TPU v7x, 128 devices: a whole 4x4x4 slice. The times are simulated.
128 devices in a mesh: ax: 4 (over y), az: 32 (over z, x, core).
Axes of the slice: x: 4, y: 4, z: 4, core: 2. Of those that a mesh axis runs over, the one named last changes fastest.
Arguments:
- noise: float32 [64, 512, 512], P('ax', 'az'), may hold values from -6 to 6
- half_width: int32 [64, 512, 512], P('ax', 'az'), may hold values from 1 to 4
- owner: int32 [32768], P(('ax', 'az')), may hold values from 0 to 127, as said below
- target_cell: int32 [32768], P(('ax', 'az')), may hold values from 0 to 511
- fields: float32 [5, 128, 512, 256], P(None, 'ax', 'az'), may hold values from -6 to 6
Outputs:
- fields_next: float32 [5, 128, 512, 256], P(None, 'ax', 'az')
Inputs may be any that keep to these rules, and one draw needn't show every extreme that they name: The owner of a device's column is the device itself, one of its two azimuthal neighbours (periodic), or one of its axial neighbours; among the 256 columns of one device no owner is named more than 128 times, and one owner is named exactly 128 times.
All inputs are finite; a program needn't handle non-finite values.
Results may differ from a plain program's by a relative error of at most 0.000067.
Values sent between devices are 32-bit elements; how exact they have to be, the bound alone decides.
No kernel may reach another device: no remote copies, remote signals or barrier semaphores. Data moves between devices by JAX's collectives and lax.ppermute only.
A program may use at most 128 MiB of HBM per device.

v0:
```python
import math

import numpy as np

import jax
import jax.numpy as jnp
from jax import lax
from jax.experimental import pallas as pl
from jax.experimental.pallas import tpu as pltpu
from jax.sharding import PartitionSpec as P

HMAX = 4
drp_coeffs = (0.770882380518, -0.166705904415, 0.02084314277)
mach_number = 0.5
time_step = 0.7
source_gain = 4.0
radial_step = 2.0
hub_ratio = 1.6

F32 = jnp.float32
BF16 = jnp.bfloat16
VM = pl.BlockSpec(memory_space=pltpu.VMEM)
PARAMS = pltpu.CompilerParams(vmem_limit_bytes=24 * 1024 * 1024)
GROUP = 8


def np_split(matrix):
    hi = matrix.astype(np.float32).astype(BF16)
    lo = (matrix - hi.astype(np.float64)).astype(np.float32).astype(BF16)
    return hi, lo


def filter_table():
    table = np.zeros((HMAX + 1, HMAX))
    for h in range(1, HMAX + 1):
        weights = [math.exp(-2.0 * k * k / (h * h)) if k <= h else 0.0 for k in range(HMAX + 1)]
        total = weights[0] + 2.0 * sum(weights[1:])
        table[:, h - 1] = [w / total for w in weights]
    return table


def radial_rows(na_total, radial):
    base = na_total / (2.0 * math.pi)
    radius = base / hub_ratio + radial_step * (np.arange(radial) + 0.5)
    return base / radius, 1.0 / radius


def radial_matrices(na_total, radial):
    diff = np.zeros((radial, radial))
    for s, a in zip((1, 2, 3), drp_coeffs):
        for j in range(radial):
            if j + s < radial:
                diff[j + s, j] += a / radial_step
            if j - s >= 0:
                diff[j - s, j] -= a / radial_step
    with_r = diff + np.diag(radial_rows(na_total, radial)[1])
    return np.stack([np.stack(np_split(with_r)), np.stack(np_split(diff))])


def azimuth_matrices(cols):
    full = np.zeros((2, GROUP * cols, GROUP * (cols + 16)))
    for which in range(2):
        place = {}
        for m in range(3):
            place[m - 3] = 1 + m + 4 * which
            place[cols + m] = 8 + m + 4 * which
        for x in range(GROUP):
            for i in range(cols):
                for s, a in zip((1, 2, 3), drp_coeffs):
                    for j, sign in ((i + s, 1.0), (i - s, -1.0)):
                        at = x * cols + j if 0 <= j < cols else GROUP * cols + x * 16 + place[j]
                        full[which, x * cols + i, at] += sign * a
    return np.stack([np.stack(np_split(full[w])) for w in range(2)])


def bin_matrix(fine, radial):
    at = (np.arange(fine) * radial) // fine
    return (source_gain * (at[:, None] == np.arange(radial)[None, :])).astype(np.float32).astype(BF16)


def split(x):
    hi = x.astype(BF16)
    return hi, (x - hi.astype(F32)).astype(BF16)


def dot(a, b):
    return lax.dot_general(a, b, (((1,), (0,)), ((), ())), preferred_element_type=F32)


def is_even(axis):
    return lax.rem(lax.axis_index(axis), 2) == 0


def swap(to_a, to_b, axis):
    devices = lax.axis_size(axis)
    pairs_a = [(i, i ^ 1) for i in range(devices)]
    pairs_b = [(i, (i - 1) % devices if i % 2 == 0 else (i + 1) % devices) for i in range(devices)]
    return lax.ppermute(to_a, axis, pairs_a), lax.ppermute(to_b, axis, pairs_b)


def call(body, outs, scratch=(), name=None, flops=0, moved=0):
    return pl.pallas_call(
        body,
        out_shape=[jax.ShapeDtypeStruct(s, d) for s, d in outs],
        out_specs=[VM] * len(outs),
        scratch_shapes=[pltpu.VMEM(s, d) for s, d in scratch],
        compiler_params=PARAMS,
        name=name,
        cost_estimate=pl.CostEstimate(flops=flops, bytes_accessed=moved, transcendentals=0),
    )


def full_specs(body, outs, args, scratch=(), name=None, moved=0):
    return pl.pallas_call(
        body,
        out_shape=[jax.ShapeDtypeStruct(s, d) for s, d in outs],
        in_specs=[VM] * len(args),
        out_specs=[VM] * len(outs),
        scratch_shapes=[pltpu.VMEM(s, d) for s, d in scratch],
        compiler_params=PARAMS,
        name=name,
        cost_estimate=pl.CostEstimate(flops=0, bytes_accessed=moved, transcendentals=0),
    )(*args)


def route_body(owner_ref, target_ref, upper_ref, pick_ref, cells_ref, own_ref):
    n_ax, n_az = lax.axis_size("ax"), lax.axis_size("az")
    ax, az = lax.axis_index("ax"), lax.axis_index("az")
    step_x = jnp.where(lax.rem(ax, 2) == 0, 1, -1)
    step_z = jnp.where(lax.rem(az, 2) == 0, 1, -1)
    me = ax * n_az + az
    b_x = ax - step_x
    ids = [
        (ax + step_x) * n_az + az,
        jnp.where((b_x >= 0) & (b_x < n_ax), b_x * n_az + az, -1),
        ax * n_az + lax.rem(az + step_z + n_az, n_az),
        ax * n_az + lax.rem(az - step_z + n_az, n_az),
    ]
    owner = owner_ref[...]
    target = target_ref[...]
    ncols = owner.shape[1]
    most = ncols // 2
    own_ref[...] = jnp.where(owner == me, target, -1)
    row = lax.broadcasted_iota(jnp.int32, (8, ncols), 0)
    marks = jnp.zeros((8, ncols), F32)
    for d, i in enumerate(ids):
        marks = jnp.where((row == d) & (owner == i), 1.0, marks)
    rank = dot(marks.astype(BF16), upper_ref[...])
    coarse = (target // 32).astype(F32)
    fine = (target % 32).astype(F32)
    digits = jnp.where(row == 0, coarse, jnp.where(row == 1, fine, 0.0)).astype(BF16)
    slot = lax.broadcasted_iota(jnp.int32, (most, ncols), 0).astype(F32)
    for d in range(4):
        wanted = jnp.where(marks[d : d + 1] > 0.0, rank[d : d + 1], -1.0)
        pick = jnp.where(slot == wanted, 1.0, 0.0).astype(BF16)
        pick_ref[d * most : (d + 1) * most, :] = pick
        found = lax.dot_general(digits, pick, (((1,), (1,)), ((), ())), preferred_element_type=F32)
        cells_ref[d, :, :] = jnp.zeros(cells_ref.shape[1:], F32)
        cells_ref[d, 0:1, 0:most] = found[0:1] * 32.0 + found[1:2]


def weights_of(h):
    table = filter_table()
    le = [h <= 1, h <= 2, h <= 3]
    out = []
    for k in range(HMAX + 1):
        value = jnp.full(h.shape, table[k, 3], F32)
        for j in (2, 1, 0):
            if j > 0 and table[k, j] == 0.0 and table[k, j - 1] == 0.0:
                value = jnp.where(le[j], 0.0, value)
                break
            value = jnp.where(le[j], table[k, j], value)
        out.append(value)
    return out


def first_body(noise_ref, half_ref, got_a_ref, got_b_ref, first_ref, to_a_ref, to_b_ref, halo):
    n_ax, ax = lax.axis_size("ax"), lax.axis_index("ax")
    even_x, even_z = is_even("ax"), is_even("az")
    rows = noise_ref.shape[0]
    halo[0] = jnp.where(ax > 0, jnp.where(even_x, got_b_ref[...], got_a_ref[...]), 0.0)
    halo[1] = jnp.where(ax < n_ax - 1, jnp.where(even_x, got_a_ref[...], got_b_ref[...]), 0.0)

    def row(x):
        if x < 0:
            return halo[0, x + HMAX]
        if x >= rows:
            return halo[1, x - rows]
        return noise_ref[x]

    for x in range(rows):
        w = weights_of(half_ref[x])
        total = w[0] * row(x)
        for k in range(1, HMAX + 1):
            total = total + w[k] * (row(x - k) + row(x + k))
        first_ref[x] = total
    half = rows // 2
    low = lax.broadcasted_iota(jnp.int32, (8, noise_ref.shape[2]), 0) < 4
    for x in range(half):
        last = jnp.where(low, pltpu.roll(first_ref[x, 8:16], 4, 0), first_ref[x + half, 8:16])
        begin = jnp.where(low, first_ref[x, 0:8], pltpu.roll(first_ref[x + half, 0:8], 4, 0))
        to_a_ref[x] = jnp.where(even_z, last, begin)
        to_b_ref[x] = jnp.where(even_z, begin, last)


def second_body(
    first_ref, half_ref, got_a_ref, got_b_ref, bins_ref, pick_ref, cells_ref,
    own_ref, to_xa, to_xb, to_za, to_zb, wide, fine_hi, fine_lo,
):
    even = is_even("az")
    rows, cols, fine = first_ref.shape
    half = rows // 2
    for x in range(half):
        got_a, got_b = got_a_ref[x], got_b_ref[x]
        before = jnp.where(even, got_b, got_a)
        after = jnp.where(even, got_a, got_b)
        wide[x, 0:8] = pltpu.roll(before, 4, 0)
        wide[x + half, 0:8] = before
        wide[x, 24:32] = after
        wide[x + half, 24:32] = pltpu.roll(after, 4, 0)
    lane = lax.broadcasted_iota(jnp.int32, (cols, fine), 1)
    for x in range(rows):
        wide[x, 8:24] = first_ref[x]
    for x in range(rows):
        w = weights_of(half_ref[x])
        total = w[0] * first_ref[x]
        for k in range(1, HMAX + 1):
            total = total + w[k] * (wide[x, 8 - k : 24 - k] + wide[x, 8 + k : 24 + k])
        result = w[0] * total
        for k in range(1, HMAX + 1):
            up = jnp.where(lane < fine - k, pltpu.roll(total, fine - k, 1), 0.0)
            down = jnp.where(lane >= k, pltpu.roll(total, k, 1), 0.0)
            result = result + w[k] * (up + down)
        hi, lo = split(result)
        fine_hi[x * cols : (x + 1) * cols] = hi
        fine_lo[x * cols : (x + 1) * cols] = lo
    bins = bins_ref[...]
    binned = dot(fine_hi[...], bins) + dot(fine_lo[...], bins)
    own_ref[...] = binned
    hi, lo = split(binned)
    most = pick_ref.shape[0] // 4
    for d, out in enumerate((to_xa, to_xb, to_za, to_zb)):
        pick = pick_ref[d * most : (d + 1) * most]
        out[0:most] = dot(pick, hi) + dot(pick, lo)
        out[most : most + 8] = cells_ref[d]


def gather_body(binned_ref, own_ref, xa, xb, za, zb, q_ref):
    cells, radial = q_ref.shape
    most = xa.shape[0] - 8

    def onehot(row):
        at = lax.broadcasted_iota(jnp.int32, (cells, row.shape[1]), 0)
        return jnp.where(at == row, 1.0, 0.0).astype(BF16)

    mats = [onehot(own_ref[...])]
    rows = [binned_ref[...]]
    for got in (xa, xb, za, zb):
        mats.append(onehot(got[most : most + 1, 0:most].astype(jnp.int32)))
        rows.append(got[0:most])
    mat = jnp.concatenate(mats, axis=1)
    hi, lo = split(jnp.concatenate(rows, axis=0))
    q_ref[...] = dot(mat, hi) + dot(mat, lo)


def write_sends(state, to_xa, to_xb, to_za, to_zb):
    even_x, even_z = is_even("ax"), is_even("az")
    rows = state.shape[1]
    for f in range(state.shape[0]):
        first, last = state[f, 0:3], state[f, rows - 3 : rows]
        to_xa[f] = jnp.where(even_x, last, first)
        to_xb[f] = jnp.where(even_x, first, last)
    low = lax.broadcasted_iota(jnp.int32, (8, state.shape[3]), 0) < 4
    for x in range(rows):
        last = jnp.where(low, pltpu.roll(state[2, x, 8:16], 4, 0), state[4, x, 8:16])
        first = jnp.where(low, state[2, x, 0:8], pltpu.roll(state[4, x, 0:8], 4, 0))
        to_za[x] = jnp.where(even_z, last, first)
        to_zb[x] = jnp.where(even_z, first, last)


def send_shapes(rows, cols, radial):
    ax, az = ((5, 3, cols, radial), F32), ((rows, 8, radial), F32)
    return [ax, ax, az, az]


def edges_body(state, to_xa, to_xb, to_za, to_zb):
    write_sends(state, to_xa, to_xb, to_za, to_zb)


def apply_operator(state, xa, xb, za, zb, tmat, rmat, inv_h_ref, halo, side, finish):
    n_ax, ax = lax.axis_size("ax"), lax.axis_index("ax")
    even_x, even_z = is_even("ax"), is_even("az")
    _, rows, cols, radial = state.shape
    for f in range(5):
        halo[0, f] = jnp.where(ax > 0, jnp.where(even_x, xb[f], xa[f]), 0.0)
        halo[1, f] = jnp.where(ax < n_ax - 1, jnp.where(even_x, xa[f], xb[f]), 0.0)
    side[:, 0:8] = jnp.where(even_z, zb[...], za[...])
    side[:, 8:16] = jnp.where(even_z, za[...], zb[...])
    inv_h = inv_h_ref[...]

    def row(f, x):
        if x < 0:
            return halo[0, f, x + 3]
        if x >= rows:
            return halo[1, f, x - rows]
        return state[f, x]

    def dx(f, x):
        total = drp_coeffs[0] * (row(f, x + 1) - row(f, x - 1))
        for s in (2, 3):
            total = total + drp_coeffs[s - 1] * (row(f, x + s) - row(f, x - s))
        return total

    size = GROUP * cols
    for g in range(rows // GROUP):
        at = slice(g * GROUP, (g + 1) * GROUP)
        halo_hi, halo_lo = split(side[at].reshape(GROUP * 16, radial))
        p_hi, p_lo = split(state[4, at].reshape(size, radial))
        ut_hi, ut_lo = split(state[2, at].reshape(size, radial))
        ur_hi, ur_lo = split(state[3, at].reshape(size, radial))

        def across(which, hi, lo):
            hi = jnp.concatenate([hi, halo_hi], axis=0)
            lo = jnp.concatenate([lo, halo_lo], axis=0)
            return dot(tmat[which, 0], hi) + dot(tmat[which, 0], lo) + dot(tmat[which, 1], hi)

        def outward(which, hi, lo):
            return dot(hi, rmat[which, 0]) + dot(lo, rmat[which, 0]) + dot(hi, rmat[which, 1])

        div_tr = across(0, ut_hi, ut_lo) * inv_h + outward(0, ur_hi, ur_lo)
        p_t = across(1, p_hi, p_lo) * inv_h
        p_r = outward(1, p_hi, p_lo)
        for i in range(GROUP):
            x = g * GROUP + i
            part = slice(i * cols, (i + 1) * cols)
            d = [dx(f, x) for f in range(5)]
            div = d[1] + div_tr[part]
            finish(
                x,
                [
                    -mach_number * d[0] - div,
                    -mach_number * d[1] - d[4],
                    -mach_number * d[2] - p_t[part],
                    -mach_number * d[3] - p_r[part],
                    -mach_number * d[4] - div,
                ],
            )


def start_body(state, xa, xb, za, zb, tmat, rmat, inv_h, out, halo, side):
    def finish(x, tend):
        for f in range(5):
            out[f, x] = tend[f]

    apply_operator(state, xa, xb, za, zb, tmat, rmat, inv_h, halo, side, finish)


def stage_body(factor, state, xa, xb, za, zb, tmat, rmat, inv_h, base, out, to_xa, to_xb, to_za, to_zb, halo, side):
    def finish(x, tend):
        for f in range(5):
            out[f, x] = base[f, x] + factor * tend[f]

    apply_operator(state, xa, xb, za, zb, tmat, rmat, inv_h, halo, side, finish)
    write_sends(out, to_xa, to_xb, to_za, to_zb)


def last_body(state, xa, xb, za, zb, tmat, rmat, inv_h, k, fields, out, halo, side):
    def finish(x, tend):
        for f in range(5):
            out[f, x] = fields[f, x] + time_step * k[f, x] + (0.5 * time_step * time_step) * tend[f]

    apply_operator(state, xa, xb, za, zb, tmat, rmat, inv_h, halo, side, finish)


def local(noise, half_width, owner, target_cell, fields):
    px, pa, fine = noise.shape
    cx, ca, radial = fields.shape[1:]
    ncols = px * pa
    most = ncols // 2
    n_az = lax.axis_size("az")
    even_x = is_even("ax")

    first, last = noise[:HMAX], noise[px - HMAX :]
    noise_a, noise_b = swap(jnp.where(even_x, last, first), jnp.where(even_x, first, last), "ax")
    sends = send_shapes(cx, ca, radial)
    xa, xb, za, zb = full_specs(edges_body, sends, [fields], name="edges")
    uza, uzb = swap(za, zb, "az")
    uxa, uxb = swap(xa, xb, "ax")

    upper = jnp.asarray(np.triu(np.ones((ncols, ncols), np.float32), 1).astype(BF16))
    pick, cells, own = full_specs(
        route_body,
        [((4 * most, ncols), BF16), ((4, 8, radial), F32), ((1, ncols), jnp.int32)],
        [owner.reshape(1, ncols), target_cell.reshape(1, ncols), upper],
        name="route",
    )
    filtered, to_a, to_b = full_specs(
        first_body,
        [((px, pa, fine), F32), ((px // 2, 8, fine), F32), ((px // 2, 8, fine), F32)],
        [noise, half_width, noise_a, noise_b],
        [((2, HMAX, pa, fine), F32)],
        name="filter_axial",
    )
    got_a, got_b = swap(to_a, to_b, "az")

    tmat = jnp.asarray(azimuth_matrices(ca))
    rmat = jnp.asarray(radial_matrices(float(ca * n_az), radial))
    inv_h = jnp.asarray(radial_rows(float(ca * n_az), radial)[0].astype(np.float32)[None, :])
    state = ((5, cx, ca, radial), F32)
    spare = [((2, 5, 3, ca, radial), F32), ((cx, 16, radial), F32)]
    (k,) = full_specs(start_body, [state], [fields, uxa, uxb, uza, uzb, tmat, rmat, inv_h], spare, name="operator")

    bins = jnp.asarray(bin_matrix(fine, radial))
    packet = ((most + 8, radial), F32)
    binned, xa, xb, za, zb = full_specs(
        second_body,
        [((ncols, radial), F32), packet, packet, packet, packet],
        [filtered, half_width, got_a, got_b, bins, pick, cells],
        [((px, 32, fine), F32), ((ncols, fine), BF16), ((ncols, fine), BF16)],
        name="filter_rest",
    )
    xa, xb = swap(xa, xb, "ax")
    za, zb = swap(za, zb, "az")
    (q,) = full_specs(gather_body, [((cx * ca, radial), F32)], [binned, own, xa, xb, za, zb], name="gather")

    k = k.at[4].add(q.reshape(cx, ca, radial))
    xa, xb, za, zb = full_specs(edges_body, sends, [k], name="edges_k")
    level = k
    for factor in (time_step / 4.0, time_step / 3.0):
        za, zb = swap(za, zb, "az")
        xa, xb = swap(xa, xb, "ax")

        def body(*refs, factor=factor):
            stage_body(factor, *refs)

        level, xa, xb, za, zb = full_specs(
            body, [state] + sends, [level, xa, xb, za, zb, tmat, rmat, inv_h, k], spare, name="stage"
        )
    za, zb = swap(za, zb, "az")
    xa, xb = swap(xa, xb, "ax")
    (out,) = full_specs(
        last_body, [state], [level, xa, xb, za, zb, tmat, rmat, inv_h, k, fields], spare, name="final"
    )
    return out


def solution(mesh):
    return jax.shard_map(
        local,
        mesh=mesh,
        in_specs=(
            P("ax", "az", None),
            P("ax", "az", None),
            P(("ax", "az")),
            P(("ax", "az")),
            P(None, "ax", "az", None),
        ),
        out_specs=P(None, "ax", "az", None),
        check_vma=False,
    )
```

profile of v0, /device:TPU:0, one launch (start us, length us, event | category | flops | bytes accessed | tf_op | source)
XLA Modules:
  0.0 76.9 jit_solution(15395775504758777040)
XLA Ops:
  0.0 1.0 %slice_select_fusion = (f32[4,16,512]{2,1,0:T(8,128)S(1)}, f32[4,16,512]{2,1,0:T(8,128)S(1)}) fusion(f32[16,16,512]{2,1,0:T(8,128)} %noise_ref.1, pred[]{:T(512)S(6)} %eq.3), kind=kLoop, calls=%fused_computation.2 | loop fusion | flops 65536 | bytes 524289 | tf_op jit(solution)/shard_map/jit(_where)/select_n | solution.py:384
  1.1 3.2 %collective-permute-start.5 = (f32[4,16,512]{2,1,0:T(8,128)S(1)}, f32[4,16,512]{2,1,0:T(8,128)S(1)}, u32[]{:S(2)}, u32[]{:S(2)}) collective-permute-start(f32[4,16,512]{2,1,0:T(8,128)S(1)} %get-tuple-element.75), channel_id=1, source_target_pairs={{0,96},{32,64},{64,32},{96,0},{1,97},{33,65},{65,33},{97,1},{2,98}... | collective-permute-start | bytes 393224 | tf_op jit(solution)/shard_map/ppermute | solution.py:98
  4.2 0.1 collective-permute-start.4
  4.4 1.7 %copy-done = f32[5,32,16,256]{3,2,1,0:T(8,128)S(1)} copy-done((f32[5,32,16,256]{3,2,1,0:T(8,128)S(1)}, f32[5,32,16,256]{3,2,1,0:T(8,128)}, u32[]{:S(2)}) %copy-start) | copy-done | bytes 2621464
  6.1 0.1 edges.1
  6.2 0.1 collective-permute-start.2
  6.3 1.4 %collective-permute-done.5.got_b_ref = f32[4,16,512]{2,1,0:T(8,128)S(1)} collective-permute-done((f32[4,16,512]{2,1,0:T(8,128)S(1)}, f32[4,16,512]{2,1,0:T(8,128)S(1)}, u32[]{:S(2)}, u32[]{:S(2)}) %collective-permute-start.5) | collective-permute-done | bytes 131104 | tf_op jit(solution)/shard_map/ppermute | solution.py:98
  7.7 1.5 %collective-permute-done.4.got_a_ref = f32[4,16,512]{2,1,0:T(8,128)S(1)} collective-permute-done((f32[4,16,512]{2,1,0:T(8,128)S(1)}, f32[4,16,512]{2,1,0:T(8,128)S(1)}, u32[]{:S(2)}, u32[]{:S(2)}) %collective-permute-start.4) | collective-permute-done | bytes 131104 | tf_op jit(solution)/shard_map/ppermute | solution.py:98
  9.2 1.0 %copy-done.5 = f32[16,16,512]{2,1,0:T(8,128)S(1)} copy-done((f32[16,16,512]{2,1,0:T(8,128)S(1)}, f32[16,16,512]{2,1,0:T(8,128)}, u32[]{:S(2)}) %copy-start.5) | copy-done | bytes 524312
  10.3 0.6 filter_axial.1
  10.9 0.1 collective-permute-start.6
  11.0 0.4 collective-permute-start
  11.4 1.3 %collective-permute-start.1 = (f32[5,3,16,256]{3,2,1,0:T(8,128)S(1)}, f32[5,3,16,256]{3,2,1,0:T(8,128)S(1)}, u32[]{:S(2)}, u32[]{:S(2)}) collective-permute-start(f32[5,3,16,256]{3,2,1,0:T(8,128)S(1)} %get-tuple-element.47), channel_id=1, source_target_pairs={{0,96},{32,64},{64,32},{96,0},{1,97},{33,65},{65,33},{97,1},{2,98}... | collective-permute-start | bytes 737288 | tf_op jit(solution)/shard_map/ppermute | solution.py:98
  12.7 5.9 %collective-permute-start.7 = (f32[8,8,512]{2,1,0:T(8,128)S(1)}, f32[8,8,512]{2,1,0:T(8,128)S(1)}, u32[]{:S(2)}, u32[]{:S(2)}) collective-permute-start(f32[8,8,512]{2,1,0:T(8,128)S(1)} %get-tuple-element.52), channel_id=1, source_target_pairs={{0,31},{1,2},{2,1},{3,4},{4,3},{5,6},{6,5},{7,8},{8,7},{9,10},{10,... | collective-permute-start | bytes 393224 | tf_op jit(solution)/shard_map/ppermute | solution.py:98
  18.5 0.0 collective-permute-done.6.got_a_ref
  18.5 0.0 collective-permute-start.3
  18.6 0.9 %copy-done.7 = bf16[256,256]{1,0:T(8,128)(2,1)S(1)} copy-done((bf16[256,256]{1,0:T(8,128)(2,1)S(1)}, bf16[256,256]{1,0:T(8,128)(2,1)}, u32[]{:S(2)}) %copy-start.7) | copy-done | bytes 131096
  19.5 0.3 route.1
  19.8 1.4 %collective-permute-done.7.got_b_ref = f32[8,8,512]{2,1,0:T(8,128)S(1)} collective-permute-done((f32[8,8,512]{2,1,0:T(8,128)S(1)}, f32[8,8,512]{2,1,0:T(8,128)S(1)}, u32[]{:S(2)}, u32[]{:S(2)}) %collective-permute-start.7) | collective-permute-done | bytes 131104 | tf_op jit(solution)/shard_map/ppermute | solution.py:98
  21.2 0.9 %copy-done.6 = bf16[512,256]{1,0:T(8,128)(2,1)S(1)} copy-done((bf16[512,256]{1,0:T(8,128)(2,1)S(1)}, bf16[512,256]{1,0:T(8,128)(2,1)}, u32[]{:S(2)}) %copy-start.6) | copy-done | bytes 262168
  22.1 2.2 %filter_rest.1 = (f32[256,256]{1,0:T(8,128)S(1)}, f32[136,256]{1,0:T(8,128)S(1)}, f32[136,256]{1,0:T(8,128)S(1)}, f32[136,256]{1,0:T(8,128)S(1)}, f32[136,256]{1,0:T(8,128)S(1)}) custom-call(f32[16,16,512]{2,1,0:T(8,128)S(1)} %get-tuple-element.50.first_ref, s32[16,16,512]{2,1,0:T(8,128)S(1)} %copy-done.4, ...), custom_call_target="tpu_custom_call" | custom-call | tf_op jit(solution)/shard_map/filter_rest/pallas_call | solution.py:114
  24.3 1.2 %collective-permute-start.8 = (f32[136,256]{1,0:T(8,128)S(1)}, f32[136,256]{1,0:T(8,128)S(1)}, u32[]{:S(2)}, u32[]{:S(2)}) collective-permute-start(f32[136,256]{1,0:T(8,128)S(1)} %get-tuple-element.57), channel_id=1, source_target_pairs={{0,32},{32,0},{64,96},{96,64},{1,33},{33,1},{65,97},{97,65},{2,34}... | collective-permute-start | bytes 417800 | tf_op jit(solution)/shard_map/ppermute | solution.py:98
  25.6 0.0 collective-permute-done.xa
  25.6 1.8 %collective-permute-start.9 = (f32[136,256]{1,0:T(8,128)S(1)}, f32[136,256]{1,0:T(8,128)S(1)}, u32[]{:S(2)}, u32[]{:S(2)}) collective-permute-start(f32[136,256]{1,0:T(8,128)S(1)} %get-tuple-element.58), channel_id=1, source_target_pairs={{0,96},{32,64},{64,32},{96,0},{1,97},{33,65},{65,33},{97,1},{2,98}... | collective-permute-start | bytes 417800 | tf_op jit(solution)/shard_map/ppermute | solution.py:98
  27.3 0.0 collective-permute-done.1.xb
  27.3 0.0 collective-permute-start.10
  27.3 0.0 collective-permute-done.2.za
  27.3 4.6 %collective-permute-start.11 = (f32[136,256]{1,0:T(8,128)S(1)}, f32[136,256]{1,0:T(8,128)S(1)}, u32[]{:S(2)}, u32[]{:S(2)}) collective-permute-start(f32[136,256]{1,0:T(8,128)S(1)} %get-tuple-element.60), channel_id=1, source_target_pairs={{0,31},{1,2},{2,1},{3,4},{4,3},{5,6},{6,5},{7,8},{8,7},{9,10},{10,... | collective-permute-start | bytes 417800 | tf_op jit(solution)/shard_map/ppermute | solution.py:98
  31.9 0.0 collective-permute-done.3.zb
  32.0 1.8 %operator.1 = f32[5,32,16,256]{3,2,1,0:T(8,128)S(1)} custom-call(f32[5,32,16,256]{3,2,1,0:T(8,128)S(1)} %copy-done.1, f32[5,3,16,256]{3,2,1,0:T(8,128)S(1)} %collective-permute-done.xa, f32[5,3,16,256]{3,2,1,0:T(8,128)S(1)} %collective-permute-done.1.xb, f32[32,8,256]{2,1,0:T(8,128)S(1)} %collective-permute-done.2.za, ...), custom_call_target="tpu_custom_call" | custom-call | tf_op jit(solution)/shard_map/operator/pallas_call | solution.py:114
  33.8 0.0 collective-permute-done.8.xa
  33.8 0.0 collective-permute-done.9.xb
  33.8 0.0 collective-permute-done.10.za
  33.8 1.4 %collective-permute-done.11.zb = f32[136,256]{1,0:T(8,128)S(1)} collective-permute-done((f32[136,256]{1,0:T(8,128)S(1)}, f32[136,256]{1,0:T(8,128)S(1)}, u32[]{:S(2)}, u32[]{:S(2)}) %collective-permute-start.11) | collective-permute-done | bytes 139296 | tf_op jit(solution)/shard_map/ppermute | solution.py:98
  35.2 0.6 gather.1
  35.8 0.1 fusion.state.refs_0_.refs_8_.k
  36.0 0.1 edges_k.1
  36.1 0.1 collective-permute-start.14
  36.2 4.6 %collective-permute-start.15 = (f32[32,8,256]{2,1,0:T(8,128)S(1)}, f32[32,8,256]{2,1,0:T(8,128)S(1)}, u32[]{:S(2)}, u32[]{:S(2)}) collective-permute-start(f32[32,8,256]{2,1,0:T(8,128)S(1)} %get-tuple-element.64), channel_id=1, source_target_pairs={{0,31},{1,2},{2,1},{3,4},{4,3},{5,6},{6,5},{7,8},{8,7},{9,10},{10,... | collective-permute-start | bytes 786440 | tf_op jit(solution)/shard_map/ppermute | solution.py:98
  40.7 0.3 collective-permute-start.12
  41.0 1.5 %collective-permute-start.13 = (f32[5,3,16,256]{3,2,1,0:T(8,128)S(1)}, f32[5,3,16,256]{3,2,1,0:T(8,128)S(1)}, u32[]{:S(2)}, u32[]{:S(2)}) collective-permute-start(f32[5,3,16,256]{3,2,1,0:T(8,128)S(1)} %get-tuple-element.62), channel_id=1, source_target_pairs={{0,96},{32,64},{64,32},{96,0},{1,97},{33,65},{65,33},{97,1},{2,98}... | collective-permute-start | bytes 737288 | tf_op jit(solution)/shard_map/ppermute | solution.py:98
  42.5 4.4 %collective-permute-done.12.refs_1_ = f32[5,3,16,256]{3,2,1,0:T(8,128)S(1)} collective-permute-done((f32[5,3,16,256]{3,2,1,0:T(8,128)S(1)}, f32[5,3,16,256]{3,2,1,0:T(8,128)S(1)}, u32[]{:S(2)}, u32[]{:S(2)}) %collective-permute-start.12) | collective-permute-done | bytes 245792 | tf_op jit(solution)/shard_map/ppermute | solution.py:98
  46.9 1.5 %collective-permute-done.13.refs_2_ = f32[5,3,16,256]{3,2,1,0:T(8,128)S(1)} collective-permute-done((f32[5,3,16,256]{3,2,1,0:T(8,128)S(1)}, f32[5,3,16,256]{3,2,1,0:T(8,128)S(1)}, u32[]{:S(2)}, u32[]{:S(2)}) %collective-permute-start.13) | collective-permute-done | bytes 245792 | tf_op jit(solution)/shard_map/ppermute | solution.py:98
  48.4 0.0 collective-permute-done.14.refs_3_
  48.4 0.0 collective-permute-done.15.refs_4_
  48.4 2.1 %stage.2 = (f32[5,32,16,256]{3,2,1,0:T(8,128)S(1)}, f32[5,3,16,256]{3,2,1,0:T(8,128)S(1)}, f32[5,3,16,256]{3,2,1,0:T(8,128)S(1)}, f32[32,8,256]{2,1,0:T(8,128)S(1)}, f32[32,8,256]{2,1,0:T(8,128)S(1)}) custom-call(f32[5,32,16,256]{3,2,1,0:T(8,128)S(1)} %fusion.state.refs_0_.refs_8_.k, f32[5,3,16,256]{3,2,1,0:T(8,128)S(1)} %collective-permute-done.12.refs_1_, ...), custom_call_target="tpu_custom_call" | custom-call | tf_op jit(solution)/shard_map/stage/pallas_call | solution.py:114
  50.5 0.1 collective-permute-start.18
  50.6 2.5 %collective-permute-start.19 = (f32[32,8,256]{2,1,0:T(8,128)S(1)}, f32[32,8,256]{2,1,0:T(8,128)S(1)}, u32[]{:S(2)}, u32[]{:S(2)}) collective-permute-start(f32[32,8,256]{2,1,0:T(8,128)S(1)} %get-tuple-element.69), channel_id=1, source_target_pairs={{0,31},{1,2},{2,1},{3,4},{4,3},{5,6},{6,5},{7,8},{8,7},{9,10},{10,... | collective-permute-start | bytes 786440 | tf_op jit(solution)/shard_map/ppermute | solution.py:98
  53.0 0.5 collective-permute-start.16
  53.6 1.5 %collective-permute-start.17 = (f32[5,3,16,256]{3,2,1,0:T(8,128)S(1)}, f32[5,3,16,256]{3,2,1,0:T(8,128)S(1)}, u32[]{:S(2)}, u32[]{:S(2)}) collective-permute-start(f32[5,3,16,256]{3,2,1,0:T(8,128)S(1)} %get-tuple-element.67), channel_id=1, source_target_pairs={{0,96},{32,64},{64,32},{96,0},{1,97},{33,65},{65,33},{97,1},{2,98}... | collective-permute-start | bytes 737288 | tf_op jit(solution)/shard_map/ppermute | solution.py:98
  55.1 4.2 %collective-permute-done.16.refs_1_ = f32[5,3,16,256]{3,2,1,0:T(8,128)S(1)} collective-permute-done((f32[5,3,16,256]{3,2,1,0:T(8,128)S(1)}, f32[5,3,16,256]{3,2,1,0:T(8,128)S(1)}, u32[]{:S(2)}, u32[]{:S(2)}) %collective-permute-start.16) | collective-permute-done | bytes 245792 | tf_op jit(solution)/shard_map/ppermute | solution.py:98
  59.2 1.7 %collective-permute-done.17.refs_2_ = f32[5,3,16,256]{3,2,1,0:T(8,128)S(1)} collective-permute-done((f32[5,3,16,256]{3,2,1,0:T(8,128)S(1)}, f32[5,3,16,256]{3,2,1,0:T(8,128)S(1)}, u32[]{:S(2)}, u32[]{:S(2)}) %collective-permute-start.17) | collective-permute-done | bytes 245792 | tf_op jit(solution)/shard_map/ppermute | solution.py:98
  61.0 0.0 collective-permute-done.18.refs_3_
  61.0 0.0 collective-permute-done.19.refs_4_
  61.0 2.1 %stage.3 = (f32[5,32,16,256]{3,2,1,0:T(8,128)S(1)}, f32[5,3,16,256]{3,2,1,0:T(8,128)S(1)}, f32[5,3,16,256]{3,2,1,0:T(8,128)S(1)}, f32[32,8,256]{2,1,0:T(8,128)S(1)}, f32[32,8,256]{2,1,0:T(8,128)S(1)}) custom-call(f32[5,32,16,256]{3,2,1,0:T(8,128)S(1)} %get-tuple-element.65.refs_0_, f32[5,3,16,256]{3,2,1,0:T(8,128)S(1)} %collective-permute-done.16.refs_1_, ...), custom_call_target="tpu_custom_call" | custom-call | tf_op jit(solution)/shard_map/stage/pallas_call | solution.py:114
  63.1 0.1 collective-permute-start.22
  63.2 2.4 %collective-permute-start.23 = (f32[32,8,256]{2,1,0:T(8,128)S(1)}, f32[32,8,256]{2,1,0:T(8,128)S(1)}, u32[]{:S(2)}, u32[]{:S(2)}) collective-permute-start(f32[32,8,256]{2,1,0:T(8,128)S(1)} %get-tuple-element.74), channel_id=1, source_target_pairs={{0,31},{1,2},{2,1},{3,4},{4,3},{5,6},{6,5},{7,8},{8,7},{9,10},{10,... | collective-permute-start | bytes 786440 | tf_op jit(solution)/shard_map/ppermute | solution.py:98
  65.5 0.3 collective-permute-start.20
  65.8 1.5 %collective-permute-start.21 = (f32[5,3,16,256]{3,2,1,0:T(8,128)S(1)}, f32[5,3,16,256]{3,2,1,0:T(8,128)S(1)}, u32[]{:S(2)}, u32[]{:S(2)}) collective-permute-start(f32[5,3,16,256]{3,2,1,0:T(8,128)S(1)} %get-tuple-element.72), channel_id=1, source_target_pairs={{0,96},{32,64},{64,32},{96,0},{1,97},{33,65},{65,33},{97,1},{2,98}... | collective-permute-start | bytes 737288 | tf_op jit(solution)/shard_map/ppermute | solution.py:98
  67.3 4.4 %collective-permute-done.20.xa = f32[5,3,16,256]{3,2,1,0:T(8,128)S(1)} collective-permute-done((f32[5,3,16,256]{3,2,1,0:T(8,128)S(1)}, f32[5,3,16,256]{3,2,1,0:T(8,128)S(1)}, u32[]{:S(2)}, u32[]{:S(2)}) %collective-permute-start.20) | collective-permute-done | bytes 245792 | tf_op jit(solution)/shard_map/ppermute | solution.py:98
  71.7 1.5 %collective-permute-done.21.xb = f32[5,3,16,256]{3,2,1,0:T(8,128)S(1)} collective-permute-done((f32[5,3,16,256]{3,2,1,0:T(8,128)S(1)}, f32[5,3,16,256]{3,2,1,0:T(8,128)S(1)}, u32[]{:S(2)}, u32[]{:S(2)}) %collective-permute-start.21) | collective-permute-done | bytes 245792 | tf_op jit(solution)/shard_map/ppermute | solution.py:98
  73.2 0.0 collective-permute-done.22.za
  73.2 0.0 collective-permute-done.23.zb
  73.2 3.7 %final.1 = f32[5,32,16,256]{3,2,1,0:T(8,128)} custom-call(f32[5,32,16,256]{3,2,1,0:T(8,128)S(1)} %get-tuple-element.70.state, f32[5,3,16,256]{3,2,1,0:T(8,128)S(1)} %collective-permute-done.20.xa, f32[5,3,16,256]{3,2,1,0:T(8,128)S(1)} %collective-permute-done.21.xb, f32[32,8,256]{2,1,0:T(8,128)S(1)} %collective-permute-done.22.za, ...), custom_call_target="tpu_custom_call" | custom-call | tf_op jit(solution)/shard_map/final/pallas_call | solution.py:114
  (18 shorter events, 0.0 us)
Async XLA Ops:
  0.0 9.2 %copy-start.4 = (s32[16,16,512]{2,1,0:T(8,128)S(1)}, s32[16,16,512]{2,1,0:T(8,128)}, u32[]{:S(2)}) copy-start(s32[16,16,512]{2,1,0:T(8,128)} %half_ref.3) | copy-start | bytes 1572868
  0.0 18.6 %copy-start.10 = (s32[256]{0:T(256)S(1)}, s32[256]{0:T(256)}, u32[]{:S(2)}) copy-start(s32[256]{0:T(256)} %param.15) | copy-start | bytes 3076
  0.0 18.6 %copy-start.9 = (s32[256]{0:T(256)S(1)}, s32[256]{0:T(256)}, u32[]{:S(2)}) copy-start(s32[256]{0:T(256)} %param.14) | copy-start | bytes 3076
  1.1 6.7 %collective-permute-start.5 = (f32[4,16,512]{2,1,0:T(8,128)S(1)}, f32[4,16,512]{2,1,0:T(8,128)S(1)}, u32[]{:S(2)}, u32[]{:S(2)}) collective-permute-start(f32[4,16,512]{2,1,0:T(8,128)S(1)} %get-tuple-element.75), channel_id=1, source_target_pairs={{0,96},{32,64},{64,32},{96,0},{1,97},{33,65},{65,33},{97,1},{2,98}... | collective-permute-start | bytes 393224 | tf_op jit(solution)/shard_map/ppermute | solution.py:98
  4.2 27.7 %copy-start.8 = (f32[1,256]{1,0:T(1,128)S(1)}, f32[1,256]{1,0:T(1,128)}, u32[]{:S(2)}) copy-start(f32[1,256]{1,0:T(1,128)} %constant.53.clone.inv_h.refs_7_) | copy-start | bytes 3076
  4.2 5.0 %collective-permute-start.4 = (f32[4,16,512]{2,1,0:T(8,128)S(1)}, f32[4,16,512]{2,1,0:T(8,128)S(1)}, u32[]{:S(2)}, u32[]{:S(2)}) collective-permute-start(f32[4,16,512]{2,1,0:T(8,128)S(1)} %get-tuple-element.76), channel_id=1, source_target_pairs={{0,32},{32,0},{64,96},{96,64},{1,33},{33,1},{65,97},{97,65},{2,34}... | collective-permute-start | bytes 393224 | tf_op jit(solution)/shard_map/ppermute | solution.py:98
  4.4 1.7 %copy-start = (f32[5,32,16,256]{3,2,1,0:T(8,128)S(1)}, f32[5,32,16,256]{3,2,1,0:T(8,128)}, u32[]{:S(2)}) copy-start(f32[5,32,16,256]{3,2,1,0:T(8,128)} %fields.1) | copy-start | bytes 7864324
  6.1 25.8 %copy-start.1 = (f32[5,32,16,256]{3,2,1,0:T(8,128)S(1)}, f32[5,32,16,256]{3,2,1,0:T(8,128)}, u32[]{:S(2)}) copy-start(f32[5,32,16,256]{3,2,1,0:T(8,128)} %fields.1) | copy-start | bytes 7864324
  6.1 25.8 %copy-start.2 = (bf16[2,2,256,256]{3,2,1,0:T(8,128)(2,1)S(1)}, bf16[2,2,256,256]{3,2,1,0:T(8,128)(2,1)}, u32[]{:S(2)}) copy-start(bf16[2,2,256,256]{3,2,1,0:T(8,128)(2,1)} %constant.52.clone.rmat.refs_6_) | copy-start | bytes 1572868
  6.1 25.8 %copy-start.3 = (bf16[2,2,128,256]{3,2,1,0:T(8,128)(2,1)S(1)}, bf16[2,2,128,256]{3,2,1,0:T(8,128)(2,1)}, u32[]{:S(2)}) copy-start(bf16[2,2,128,256]{3,2,1,0:T(8,128)(2,1)} %constant.51.clone.tmat.refs_5_) | copy-start | bytes 786436
  6.2 21.1 %collective-permute-start.2 = (f32[32,8,256]{2,1,0:T(8,128)S(1)}, f32[32,8,256]{2,1,0:T(8,128)S(1)}, u32[]{:S(2)}, u32[]{:S(2)}) collective-permute-start(f32[32,8,256]{2,1,0:T(8,128)S(1)} %get-tuple-element.48), channel_id=1, source_target_pairs={{0,1},{1,0},{2,3},{3,2},{4,5},{5,4},{6,7},{7,6},{8,9},{9,8},{10,11... | collective-permute-start | bytes 786440 | tf_op jit(solution)/shard_map/ppermute | solution.py:98
  9.2 1.0 %copy-start.5 = (f32[16,16,512]{2,1,0:T(8,128)S(1)}, f32[16,16,512]{2,1,0:T(8,128)}, u32[]{:S(2)}) copy-start(f32[16,16,512]{2,1,0:T(8,128)} %noise_ref.1) | copy-start | bytes 1572868
  10.9 7.6 %collective-permute-start.6 = (f32[8,8,512]{2,1,0:T(8,128)S(1)}, f32[8,8,512]{2,1,0:T(8,128)S(1)}, u32[]{:S(2)}, u32[]{:S(2)}) collective-permute-start(f32[8,8,512]{2,1,0:T(8,128)S(1)} %get-tuple-element.51), channel_id=1, source_target_pairs={{0,1},{1,0},{2,3},{3,2},{4,5},{5,4},{6,7},{7,6},{8,9},{9,8},{10,11... | collective-permute-start | bytes 393224 | tf_op jit(solution)/shard_map/ppermute | solution.py:98
  11.0 14.6 %collective-permute-start = (f32[5,3,16,256]{3,2,1,0:T(8,128)S(1)}, f32[5,3,16,256]{3,2,1,0:T(8,128)S(1)}, u32[]{:S(2)}, u32[]{:S(2)}) collective-permute-start(f32[5,3,16,256]{3,2,1,0:T(8,128)S(1)} %get-tuple-element.46), channel_id=1, source_target_pairs={{0,32},{32,0},{64,96},{96,64},{1,33},{33,1},{65,97},{97,65},{2,34}... | collective-permute-start | bytes 737288 | tf_op jit(solution)/shard_map/ppermute | solution.py:98
  11.4 16.0 %collective-permute-start.1 = (f32[5,3,16,256]{3,2,1,0:T(8,128)S(1)}, f32[5,3,16,256]{3,2,1,0:T(8,128)S(1)}, u32[]{:S(2)}, u32[]{:S(2)}) collective-permute-start(f32[5,3,16,256]{3,2,1,0:T(8,128)S(1)} %get-tuple-element.47), channel_id=1, source_target_pairs={{0,96},{32,64},{64,32},{96,0},{1,97},{33,65},{65,33},{97,1},{2,98}... | collective-permute-start | bytes 737288 | tf_op jit(solution)/shard_map/ppermute | solution.py:98
  12.7 8.5 %collective-permute-start.7 = (f32[8,8,512]{2,1,0:T(8,128)S(1)}, f32[8,8,512]{2,1,0:T(8,128)S(1)}, u32[]{:S(2)}, u32[]{:S(2)}) collective-permute-start(f32[8,8,512]{2,1,0:T(8,128)S(1)} %get-tuple-element.52), channel_id=1, source_target_pairs={{0,31},{1,2},{2,1},{3,4},{4,3},{5,6},{6,5},{7,8},{8,7},{9,10},{10,... | collective-permute-start | bytes 393224 | tf_op jit(solution)/shard_map/ppermute | solution.py:98
  18.5 13.4 %collective-permute-start.3 = (f32[32,8,256]{2,1,0:T(8,128)S(1)}, f32[32,8,256]{2,1,0:T(8,128)S(1)}, u32[]{:S(2)}, u32[]{:S(2)}) collective-permute-start(f32[32,8,256]{2,1,0:T(8,128)S(1)} %get-tuple-element.49), channel_id=1, source_target_pairs={{0,31},{1,2},{2,1},{3,4},{4,3},{5,6},{6,5},{7,8},{8,7},{9,10},{10,... | collective-permute-start | bytes 786440 | tf_op jit(solution)/shard_map/ppermute | solution.py:98
  18.6 0.9 %copy-start.7 = (bf16[256,256]{1,0:T(8,128)(2,1)S(1)}, bf16[256,256]{1,0:T(8,128)(2,1)}, u32[]{:S(2)}) copy-start(bf16[256,256]{1,0:T(8,128)(2,1)} %constant.50.clone.upper_ref) | copy-start | bytes 393220
  21.2 1.0 %copy-start.6 = (bf16[512,256]{1,0:T(8,128)(2,1)S(1)}, bf16[512,256]{1,0:T(8,128)(2,1)}, u32[]{:S(2)}) copy-start(bf16[512,256]{1,0:T(8,128)(2,1)} %constant.54.clone.bins_ref) | copy-start | bytes 786436
  24.3 9.4 %collective-permute-start.8 = (f32[136,256]{1,0:T(8,128)S(1)}, f32[136,256]{1,0:T(8,128)S(1)}, u32[]{:S(2)}, u32[]{:S(2)}) collective-permute-start(f32[136,256]{1,0:T(8,128)S(1)} %get-tuple-element.57), channel_id=1, source_target_pairs={{0,32},{32,0},{64,96},{96,64},{1,33},{33,1},{65,97},{97,65},{2,34}... | collective-permute-start | bytes 417800 | tf_op jit(solution)/shard_map/ppermute | solution.py:98
  25.6 8.2 %collective-permute-start.9 = (f32[136,256]{1,0:T(8,128)S(1)}, f32[136,256]{1,0:T(8,128)S(1)}, u32[]{:S(2)}, u32[]{:S(2)}) collective-permute-start(f32[136,256]{1,0:T(8,128)S(1)} %get-tuple-element.58), channel_id=1, source_target_pairs={{0,96},{32,64},{64,32},{96,0},{1,97},{33,65},{65,33},{97,1},{2,98}... | collective-permute-start | bytes 417800 | tf_op jit(solution)/shard_map/ppermute | solution.py:98
  27.3 6.5 %collective-permute-start.10 = (f32[136,256]{1,0:T(8,128)S(1)}, f32[136,256]{1,0:T(8,128)S(1)}, u32[]{:S(2)}, u32[]{:S(2)}) collective-permute-start(f32[136,256]{1,0:T(8,128)S(1)} %get-tuple-element.59), channel_id=1, source_target_pairs={{0,1},{1,0},{2,3},{3,2},{4,5},{5,4},{6,7},{7,6},{8,9},{9,8},{10,11... | collective-permute-start | bytes 417800 | tf_op jit(solution)/shard_map/ppermute | solution.py:98
  27.3 7.9 %collective-permute-start.11 = (f32[136,256]{1,0:T(8,128)S(1)}, f32[136,256]{1,0:T(8,128)S(1)}, u32[]{:S(2)}, u32[]{:S(2)}) collective-permute-start(f32[136,256]{1,0:T(8,128)S(1)} %get-tuple-element.60), channel_id=1, source_target_pairs={{0,31},{1,2},{2,1},{3,4},{4,3},{5,6},{6,5},{7,8},{8,7},{9,10},{10,... | collective-permute-start | bytes 417800 | tf_op jit(solution)/shard_map/ppermute | solution.py:98
  36.1 12.4 %collective-permute-start.14 = (f32[32,8,256]{2,1,0:T(8,128)S(1)}, f32[32,8,256]{2,1,0:T(8,128)S(1)}, u32[]{:S(2)}, u32[]{:S(2)}) collective-permute-start(f32[32,8,256]{2,1,0:T(8,128)S(1)} %get-tuple-element.63), channel_id=1, source_target_pairs={{0,1},{1,0},{2,3},{3,2},{4,5},{5,4},{6,7},{7,6},{8,9},{9,8},{10,11... | collective-permute-start | bytes 786440 | tf_op jit(solution)/shard_map/ppermute | solution.py:98
  36.2 12.3 %collective-permute-start.15 = (f32[32,8,256]{2,1,0:T(8,128)S(1)}, f32[32,8,256]{2,1,0:T(8,128)S(1)}, u32[]{:S(2)}, u32[]{:S(2)}) collective-permute-start(f32[32,8,256]{2,1,0:T(8,128)S(1)} %get-tuple-element.64), channel_id=1, source_target_pairs={{0,31},{1,2},{2,1},{3,4},{4,3},{5,6},{6,5},{7,8},{8,7},{9,10},{10,... | collective-permute-start | bytes 786440 | tf_op jit(solution)/shard_map/ppermute | solution.py:98
  40.7 6.2 %collective-permute-start.12 = (f32[5,3,16,256]{3,2,1,0:T(8,128)S(1)}, f32[5,3,16,256]{3,2,1,0:T(8,128)S(1)}, u32[]{:S(2)}, u32[]{:S(2)}) collective-permute-start(f32[5,3,16,256]{3,2,1,0:T(8,128)S(1)} %get-tuple-element.61), channel_id=1, source_target_pairs={{0,32},{32,0},{64,96},{96,64},{1,33},{33,1},{65,97},{97,65},{2,34}... | collective-permute-start | bytes 737288 | tf_op jit(solution)/shard_map/ppermute | solution.py:98
  41.0 7.4 %collective-permute-start.13 = (f32[5,3,16,256]{3,2,1,0:T(8,128)S(1)}, f32[5,3,16,256]{3,2,1,0:T(8,128)S(1)}, u32[]{:S(2)}, u32[]{:S(2)}) collective-permute-start(f32[5,3,16,256]{3,2,1,0:T(8,128)S(1)} %get-tuple-element.62), channel_id=1, source_target_pairs={{0,96},{32,64},{64,32},{96,0},{1,97},{33,65},{65,33},{97,1},{2,98}... | collective-permute-start | bytes 737288 | tf_op jit(solution)/shard_map/ppermute | solution.py:98
  50.5 10.5 %collective-permute-start.18 = (f32[32,8,256]{2,1,0:T(8,128)S(1)}, f32[32,8,256]{2,1,0:T(8,128)S(1)}, u32[]{:S(2)}, u32[]{:S(2)}) collective-permute-start(f32[32,8,256]{2,1,0:T(8,128)S(1)} %get-tuple-element.68), channel_id=1, source_target_pairs={{0,1},{1,0},{2,3},{3,2},{4,5},{5,4},{6,7},{7,6},{8,9},{9,8},{10,11... | collective-permute-start | bytes 786440 | tf_op jit(solution)/shard_map/ppermute | solution.py:98
  50.6 10.4 %collective-permute-start.19 = (f32[32,8,256]{2,1,0:T(8,128)S(1)}, f32[32,8,256]{2,1,0:T(8,128)S(1)}, u32[]{:S(2)}, u32[]{:S(2)}) collective-permute-start(f32[32,8,256]{2,1,0:T(8,128)S(1)} %get-tuple-element.69), channel_id=1, source_target_pairs={{0,31},{1,2},{2,1},{3,4},{4,3},{5,6},{6,5},{7,8},{8,7},{9,10},{10,... | collective-permute-start | bytes 786440 | tf_op jit(solution)/shard_map/ppermute | solution.py:98
  53.0 6.2 %collective-permute-start.16 = (f32[5,3,16,256]{3,2,1,0:T(8,128)S(1)}, f32[5,3,16,256]{3,2,1,0:T(8,128)S(1)}, u32[]{:S(2)}, u32[]{:S(2)}) collective-permute-start(f32[5,3,16,256]{3,2,1,0:T(8,128)S(1)} %get-tuple-element.66), channel_id=1, source_target_pairs={{0,32},{32,0},{64,96},{96,64},{1,33},{33,1},{65,97},{97,65},{2,34}... | collective-permute-start | bytes 737288 | tf_op jit(solution)/shard_map/ppermute | solution.py:98
  53.6 7.4 %collective-permute-start.17 = (f32[5,3,16,256]{3,2,1,0:T(8,128)S(1)}, f32[5,3,16,256]{3,2,1,0:T(8,128)S(1)}, u32[]{:S(2)}, u32[]{:S(2)}) collective-permute-start(f32[5,3,16,256]{3,2,1,0:T(8,128)S(1)} %get-tuple-element.67), channel_id=1, source_target_pairs={{0,96},{32,64},{64,32},{96,0},{1,97},{33,65},{65,33},{97,1},{2,98}... | collective-permute-start | bytes 737288 | tf_op jit(solution)/shard_map/ppermute | solution.py:98
  63.1 10.2 %collective-permute-start.22 = (f32[32,8,256]{2,1,0:T(8,128)S(1)}, f32[32,8,256]{2,1,0:T(8,128)S(1)}, u32[]{:S(2)}, u32[]{:S(2)}) collective-permute-start(f32[32,8,256]{2,1,0:T(8,128)S(1)} %get-tuple-element.73), channel_id=1, source_target_pairs={{0,1},{1,0},{2,3},{3,2},{4,5},{5,4},{6,7},{7,6},{8,9},{9,8},{10,11... | collective-permute-start | bytes 786440 | tf_op jit(solution)/shard_map/ppermute | solution.py:98
  63.2 10.1 %collective-permute-start.23 = (f32[32,8,256]{2,1,0:T(8,128)S(1)}, f32[32,8,256]{2,1,0:T(8,128)S(1)}, u32[]{:S(2)}, u32[]{:S(2)}) collective-permute-start(f32[32,8,256]{2,1,0:T(8,128)S(1)} %get-tuple-element.74), channel_id=1, source_target_pairs={{0,31},{1,2},{2,1},{3,4},{4,3},{5,6},{6,5},{7,8},{8,7},{9,10},{10,... | collective-permute-start | bytes 786440 | tf_op jit(solution)/shard_map/ppermute | solution.py:98
  65.5 6.2 %collective-permute-start.20 = (f32[5,3,16,256]{3,2,1,0:T(8,128)S(1)}, f32[5,3,16,256]{3,2,1,0:T(8,128)S(1)}, u32[]{:S(2)}, u32[]{:S(2)}) collective-permute-start(f32[5,3,16,256]{3,2,1,0:T(8,128)S(1)} %get-tuple-element.71), channel_id=1, source_target_pairs={{0,32},{32,0},{64,96},{96,64},{1,33},{33,1},{65,97},{97,65},{2,34}... | collective-permute-start | bytes 737288 | tf_op jit(solution)/shard_map/ppermute | solution.py:98
  65.8 7.4 %collective-permute-start.21 = (f32[5,3,16,256]{3,2,1,0:T(8,128)S(1)}, f32[5,3,16,256]{3,2,1,0:T(8,128)S(1)}, u32[]{:S(2)}, u32[]{:S(2)}) collective-permute-start(f32[5,3,16,256]{3,2,1,0:T(8,128)S(1)} %get-tuple-element.72), channel_id=1, source_target_pairs={{0,96},{32,64},{64,32},{96,0},{1,97},{33,65},{65,33},{97,1},{2,98}... | collective-permute-start | bytes 737288 | tf_op jit(solution)/shard_map/ppermute | solution.py:98
where the time goes:
time: 77.2 us; the launch traced here: 76.9 us
  starting transfers between devices  33.8 us (44%)
  waiting for transfers between devices  23.5 us (30%)
  Pallas kernels  13.5 us (17%)
  local copies, waits for them, and re-layouts  4.66 us (6%)
  other arithmetic  1.19 us (2%)
    ppermute x12, starting transfers between devices, swap(): lax.ppermute(to_b, axis, pairs_b)  30.6 us
    ppermute x12, waiting for transfers between devices, swap(): lax.ppermute(to_a, axis, pairs_a)  14.6 us
    pallas_call x10, Pallas kernels, full_specs(): pl.pallas_call(body, out_shape=[jax.ShapeDtypeStruct(s, d) for s, d in ou...  13.5 us
    ppermute x12, waiting for transfers between devices, swap(): lax.ppermute(to_b, axis, pairs_b)  8.95 us
    unnamed x22, local copies, waits for them, and re-layouts  4.66 us
    ppermute x12, starting transfers between devices, swap(): lax.ppermute(to_a, axis, pairs_a)  3.24 us
  transfers between devices with their start and end apart: 24, of which 10 were waited for; matrix products, arithmetic and copies ran while one was open for 0% of the time, Pallas kernels for 7%

commit v1 on v0

v1 whole, which is shorter than its diff:
```python
import math

import numpy as np

import jax
import jax.numpy as jnp
from jax import lax
from jax.experimental import pallas as pl
from jax.experimental.pallas import tpu as pltpu
from jax.sharding import PartitionSpec as P

HMAX = 4
drp_coeffs = (0.770882380518, -0.166705904415, 0.02084314277)
mach_number = 0.5
time_step = 0.7
source_gain = 4.0
radial_step = 2.0
hub_ratio = 1.6

F32 = jnp.float32
BF16 = jnp.bfloat16
VM = pl.BlockSpec(memory_space=pltpu.VMEM)
PARAMS = pltpu.CompilerParams(vmem_limit_bytes=24 * 1024 * 1024)
GROUP = 8


def window_matrices(span):
    one = np.zeros((span, span))
    for s, a in zip((1, 2, 3), drp_coeffs):
        one += a * (np.eye(span, k=s) - np.eye(span, k=-s))
    return np.stack(np_split(np.kron(np.eye(GROUP), one)))


def np_split(matrix):
    hi = matrix.astype(np.float32).astype(BF16)
    lo = (matrix - hi.astype(np.float64)).astype(np.float32).astype(BF16)
    return hi, lo


def filter_table():
    table = np.zeros((HMAX + 1, HMAX))
    for h in range(1, HMAX + 1):
        weights = [math.exp(-2.0 * k * k / (h * h)) if k <= h else 0.0 for k in range(HMAX + 1)]
        total = weights[0] + 2.0 * sum(weights[1:])
        table[:, h - 1] = [w / total for w in weights]
    return table


def radial_rows(na_total, radial):
    base = na_total / (2.0 * math.pi)
    radius = base / hub_ratio + radial_step * (np.arange(radial) + 0.5)
    return base / radius, 1.0 / radius


def radial_matrices(na_total, radial):
    diff = np.zeros((radial, radial))
    for s, a in zip((1, 2, 3), drp_coeffs):
        for j in range(radial):
            if j + s < radial:
                diff[j + s, j] += a / radial_step
            if j - s >= 0:
                diff[j - s, j] -= a / radial_step
    with_r = diff + np.diag(radial_rows(na_total, radial)[1])
    return np.stack([np.stack(np_split(with_r)), np.stack(np_split(diff))])


def azimuth_matrices(cols):
    full = np.zeros((2, GROUP * cols, GROUP * (cols + 16)))
    for which in range(2):
        place = {}
        for m in range(3):
            place[m - 3] = m + 4 * which
            place[cols + m] = 8 + m + 4 * which
        for x in range(GROUP):
            for i in range(cols):
                for s, a in zip((1, 2, 3), drp_coeffs):
                    for j, sign in ((i + s, 1.0), (i - s, -1.0)):
                        at = x * cols + j if 0 <= j < cols else GROUP * cols + x * 16 + place[j]
                        full[which, x * cols + i, at] += sign * a
    return np.stack([np.stack(np_split(full[w])) for w in range(2)])


def split(x):
    hi = x.astype(BF16)
    return hi, (x - hi.astype(F32)).astype(BF16)


def dot(a, b):
    return lax.dot_general(a, b, (((1,), (0,)), ((), ())), preferred_element_type=F32)


def is_even(axis):
    return lax.rem(lax.axis_index(axis), 2) == 0


def swap(to_a, to_b, axis):
    devices = lax.axis_size(axis)
    pairs_a = [(i, i ^ 1) for i in range(devices)]
    pairs_b = [(i, (i - 1) % devices if i % 2 == 0 else (i + 1) % devices) for i in range(devices)]
    return lax.ppermute(to_a, axis, pairs_a), lax.ppermute(to_b, axis, pairs_b)


def full_specs(body, outs, args, scratch=(), name=None, out_specs=None):
    return pl.pallas_call(
        body,
        out_shape=[jax.ShapeDtypeStruct(s, d) for s, d in outs],
        in_specs=[VM] * len(args),
        out_specs=out_specs or [VM] * len(outs),
        scratch_shapes=[pltpu.VMEM(*s) if isinstance(s, tuple) else s for s in scratch],
        compiler_params=PARAMS,
        name=name,
    )(*args)


def route_body(owner_ref, target_ref, pick_ref, cells_ref, own_ref):
    n_ax, n_az = lax.axis_size("ax"), lax.axis_size("az")
    ax, az = lax.axis_index("ax"), lax.axis_index("az")
    step_x = jnp.where(lax.rem(ax, 2) == 0, 1, -1)
    step_z = jnp.where(lax.rem(az, 2) == 0, 1, -1)
    me = ax * n_az + az
    b_x = ax - step_x
    ids = [
        (ax + step_x) * n_az + az,
        jnp.where((b_x >= 0) & (b_x < n_ax), b_x * n_az + az, -1),
        ax * n_az + lax.rem(az + step_z + n_az, n_az),
        ax * n_az + lax.rem(az - step_z + n_az, n_az),
    ]
    owner = owner_ref[...]
    target = target_ref[...]
    ncols = owner.shape[1]
    most = ncols // 2
    own_ref[...] = jnp.where(owner == me, target, -1)
    row = lax.broadcasted_iota(jnp.int32, (8, ncols), 0)
    marks = jnp.zeros((8, ncols), F32)
    for d, i in enumerate(ids):
        marks = jnp.where((row == d) & (owner == i), 1.0, marks)
    before = lax.broadcasted_iota(jnp.int32, (ncols, ncols), 0) < lax.broadcasted_iota(jnp.int32, (ncols, ncols), 1)
    rank = dot(marks.astype(BF16), jnp.where(before, 1.0, 0.0).astype(BF16))
    coarse = (target // 32).astype(F32)
    fine = (target % 32).astype(F32)
    digits = jnp.where(row == 0, coarse, jnp.where(row == 1, fine, 0.0)).astype(BF16)
    slot = lax.broadcasted_iota(jnp.int32, (most, ncols), 0).astype(F32)
    for d in range(4):
        wanted = jnp.where(marks[d : d + 1] > 0.0, rank[d : d + 1], -1.0)
        pick = jnp.where(slot == wanted, 1.0, 0.0).astype(BF16)
        pick_ref[d * most : (d + 1) * most, :] = pick
        found = lax.dot_general(digits, pick, (((1,), (1,)), ((), ())), preferred_element_type=F32)
        cells_ref[d, :, :] = jnp.zeros(cells_ref.shape[1:], F32)
        cells_ref[d, 0:1, 0:most] = found[0:1] * 32.0 + found[1:2]


def weights_of(h):
    table = filter_table()
    le = [h <= 1, h <= 2, h <= 3]
    out = []
    for k in range(HMAX + 1):
        value = jnp.full(h.shape, table[k, 3], F32)
        for j in (2, 1, 0):
            if j > 0 and table[k, j] == 0.0 and table[k, j - 1] == 0.0:
                value = jnp.where(le[j], 0.0, value)
                break
            value = jnp.where(le[j], table[k, j], value)
        out.append(value)
    return out


def inner_body(noise_ref, half_ref, first_ref):
    rows = noise_ref.shape[0]
    for x in range(rows):
        w = weights_of(half_ref[x])
        total = w[0] * noise_ref[x]
        for k in range(1, HMAX + 1):
            near = [noise_ref[y] for y in (x - k, x + k) if 0 <= y < rows]
            if near:
                total = total + w[k] * (near[0] + near[1] if len(near) == 2 else near[0])
        first_ref[x] = total


def first_body(inner_ref, half_ref, got_a_ref, got_b_ref, first_ref, to_a_ref, to_b_ref, halo):
    n_ax, ax = lax.axis_size("ax"), lax.axis_index("ax")
    even_x, even_z = is_even("ax"), is_even("az")
    rows = half_ref.shape[0]
    halo[0] = jnp.where(ax > 0, jnp.where(even_x, got_b_ref[...], got_a_ref[...]), 0.0)
    halo[1] = jnp.where(ax < n_ax - 1, jnp.where(even_x, got_a_ref[...], got_b_ref[...]), 0.0)
    for x in range(HMAX, rows - HMAX):
        first_ref[x] = inner_ref[x]
    for i in range(HMAX):
        w = weights_of(half_ref[i])
        total = inner_ref[i]
        for k in range(i + 1, HMAX + 1):
            total = total + w[k] * halo[0, HMAX + i - k]
        first_ref[i] = total
        x = rows - 1 - i
        w = weights_of(half_ref[x])
        total = inner_ref[x]
        for k in range(i + 1, HMAX + 1):
            total = total + w[k] * halo[1, k - i - 1]
        first_ref[x] = total
    half = rows // 2
    low = lax.broadcasted_iota(jnp.int32, (8, half_ref.shape[2]), 0) < 4
    for x in range(half):
        last = jnp.where(low, pltpu.roll(first_ref[x, 8:16], 4, 0), first_ref[x + half, 8:16])
        begin = jnp.where(low, first_ref[x, 0:8], pltpu.roll(first_ref[x + half, 0:8], 4, 0))
        to_a_ref[x] = jnp.where(even_z, last, begin)
        to_b_ref[x] = jnp.where(even_z, begin, last)


def second_body(
    first_ref, half_ref, got_a_ref, got_b_ref, pick_ref, cells_ref,
    own_ref, to_xa, to_xb, to_za, to_zb, wide, fine_hi, fine_lo,
):
    even = is_even("az")
    rows, cols, fine = first_ref.shape
    half = rows // 2
    for x in range(half):
        got_a, got_b = got_a_ref[x], got_b_ref[x]
        before = jnp.where(even, got_b, got_a)
        after = jnp.where(even, got_a, got_b)
        wide[x, 0:8] = pltpu.roll(before, 4, 0)
        wide[x + half, 0:8] = before
        wide[x, 24:32] = after
        wide[x + half, 24:32] = pltpu.roll(after, 4, 0)
    lane = lax.broadcasted_iota(jnp.int32, (cols, fine), 1)
    for x in range(rows):
        wide[x, 8:24] = first_ref[x]
    for x in range(rows):
        w = weights_of(half_ref[x])
        total = w[0] * first_ref[x]
        for k in range(1, HMAX + 1):
            total = total + w[k] * (wide[x, 8 - k : 24 - k] + wide[x, 8 + k : 24 + k])
        result = w[0] * total
        for k in range(1, HMAX + 1):
            up = jnp.where(lane < fine - k, pltpu.roll(total, fine - k, 1), 0.0)
            down = jnp.where(lane >= k, pltpu.roll(total, k, 1), 0.0)
            result = result + w[k] * (up + down)
        hi, lo = split(result)
        fine_hi[x * cols : (x + 1) * cols] = hi
        fine_lo[x * cols : (x + 1) * cols] = lo
    radial = own_ref.shape[1]
    above = lax.broadcasted_iota(jnp.int32, (fine, radial), 0) - lax.broadcasted_iota(
        jnp.int32, (fine, radial), 1
    ) * (fine // radial)
    bins = jnp.where((above >= 0) & (above < fine // radial), source_gain, 0.0).astype(BF16)
    binned = dot(fine_hi[...], bins) + dot(fine_lo[...], bins)
    own_ref[...] = binned
    hi, lo = split(binned)
    most = pick_ref.shape[0] // 4
    for d, out in enumerate((to_xa, to_xb, to_za, to_zb)):
        pick = pick_ref[d * most : (d + 1) * most]
        out[0:most] = dot(pick, hi) + dot(pick, lo)
        out[most : most + 8] = cells_ref[d]


def gather_body(binned_ref, own_ref, xa, xb, za, zb, q_ref, to_xa, to_xb):
    rows, cols, radial = q_ref.shape
    cells = rows * cols
    most = xa.shape[0] - 8
    even = is_even("ax")

    def onehot(row):
        at = lax.broadcasted_iota(jnp.int32, (cells, row.shape[1]), 0)
        return jnp.where(at == row, 1.0, 0.0).astype(BF16)

    mats = [onehot(own_ref[...])]
    packets = [binned_ref[...]]
    for got in (xa, xb, za, zb):
        mats.append(onehot(got[most : most + 1, 0:most].astype(jnp.int32)))
        packets.append(got[0:most])
    mat = jnp.concatenate(mats, axis=1)
    hi, lo = split(jnp.concatenate(packets, axis=0))
    q_ref[...] = (dot(mat, hi) + dot(mat, lo)).reshape(rows, cols, radial)
    first, last = q_ref[0:REACH], q_ref[rows - REACH :]
    to_xa[...] = jnp.where(even, last, first)
    to_xb[...] = jnp.where(even, first, last)


def join_last(ut, p):
    low = lax.broadcasted_iota(jnp.int32, ut.shape, 0) < 4
    return jnp.where(low, pltpu.roll(ut, 3, 0), pltpu.roll(p, 7, 0))


def join_first(ut, p):
    low = lax.broadcasted_iota(jnp.int32, ut.shape, 0) < 4
    return jnp.where(low, ut, pltpu.roll(p, 4, 0))


def write_sends(state, to_xa, to_xb, to_za, to_zb):
    even_x, even_z = is_even("ax"), is_even("az")
    rows = state.shape[1]
    for f in range(state.shape[0]):
        first, last = state[f, 0:3], state[f, rows - 3 : rows]
        to_xa[f] = jnp.where(even_x, last, first)
        to_xb[f] = jnp.where(even_x, first, last)
    for x in range(rows):
        last = join_last(state[2, x, 8:16], state[4, x, 8:16])[0:7]
        first = join_first(state[2, x, 0:8], state[4, x, 0:8])[0:7]
        to_za[x] = jnp.where(even_z, last, first)
        to_zb[x] = jnp.where(even_z, first, last)


def send_shapes(rows, cols, radial):
    ax, az = ((5, 3, cols, radial), F32), ((rows, 7, radial), F32)
    return [ax, ax, az, az]


def edges_body(state, to_xa, to_xb, to_za, to_zb):
    write_sends(state, to_xa, to_xb, to_za, to_zb)


def fill_side(side, za, zb):
    even = is_even("az")
    side[:, 0:7] = jnp.where(even, zb[...], za[...])
    side[:, 8:15] = jnp.where(even, za[...], zb[...])
    blank = jnp.zeros((side.shape[0], 1, side.shape[2]), F32)
    side[:, 7:8] = blank
    side[:, 15:16] = blank


def inverse_step(cols, radial):
    base = cols * lax.axis_size("az") / (2.0 * math.pi)
    at = lax.broadcasted_iota(jnp.int32, (1, radial), 1).astype(F32)
    return base / (base / hub_ratio + radial_step * (at + 0.5))


def outward(rmat, which, hi, lo):
    return dot(hi, rmat[which, 0]) + dot(lo, rmat[which, 0]) + dot(hi, rmat[which, 1])


def along(row, x):
    total = drp_coeffs[0] * (row(x + 1) - row(x - 1))
    for s in (2, 3):
        total = total + drp_coeffs[s - 1] * (row(x + s) - row(x - s))
    return total


def apply_operator(state, row, side, tmat, rmat, finish):
    _, rows, cols, radial = state.shape
    inv_h = inverse_step(cols, radial)
    size = GROUP * cols
    for g in range(rows // GROUP):
        at = slice(g * GROUP, (g + 1) * GROUP)
        halo_hi, halo_lo = split(side[at].reshape(GROUP * 16, radial))
        p_hi, p_lo = split(state[4, at].reshape(size, radial))
        ut_hi, ut_lo = split(state[2, at].reshape(size, radial))
        ur_hi, ur_lo = split(state[3, at].reshape(size, radial))

        def across(which, hi, lo):
            hi = jnp.concatenate([hi, halo_hi], axis=0)
            lo = jnp.concatenate([lo, halo_lo], axis=0)
            return dot(tmat[which, 0], hi) + dot(tmat[which, 0], lo) + dot(tmat[which, 1], hi)

        div_tr = across(0, ut_hi, ut_lo) * inv_h + outward(rmat, 0, ur_hi, ur_lo)
        p_t = across(1, p_hi, p_lo) * inv_h
        p_r = outward(rmat, 1, p_hi, p_lo)
        for i in range(GROUP):
            x = g * GROUP + i
            part = slice(i * cols, (i + 1) * cols)
            d = [along(lambda y: row(f, y), x) for f in range(5)]
            div = d[1] + div_tr[part]
            finish(
                x,
                [
                    -mach_number * d[0] - div,
                    -mach_number * d[1] - d[4],
                    -mach_number * d[2] - p_t[part],
                    -mach_number * d[3] - p_r[part],
                    -mach_number * d[4] - div,
                ],
            )


def fill_halo(halo, xa, xb):
    n_ax, ax = lax.axis_size("ax"), lax.axis_index("ax")
    even = is_even("ax")
    for f in range(halo.shape[1]):
        halo[0, f] = jnp.where(ax > 0, jnp.where(even, xb[f], xa[f]), 0.0)
        halo[1, f] = jnp.where(ax < n_ax - 1, jnp.where(even, xa[f], xb[f]), 0.0)


def with_halos(state, halo):
    rows = state.shape[1]

    def row(f, x):
        if x < 0:
            return halo[0, f, x + 3]
        if x >= rows:
            return halo[1, f, x - rows]
        return state[f, x]

    return row


def stage_body(factor, refs):
    state, za, zb, xa, xb, tmat, rmat, *rest = refs
    base = rest.pop(0) if len(rest) == 8 else None
    out, to_xa, to_xb, to_za, to_zb, halo, side = rest
    fill_halo(halo, xa, xb)
    fill_side(side, za, zb)

    def finish(x, tend):
        for f in range(5):
            out[f, x] = tend[f] if base is None else base[f, x] + factor * tend[f]

    apply_operator(state, with_halos(state, halo), side, tmat, rmat, finish)
    write_sends(out, to_xa, to_xb, to_za, to_zb)


def last_body(
    state, za, zb, xa, xb, tmat, rmat, k, fields, extra, extra_side, q, out, halo, side, both, result, sems
):
    _, rows, cols, radial = state.shape
    fill_halo(halo, xa, xb)
    fill_side(side, za, zb)
    side[...] = side[...] + extra_side[...]
    for f in range(5):
        halo[0, f] = halo[0, f] + extra[f, 0:3]
        halo[1, f] = halo[1, f] + extra[f, rows + 3 : rows + 6]
        for x in range(rows):
            both[f, x] = state[f, x] + extra[f, x + 3]

    def finish(x, tend):
        for f in range(5):
            slope = k[f, x] + q[x] if f == 4 else k[f, x]
            result[f, x] = fields[f, x] + time_step * slope + (0.5 * time_step * time_step) * tend[f]
        if x % GROUP == GROUP - 1:
            copy(x // GROUP).start()

    def copy(g):
        at = pl.ds(g * GROUP, GROUP)
        return pltpu.make_async_copy(result.at[:, at], out.at[:, at], sems.at[g])

    apply_operator(both, with_halos(both, halo), side, tmat, rmat, finish)
    for g in range(rows // GROUP):
        copy(g).wait()


REACH = 9


def widen_body(q, xa, xb, wide, to_za, to_zb):
    n_ax, ax = lax.axis_size("ax"), lax.axis_index("ax")
    even_x, even_z = is_even("ax"), is_even("az")
    rows, _, radial = q.shape
    wide[0:REACH] = jnp.where(ax > 0, jnp.where(even_x, xb[...], xa[...]), 0.0)
    wide[REACH : REACH + rows] = q[...]
    wide[REACH + rows :] = jnp.where(ax < n_ax - 1, jnp.where(even_x, xa[...], xb[...]), 0.0)
    total = rows + 2 * REACH
    place = lax.broadcasted_iota(jnp.int32, (8, radial), 0)
    for start in range(0, total, 8):
        last, first = jnp.zeros((8, radial), F32), jnp.zeros((8, radial), F32)
        for x in range(start, min(start + 8, total)):
            low, high = wide[x, 0:8], wide[x, 8:16]
            to_za[x] = jnp.where(even_z, high, low)
            to_zb[x] = jnp.where(even_z, low, high)
            at = x - start
            last = jnp.where(place == at, pltpu.roll(low, (at + 1) % 8, 0), last)
            first = jnp.where(place == at, pltpu.roll(high, at, 0) if at else high, first)
        to_za[total + start // 8] = jnp.where(even_z, last, first)
        to_zb[total + start // 8] = jnp.where(even_z, first, last)


def source_body(wide, za, zb, tmat, rmat, out, out_side, full, far, w3):
    n_ax, ax = lax.axis_size("ax"), lax.axis_index("ax")
    even = is_even("az")
    total, cols, radial = wide.shape
    rows = total - 2 * REACH

    def inside(value, x):
        if x < 0:
            return jnp.where(ax > 0, value, 0.0)
        if x >= rows:
            return jnp.where(ax < n_ax - 1, value, 0.0)
        return value

    before, after = 8, 8 + cols
    full[:, 0:8] = jnp.where(even, zb[0:total], za[0:total])
    full[:, 8:after] = wide[...]
    full[:, after : after + 8] = jnp.where(even, za[0:total], zb[0:total])
    far[0] = jnp.where(even, zb[total:], za[total:])
    far[1] = jnp.where(even, za[total:], zb[total:])
    inv_h = inverse_step(cols, radial)
    span = cols + 16
    size = GROUP * span
    place = lax.broadcasted_iota(jnp.int32, (8, radial), 0)
    edge = drp_coeffs[2]

    def across(hi, lo):
        return dot(tmat[0], hi) + dot(tmat[0], lo) + dot(tmat[1], hi)

    def groups(start, count):
        done = start
        while done < start + count:
            at = min(done, start + count - GROUP)
            yield at, range(done, at + GROUP)
            done = at + GROUP

    c = time_step / 4.0
    for at, todo in groups(3, rows + 12):
        hi, lo = split(full[at : at + GROUP].reshape(size, radial))
        q_t = across(hi, lo)
        q_r = outward(rmat, 1, hi, lo)
        for x in todo:
            part = slice((x - at) * span, (x - at + 1) * span)
            d = along(lambda y: full[y], x)
            w3[0, x - 3] = inside(-c * d, x - REACH)
            turn = q_t[part]
            low = jnp.where(place == 2, -edge * far[0, x // 8, x % 8 : x % 8 + 1], 0.0)
            high = jnp.where(place == 5, edge * far[1, x // 8, x % 8 : x % 8 + 1], 0.0)
            turn = jnp.concatenate([turn[0:8] + low, turn[8:after], turn[after:span] + high], axis=0)
            w3[1, x - 3] = inside((-c) * inv_h * turn, x - REACH)
            w3[2, x - 3] = inside(-c * q_r[part], x - REACH)
            w3[3, x - 3] = inside(full[x] - (c * mach_number) * d, x - REACH)

    c = time_step / 3.0
    for at, todo in groups(3, rows + 6):
        ut_hi, ut_lo = split(w3[1, at : at + GROUP].reshape(size, radial))
        ur_hi, ur_lo = split(w3[2, at : at + GROUP].reshape(size, radial))
        p_hi, p_lo = split(w3[3, at : at + GROUP].reshape(size, radial))
        div_tr = across(ut_hi, ut_lo) * inv_h + outward(rmat, 0, ur_hi, ur_lo)
        p_t = across(p_hi, p_lo) * inv_h
        p_r = outward(rmat, 1, p_hi, p_lo)
        for x in todo:
            o = x - 3
            begin = (x - at) * span
            part = slice(begin + 8, begin + 8 + cols)
            d = [along(lambda y: w3[f, y, 8:after], x) for f in range(4)]
            div = d[0] + div_tr[part]
            out[0, o] = inside(-c * div, o - 3)
            out[1, o] = inside(-c * (mach_number * d[0] + d[3]), o - 3)
            out[2, o] = inside(-c * (mach_number * d[1] + p_t[part]), o - 3)
            out[3, o] = inside(-c * (mach_number * d[2] + p_r[part]), o - 3)
            out[4, o] = inside(full[x + 3, 8:after] - c * (mach_number * d[3] + div), o - 3)
            if 3 <= o < 3 + rows:
                tiles = []
                for lanes in (slice(0, 8), slice(after, after + 8)):
                    part = slice(begin + lanes.start, begin + lanes.stop)
                    d0, d1, d3 = [along(lambda y: w3[f, y, lanes], x) for f in (0, 1, 3)]
                    ut = -c * (mach_number * d1 + p_t[part])
                    p = full[x + 3, lanes] - c * (mach_number * d3 + d0 + div_tr[part])
                    tiles.append((ut, p))
                out_side[o - 3, 0:8] = jnp.where(place == 7, 0.0, join_last(*tiles[0]))
                out_side[o - 3, 8:16] = jnp.where(place == 7, 0.0, join_first(*tiles[1]))


def local(noise, half_width, owner, target_cell, fields):
    px, pa, fine = noise.shape
    cx, ca, radial = fields.shape[1:]
    ncols = px * pa
    most = ncols // 2
    n_az = lax.axis_size("az")
    even_x = is_even("ax")

    first, last = noise[:HMAX], noise[px - HMAX :]
    to_a, to_b = jnp.where(even_x, last, first), jnp.where(even_x, first, last)
    to_a, to_b, late = lax.optimization_barrier((to_a, to_b, fields))
    noise_a, noise_b = swap(to_a, to_b, "ax")
    sends = send_shapes(cx, ca, radial)
    xa, xb, za, zb = full_specs(edges_body, sends, [late], name="edges")
    uza, uzb = swap(za, zb, "az")
    uxa, uxb = swap(xa, xb, "ax")

    pick, cells, own = full_specs(
        route_body,
        [((4 * most, ncols), BF16), ((4, 8, radial), F32), ((1, ncols), jnp.int32)],
        [owner.reshape(1, ncols), target_cell.reshape(1, ncols)],
        name="route",
    )
    (inner,) = full_specs(inner_body, [((px, pa, fine), F32)], [noise, half_width], name="filter_inner")
    filtered, to_a, to_b = full_specs(
        first_body,
        [((px, pa, fine), F32), ((px // 2, 8, fine), F32), ((px // 2, 8, fine), F32)],
        [inner, half_width, noise_a, noise_b],
        [((2, HMAX, pa, fine), F32)],
        name="filter_axial",
    )
    got_a, got_b = swap(to_a, to_b, "az")

    tmat = jnp.asarray(azimuth_matrices(ca))
    rmat = jnp.asarray(radial_matrices(float(ca * n_az), radial))
    state = ((5, cx, ca, radial), F32)
    spare = [((2, 5, 3, ca, radial), F32), ((cx, 16, radial), F32)]
    packet = ((most + 8, radial), F32)
    binned, xa, xb, za, zb = full_specs(
        second_body,
        [((ncols, radial), F32), packet, packet, packet, packet],
        [filtered, half_width, got_a, got_b, pick, cells],
        [((px, 32, fine), F32), ((ncols, fine), BF16), ((ncols, fine), BF16)],
        name="filter_rest",
    )
    xa, xb = swap(xa, xb, "ax")
    za, zb = swap(za, zb, "az")
    edge = ((REACH, ca, radial), F32)
    q, qxa, qxb = full_specs(
        gather_body, [((cx, ca, radial), F32), edge, edge], [binned, own, xa, xb, za, zb], name="gather"
    )
    qxa, qxb = swap(qxa, qxb, "ax")
    total = cx + 2 * REACH
    strip = ((total + pl.cdiv(total, 8), 8, radial), F32)
    wide, qza, qzb = full_specs(
        widen_body, [((total, ca, radial), F32), strip, strip], [q, qxa, qxb], name="widen"
    )
    qza, qzb = swap(qza, qzb, "az")

    def stage(factor, level, halos, base, name):
        def body(*refs):
            stage_body(factor, refs)

        args = [level, *halos, tmat, rmat] + ([] if base is None else [base])
        out, xa, xb, za, zb = full_specs(body, [state] + sends, args, spare, name=name)
        return out, (*swap(za, zb, "az"), *swap(xa, xb, "ax"))

    k, halos = stage(1.0, late, (uza, uzb, uxa, uxb), None, "operator")
    level, halos = stage(time_step / 4.0, k, halos, k, "stage")
    level, halos = stage(time_step / 3.0, level, halos, k, "stage")

    span = ca + 16
    extra, extra_side = full_specs(
        source_body,
        [((5, cx + 6, ca, radial), F32), ((cx, 16, radial), F32)],
        [wide, qza, qzb, jnp.asarray(window_matrices(span)), rmat],
        [
            ((total, span, radial), F32),
            ((2, pl.cdiv(total, 8), 8, radial), F32),
            ((4, cx + 12, span, radial), F32),
        ],
        name="source",
    )
    (out,) = full_specs(
        last_body,
        [state],
        [level, *halos, tmat, rmat, k, late, extra, extra_side, q],
        spare + [state, state, pltpu.SemaphoreType.DMA((cx // GROUP,))],
        name="final",
        out_specs=[pl.BlockSpec(memory_space=pl.ANY)],
    )
    return out


def solution(mesh):
    return jax.shard_map(
        local,
        mesh=mesh,
        in_specs=(
            P("ax", "az", None),
            P("ax", "az", None),
            P(("ax", "az")),
            P(("ax", "az")),
            P(None, "ax", "az", None),
        ),
        out_specs=P(None, "ax", "az", None),
        check_vma=False,
    )
```

time: 77.2 us -> 79.2 us (1.026)
  Pallas kernels: 13.5 us -> 18.2 us
  waiting for transfers between devices: 23.5 us -> 19.2 us
  starting transfers between devices: 33.8 us -> 36.8 us
  local copies, waits for them, and re-layouts: 4.66 us -> 3.15 us
    ppermute x12 -> x14, waiting for transfers between devices: 14.6 us -> 0.04 us  [swap(): lax.ppermute(to_a, axis, pairs_a)]
    ppermute x12 -> x14, waiting for transfers between devices: 8.95 us -> 19.2 us  [swap(): lax.ppermute(to_b, axis, pairs_b)]
    pallas_call x10 -> x12, Pallas kernels: 13.5 us -> 18.2 us  [full_specs(): pl.pallas_call(body, out_shape=[jax.ShapeDtypeStruct(s, d) for s, d in ou...]
    ppermute x12 -> x14, starting transfers between devices: 3.24 us -> 7.19 us  [swap(): lax.ppermute(to_a, axis, pairs_a)]
    unnamed x22 -> x20, local copies, waits for them, and re-layouts: 4.66 us -> 3.15 us
    ppermute x12 -> x14, starting transfers between devices: 30.6 us -> 29.6 us  [swap(): lax.ppermute(to_b, axis, pairs_b)]
  transfers between devices with their start and end apart: 24 -> 28, of which waited for: 10 -> 7; matrix products, arithmetic and copies ran while one was open for 0% -> 0% of each run, Pallas kernels for 7% -> 19%
where the time goes in v1:
time: 79.2 us; the launch traced here: 78.9 us
  starting transfers between devices  36.8 us (46%)
  waiting for transfers between devices  19.2 us (24%)
  Pallas kernels  18.2 us (23%)
  local copies, waits for them, and re-layouts  3.15 us (4%)
  other arithmetic  1.14 us (1%)
    ppermute x14, starting transfers between devices, swap(): lax.ppermute(to_b, axis, pairs_b)  29.6 us
    ppermute x14, waiting for transfers between devices, swap(): lax.ppermute(to_b, axis, pairs_b)  19.2 us
    pallas_call x12, Pallas kernels, full_specs(): pl.pallas_call(body, out_shape=[jax.ShapeDtypeStruct(s, d) for s, d in ou...  18.2 us
    ppermute x14, starting transfers between devices, swap(): lax.ppermute(to_a, axis, pairs_a)  7.19 us
    unnamed x20, local copies, waits for them, and re-layouts  3.15 us
  transfers between devices with their start and end apart: 28, of which 7 were waited for; matrix products, arithmetic and copies ran while one was open for 0% of the time, Pallas kernels for 19%

profile of v1, /device:TPU:0, one launch (start us, length us, event | category | flops | bytes accessed | tf_op | source)
XLA Modules:
  0.0 78.9 jit_solution(18358863198674519104)
XLA Ops:
  0.0 1.1 %slice_select_fusion = (f32[4,16,512]{2,1,0:T(8,128)S(1)}, f32[4,16,512]{2,1,0:T(8,128)S(1)}) fusion(f32[16,16,512]{2,1,0:T(8,128)} %noise_ref.1, pred[]{:T(512)S(6)} %eq.3), kind=kLoop, calls=%fused_computation | loop fusion | flops 65536 | bytes 524289 | tf_op jit(solution)/shard_map/jit(_where)/select_n | solution.py:554
  1.1 1.7 %collective-permute-start.16 = (f32[4,16,512]{2,1,0:T(8,128)S(1)}, f32[4,16,512]{2,1,0:T(8,128)S(1)}, u32[]{:S(2)}, u32[]{:S(2)}) collective-permute-start(f32[4,16,512]{2,1,0:T(8,128)S(1)} %get-tuple-element.66), channel_id=1, source_target_pairs={{0,32},{32,0},{64,96},{96,64},{1,33},{33,1},{65,97},{97,65},{2,34}... | collective-permute-start | bytes 393224 | tf_op jit(solution)/shard_map/ppermute | solution.py:100
  2.9 2.2 %collective-permute-start.17 = (f32[4,16,512]{2,1,0:T(8,128)S(1)}, f32[4,16,512]{2,1,0:T(8,128)S(1)}, u32[]{:S(2)}, u32[]{:S(2)}) collective-permute-start(f32[4,16,512]{2,1,0:T(8,128)S(1)} %get-tuple-element.67), channel_id=1, source_target_pairs={{0,96},{32,64},{64,32},{96,0},{1,97},{33,65},{65,33},{97,1},{2,98}... | collective-permute-start | bytes 393224 | tf_op jit(solution)/shard_map/ppermute | solution.py:100
  5.1 1.0 %copy-done.2 = s32[16,16,512]{2,1,0:T(8,128)S(1)} copy-done((s32[16,16,512]{2,1,0:T(8,128)S(1)}, s32[16,16,512]{2,1,0:T(8,128)}, u32[]{:S(2)}) %copy-start.2) | copy-done | bytes 524312
  6.1 1.0 %copy-done.6 = f32[16,16,512]{2,1,0:T(8,128)S(1)} copy-done((f32[16,16,512]{2,1,0:T(8,128)S(1)}, f32[16,16,512]{2,1,0:T(8,128)}, u32[]{:S(2)}) %copy-start.6) | copy-done | bytes 524312
  7.1 0.5 filter_inner.1.inner_ref
  7.6 0.0 copy-start.1
  7.6 0.0 collective-permute-done.16.got_a_ref
  7.6 1.4 %collective-permute-done.17.got_b_ref = f32[4,16,512]{2,1,0:T(8,128)S(1)} collective-permute-done((f32[4,16,512]{2,1,0:T(8,128)S(1)}, f32[4,16,512]{2,1,0:T(8,128)S(1)}, u32[]{:S(2)}, u32[]{:S(2)}) %collective-permute-start.17) | collective-permute-done | bytes 131104 | tf_op jit(solution)/shard_map/ppermute | solution.py:100
  9.1 1.0 %copy-done.3 = s32[16,16,512]{2,1,0:T(8,128)S(1)} copy-done((s32[16,16,512]{2,1,0:T(8,128)S(1)}, s32[16,16,512]{2,1,0:T(8,128)}, u32[]{:S(2)}) %copy-start.3) | copy-done | bytes 524312
  10.1 0.2 filter_axial.1
  10.3 0.1 collective-permute-start.18
  10.4 0.1 edges.1
  10.5 0.1 collective-permute-start.2
  10.6 2.3 %collective-permute-start.3 = (f32[5,3,16,256]{3,2,1,0:T(8,128)S(1)}, f32[5,3,16,256]{3,2,1,0:T(8,128)S(1)}, u32[]{:S(2)}, u32[]{:S(2)}) collective-permute-start(f32[5,3,16,256]{3,2,1,0:T(8,128)S(1)} %get-tuple-element.50), channel_id=1, source_target_pairs={{0,96},{32,64},{64,32},{96,0},{1,97},{33,65},{65,33},{97,1},{2,98}... | collective-permute-start | bytes 737288 | tf_op jit(solution)/shard_map/ppermute | solution.py:100
  12.9 0.2 collective-permute-start
  13.1 6.1 %collective-permute-start.1 = (f32[32,7,256]{2,1,0:T(8,128)S(1)}, f32[32,7,256]{2,1,0:T(8,128)S(1)}, u32[]{:S(2)}, u32[]{:S(2)}) collective-permute-start(f32[32,7,256]{2,1,0:T(8,128)S(1)} %get-tuple-element.48), channel_id=1, source_target_pairs={{0,31},{1,2},{2,1},{3,4},{4,3},{5,6},{6,5},{7,8},{8,7},{9,10},{10,... | collective-permute-start | bytes 688136 | tf_op jit(solution)/shard_map/ppermute | solution.py:100
  19.2 0.0 collective-permute-start.19
  19.3 0.3 route.1
  19.6 7.4 %collective-permute-done.19.got_b_ref = f32[8,8,512]{2,1,0:T(8,128)S(1)} collective-permute-done((f32[8,8,512]{2,1,0:T(8,128)S(1)}, f32[8,8,512]{2,1,0:T(8,128)S(1)}, u32[]{:S(2)}, u32[]{:S(2)}) %collective-permute-start.19) | collective-permute-done | bytes 131104 | tf_op jit(solution)/shard_map/ppermute | solution.py:100
  27.0 2.3 %filter_rest.1 = (f32[256,256]{1,0:T(8,128)S(1)}, f32[136,256]{1,0:T(8,128)S(1)}, f32[136,256]{1,0:T(8,128)S(1)}, f32[136,256]{1,0:T(8,128)S(1)}, f32[136,256]{1,0:T(8,128)S(1)}) custom-call(f32[16,16,512]{2,1,0:T(8,128)S(1)} %get-tuple-element.68.first_ref, s32[16,16,512]{2,1,0:T(8,128)S(1)} %copy-done.4, ...), custom_call_target="tpu_custom_call" | custom-call | tf_op jit(solution)/shard_map/filter_rest/pallas_call | solution.py:104
  29.3 1.4 %collective-permute-start.20 = (f32[136,256]{1,0:T(8,128)S(1)}, f32[136,256]{1,0:T(8,128)S(1)}, u32[]{:S(2)}, u32[]{:S(2)}) collective-permute-start(f32[136,256]{1,0:T(8,128)S(1)} %get-tuple-element.75), channel_id=1, source_target_pairs={{0,32},{32,0},{64,96},{96,64},{1,33},{33,1},{65,97},{97,65},{2,34}... | collective-permute-start | bytes 417800 | tf_op jit(solution)/shard_map/ppermute | solution.py:100
  30.7 1.1 %collective-permute-start.21 = (f32[136,256]{1,0:T(8,128)S(1)}, f32[136,256]{1,0:T(8,128)S(1)}, u32[]{:S(2)}, u32[]{:S(2)}) collective-permute-start(f32[136,256]{1,0:T(8,128)S(1)} %get-tuple-element.76), channel_id=1, source_target_pairs={{0,96},{32,64},{64,32},{96,0},{1,97},{33,65},{65,33},{97,1},{2,98}... | collective-permute-start | bytes 417800 | tf_op jit(solution)/shard_map/ppermute | solution.py:100
  31.8 1.8 %operator.1 = (f32[5,32,16,256]{3,2,1,0:T(8,128)S(1)}, f32[5,3,16,256]{3,2,1,0:T(8,128)S(1)}, f32[5,3,16,256]{3,2,1,0:T(8,128)S(1)}, f32[32,7,256]{2,1,0:T(8,128)S(1)}, f32[32,7,256]{2,1,0:T(8,128)S(1)}) custom-call(f32[5,32,16,256]{3,2,1,0:T(8,128)S(1)} %copy-done, f32[32,7,256]{2,1,0:T(8,128)S(1)} %collective-permute-done.refs_1_, ...), custom_call_target="tpu_custom_call" | custom-call | tf_op jit(solution)/shard_map/operator/pallas_call | solution.py:104
  33.6 0.1 collective-permute-start.4
  33.7 0.5 collective-permute-start.22
  34.2 2.2 %collective-permute-start.23 = (f32[136,256]{1,0:T(8,128)S(1)}, f32[136,256]{1,0:T(8,128)S(1)}, u32[]{:S(2)}, u32[]{:S(2)}) collective-permute-start(f32[136,256]{1,0:T(8,128)S(1)} %get-tuple-element.78), channel_id=1, source_target_pairs={{0,31},{1,2},{2,1},{3,4},{4,3},{5,6},{6,5},{7,8},{8,7},{9,10},{10,... | collective-permute-start | bytes 417800 | tf_op jit(solution)/shard_map/ppermute | solution.py:100
  36.4 0.0 collective-permute-done.20.xa
  36.4 0.1 collective-permute-start.6
  36.5 0.4 collective-permute-done.21.xb
  37.0 1.7 %collective-permute-start.7 = (f32[5,3,16,256]{3,2,1,0:T(8,128)S(1)}, f32[5,3,16,256]{3,2,1,0:T(8,128)S(1)}, u32[]{:S(2)}, u32[]{:S(2)}) collective-permute-start(f32[5,3,16,256]{3,2,1,0:T(8,128)S(1)} %get-tuple-element.55), channel_id=1, source_target_pairs={{0,96},{32,64},{64,32},{96,0},{1,97},{33,65},{65,33},{97,1},{2,98}... | collective-permute-start | bytes 737288 | tf_op jit(solution)/shard_map/ppermute | solution.py:100
  38.7 2.5 %collective-permute-start.5 = (f32[32,7,256]{2,1,0:T(8,128)S(1)}, f32[32,7,256]{2,1,0:T(8,128)S(1)}, u32[]{:S(2)}, u32[]{:S(2)}) collective-permute-start(f32[32,7,256]{2,1,0:T(8,128)S(1)} %get-tuple-element.53), channel_id=1, source_target_pairs={{0,31},{1,2},{2,1},{3,4},{4,3},{5,6},{6,5},{7,8},{8,7},{9,10},{10,... | collective-permute-start | bytes 688136 | tf_op jit(solution)/shard_map/ppermute | solution.py:100
  41.3 0.7 collective-permute-done.23.zb
  42.0 0.6 gather.1
  42.6 0.4 collective-permute-start.24
  43.0 0.0 collective-permute-done.4.refs_1_
  43.0 2.1 %collective-permute-start.25 = (f32[9,16,256]{2,1,0:T(8,128)S(1)}, f32[9,16,256]{2,1,0:T(8,128)S(1)}, u32[]{:S(2)}, u32[]{:S(2)}) collective-permute-start(f32[9,16,256]{2,1,0:T(8,128)S(1)} %get-tuple-element.81), channel_id=1, source_target_pairs={{0,96},{32,64},{64,32},{96,0},{1,97},{33,65},{65,33},{97,1},{2,98}... | collective-permute-start | bytes 442376 | tf_op jit(solution)/shard_map/ppermute | solution.py:100
  45.1 2.7 %collective-permute-done.5.refs_2_ = f32[32,7,256]{2,1,0:T(8,128)S(1)} collective-permute-done((f32[32,7,256]{2,1,0:T(8,128)S(1)}, f32[32,7,256]{2,1,0:T(8,128)S(1)}, u32[]{:S(2)}, u32[]{:S(2)}) %collective-permute-start.5) | collective-permute-done | bytes 229408 | tf_op jit(solution)/shard_map/ppermute | solution.py:100
  47.8 0.0 collective-permute-done.6.refs_3_
  47.8 0.0 collective-permute-done.7.refs_4_
  47.8 2.0 %stage.2 = (f32[5,32,16,256]{3,2,1,0:T(8,128)S(1)}, f32[5,3,16,256]{3,2,1,0:T(8,128)S(1)}, f32[5,3,16,256]{3,2,1,0:T(8,128)S(1)}, f32[32,7,256]{2,1,0:T(8,128)S(1)}, f32[32,7,256]{2,1,0:T(8,128)S(1)}) custom-call(f32[5,32,16,256]{3,2,1,0:T(8,128)S(1)} %get-tuple-element.51.refs_0_.refs_7_.k, f32[32,7,256]{2,1,0:T(8,128)S(1)} %collective-permute-done.4.refs_1_, ...), custom_call_target="tpu_custom_call" | custom-call | tf_op jit(solution)/shard_map/stage/pallas_call | solution.py:104
  49.8 0.1 collective-permute-start.8
  49.9 0.0 collective-permute-done.24.xa
  49.9 0.0 collective-permute-done.25.xb
  50.0 0.2 widen.1
  50.1 0.6 collective-permute-start.26
  50.7 1.3 %collective-permute-start.10 = (f32[5,3,16,256]{3,2,1,0:T(8,128)S(1)}, f32[5,3,16,256]{3,2,1,0:T(8,128)S(1)}, u32[]{:S(2)}, u32[]{:S(2)}) collective-permute-start(f32[5,3,16,256]{3,2,1,0:T(8,128)S(1)} %get-tuple-element.59), channel_id=1, source_target_pairs={{0,32},{32,0},{64,96},{96,64},{1,33},{33,1},{65,97},{97,65},{2,34}... | collective-permute-start | bytes 737288 | tf_op jit(solution)/shard_map/ppermute | solution.py:100
  52.0 1.1 %collective-permute-start.11 = (f32[5,3,16,256]{3,2,1,0:T(8,128)S(1)}, f32[5,3,16,256]{3,2,1,0:T(8,128)S(1)}, u32[]{:S(2)}, u32[]{:S(2)}) collective-permute-start(f32[5,3,16,256]{3,2,1,0:T(8,128)S(1)} %get-tuple-element.60), channel_id=1, source_target_pairs={{0,96},{32,64},{64,32},{96,0},{1,97},{33,65},{65,33},{97,1},{2,98}... | collective-permute-start | bytes 737288 | tf_op jit(solution)/shard_map/ppermute | solution.py:100
  53.1 1.7 %collective-permute-start.9 = (f32[32,7,256]{2,1,0:T(8,128)S(1)}, f32[32,7,256]{2,1,0:T(8,128)S(1)}, u32[]{:S(2)}, u32[]{:S(2)}) collective-permute-start(f32[32,7,256]{2,1,0:T(8,128)S(1)} %get-tuple-element.58), channel_id=1, source_target_pairs={{0,31},{1,2},{2,1},{3,4},{4,3},{5,6},{6,5},{7,8},{8,7},{9,10},{10,... | collective-permute-start | bytes 688136 | tf_op jit(solution)/shard_map/ppermute | solution.py:100
  54.8 0.0 collective-permute-done.8.refs_1_
  54.8 3.4 %collective-permute-start.27 = (f32[57,8,256]{2,1,0:T(8,128)S(1)}, f32[57,8,256]{2,1,0:T(8,128)S(1)}, u32[]{:S(2)}, u32[]{:S(2)}) collective-permute-start(f32[57,8,256]{2,1,0:T(8,128)S(1)} %get-tuple-element.84), channel_id=1, source_target_pairs={{0,31},{1,2},{2,1},{3,4},{4,3},{5,6},{6,5},{7,8},{8,7},{9,10},{10,... | collective-permute-start | bytes 1400840 | tf_op jit(solution)/shard_map/ppermute | solution.py:100
  58.1 4.0 %collective-permute-done.9.refs_2_ = f32[32,7,256]{2,1,0:T(8,128)S(1)} collective-permute-done((f32[32,7,256]{2,1,0:T(8,128)S(1)}, f32[32,7,256]{2,1,0:T(8,128)S(1)}, u32[]{:S(2)}, u32[]{:S(2)}) %collective-permute-start.9) | collective-permute-done | bytes 229408 | tf_op jit(solution)/shard_map/ppermute | solution.py:100
  62.2 0.0 collective-permute-done.10.refs_3_
  62.2 0.0 collective-permute-done.11.refs_4_
  62.2 2.0 %stage.3 = (f32[5,32,16,256]{3,2,1,0:T(8,128)S(1)}, f32[5,3,16,256]{3,2,1,0:T(8,128)S(1)}, f32[5,3,16,256]{3,2,1,0:T(8,128)S(1)}, f32[32,7,256]{2,1,0:T(8,128)S(1)}, f32[32,7,256]{2,1,0:T(8,128)S(1)}) custom-call(f32[5,32,16,256]{3,2,1,0:T(8,128)S(1)} %get-tuple-element.56.refs_0_, f32[32,7,256]{2,1,0:T(8,128)S(1)} %collective-permute-done.8.refs_1_, ...), custom_call_target="tpu_custom_call" | custom-call | tf_op jit(solution)/shard_map/stage/pallas_call | solution.py:104
  64.2 0.6 collective-permute-start.14
  64.8 1.8 %collective-permute-start.15 = (f32[5,3,16,256]{3,2,1,0:T(8,128)S(1)}, f32[5,3,16,256]{3,2,1,0:T(8,128)S(1)}, u32[]{:S(2)}, u32[]{:S(2)}) collective-permute-start(f32[5,3,16,256]{3,2,1,0:T(8,128)S(1)} %get-tuple-element.65), channel_id=1, source_target_pairs={{0,96},{32,64},{64,32},{96,0},{1,97},{33,65},{65,33},{97,1},{2,98}... | collective-permute-start | bytes 737288 | tf_op jit(solution)/shard_map/ppermute | solution.py:100
  66.5 1.4 %collective-permute-start.13 = (f32[32,7,256]{2,1,0:T(8,128)S(1)}, f32[32,7,256]{2,1,0:T(8,128)S(1)}, u32[]{:S(2)}, u32[]{:S(2)}) collective-permute-start(f32[32,7,256]{2,1,0:T(8,128)S(1)} %get-tuple-element.63), channel_id=1, source_target_pairs={{0,31},{1,2},{2,1},{3,4},{4,3},{5,6},{6,5},{7,8},{8,7},{9,10},{10,... | collective-permute-start | bytes 688136 | tf_op jit(solution)/shard_map/ppermute | solution.py:100
  68.0 0.0 collective-permute-done.27.zb
  68.0 5.2 %source.1 = (f32[5,38,16,256]{3,2,1,0:T(8,128)S(1)}, f32[32,16,256]{2,1,0:T(8,128)S(1)}) custom-call(f32[50,16,256]{2,1,0:T(8,128)S(1)} %get-tuple-element.82.wide, f32[57,8,256]{2,1,0:T(8,128)S(1)} %collective-permute-done.26.za, f32[57,8,256]{2,1,0:T(8,128)S(1)} %collective-permute-done.27.zb, bf16[2,256,256]{2,1,0:T(8,128)(2,1)S(1)} %copy-done.7, ...), custom_call_target="tpu_custom_call" | custom-call | tf_op jit(solution)/shard_map/source/pallas_call | solution.py:104
  73.2 2.5 %collective-permute-done.13.zb = f32[32,7,256]{2,1,0:T(8,128)S(1)} collective-permute-done((f32[32,7,256]{2,1,0:T(8,128)S(1)}, f32[32,7,256]{2,1,0:T(8,128)S(1)}, u32[]{:S(2)}, u32[]{:S(2)}) %collective-permute-start.13) | collective-permute-done | bytes 229408 | tf_op jit(solution)/shard_map/ppermute | solution.py:100
  75.7 0.0 collective-permute-done.14.xa
  75.7 0.0 collective-permute-done.15.xb
  75.7 3.1 %final.1 = f32[5,32,16,256]{3,2,1,0:T(8,128)} custom-call(f32[5,32,16,256]{3,2,1,0:T(8,128)S(1)} %get-tuple-element.61.state, f32[32,7,256]{2,1,0:T(8,128)S(1)} %collective-permute-done.12.za, f32[32,7,256]{2,1,0:T(8,128)S(1)} %collective-permute-done.13.zb, f32[5,3,16,256]{3,2,1,0:T(8,128)S(1)} %collective-permute-done.14.xa, ...), custom_call_target="tpu_custom_call" | custom-call | tf_op jit(solution)/shard_map/final/pallas_call | solution.py:104
  (25 shorter events, 0.1 us)
Async XLA Ops:
  0.0 10.4 %copy-start = (f32[5,32,16,256]{3,2,1,0:T(8,128)S(1)}, f32[5,32,16,256]{3,2,1,0:T(8,128)}, u32[]{:S(2)}) copy-start(f32[5,32,16,256]{3,2,1,0:T(8,128)} %fields) | copy-start | bytes 7864324
  1.1 6.5 %collective-permute-start.16 = (f32[4,16,512]{2,1,0:T(8,128)S(1)}, f32[4,16,512]{2,1,0:T(8,128)S(1)}, u32[]{:S(2)}, u32[]{:S(2)}) collective-permute-start(f32[4,16,512]{2,1,0:T(8,128)S(1)} %get-tuple-element.66), channel_id=1, source_target_pairs={{0,32},{32,0},{64,96},{96,64},{1,33},{33,1},{65,97},{97,65},{2,34}... | collective-permute-start | bytes 393224 | tf_op jit(solution)/shard_map/ppermute | solution.py:100
  2.9 6.2 %collective-permute-start.17 = (f32[4,16,512]{2,1,0:T(8,128)S(1)}, f32[4,16,512]{2,1,0:T(8,128)S(1)}, u32[]{:S(2)}, u32[]{:S(2)}) collective-permute-start(f32[4,16,512]{2,1,0:T(8,128)S(1)} %get-tuple-element.67), channel_id=1, source_target_pairs={{0,96},{32,64},{64,32},{96,0},{1,97},{33,65},{65,33},{97,1},{2,98}... | collective-permute-start | bytes 393224 | tf_op jit(solution)/shard_map/ppermute | solution.py:100
  5.1 1.0 %copy-start.2 = (s32[16,16,512]{2,1,0:T(8,128)S(1)}, s32[16,16,512]{2,1,0:T(8,128)}, u32[]{:S(2)}) copy-start(s32[16,16,512]{2,1,0:T(8,128)} %half_ref.5) | copy-start | bytes 1572868
  6.1 1.0 %copy-start.6 = (f32[16,16,512]{2,1,0:T(8,128)S(1)}, f32[16,16,512]{2,1,0:T(8,128)}, u32[]{:S(2)}) copy-start(f32[16,16,512]{2,1,0:T(8,128)} %noise_ref.1) | copy-start | bytes 1572868
  7.6 24.2 %copy-start.1 = (bf16[2,2,256,256]{3,2,1,0:T(8,128)(2,1)S(1)}, bf16[2,2,256,256]{3,2,1,0:T(8,128)(2,1)}, u32[]{:S(2)}) copy-start(bf16[2,2,256,256]{3,2,1,0:T(8,128)(2,1)} %constant.19.clone.refs_6_.rmat) | copy-start | bytes 1572868
  9.1 1.0 %copy-start.3 = (s32[16,16,512]{2,1,0:T(8,128)S(1)}, s32[16,16,512]{2,1,0:T(8,128)}, u32[]{:S(2)}) copy-start(s32[16,16,512]{2,1,0:T(8,128)} %half_ref.5) | copy-start | bytes 1572868
  10.1 9.2 %copy-start.8 = (s32[256]{0:T(256)S(1)}, s32[256]{0:T(256)}, u32[]{:S(2)}) copy-start(s32[256]{0:T(256)} %param.10) | copy-start | bytes 3076
  10.1 9.2 %copy-start.9 = (s32[256]{0:T(256)S(1)}, s32[256]{0:T(256)}, u32[]{:S(2)}) copy-start(s32[256]{0:T(256)} %param.11) | copy-start | bytes 3076
  10.1 16.9 %copy-start.4 = (s32[16,16,512]{2,1,0:T(8,128)S(1)}, s32[16,16,512]{2,1,0:T(8,128)}, u32[]{:S(2)}) copy-start(s32[16,16,512]{2,1,0:T(8,128)} %half_ref.5) | copy-start | bytes 1572868
  10.1 21.7 %copy-start.5 = (bf16[2,2,128,256]{3,2,1,0:T(8,128)(2,1)S(1)}, bf16[2,2,128,256]{3,2,1,0:T(8,128)(2,1)}, u32[]{:S(2)}) copy-start(bf16[2,2,128,256]{3,2,1,0:T(8,128)(2,1)} %constant.18.clone.refs_5_.tmat) | copy-start | bytes 786436
  10.3 8.9 %collective-permute-start.18 = (f32[8,8,512]{2,1,0:T(8,128)S(1)}, f32[8,8,512]{2,1,0:T(8,128)S(1)}, u32[]{:S(2)}, u32[]{:S(2)}) collective-permute-start(f32[8,8,512]{2,1,0:T(8,128)S(1)} %get-tuple-element.69), channel_id=1, source_target_pairs={{0,1},{1,0},{2,3},{3,2},{4,5},{5,4},{6,7},{7,6},{8,9},{9,8},{10,11... | collective-permute-start | bytes 393224 | tf_op jit(solution)/shard_map/ppermute | solution.py:100
  10.5 21.2 %collective-permute-start.2 = (f32[5,3,16,256]{3,2,1,0:T(8,128)S(1)}, f32[5,3,16,256]{3,2,1,0:T(8,128)S(1)}, u32[]{:S(2)}, u32[]{:S(2)}) collective-permute-start(f32[5,3,16,256]{3,2,1,0:T(8,128)S(1)} %get-tuple-element.49), channel_id=1, source_target_pairs={{0,32},{32,0},{64,96},{96,64},{1,33},{33,1},{65,97},{97,65},{2,34}... | collective-permute-start | bytes 737288 | tf_op jit(solution)/shard_map/ppermute | solution.py:100
  10.6 21.1 %collective-permute-start.3 = (f32[5,3,16,256]{3,2,1,0:T(8,128)S(1)}, f32[5,3,16,256]{3,2,1,0:T(8,128)S(1)}, u32[]{:S(2)}, u32[]{:S(2)}) collective-permute-start(f32[5,3,16,256]{3,2,1,0:T(8,128)S(1)} %get-tuple-element.50), channel_id=1, source_target_pairs={{0,96},{32,64},{64,32},{96,0},{1,97},{33,65},{65,33},{97,1},{2,98}... | collective-permute-start | bytes 737288 | tf_op jit(solution)/shard_map/ppermute | solution.py:100
  12.9 17.8 %collective-permute-start = (f32[32,7,256]{2,1,0:T(8,128)S(1)}, f32[32,7,256]{2,1,0:T(8,128)S(1)}, u32[]{:S(2)}, u32[]{:S(2)}) collective-permute-start(f32[32,7,256]{2,1,0:T(8,128)S(1)} %get-tuple-element.47), channel_id=1, source_target_pairs={{0,1},{1,0},{2,3},{3,2},{4,5},{5,4},{6,7},{7,6},{8,9},{9,8},{10,11... | collective-permute-start | bytes 688136 | tf_op jit(solution)/shard_map/ppermute | solution.py:100
  13.1 18.7 %collective-permute-start.1 = (f32[32,7,256]{2,1,0:T(8,128)S(1)}, f32[32,7,256]{2,1,0:T(8,128)S(1)}, u32[]{:S(2)}, u32[]{:S(2)}) collective-permute-start(f32[32,7,256]{2,1,0:T(8,128)S(1)} %get-tuple-element.48), channel_id=1, source_target_pairs={{0,31},{1,2},{2,1},{3,4},{4,3},{5,6},{6,5},{7,8},{8,7},{9,10},{10,... | collective-permute-start | bytes 688136 | tf_op jit(solution)/shard_map/ppermute | solution.py:100
  19.2 7.7 %collective-permute-start.19 = (f32[8,8,512]{2,1,0:T(8,128)S(1)}, f32[8,8,512]{2,1,0:T(8,128)S(1)}, u32[]{:S(2)}, u32[]{:S(2)}) collective-permute-start(f32[8,8,512]{2,1,0:T(8,128)S(1)} %get-tuple-element.70), channel_id=1, source_target_pairs={{0,31},{1,2},{2,1},{3,4},{4,3},{5,6},{6,5},{7,8},{8,7},{9,10},{10,... | collective-permute-start | bytes 393224 | tf_op jit(solution)/shard_map/ppermute | solution.py:100
  29.3 7.1 %collective-permute-start.20 = (f32[136,256]{1,0:T(8,128)S(1)}, f32[136,256]{1,0:T(8,128)S(1)}, u32[]{:S(2)}, u32[]{:S(2)}) collective-permute-start(f32[136,256]{1,0:T(8,128)S(1)} %get-tuple-element.75), channel_id=1, source_target_pairs={{0,32},{32,0},{64,96},{96,64},{1,33},{33,1},{65,97},{97,65},{2,34}... | collective-permute-start | bytes 417800 | tf_op jit(solution)/shard_map/ppermute | solution.py:100
  30.7 6.3 %collective-permute-start.21 = (f32[136,256]{1,0:T(8,128)S(1)}, f32[136,256]{1,0:T(8,128)S(1)}, u32[]{:S(2)}, u32[]{:S(2)}) collective-permute-start(f32[136,256]{1,0:T(8,128)S(1)} %get-tuple-element.76), channel_id=1, source_target_pairs={{0,96},{32,64},{64,32},{96,0},{1,97},{33,65},{65,33},{97,1},{2,98}... | collective-permute-start | bytes 417800 | tf_op jit(solution)/shard_map/ppermute | solution.py:100
  33.6 9.4 %collective-permute-start.4 = (f32[32,7,256]{2,1,0:T(8,128)S(1)}, f32[32,7,256]{2,1,0:T(8,128)S(1)}, u32[]{:S(2)}, u32[]{:S(2)}) collective-permute-start(f32[32,7,256]{2,1,0:T(8,128)S(1)} %get-tuple-element.52), channel_id=1, source_target_pairs={{0,1},{1,0},{2,3},{3,2},{4,5},{5,4},{6,7},{7,6},{8,9},{9,8},{10,11... | collective-permute-start | bytes 688136 | tf_op jit(solution)/shard_map/ppermute | solution.py:100
  33.7 5.0 %collective-permute-start.22 = (f32[136,256]{1,0:T(8,128)S(1)}, f32[136,256]{1,0:T(8,128)S(1)}, u32[]{:S(2)}, u32[]{:S(2)}) collective-permute-start(f32[136,256]{1,0:T(8,128)S(1)} %get-tuple-element.77), channel_id=1, source_target_pairs={{0,1},{1,0},{2,3},{3,2},{4,5},{5,4},{6,7},{7,6},{8,9},{9,8},{10,11... | collective-permute-start | bytes 417800 | tf_op jit(solution)/shard_map/ppermute | solution.py:100
  34.2 7.8 %collective-permute-start.23 = (f32[136,256]{1,0:T(8,128)S(1)}, f32[136,256]{1,0:T(8,128)S(1)}, u32[]{:S(2)}, u32[]{:S(2)}) collective-permute-start(f32[136,256]{1,0:T(8,128)S(1)} %get-tuple-element.78), channel_id=1, source_target_pairs={{0,31},{1,2},{2,1},{3,4},{4,3},{5,6},{6,5},{7,8},{8,7},{9,10},{10,... | collective-permute-start | bytes 417800 | tf_op jit(solution)/shard_map/ppermute | solution.py:100
  36.4 11.4 %collective-permute-start.6 = (f32[5,3,16,256]{3,2,1,0:T(8,128)S(1)}, f32[5,3,16,256]{3,2,1,0:T(8,128)S(1)}, u32[]{:S(2)}, u32[]{:S(2)}) collective-permute-start(f32[5,3,16,256]{3,2,1,0:T(8,128)S(1)} %get-tuple-element.54), channel_id=1, source_target_pairs={{0,32},{32,0},{64,96},{96,64},{1,33},{33,1},{65,97},{97,65},{2,34}... | collective-permute-start | bytes 737288 | tf_op jit(solution)/shard_map/ppermute | solution.py:100
  37.0 10.9 %collective-permute-start.7 = (f32[5,3,16,256]{3,2,1,0:T(8,128)S(1)}, f32[5,3,16,256]{3,2,1,0:T(8,128)S(1)}, u32[]{:S(2)}, u32[]{:S(2)}) collective-permute-start(f32[5,3,16,256]{3,2,1,0:T(8,128)S(1)} %get-tuple-element.55), channel_id=1, source_target_pairs={{0,96},{32,64},{64,32},{96,0},{1,97},{33,65},{65,33},{97,1},{2,98}... | collective-permute-start | bytes 737288 | tf_op jit(solution)/shard_map/ppermute | solution.py:100
  38.7 9.1 %collective-permute-start.5 = (f32[32,7,256]{2,1,0:T(8,128)S(1)}, f32[32,7,256]{2,1,0:T(8,128)S(1)}, u32[]{:S(2)}, u32[]{:S(2)}) collective-permute-start(f32[32,7,256]{2,1,0:T(8,128)S(1)} %get-tuple-element.53), channel_id=1, source_target_pairs={{0,31},{1,2},{2,1},{3,4},{4,3},{5,6},{6,5},{7,8},{8,7},{9,10},{10,... | collective-permute-start | bytes 688136 | tf_op jit(solution)/shard_map/ppermute | solution.py:100
  42.6 7.4 %collective-permute-start.24 = (f32[9,16,256]{2,1,0:T(8,128)S(1)}, f32[9,16,256]{2,1,0:T(8,128)S(1)}, u32[]{:S(2)}, u32[]{:S(2)}) collective-permute-start(f32[9,16,256]{2,1,0:T(8,128)S(1)} %get-tuple-element.80), channel_id=1, source_target_pairs={{0,32},{32,0},{64,96},{96,64},{1,33},{33,1},{65,97},{97,65},{2,34}... | collective-permute-start | bytes 442376 | tf_op jit(solution)/shard_map/ppermute | solution.py:100
  43.0 7.0 %collective-permute-start.25 = (f32[9,16,256]{2,1,0:T(8,128)S(1)}, f32[9,16,256]{2,1,0:T(8,128)S(1)}, u32[]{:S(2)}, u32[]{:S(2)}) collective-permute-start(f32[9,16,256]{2,1,0:T(8,128)S(1)} %get-tuple-element.81), channel_id=1, source_target_pairs={{0,96},{32,64},{64,32},{96,0},{1,97},{33,65},{65,33},{97,1},{2,98}... | collective-permute-start | bytes 442376 | tf_op jit(solution)/shard_map/ppermute | solution.py:100
  49.8 4.9 %collective-permute-start.8 = (f32[32,7,256]{2,1,0:T(8,128)S(1)}, f32[32,7,256]{2,1,0:T(8,128)S(1)}, u32[]{:S(2)}, u32[]{:S(2)}) collective-permute-start(f32[32,7,256]{2,1,0:T(8,128)S(1)} %get-tuple-element.57), channel_id=1, source_target_pairs={{0,1},{1,0},{2,3},{3,2},{4,5},{5,4},{6,7},{7,6},{8,9},{9,8},{10,11... | collective-permute-start | bytes 688136 | tf_op jit(solution)/shard_map/ppermute | solution.py:100
  50.1 16.4 %collective-permute-start.26 = (f32[57,8,256]{2,1,0:T(8,128)S(1)}, f32[57,8,256]{2,1,0:T(8,128)S(1)}, u32[]{:S(2)}, u32[]{:S(2)}) collective-permute-start(f32[57,8,256]{2,1,0:T(8,128)S(1)} %get-tuple-element.83), channel_id=1, source_target_pairs={{0,1},{1,0},{2,3},{3,2},{4,5},{5,4},{6,7},{7,6},{8,9},{9,8},{10,11... | collective-permute-start | bytes 1400840 | tf_op jit(solution)/shard_map/ppermute | solution.py:100
  50.7 11.5 %collective-permute-start.10 = (f32[5,3,16,256]{3,2,1,0:T(8,128)S(1)}, f32[5,3,16,256]{3,2,1,0:T(8,128)S(1)}, u32[]{:S(2)}, u32[]{:S(2)}) collective-permute-start(f32[5,3,16,256]{3,2,1,0:T(8,128)S(1)} %get-tuple-element.59), channel_id=1, source_target_pairs={{0,32},{32,0},{64,96},{96,64},{1,33},{33,1},{65,97},{97,65},{2,34}... | collective-permute-start | bytes 737288 | tf_op jit(solution)/shard_map/ppermute | solution.py:100
  52.0 10.2 %collective-permute-start.11 = (f32[5,3,16,256]{3,2,1,0:T(8,128)S(1)}, f32[5,3,16,256]{3,2,1,0:T(8,128)S(1)}, u32[]{:S(2)}, u32[]{:S(2)}) collective-permute-start(f32[5,3,16,256]{3,2,1,0:T(8,128)S(1)} %get-tuple-element.60), channel_id=1, source_target_pairs={{0,96},{32,64},{64,32},{96,0},{1,97},{33,65},{65,33},{97,1},{2,98}... | collective-permute-start | bytes 737288 | tf_op jit(solution)/shard_map/ppermute | solution.py:100
  53.1 9.1 %collective-permute-start.9 = (f32[32,7,256]{2,1,0:T(8,128)S(1)}, f32[32,7,256]{2,1,0:T(8,128)S(1)}, u32[]{:S(2)}, u32[]{:S(2)}) collective-permute-start(f32[32,7,256]{2,1,0:T(8,128)S(1)} %get-tuple-element.58), channel_id=1, source_target_pairs={{0,31},{1,2},{2,1},{3,4},{4,3},{5,6},{6,5},{7,8},{8,7},{9,10},{10,... | collective-permute-start | bytes 688136 | tf_op jit(solution)/shard_map/ppermute | solution.py:100
  54.8 13.2 %collective-permute-start.27 = (f32[57,8,256]{2,1,0:T(8,128)S(1)}, f32[57,8,256]{2,1,0:T(8,128)S(1)}, u32[]{:S(2)}, u32[]{:S(2)}) collective-permute-start(f32[57,8,256]{2,1,0:T(8,128)S(1)} %get-tuple-element.84), channel_id=1, source_target_pairs={{0,31},{1,2},{2,1},{3,4},{4,3},{5,6},{6,5},{7,8},{8,7},{9,10},{10,... | collective-permute-start | bytes 1400840 | tf_op jit(solution)/shard_map/ppermute | solution.py:100
  62.2 5.8 %copy-start.7 = (bf16[2,256,256]{2,1,0:T(8,128)(2,1)S(1)}, bf16[2,256,256]{2,1,0:T(8,128)(2,1)}, u32[]{:S(2)}) copy-start(bf16[2,256,256]{2,1,0:T(8,128)(2,1)} %constant.20.clone.tmat) | copy-start | bytes 786436
  64.2 11.5 %collective-permute-start.14 = (f32[5,3,16,256]{3,2,1,0:T(8,128)S(1)}, f32[5,3,16,256]{3,2,1,0:T(8,128)S(1)}, u32[]{:S(2)}, u32[]{:S(2)}) collective-permute-start(f32[5,3,16,256]{3,2,1,0:T(8,128)S(1)} %get-tuple-element.64), channel_id=1, source_target_pairs={{0,32},{32,0},{64,96},{96,64},{1,33},{33,1},{65,97},{97,65},{2,34}... | collective-permute-start | bytes 737288 | tf_op jit(solution)/shard_map/ppermute | solution.py:100
  64.8 10.9 %collective-permute-start.15 = (f32[5,3,16,256]{3,2,1,0:T(8,128)S(1)}, f32[5,3,16,256]{3,2,1,0:T(8,128)S(1)}, u32[]{:S(2)}, u32[]{:S(2)}) collective-permute-start(f32[5,3,16,256]{3,2,1,0:T(8,128)S(1)} %get-tuple-element.65), channel_id=1, source_target_pairs={{0,96},{32,64},{64,32},{96,0},{1,97},{33,65},{65,33},{97,1},{2,98}... | collective-permute-start | bytes 737288 | tf_op jit(solution)/shard_map/ppermute | solution.py:100
  66.5 6.7 %collective-permute-start.12 = (f32[32,7,256]{2,1,0:T(8,128)S(1)}, f32[32,7,256]{2,1,0:T(8,128)S(1)}, u32[]{:S(2)}, u32[]{:S(2)}) collective-permute-start(f32[32,7,256]{2,1,0:T(8,128)S(1)} %get-tuple-element.62), channel_id=1, source_target_pairs={{0,1},{1,0},{2,3},{3,2},{4,5},{5,4},{6,7},{7,6},{8,9},{9,8},{10,11... | collective-permute-start | bytes 688136 | tf_op jit(solution)/shard_map/ppermute | solution.py:100
  66.5 9.1 %collective-permute-start.13 = (f32[32,7,256]{2,1,0:T(8,128)S(1)}, f32[32,7,256]{2,1,0:T(8,128)S(1)}, u32[]{:S(2)}, u32[]{:S(2)}) collective-permute-start(f32[32,7,256]{2,1,0:T(8,128)S(1)} %get-tuple-element.63), channel_id=1, source_target_pairs={{0,31},{1,2},{2,1},{3,4},{4,3},{5,6},{6,5},{7,8},{8,7},{9,10},{10,... | collective-permute-start | bytes 688136 | tf_op jit(solution)/shard_map/ppermute | solution.py:100

commit v2 on v1

--- a/solution.py
+++ b/solution.py
@@ -20,6 +20,7 @@
 F32 = jnp.float32
 BF16 = jnp.bfloat16
 VM = pl.BlockSpec(memory_space=pltpu.VMEM)
+ANY = pl.BlockSpec(memory_space=pl.ANY)
 PARAMS = pltpu.CompilerParams(vmem_limit_bytes=24 * 1024 * 1024)
 GROUP = 8
 
@@ -100,16 +101,22 @@
     return lax.ppermute(to_a, axis, pairs_a), lax.ppermute(to_b, axis, pairs_b)
 
 
-def full_specs(body, outs, args, scratch=(), name=None, out_specs=None):
+def full_specs(body, outs, args, scratch=(), name=None, out_specs=None, after=(), cost=0):
+    skip = len(args)
+
+    def run(*refs):
+        body(*refs[:skip], *refs[skip + len(after) :])
+
     return pl.pallas_call(
-        body,
+        run,
         out_shape=[jax.ShapeDtypeStruct(s, d) for s, d in outs],
-        in_specs=[VM] * len(args),
+        in_specs=[VM] * skip + [ANY] * len(after),
         out_specs=out_specs or [VM] * len(outs),
         scratch_shapes=[pltpu.VMEM(*s) if isinstance(s, tuple) else s for s in scratch],
         compiler_params=PARAMS,
         name=name,
-    )(*args)
+        cost_estimate=pl.CostEstimate(flops=0, bytes_accessed=cost, transcendentals=0),
+    )(*args, *after)
 
 
 def route_body(owner_ref, target_ref, pick_ref, cells_ref, own_ref):
@@ -164,8 +171,9 @@
     return out
 
 
-def inner_body(noise_ref, half_ref, first_ref):
+def inner_body(noise_ref, half_ref, first_ref, kept_ref):
     rows = noise_ref.shape[0]
+    kept_ref[...] = half_ref[...]
     for x in range(rows):
         w = weights_of(half_ref[x])
         total = w[0] * noise_ref[x]
@@ -247,14 +255,15 @@
     most = pick_ref.shape[0] // 4
     for d, out in enumerate((to_xa, to_xb, to_za, to_zb)):
         pick = pick_ref[d * most : (d + 1) * most]
-        out[0:most] = dot(pick, hi) + dot(pick, lo)
-        out[most : most + 8] = cells_ref[d]
+        tile = out.shape[1]
+        out[0 : most // tile] = (dot(pick, hi) + dot(pick, lo)).reshape(most // tile, tile, radial)
+        out[most // tile] = jnp.concatenate([cells_ref[d]] * (tile // 8), axis=0)
 
 
 def gather_body(binned_ref, own_ref, xa, xb, za, zb, q_ref, to_xa, to_xb):
     rows, cols, radial = q_ref.shape
     cells = rows * cols
-    most = xa.shape[0] - 8
+    most = binned_ref.shape[0] // 2
     even = is_even("ax")
 
     def onehot(row):
@@ -264,8 +273,9 @@
     mats = [onehot(own_ref[...])]
     packets = [binned_ref[...]]
     for got in (xa, xb, za, zb):
-        mats.append(onehot(got[most : most + 1, 0:most].astype(jnp.int32)))
-        packets.append(got[0:most])
+        layers, tile = got.shape[0], got.shape[1]
+        mats.append(onehot(got[layers - 1, 0:1, 0:most].astype(jnp.int32)))
+        packets.append(got[layers - 1 - most // tile : layers - 1].reshape(most, radial))
     mat = jnp.concatenate(mats, axis=1)
     hi, lo = split(jnp.concatenate(packets, axis=0))
     q_ref[...] = (dot(mat, hi) + dot(mat, lo)).reshape(rows, cols, radial)
@@ -284,34 +294,31 @@
     return jnp.where(low, ut, pltpu.roll(p, 4, 0))
 
 
-def write_sends(state, to_xa, to_xb, to_za, to_zb):
-    even_x, even_z = is_even("ax"), is_even("az")
-    rows = state.shape[1]
-    for f in range(state.shape[0]):
+def write_x(state, to_xa, to_xb):
+    even = is_even("ax")
+    fields, rows = state.shape[:2]
+    for f in range(fields):
         first, last = state[f, 0:3], state[f, rows - 3 : rows]
-        to_xa[f] = jnp.where(even_x, last, first)
-        to_xb[f] = jnp.where(even_x, first, last)
-    for x in range(rows):
-        last = join_last(state[2, x, 8:16], state[4, x, 8:16])[0:7]
-        first = join_first(state[2, x, 0:8], state[4, x, 0:8])[0:7]
-        to_za[x] = jnp.where(even_z, last, first)
-        to_zb[x] = jnp.where(even_z, first, last)
-
-
-def send_shapes(rows, cols, radial):
-    ax, az = ((5, 3, cols, radial), F32), ((rows, 7, radial), F32)
-    return [ax, ax, az, az]
-
-
-def edges_body(state, to_xa, to_xb, to_za, to_zb):
-    write_sends(state, to_xa, to_xb, to_za, to_zb)
+        to_xa[3 * f : 3 * f + 3] = jnp.where(even, last, first)
+        to_xb[3 * f : 3 * f + 3] = jnp.where(even, first, last)
+
+
+def write_z(state, to_za, to_zb):
+    even = is_even("az")
+    for x in range(state.shape[1]):
+        last = join_last(state[2, x, 8:16], state[4, x, 8:16])
+        first = join_first(state[2, x, 0:8], state[4, x, 0:8])
+        to_za[x] = jnp.where(even, last, first)[0 : to_za.shape[1]]
+        to_zb[x] = jnp.where(even, first, last)[0 : to_zb.shape[1]]
 
 
 def fill_side(side, za, zb):
     even = is_even("az")
-    side[:, 0:7] = jnp.where(even, zb[...], za[...])
-    side[:, 8:15] = jnp.where(even, za[...], zb[...])
-    blank = jnp.zeros((side.shape[0], 1, side.shape[2]), F32)
+    rows = side.shape[0]
+    a, b = za[0:rows, 0:7], zb[0:rows, 0:7]
+    side[:, 0:7] = jnp.where(even, b, a)
+    side[:, 8:15] = jnp.where(even, a, b)
+    blank = jnp.zeros((rows, 1, side.shape[2]), F32)
     side[:, 7:8] = blank
     side[:, 15:16] = blank
 
@@ -373,8 +380,9 @@
     n_ax, ax = lax.axis_size("ax"), lax.axis_index("ax")
     even = is_even("ax")
     for f in range(halo.shape[1]):
-        halo[0, f] = jnp.where(ax > 0, jnp.where(even, xb[f], xa[f]), 0.0)
-        halo[1, f] = jnp.where(ax < n_ax - 1, jnp.where(even, xa[f], xb[f]), 0.0)
+        a, b = xa[3 * f : 3 * f + 3], xb[3 * f : 3 * f + 3]
+        halo[0, f] = jnp.where(ax > 0, jnp.where(even, b, a), 0.0)
+        halo[1, f] = jnp.where(ax < n_ax - 1, jnp.where(even, a, b), 0.0)
 
 
 def with_halos(state, halo):
@@ -390,19 +398,34 @@
     return row
 
 
-def stage_body(factor, refs):
-    state, za, zb, xa, xb, tmat, rmat, *rest = refs
-    base = rest.pop(0) if len(rest) == 8 else None
-    out, to_xa, to_xb, to_za, to_zb, halo, side = rest
+def start_body(state, za, zb, xa, xb, tmat, rmat, px_a, px_b, pz_a, pz_b, out, to_xa, to_xb, to_za, to_zb, halo, side):
     fill_halo(halo, xa, xb)
     fill_side(side, za, zb)
 
     def finish(x, tend):
         for f in range(5):
-            out[f, x] = tend[f] if base is None else base[f, x] + factor * tend[f]
+            out[f, x] = tend[f]
 
     apply_operator(state, with_halos(state, halo), side, tmat, rmat, finish)
-    write_sends(out, to_xa, to_xb, to_za, to_zb)
+    write_x(out, to_xa, to_xb)
+    write_z(out, to_za, to_zb)
+    for ref in (to_xa, to_xb):
+        ref[15] = jnp.zeros(ref.shape[1:], F32)
+    for packet, out_ref in ((px_a, to_xa), (px_b, to_xb), (pz_a, to_za), (pz_b, to_zb)):
+        out_ref[out_ref.shape[0] - packet.shape[0] :] = packet[...]
+
+
+def stage_body(factor, state, za, zb, xa, xb, tmat, rmat, base, out, to_xa, to_xb, to_za, to_zb, halo, side):
+    fill_halo(halo, xa, xb)
+    fill_side(side, za, zb)
+
+    def finish(x, tend):
+        for f in range(5):
+            out[f, x] = base[f, x] + factor * tend[f]
+
+    apply_operator(state, with_halos(state, halo), side, tmat, rmat, finish)
+    write_x(out, to_xa, to_xb)
+    write_z(out, to_za, to_zb)
 
 
 def last_body(
@@ -434,6 +457,7 @@
         copy(g).wait()
 
 
+COST = 1 << 27
 REACH = 9
 
 
@@ -548,24 +572,17 @@
     ncols = px * pa
     most = ncols // 2
     n_az = lax.axis_size("az")
-    even_x = is_even("ax")
-
-    first, last = noise[:HMAX], noise[px - HMAX :]
-    to_a, to_b = jnp.where(even_x, last, first), jnp.where(even_x, first, last)
-    to_a, to_b, late = lax.optimization_barrier((to_a, to_b, fields))
+    block = ((px, pa, fine), F32)
+    even = is_even("ax")
+    to_a = jnp.where(even, noise[px - HMAX :], noise[:HMAX])
+    to_b = jnp.where(even, noise[:HMAX], noise[px - HMAX :])
     noise_a, noise_b = swap(to_a, to_b, "ax")
-    sends = send_shapes(cx, ca, radial)
-    xa, xb, za, zb = full_specs(edges_body, sends, [late], name="edges")
-    uza, uzb = swap(za, zb, "az")
-    uxa, uxb = swap(xa, xb, "ax")
-
-    pick, cells, own = full_specs(
-        route_body,
-        [((4 * most, ncols), BF16), ((4, 8, radial), F32), ((1, ncols), jnp.int32)],
-        [owner.reshape(1, ncols), target_cell.reshape(1, ncols)],
-        name="route",
-    )
-    (inner,) = full_specs(inner_body, [((px, pa, fine), F32)], [noise, half_width], name="filter_inner")
+    send_x, send_z = ((15, ca, radial), F32), ((cx, 7, radial), F32)
+    to_xa, to_xb = full_specs(write_x, [send_x, send_x], [fields], name="edges", after=[to_a])
+    uxa, uxb = swap(to_xa, to_xb, "ax")
+    inner, half_width = full_specs(
+        inner_body, [block, ((px, pa, fine), jnp.int32)], [noise, half_width], name="filter_inner", after=[to_xa]
+    )
     filtered, to_a, to_b = full_specs(
         first_body,
         [((px, pa, fine), F32), ((px // 2, 8, fine), F32), ((px // 2, 8, fine), F32)],
@@ -574,44 +591,78 @@
         name="filter_axial",
     )
     got_a, got_b = swap(to_a, to_b, "az")
-
+    uza, uzb = full_specs(write_z, [send_z, send_z], [fields], name="late_edges", after=[filtered])
+    pick, cells, own = full_specs(
+        route_body,
+        [((4 * most, ncols), BF16), ((4, 8, radial), F32), ((1, ncols), jnp.int32)],
+        [owner.reshape(1, ncols), target_cell.reshape(1, ncols)],
+        name="route",
+        after=[uzb],
+    )
+    uza, uzb = swap(uza, uzb, "az")
     tmat = jnp.asarray(azimuth_matrices(ca))
     rmat = jnp.asarray(radial_matrices(float(ca * n_az), radial))
     state = ((5, cx, ca, radial), F32)
     spare = [((2, 5, 3, ca, radial), F32), ((cx, 16, radial), F32)]
-    packet = ((most + 8, radial), F32)
-    binned, xa, xb, za, zb = full_specs(
+
+    packet_x = ((most // ca + 1, ca, radial), F32)
+    packet_z = ((most // 8 + 1, 8, radial), F32)
+    binned, *packets = full_specs(
         second_body,
-        [((ncols, radial), F32), packet, packet, packet, packet],
+        [((ncols, radial), F32), packet_x, packet_x, packet_z, packet_z],
         [filtered, half_width, got_a, got_b, pick, cells],
         [((px, 32, fine), F32), ((ncols, fine), BF16), ((ncols, fine), BF16)],
         name="filter_rest",
+    )
+    long_x = ((16 + packet_x[0][0], ca, radial), F32)
+    long_z = ((cx + packet_z[0][0], 8, radial), F32)
+    k, xa, xb, za, zb = full_specs(
+        start_body,
+        [state, long_x, long_x, long_z, long_z],
+        [fields, uza, uzb, uxa, uxb, tmat, rmat, *packets],
+        spare,
+        name="operator",
     )
     xa, xb = swap(xa, xb, "ax")
     za, zb = swap(za, zb, "az")
     edge = ((REACH, ca, radial), F32)
     q, qxa, qxb = full_specs(
-        gather_body, [((cx, ca, radial), F32), edge, edge], [binned, own, xa, xb, za, zb], name="gather"
-    )
+        gather_body,
+        [((cx, ca, radial), F32), edge, edge],
+        [binned, own, xa, xb, za, zb],
+        name="gather",
+    )
+
+    def stage(factor, level, halos, name, after, cost=0):
+        def body(*refs):
+            stage_body(factor, *refs)
+
+        return full_specs(
+            body,
+            [state, send_x, send_x, send_z, send_z],
+            [level, *halos, tmat, rmat, k],
+            spare,
+            name=name,
+            after=after,
+            cost=cost,
+        )
+
+    level, xa, xb, za, zb = stage(time_step / 4.0, k, (za, zb, xa, xb), "stage_3", [qxa])
     qxa, qxb = swap(qxa, qxb, "ax")
     total = cx + 2 * REACH
-    strip = ((total + pl.cdiv(total, 8), 8, radial), F32)
+    count = total + pl.cdiv(total, 8)
+    xa, xb = swap(xa, xb, "ax")
     wide, qza, qzb = full_specs(
-        widen_body, [((total, ca, radial), F32), strip, strip], [q, qxa, qxb], name="widen"
-    )
+        widen_body,
+        [((total, ca, radial), F32), ((count, 8, radial), F32), ((count, 8, radial), F32)],
+        [q, qxa, qxb],
+        name="widen",
+    )
+    za, zb = swap(za, zb, "az")
+    qza_sent = qza
     qza, qzb = swap(qza, qzb, "az")
-
-    def stage(factor, level, halos, base, name):
-        def body(*refs):
-            stage_body(factor, refs)
-
-        args = [level, *halos, tmat, rmat] + ([] if base is None else [base])
-        out, xa, xb, za, zb = full_specs(body, [state] + sends, args, spare, name=name)
-        return out, (*swap(za, zb, "az"), *swap(xa, xb, "ax"))
-
-    k, halos = stage(1.0, late, (uza, uzb, uxa, uxb), None, "operator")
-    level, halos = stage(time_step / 4.0, k, halos, k, "stage")
-    level, halos = stage(time_step / 3.0, level, halos, k, "stage")
+    level, xa, xb, za, zb = stage(time_step / 3.0, level, (za, zb, xa, xb), "stage_2", [qza_sent], COST)
+    halos = (*swap(za, zb, "az"), *swap(xa, xb, "ax"))
 
     span = ca + 16
     extra, extra_side = full_specs(
@@ -624,14 +675,15 @@
             ((4, cx + 12, span, radial), F32),
         ],
         name="source",
+        after=[level],
     )
     (out,) = full_specs(
         last_body,
         [state],
-        [level, *halos, tmat, rmat, k, late, extra, extra_side, q],
+        [level, *halos, tmat, rmat, k, fields, extra, extra_side, q],
         spare + [state, state, pltpu.SemaphoreType.DMA((cx // GROUP,))],
         name="final",
-        out_specs=[pl.BlockSpec(memory_space=pl.ANY)],
+        out_specs=[ANY],
     )
     return out
 

time: 79.2 us -> 82.7 us (1.044)
  waiting for transfers between devices: 19.2 us -> 29.8 us
  starting transfers between devices: 36.8 us -> 29.7 us
    ppermute x14 -> x12, waiting for transfers between devices: 19.2 us -> 28.2 us  [swap(): lax.ppermute(to_b, axis, pairs_b)]
    ppermute x14 -> x12, starting transfers between devices: 7.19 us -> 3.01 us  [swap(): lax.ppermute(to_a, axis, pairs_a)]
    ppermute x14 -> x12, starting transfers between devices: 29.6 us -> 26.6 us  [swap(): lax.ppermute(to_b, axis, pairs_b)]
    ppermute x14 -> x12, waiting for transfers between devices: 0.04 us -> 1.63 us  [swap(): lax.ppermute(to_a, axis, pairs_a)]
    pallas_call x12 -> x13, Pallas kernels: 18.2 us -> 18.7 us  [full_specs(): pl.pallas_call(run, out_shape=[jax.ShapeDtypeStruct(s, d) for s, d in out...]
    unnamed x20 -> x18, local copies, waits for them, and re-layouts: 3.15 us -> 2.96 us
  transfers between devices with their start and end apart: 28 -> 24, of which waited for: 7 -> 7; matrix products, arithmetic and copies ran while one was open for 0% -> 0% of each run, Pallas kernels for 19% -> 16%
where the time goes in v2:
time: 82.7 us; the launch traced here: 82.6 us
  waiting for transfers between devices  29.8 us (36%)
  starting transfers between devices  29.7 us (36%)
  Pallas kernels  18.7 us (23%)
  local copies, waits for them, and re-layouts  2.96 us (4%)
  other arithmetic  1.05 us (1%)
    ppermute x12, waiting for transfers between devices, swap(): lax.ppermute(to_b, axis, pairs_b)  28.2 us
    ppermute x12, starting transfers between devices, swap(): lax.ppermute(to_b, axis, pairs_b)  26.6 us
    pallas_call x13, Pallas kernels, full_specs(): pl.pallas_call(run, out_shape=[jax.ShapeDtypeStruct(s, d) for s, d in out...  18.7 us
    ppermute x12, starting transfers between devices, swap(): lax.ppermute(to_a, axis, pairs_a)  3.01 us
    unnamed x18, local copies, waits for them, and re-layouts  2.96 us
  transfers between devices with their start and end apart: 24, of which 7 were waited for; matrix products, arithmetic and copies ran while one was open for 0% of the time, Pallas kernels for 16%

profile of v2, /device:TPU:0, one launch (start us, length us, event | category | flops | bytes accessed | tf_op | source)
XLA Modules:
  0.0 82.6 jit_solution(6253571438187999507)
XLA Ops:
  0.0 1.0 %slice_select_fusion = (f32[4,16,512]{2,1,0:T(8,128)S(1)}, f32[4,16,512]{2,1,0:T(8,128)S(1)}) fusion(f32[16,16,512]{2,1,0:T(8,128)} %refs_0_.5, pred[]{:T(512)S(6)} %eq.3), kind=kLoop, calls=%fused_computation | loop fusion | flops 65536 | bytes 524289 | tf_op jit(solution)/shard_map/jit(_where)/select_n | solution.py:578
  1.1 3.2 %collective-permute-start.1 = (f32[4,16,512]{2,1,0:T(8,128)S(1)}, f32[4,16,512]{2,1,0:T(8,128)S(1)}, u32[]{:S(2)}, u32[]{:S(2)}) collective-permute-start(f32[4,16,512]{2,1,0:T(8,128)S(1)} %get-tuple-element.85), channel_id=1, source_target_pairs={{0,96},{32,64},{64,32},{96,0},{1,97},{33,65},{65,33},{97,1},{2,98}... | collective-permute-start | bytes 393224 | tf_op jit(solution)/shard_map/ppermute | solution.py:101
  4.2 0.1 collective-permute-start
  4.4 1.7 %copy-done = f32[5,32,16,256]{3,2,1,0:T(8,128)S(1)} copy-done((f32[5,32,16,256]{3,2,1,0:T(8,128)S(1)}, f32[5,32,16,256]{3,2,1,0:T(8,128)}, u32[]{:S(2)}) %copy-start) | copy-done | bytes 2621464
  6.2 0.0 copy-start.5
  6.2 1.2 %copy-done.5 = s32[16,16,512]{2,1,0:T(8,128)S(1)} copy-done((s32[16,16,512]{2,1,0:T(8,128)S(1)}, s32[16,16,512]{2,1,0:T(8,128)}, u32[]{:S(2)}) %copy-start.5) | copy-done | bytes 524312
  7.4 0.5 filter_inner.1
  7.9 0.0 collective-permute-done.1.refs_3_
  7.9 1.3 %collective-permute-done.refs_2_ = f32[4,16,512]{2,1,0:T(8,128)S(1)} collective-permute-done((f32[4,16,512]{2,1,0:T(8,128)S(1)}, f32[4,16,512]{2,1,0:T(8,128)S(1)}, u32[]{:S(2)}, u32[]{:S(2)}) %collective-permute-start) | collective-permute-done | bytes 131104 | tf_op jit(solution)/shard_map/ppermute | solution.py:101
  9.2 0.2 filter_axial.1
  9.4 0.0 copy-start.2
  9.4 0.0 copy-start.3
  9.4 0.1 collective-permute-start.6
  9.5 1.6 %collective-permute-start.5 = (f32[15,16,256]{2,1,0:T(8,128)S(1)}, f32[15,16,256]{2,1,0:T(8,128)S(1)}, u32[]{:S(2)}, u32[]{:S(2)}) collective-permute-start(f32[15,16,256]{2,1,0:T(8,128)S(1)} %get-tuple-element.51), channel_id=1, source_target_pairs={{0,96},{32,64},{64,32},{96,0},{1,97},{33,65},{65,33},{97,1},{2,98}... | collective-permute-start | bytes 737288 | tf_op jit(solution)/shard_map/ppermute | solution.py:101
  11.1 0.0 collective-permute-start.4
  11.1 0.1 late_edges.1
  11.2 0.2 collective-permute-start.2
  11.4 6.2 %collective-permute-start.3 = (f32[32,7,256]{2,1,0:T(8,128)S(1)}, f32[32,7,256]{2,1,0:T(8,128)S(1)}, u32[]{:S(2)}, u32[]{:S(2)}) collective-permute-start(f32[32,7,256]{2,1,0:T(8,128)S(1)} %get-tuple-element.50.refs_2_), channel_id=1, source_target_pairs={{0,31},{1,2},{2,1},{3,4},{4,3},{5,6},{6,5},{7,8},{8,7},{9,10},{10,... | collective-permute-start | bytes 688136 | tf_op jit(solution)/shard_map/ppermute | solution.py:101
  17.6 0.0 collective-permute-done.6.refs_2_
  17.6 0.0 collective-permute-start.7
  17.6 0.3 route.1
  17.9 7.4 %collective-permute-done.7.refs_3_ = f32[8,8,512]{2,1,0:T(8,128)S(1)} collective-permute-done((f32[8,8,512]{2,1,0:T(8,128)S(1)}, f32[8,8,512]{2,1,0:T(8,128)S(1)}, u32[]{:S(2)}, u32[]{:S(2)}) %collective-permute-start.7) | collective-permute-done | bytes 131104 | tf_op jit(solution)/shard_map/ppermute | solution.py:101
  25.3 2.3 %filter_rest.1 = (f32[256,256]{1,0:T(8,128)S(1)}, f32[9,16,256]{2,1,0:T(8,128)S(1)}, f32[9,16,256]{2,1,0:T(8,128)S(1)}, f32[17,8,256]{2,1,0:T(8,128)S(1)}, f32[17,8,256]{2,1,0:T(8,128)S(1)}) custom-call(f32[16,16,512]{2,1,0:T(8,128)S(1)} %get-tuple-element.48.refs_1_.refs_0_, s32[16,16,512]{2,1,0:T(8,128)S(1)} %get-tuple-element.47.refs_1_, ...), custom_call_target="tpu_custom_call" | custom-call | tf_op jit(solution)/shard_map/filter_rest/pallas_call | solution.py:110
  27.6 0.0 collective-permute-done.5.refs_4_
  27.6 0.0 collective-permute-done.4.refs_3_
  27.7 0.0 collective-permute-done.2.refs_1_
  27.7 0.0 collective-permute-done.3.refs_2_
  27.7 1.8 %operator.1 = (f32[5,32,16,256]{3,2,1,0:T(8,128)S(1)}, f32[25,16,256]{2,1,0:T(8,128)S(1)}, f32[25,16,256]{2,1,0:T(8,128)S(1)}, f32[49,8,256]{2,1,0:T(8,128)S(1)}, f32[49,8,256]{2,1,0:T(8,128)S(1)}) custom-call(f32[5,32,16,256]{3,2,1,0:T(8,128)S(1)} %copy-done.1, f32[32,7,256]{2,1,0:T(8,128)S(1)} %collective-permute-done.2.refs_1_, ...), custom_call_target="tpu_custom_call" | custom-call | tf_op jit(solution)/shard_map/operator/pallas_call | solution.py:110
  29.6 2.1 %collective-permute-start.10 = (f32[25,16,256]{2,1,0:T(8,128)S(1)}, f32[25,16,256]{2,1,0:T(8,128)S(1)}, u32[]{:S(2)}, u32[]{:S(2)}) collective-permute-start(f32[25,16,256]{2,1,0:T(8,128)S(1)} %get-tuple-element.63), channel_id=1, source_target_pairs={{0,32},{32,0},{64,96},{96,64},{1,33},{33,1},{65,97},{97,65},{2,34}... | collective-permute-start | bytes 1228808 | tf_op jit(solution)/shard_map/ppermute | solution.py:101
  31.7 1.8 %collective-permute-start.11 = (f32[25,16,256]{2,1,0:T(8,128)S(1)}, f32[25,16,256]{2,1,0:T(8,128)S(1)}, u32[]{:S(2)}, u32[]{:S(2)}) collective-permute-start(f32[25,16,256]{2,1,0:T(8,128)S(1)} %get-tuple-element.64), channel_id=1, source_target_pairs={{0,96},{32,64},{64,32},{96,0},{1,97},{33,65},{65,33},{97,1},{2,98}... | collective-permute-start | bytes 1228808 | tf_op jit(solution)/shard_map/ppermute | solution.py:101
  33.4 0.0 collective-permute-start.8
  33.4 2.2 %collective-permute-start.9 = (f32[49,8,256]{2,1,0:T(8,128)S(1)}, f32[49,8,256]{2,1,0:T(8,128)S(1)}, u32[]{:S(2)}, u32[]{:S(2)}) collective-permute-start(f32[49,8,256]{2,1,0:T(8,128)S(1)} %get-tuple-element.62), channel_id=1, source_target_pairs={{0,31},{1,2},{2,1},{3,4},{4,3},{5,6},{6,5},{7,8},{8,7},{9,10},{10,... | collective-permute-start | bytes 1204232 | tf_op jit(solution)/shard_map/ppermute | solution.py:101
  35.7 0.0 collective-permute-done.8.refs_4_.refs_1_
  35.7 8.4 %collective-permute-done.9.refs_5_.refs_2_ = f32[49,8,256]{2,1,0:T(8,128)S(1)} collective-permute-done((f32[49,8,256]{2,1,0:T(8,128)S(1)}, f32[49,8,256]{2,1,0:T(8,128)S(1)}, u32[]{:S(2)}, u32[]{:S(2)}) %collective-permute-start.9) | collective-permute-done | bytes 401440 | tf_op jit(solution)/shard_map/ppermute | solution.py:101
  44.0 0.0 collective-permute-done.10.refs_2_.refs_3_
  44.0 0.0 collective-permute-done.11.refs_3_.refs_4_
  44.0 0.6 gather.1
  44.6 1.6 %collective-permute-start.17 = (f32[9,16,256]{2,1,0:T(8,128)S(1)}, f32[9,16,256]{2,1,0:T(8,128)S(1)}, u32[]{:S(2)}, u32[]{:S(2)}) collective-permute-start(f32[9,16,256]{2,1,0:T(8,128)S(1)} %get-tuple-element.74), channel_id=1, source_target_pairs={{0,96},{32,64},{64,32},{96,0},{1,97},{33,65},{65,33},{97,1},{2,98}... | collective-permute-start | bytes 442376 | tf_op jit(solution)/shard_map/ppermute | solution.py:101
  46.2 0.0 collective-permute-start.16
  46.2 2.0 %stage_3.1 = (f32[5,32,16,256]{3,2,1,0:T(8,128)S(1)}, f32[15,16,256]{2,1,0:T(8,128)S(1)}, f32[15,16,256]{2,1,0:T(8,128)S(1)}, f32[32,7,256]{2,1,0:T(8,128)S(1)}, f32[32,7,256]{2,1,0:T(8,128)S(1)}) custom-call(f32[5,32,16,256]{3,2,1,0:T(8,128)S(1)} %get-tuple-element.60.refs_0_.refs_7_, f32[49,8,256]{2,1,0:T(8,128)S(1)} %collective-permute-done.8.refs_4_.refs_1_, ...), custom_call_target="tpu_custom_call" | custom-call | tf_op jit(solution)/shard_map/stage_3/pallas_call | solution.py:110
  48.2 0.1 collective-permute-start.12
  48.3 2.7 %collective-permute-done.17.refs_2_ = f32[9,16,256]{2,1,0:T(8,128)S(1)} collective-permute-done((f32[9,16,256]{2,1,0:T(8,128)S(1)}, f32[9,16,256]{2,1,0:T(8,128)S(1)}, u32[]{:S(2)}, u32[]{:S(2)}) %collective-permute-start.17) | collective-permute-done | bytes 147488 | tf_op jit(solution)/shard_map/ppermute | solution.py:101
  51.1 0.3 collective-permute-done.16.refs_1_
  51.3 0.2 widen.1
  51.5 1.1 %collective-permute-start.23 = (f32[57,8,256]{2,1,0:T(8,128)S(1)}, f32[57,8,256]{2,1,0:T(8,128)S(1)}, u32[]{:S(2)}, u32[]{:S(2)}) collective-permute-start(f32[57,8,256]{2,1,0:T(8,128)S(1)} %get-tuple-element.82), channel_id=1, source_target_pairs={{0,31},{1,2},{2,1},{3,4},{4,3},{5,6},{6,5},{7,8},{8,7},{9,10},{10,... | collective-permute-start | bytes 1400840 | tf_op jit(solution)/shard_map/ppermute | solution.py:101
  52.6 0.3 collective-permute-start.14
  52.8 1.8 %collective-permute-start.15 = (f32[15,16,256]{2,1,0:T(8,128)S(1)}, f32[15,16,256]{2,1,0:T(8,128)S(1)}, u32[]{:S(2)}, u32[]{:S(2)}) collective-permute-start(f32[15,16,256]{2,1,0:T(8,128)S(1)} %get-tuple-element.72), channel_id=1, source_target_pairs={{0,96},{32,64},{64,32},{96,0},{1,97},{33,65},{65,33},{97,1},{2,98}... | collective-permute-start | bytes 737288 | tf_op jit(solution)/shard_map/ppermute | solution.py:101
  54.6 3.7 %collective-permute-start.13 = (f32[32,7,256]{2,1,0:T(8,128)S(1)}, f32[32,7,256]{2,1,0:T(8,128)S(1)}, u32[]{:S(2)}, u32[]{:S(2)}) collective-permute-start(f32[32,7,256]{2,1,0:T(8,128)S(1)} %get-tuple-element.70), channel_id=1, source_target_pairs={{0,31},{1,2},{2,1},{3,4},{4,3},{5,6},{6,5},{7,8},{8,7},{9,10},{10,... | collective-permute-start | bytes 688136 | tf_op jit(solution)/shard_map/ppermute | solution.py:101
  58.3 0.0 collective-permute-done.12.refs_1_
  58.3 0.0 collective-permute-start.22
  58.3 7.6 %collective-permute-done.13.refs_2_ = f32[32,7,256]{2,1,0:T(8,128)S(1)} collective-permute-done((f32[32,7,256]{2,1,0:T(8,128)S(1)}, f32[32,7,256]{2,1,0:T(8,128)S(1)}, u32[]{:S(2)}, u32[]{:S(2)}) %collective-permute-start.13) | collective-permute-done | bytes 229408 | tf_op jit(solution)/shard_map/ppermute | solution.py:101
  65.9 0.0 collective-permute-done.15.refs_4_
  65.9 2.3 %stage_2.1 = (f32[5,32,16,256]{3,2,1,0:T(8,128)S(1)}, f32[15,16,256]{2,1,0:T(8,128)S(1)}, f32[15,16,256]{2,1,0:T(8,128)S(1)}, f32[32,7,256]{2,1,0:T(8,128)S(1)}, f32[32,7,256]{2,1,0:T(8,128)S(1)}) custom-call(f32[5,32,16,256]{3,2,1,0:T(8,128)S(1)} %get-tuple-element.68.refs_0_, f32[32,7,256]{2,1,0:T(8,128)S(1)} %collective-permute-done.12.refs_1_, ...), custom_call_target="tpu_custom_call" | custom-call | bytes 134217728 | tf_op jit(solution)/shard_map/stage_2/pallas_call | solution.py:110
  68.2 0.1 collective-permute-start.20
  68.3 1.8 %collective-permute-start.21 = (f32[15,16,256]{2,1,0:T(8,128)S(1)}, f32[15,16,256]{2,1,0:T(8,128)S(1)}, u32[]{:S(2)}, u32[]{:S(2)}) collective-permute-start(f32[15,16,256]{2,1,0:T(8,128)S(1)} %get-tuple-element.80), channel_id=1, source_target_pairs={{0,96},{32,64},{64,32},{96,0},{1,97},{33,65},{65,33},{97,1},{2,98}... | collective-permute-start | bytes 737288 | tf_op jit(solution)/shard_map/ppermute | solution.py:101
  70.1 0.0 collective-permute-start.18
  70.1 0.0 collective-permute-done.23.refs_2_
  70.1 1.8 %collective-permute-start.19 = (f32[32,7,256]{2,1,0:T(8,128)S(1)}, f32[32,7,256]{2,1,0:T(8,128)S(1)}, u32[]{:S(2)}, u32[]{:S(2)}) collective-permute-start(f32[32,7,256]{2,1,0:T(8,128)S(1)} %get-tuple-element.78), channel_id=1, source_target_pairs={{0,31},{1,2},{2,1},{3,4},{4,3},{5,6},{6,5},{7,8},{8,7},{9,10},{10,... | collective-permute-start | bytes 688136 | tf_op jit(solution)/shard_map/ppermute | solution.py:101
  71.9 0.0 collective-permute-done.22.refs_1_
  71.9 5.2 %source.1 = (f32[5,38,16,256]{3,2,1,0:T(8,128)S(1)}, f32[32,16,256]{2,1,0:T(8,128)S(1)}) custom-call(f32[50,16,256]{2,1,0:T(8,128)S(1)} %get-tuple-element.81.refs_0_, f32[57,8,256]{2,1,0:T(8,128)S(1)} %collective-permute-done.22.refs_1_, f32[57,8,256]{2,1,0:T(8,128)S(1)} %collective-permute-done.23.refs_2_, bf16[2,256,256]{2,1,0:T(8,128)(2,1)S(1)} %copy-done.6, ...), custom_call_target="tpu_custom_call" | custom-call | tf_op jit(solution)/shard_map/source/pallas_call | solution.py:110
  77.1 2.1 %collective-permute-done.19.refs_2_ = f32[32,7,256]{2,1,0:T(8,128)S(1)} collective-permute-done((f32[32,7,256]{2,1,0:T(8,128)S(1)}, f32[32,7,256]{2,1,0:T(8,128)S(1)}, u32[]{:S(2)}, u32[]{:S(2)}) %collective-permute-start.19) | collective-permute-done | bytes 229408 | tf_op jit(solution)/shard_map/ppermute | solution.py:101
  79.2 0.0 collective-permute-done.20.refs_3_
  79.2 0.0 collective-permute-done.21.refs_4_
  79.2 3.2 %final.1 = f32[5,32,16,256]{3,2,1,0:T(8,128)} custom-call(f32[5,32,16,256]{3,2,1,0:T(8,128)S(1)} %get-tuple-element.76.refs_5_.refs_0_, f32[32,7,256]{2,1,0:T(8,128)S(1)} %collective-permute-done.18.refs_1_, f32[32,7,256]{2,1,0:T(8,128)S(1)} %collective-permute-done.19.refs_2_, f32[15,16,256]{2,1,0:T(8,128)S(1)} %collective-permute-done.20.refs_3_, ...), custom_call_target="tpu_custom_call" | custom-call | tf_op jit(solution)/shard_map/final/pallas_call | solution.py:110
  (16 shorter events, 0.1 us)
Async XLA Ops:
  0.0 6.2 %copy-start.4 = (f32[16,16,512]{2,1,0:T(8,128)S(1)}, f32[16,16,512]{2,1,0:T(8,128)}, u32[]{:S(2)}) copy-start(f32[16,16,512]{2,1,0:T(8,128)} %refs_0_.5) | copy-start | bytes 1572868
  1.1 6.8 %collective-permute-start.1 = (f32[4,16,512]{2,1,0:T(8,128)S(1)}, f32[4,16,512]{2,1,0:T(8,128)S(1)}, u32[]{:S(2)}, u32[]{:S(2)}) collective-permute-start(f32[4,16,512]{2,1,0:T(8,128)S(1)} %get-tuple-element.85), channel_id=1, source_target_pairs={{0,96},{32,64},{64,32},{96,0},{1,97},{33,65},{65,33},{97,1},{2,98}... | collective-permute-start | bytes 393224 | tf_op jit(solution)/shard_map/ppermute | solution.py:101
  4.2 5.0 %collective-permute-start = (f32[4,16,512]{2,1,0:T(8,128)S(1)}, f32[4,16,512]{2,1,0:T(8,128)S(1)}, u32[]{:S(2)}, u32[]{:S(2)}) collective-permute-start(f32[4,16,512]{2,1,0:T(8,128)S(1)} %get-tuple-element.86.refs_1_), channel_id=1, source_target_pairs={{0,32},{32,0},{64,96},{96,64},{1,33},{33,1},{65,97},{97,65},{2,34}... | collective-permute-start | bytes 393224 | tf_op jit(solution)/shard_map/ppermute | solution.py:101
  4.4 1.7 %copy-start = (f32[5,32,16,256]{3,2,1,0:T(8,128)S(1)}, f32[5,32,16,256]{3,2,1,0:T(8,128)}, u32[]{:S(2)}) copy-start(f32[5,32,16,256]{3,2,1,0:T(8,128)} %refs_8_.1) | copy-start | bytes 7864324
  6.1 5.0 %copy-start.1 = (f32[5,32,16,256]{3,2,1,0:T(8,128)S(1)}, f32[5,32,16,256]{3,2,1,0:T(8,128)}, u32[]{:S(2)}) copy-start(f32[5,32,16,256]{3,2,1,0:T(8,128)} %refs_8_.1) | copy-start | bytes 7864324
  6.2 1.2 %copy-start.5 = (s32[16,16,512]{2,1,0:T(8,128)S(1)}, s32[16,16,512]{2,1,0:T(8,128)}, u32[]{:S(2)}) copy-start(s32[16,16,512]{2,1,0:T(8,128)} %refs_1_.1) | copy-start | bytes 1572868
  7.4 10.2 %copy-start.7 = (s32[256]{0:T(256)S(1)}, s32[256]{0:T(256)}, u32[]{:S(2)}) copy-start(s32[256]{0:T(256)} %param.10) | copy-start | bytes 3076
  7.4 10.2 %copy-start.8 = (s32[256]{0:T(256)S(1)}, s32[256]{0:T(256)}, u32[]{:S(2)}) copy-start(s32[256]{0:T(256)} %param.11) | copy-start | bytes 3076
  9.4 18.3 %copy-start.2 = (bf16[2,2,256,256]{3,2,1,0:T(8,128)(2,1)S(1)}, bf16[2,2,256,256]{3,2,1,0:T(8,128)(2,1)}, u32[]{:S(2)}) copy-start(bf16[2,2,256,256]{3,2,1,0:T(8,128)(2,1)} %constant.19.clone.refs_6_.refs_4_) | copy-start | bytes 1572868
  9.4 18.3 %copy-start.3 = (bf16[2,2,128,256]{3,2,1,0:T(8,128)(2,1)S(1)}, bf16[2,2,128,256]{3,2,1,0:T(8,128)(2,1)}, u32[]{:S(2)}) copy-start(bf16[2,2,128,256]{3,2,1,0:T(8,128)(2,1)} %constant.18.clone.refs_5_) | copy-start | bytes 786436
  9.4 8.2 %collective-permute-start.6 = (f32[8,8,512]{2,1,0:T(8,128)S(1)}, f32[8,8,512]{2,1,0:T(8,128)S(1)}, u32[]{:S(2)}, u32[]{:S(2)}) collective-permute-start(f32[8,8,512]{2,1,0:T(8,128)S(1)} %get-tuple-element.52), channel_id=1, source_target_pairs={{0,1},{1,0},{2,3},{3,2},{4,5},{5,4},{6,7},{7,6},{8,9},{9,8},{10,11... | collective-permute-start | bytes 393224 | tf_op jit(solution)/shard_map/ppermute | solution.py:101
  9.5 18.1 %collective-permute-start.5 = (f32[15,16,256]{2,1,0:T(8,128)S(1)}, f32[15,16,256]{2,1,0:T(8,128)S(1)}, u32[]{:S(2)}, u32[]{:S(2)}) collective-permute-start(f32[15,16,256]{2,1,0:T(8,128)S(1)} %get-tuple-element.51), channel_id=1, source_target_pairs={{0,96},{32,64},{64,32},{96,0},{1,97},{33,65},{65,33},{97,1},{2,98}... | collective-permute-start | bytes 737288 | tf_op jit(solution)/shard_map/ppermute | solution.py:101
  11.1 16.6 %collective-permute-start.4 = (f32[15,16,256]{2,1,0:T(8,128)S(1)}, f32[15,16,256]{2,1,0:T(8,128)S(1)}, u32[]{:S(2)}, u32[]{:S(2)}) collective-permute-start(f32[15,16,256]{2,1,0:T(8,128)S(1)} %get-tuple-element.45.refs_2_), channel_id=1, source_target_pairs={{0,32},{32,0},{64,96},{96,64},{1,33},{33,1},{65,97},{97,65},{2,34}... | collective-permute-start | bytes 737288 | tf_op jit(solution)/shard_map/ppermute | solution.py:101
  11.2 16.5 %collective-permute-start.2 = (f32[32,7,256]{2,1,0:T(8,128)S(1)}, f32[32,7,256]{2,1,0:T(8,128)S(1)}, u32[]{:S(2)}, u32[]{:S(2)}) collective-permute-start(f32[32,7,256]{2,1,0:T(8,128)S(1)} %get-tuple-element.49), channel_id=1, source_target_pairs={{0,1},{1,0},{2,3},{3,2},{4,5},{5,4},{6,7},{7,6},{8,9},{9,8},{10,11... | collective-permute-start | bytes 688136 | tf_op jit(solution)/shard_map/ppermute | solution.py:101
  11.4 16.3 %collective-permute-start.3 = (f32[32,7,256]{2,1,0:T(8,128)S(1)}, f32[32,7,256]{2,1,0:T(8,128)S(1)}, u32[]{:S(2)}, u32[]{:S(2)}) collective-permute-start(f32[32,7,256]{2,1,0:T(8,128)S(1)} %get-tuple-element.50.refs_2_), channel_id=1, source_target_pairs={{0,31},{1,2},{2,1},{3,4},{4,3},{5,6},{6,5},{7,8},{8,7},{9,10},{10,... | collective-permute-start | bytes 688136 | tf_op jit(solution)/shard_map/ppermute | solution.py:101
  17.6 7.7 %collective-permute-start.7 = (f32[8,8,512]{2,1,0:T(8,128)S(1)}, f32[8,8,512]{2,1,0:T(8,128)S(1)}, u32[]{:S(2)}, u32[]{:S(2)}) collective-permute-start(f32[8,8,512]{2,1,0:T(8,128)S(1)} %get-tuple-element.53), channel_id=1, source_target_pairs={{0,31},{1,2},{2,1},{3,4},{4,3},{5,6},{6,5},{7,8},{8,7},{9,10},{10,... | collective-permute-start | bytes 393224 | tf_op jit(solution)/shard_map/ppermute | solution.py:101
  29.6 14.5 %collective-permute-start.10 = (f32[25,16,256]{2,1,0:T(8,128)S(1)}, f32[25,16,256]{2,1,0:T(8,128)S(1)}, u32[]{:S(2)}, u32[]{:S(2)}) collective-permute-start(f32[25,16,256]{2,1,0:T(8,128)S(1)} %get-tuple-element.63), channel_id=1, source_target_pairs={{0,32},{32,0},{64,96},{96,64},{1,33},{33,1},{65,97},{97,65},{2,34}... | collective-permute-start | bytes 1228808 | tf_op jit(solution)/shard_map/ppermute | solution.py:101
  31.7 12.4 %collective-permute-start.11 = (f32[25,16,256]{2,1,0:T(8,128)S(1)}, f32[25,16,256]{2,1,0:T(8,128)S(1)}, u32[]{:S(2)}, u32[]{:S(2)}) collective-permute-start(f32[25,16,256]{2,1,0:T(8,128)S(1)} %get-tuple-element.64), channel_id=1, source_target_pairs={{0,96},{32,64},{64,32},{96,0},{1,97},{33,65},{65,33},{97,1},{2,98}... | collective-permute-start | bytes 1228808 | tf_op jit(solution)/shard_map/ppermute | solution.py:101
  33.4 2.2 %collective-permute-start.8 = (f32[49,8,256]{2,1,0:T(8,128)S(1)}, f32[49,8,256]{2,1,0:T(8,128)S(1)}, u32[]{:S(2)}, u32[]{:S(2)}) collective-permute-start(f32[49,8,256]{2,1,0:T(8,128)S(1)} %get-tuple-element.61), channel_id=1, source_target_pairs={{0,1},{1,0},{2,3},{3,2},{4,5},{5,4},{6,7},{7,6},{8,9},{9,8},{10,11... | collective-permute-start | bytes 1204232 | tf_op jit(solution)/shard_map/ppermute | solution.py:101
  33.4 10.6 %collective-permute-start.9 = (f32[49,8,256]{2,1,0:T(8,128)S(1)}, f32[49,8,256]{2,1,0:T(8,128)S(1)}, u32[]{:S(2)}, u32[]{:S(2)}) collective-permute-start(f32[49,8,256]{2,1,0:T(8,128)S(1)} %get-tuple-element.62), channel_id=1, source_target_pairs={{0,31},{1,2},{2,1},{3,4},{4,3},{5,6},{6,5},{7,8},{8,7},{9,10},{10,... | collective-permute-start | bytes 1204232 | tf_op jit(solution)/shard_map/ppermute | solution.py:101
  44.6 6.4 %collective-permute-start.17 = (f32[9,16,256]{2,1,0:T(8,128)S(1)}, f32[9,16,256]{2,1,0:T(8,128)S(1)}, u32[]{:S(2)}, u32[]{:S(2)}) collective-permute-start(f32[9,16,256]{2,1,0:T(8,128)S(1)} %get-tuple-element.74), channel_id=1, source_target_pairs={{0,96},{32,64},{64,32},{96,0},{1,97},{33,65},{65,33},{97,1},{2,98}... | collective-permute-start | bytes 442376 | tf_op jit(solution)/shard_map/ppermute | solution.py:101
  46.2 5.1 %collective-permute-start.16 = (f32[9,16,256]{2,1,0:T(8,128)S(1)}, f32[9,16,256]{2,1,0:T(8,128)S(1)}, u32[]{:S(2)}, u32[]{:S(2)}) collective-permute-start(f32[9,16,256]{2,1,0:T(8,128)S(1)} %get-tuple-element.67.refs_8_), channel_id=1, source_target_pairs={{0,32},{32,0},{64,96},{96,64},{1,33},{33,1},{65,97},{97,65},{2,34}... | collective-permute-start | bytes 442376 | tf_op jit(solution)/shard_map/ppermute | solution.py:101
  48.2 10.1 %collective-permute-start.12 = (f32[32,7,256]{2,1,0:T(8,128)S(1)}, f32[32,7,256]{2,1,0:T(8,128)S(1)}, u32[]{:S(2)}, u32[]{:S(2)}) collective-permute-start(f32[32,7,256]{2,1,0:T(8,128)S(1)} %get-tuple-element.69), channel_id=1, source_target_pairs={{0,1},{1,0},{2,3},{3,2},{4,5},{5,4},{6,7},{7,6},{8,9},{9,8},{10,11... | collective-permute-start | bytes 688136 | tf_op jit(solution)/shard_map/ppermute | solution.py:101
  51.5 18.6 %collective-permute-start.23 = (f32[57,8,256]{2,1,0:T(8,128)S(1)}, f32[57,8,256]{2,1,0:T(8,128)S(1)}, u32[]{:S(2)}, u32[]{:S(2)}) collective-permute-start(f32[57,8,256]{2,1,0:T(8,128)S(1)} %get-tuple-element.82), channel_id=1, source_target_pairs={{0,31},{1,2},{2,1},{3,4},{4,3},{5,6},{6,5},{7,8},{8,7},{9,10},{10,... | collective-permute-start | bytes 1400840 | tf_op jit(solution)/shard_map/ppermute | solution.py:101
  52.6 13.3 %collective-permute-start.14 = (f32[15,16,256]{2,1,0:T(8,128)S(1)}, f32[15,16,256]{2,1,0:T(8,128)S(1)}, u32[]{:S(2)}, u32[]{:S(2)}) collective-permute-start(f32[15,16,256]{2,1,0:T(8,128)S(1)} %get-tuple-element.71), channel_id=1, source_target_pairs={{0,32},{32,0},{64,96},{96,64},{1,33},{33,1},{65,97},{97,65},{2,34}... | collective-permute-start | bytes 737288 | tf_op jit(solution)/shard_map/ppermute | solution.py:101
  52.8 13.0 %collective-permute-start.15 = (f32[15,16,256]{2,1,0:T(8,128)S(1)}, f32[15,16,256]{2,1,0:T(8,128)S(1)}, u32[]{:S(2)}, u32[]{:S(2)}) collective-permute-start(f32[15,16,256]{2,1,0:T(8,128)S(1)} %get-tuple-element.72), channel_id=1, source_target_pairs={{0,96},{32,64},{64,32},{96,0},{1,97},{33,65},{65,33},{97,1},{2,98}... | collective-permute-start | bytes 737288 | tf_op jit(solution)/shard_map/ppermute | solution.py:101
  54.6 11.3 %collective-permute-start.13 = (f32[32,7,256]{2,1,0:T(8,128)S(1)}, f32[32,7,256]{2,1,0:T(8,128)S(1)}, u32[]{:S(2)}, u32[]{:S(2)}) collective-permute-start(f32[32,7,256]{2,1,0:T(8,128)S(1)} %get-tuple-element.70), channel_id=1, source_target_pairs={{0,31},{1,2},{2,1},{3,4},{4,3},{5,6},{6,5},{7,8},{8,7},{9,10},{10,... | collective-permute-start | bytes 688136 | tf_op jit(solution)/shard_map/ppermute | solution.py:101
  58.3 13.6 %collective-permute-start.22 = (f32[57,8,256]{2,1,0:T(8,128)S(1)}, f32[57,8,256]{2,1,0:T(8,128)S(1)}, u32[]{:S(2)}, u32[]{:S(2)}) collective-permute-start(f32[57,8,256]{2,1,0:T(8,128)S(1)} %get-tuple-element.75.refs_8_), channel_id=1, source_target_pairs={{0,1},{1,0},{2,3},{3,2},{4,5},{5,4},{6,7},{7,6},{8,9},{9,8},{10,11... | collective-permute-start | bytes 1400840 | tf_op jit(solution)/shard_map/ppermute | solution.py:101
  65.9 6.0 %copy-start.6 = (bf16[2,256,256]{2,1,0:T(8,128)(2,1)S(1)}, bf16[2,256,256]{2,1,0:T(8,128)(2,1)}, u32[]{:S(2)}) copy-start(bf16[2,256,256]{2,1,0:T(8,128)(2,1)} %constant.20.clone.refs_3_) | copy-start | bytes 786436
  68.2 11.1 %collective-permute-start.20 = (f32[15,16,256]{2,1,0:T(8,128)S(1)}, f32[15,16,256]{2,1,0:T(8,128)S(1)}, u32[]{:S(2)}, u32[]{:S(2)}) collective-permute-start(f32[15,16,256]{2,1,0:T(8,128)S(1)} %get-tuple-element.79), channel_id=1, source_target_pairs={{0,32},{32,0},{64,96},{96,64},{1,33},{33,1},{65,97},{97,65},{2,34}... | collective-permute-start | bytes 737288 | tf_op jit(solution)/shard_map/ppermute | solution.py:101
  68.3 11.0 %collective-permute-start.21 = (f32[15,16,256]{2,1,0:T(8,128)S(1)}, f32[15,16,256]{2,1,0:T(8,128)S(1)}, u32[]{:S(2)}, u32[]{:S(2)}) collective-permute-start(f32[15,16,256]{2,1,0:T(8,128)S(1)} %get-tuple-element.80), channel_id=1, source_target_pairs={{0,96},{32,64},{64,32},{96,0},{1,97},{33,65},{65,33},{97,1},{2,98}... | collective-permute-start | bytes 737288 | tf_op jit(solution)/shard_map/ppermute | solution.py:101
  70.1 7.0 %collective-permute-start.18 = (f32[32,7,256]{2,1,0:T(8,128)S(1)}, f32[32,7,256]{2,1,0:T(8,128)S(1)}, u32[]{:S(2)}, u32[]{:S(2)}) collective-permute-start(f32[32,7,256]{2,1,0:T(8,128)S(1)} %get-tuple-element.77), channel_id=1, source_target_pairs={{0,1},{1,0},{2,3},{3,2},{4,5},{5,4},{6,7},{7,6},{8,9},{9,8},{10,11... | collective-permute-start | bytes 688136 | tf_op jit(solution)/shard_map/ppermute | solution.py:101
  70.1 9.1 %collective-permute-start.19 = (f32[32,7,256]{2,1,0:T(8,128)S(1)}, f32[32,7,256]{2,1,0:T(8,128)S(1)}, u32[]{:S(2)}, u32[]{:S(2)}) collective-permute-start(f32[32,7,256]{2,1,0:T(8,128)S(1)} %get-tuple-element.78), channel_id=1, source_target_pairs={{0,31},{1,2},{2,1},{3,4},{4,3},{5,6},{6,5},{7,8},{8,7},{9,10},{10,... | collective-permute-start | bytes 688136 | tf_op jit(solution)/shard_map/ppermute | solution.py:101

commit v3 on v0

v3 whole, which is shorter than its diff:
```python
import math

import numpy as np

import jax
import jax.numpy as jnp
from jax import lax
from jax.experimental import pallas as pl
from jax.experimental.pallas import tpu as pltpu
from jax.sharding import PartitionSpec as P

HMAX = 4
drp_coeffs = (0.770882380518, -0.166705904415, 0.02084314277)
mach_number = 0.5
time_step = 0.7
source_gain = 4.0
radial_step = 2.0
hub_ratio = 1.6

F32 = jnp.float32
BF16 = jnp.bfloat16
VM = pl.BlockSpec(memory_space=pltpu.VMEM)
ANY = pl.BlockSpec(memory_space=pl.ANY)
PARAMS = pltpu.CompilerParams(vmem_limit_bytes=24 * 1024 * 1024)
GROUP = 8
RIM = 4
COST = 1 << 27


def np_split(matrix):
    hi = matrix.astype(np.float32).astype(BF16)
    lo = (matrix - hi.astype(np.float64)).astype(np.float32).astype(BF16)
    return hi, lo


def filter_table():
    table = np.zeros((HMAX + 1, HMAX))
    for h in range(1, HMAX + 1):
        weights = [math.exp(-2.0 * k * k / (h * h)) if k <= h else 0.0 for k in range(HMAX + 1)]
        total = weights[0] + 2.0 * sum(weights[1:])
        table[:, h - 1] = [w / total for w in weights]
    return table


def radial_rows(na_total, radial):
    base = na_total / (2.0 * math.pi)
    radius = base / hub_ratio + radial_step * (np.arange(radial) + 0.5)
    return base / radius, 1.0 / radius


def radial_matrices(na_total, radial):
    diff = np.zeros((radial, radial))
    for s, a in zip((1, 2, 3), drp_coeffs):
        for j in range(radial):
            if j + s < radial:
                diff[j + s, j] += a / radial_step
            if j - s >= 0:
                diff[j - s, j] -= a / radial_step
    with_r = diff + np.diag(radial_rows(na_total, radial)[1])
    return np.stack([np.stack(np_split(with_r)), np.stack(np_split(diff))])


def azimuth_matrices(cols):
    packed = GROUP * 6
    full = np.zeros((2, GROUP * cols, GROUP * cols + 2 * packed))
    for which in range(2):
        for x in range(GROUP):
            for i in range(cols):
                for s, a in zip((1, 2, 3), drp_coeffs):
                    for j, sign in ((i + s, 1.0), (i - s, -1.0)):
                        if 0 <= j < cols:
                            at = x * cols + j
                        else:
                            m = j + 3 if j < 0 else j - cols
                            tile, row = (x % 4, m) if x % 4 < 3 else (m, 3)
                            at = GROUP * cols + (x // 4 * 3 + tile) * 8 + row + 4 * which
                            at += packed if j >= cols else 0
                        full[which, x * cols + i, at] += sign * a
    return np.stack([np.stack(np_split(full[w])) for w in range(2)])


def split(x):
    hi = x.astype(BF16)
    return hi, (x - hi.astype(F32)).astype(BF16)


def dot(a, b):
    return lax.dot_general(a, b, (((1,), (0,)), ((), ())), preferred_element_type=F32)


def is_even(axis):
    return lax.rem(lax.axis_index(axis), 2) == 0


def swap(to_a, to_b, axis):
    devices = lax.axis_size(axis)
    pairs_a = [(i, i ^ 1) for i in range(devices)]
    pairs_b = [(i, (i - 1) % devices if i % 2 == 0 else (i + 1) % devices) for i in range(devices)]
    return lax.ppermute(to_a, axis, pairs_a), lax.ppermute(to_b, axis, pairs_b)


def swap_b(value, axis):
    devices = lax.axis_size(axis)
    pairs = [(i, (i - 1) % devices if i % 2 == 0 else (i + 1) % devices) for i in range(devices)]
    return (lax.ppermute(value, axis, pairs),)


def full_specs(body, outs, args, scratch=(), name=None, in_specs=None, out_specs=None, after=(), cost=0, alias=None):
    skip = len(args)

    def run(*refs):
        body(*refs[:skip], *refs[skip + len(after) :])

    return pl.pallas_call(
        run,
        out_shape=[jax.ShapeDtypeStruct(s, d) for s, d in outs],
        in_specs=(in_specs or [VM] * skip) + [ANY] * len(after),
        input_output_aliases=alias or {},
        out_specs=out_specs or [VM] * len(outs),
        scratch_shapes=[pltpu.VMEM(*s) if isinstance(s, tuple) else s for s in scratch],
        compiler_params=PARAMS,
        name=name,
        cost_estimate=pl.CostEstimate(flops=0, bytes_accessed=cost, transcendentals=0),
    )(*args, *after)


def route_body(owner_ref, target_ref, pick_ref, cells_ref, own_ref):
    n_ax, n_az = lax.axis_size("ax"), lax.axis_size("az")
    ax, az = lax.axis_index("ax"), lax.axis_index("az")
    step_x = jnp.where(lax.rem(ax, 2) == 0, 1, -1)
    step_z = jnp.where(lax.rem(az, 2) == 0, 1, -1)
    me = ax * n_az + az
    b_x = ax - step_x
    ids = [
        (ax + step_x) * n_az + az,
        jnp.where((b_x >= 0) & (b_x < n_ax), b_x * n_az + az, -1),
        ax * n_az + lax.rem(az + step_z + n_az, n_az),
        ax * n_az + lax.rem(az - step_z + n_az, n_az),
    ]
    owner = owner_ref[...]
    target = target_ref[...]
    ncols = owner.shape[1]
    most = ncols // 2
    own_ref[...] = jnp.where(owner == me, target, -1)
    row = lax.broadcasted_iota(jnp.int32, (8, ncols), 0)
    marks = jnp.zeros((8, ncols), F32)
    for d, i in enumerate(ids):
        marks = jnp.where((row == d) & (owner == i), 1.0, marks)
    before = lax.broadcasted_iota(jnp.int32, (ncols, ncols), 0) < lax.broadcasted_iota(jnp.int32, (ncols, ncols), 1)
    rank = dot(marks.astype(BF16), jnp.where(before, 1.0, 0.0).astype(BF16))
    coarse = (target // 32).astype(F32)
    fine = (target % 32).astype(F32)
    digits = jnp.where(row == 0, coarse, jnp.where(row == 1, fine, 0.0)).astype(BF16)
    slot = lax.broadcasted_iota(jnp.int32, (most, ncols), 0).astype(F32)
    for d in range(4):
        wanted = jnp.where(marks[d : d + 1] > 0.0, rank[d : d + 1], -1.0)
        pick = jnp.where(slot == wanted, 1.0, 0.0).astype(BF16)
        pick_ref[d * most : (d + 1) * most, :] = pick
        found = lax.dot_general(digits, pick, (((1,), (1,)), ((), ())), preferred_element_type=F32)
        cells_ref[d, :, :] = jnp.zeros(cells_ref.shape[1:], F32)
        cells_ref[d, 0:1, 0:most] = found[0:1] * 32.0 + found[1:2]


def weights_of(h):
    table = filter_table()
    le = [h <= 1, h <= 2, h <= 3]
    out = []
    for k in range(HMAX + 1):
        value = jnp.full(h.shape, table[k, 3], F32)
        for j in (2, 1, 0):
            if j > 0 and table[k, j] == 0.0 and table[k, j - 1] == 0.0:
                value = jnp.where(le[j], 0.0, value)
                break
            value = jnp.where(le[j], table[k, j], value)
        out.append(value)
    return out


def inner_body(noise_ref, half_ref, first_ref, kept_ref):
    rows = noise_ref.shape[0]
    kept_ref[...] = half_ref[...]
    for x in range(rows):
        w = weights_of(half_ref[x])
        total = w[0] * noise_ref[x]
        for k in range(1, HMAX + 1):
            near = [noise_ref[y] for y in (x - k, x + k) if 0 <= y < rows]
            if near:
                total = total + w[k] * (near[0] + near[1] if len(near) == 2 else near[0])
        first_ref[x] = total


def first_body(inner_ref, half_ref, got_a_ref, got_b_ref, edge_a_ref, first_ref, to_a_ref, to_b_ref, halo):
    n_ax, ax = lax.axis_size("ax"), lax.axis_index("ax")
    even_x, even_z = is_even("ax"), is_even("az")
    rows, _, fine = half_ref.shape
    halo[0] = jnp.where(ax > 0, jnp.where(even_x, got_b_ref[...], got_a_ref[...]), 0.0)
    halo[1] = jnp.where(ax < n_ax - 1, jnp.where(even_x, got_a_ref[...], got_b_ref[...]), 0.0)
    for x in range(HMAX, rows - HMAX):
        first_ref[x] = inner_ref[x]
    for i in range(HMAX):
        w = weights_of(half_ref[i])
        total = inner_ref[i]
        for k in range(i + 1, HMAX + 1):
            total = total + w[k] * halo[0, HMAX + i - k]
        first_ref[i] = total
        x = rows - 1 - i
        w = weights_of(half_ref[x])
        total = inner_ref[x]
        for k in range(i + 1, HMAX + 1):
            total = total + w[k] * halo[1, k - i - 1]
        first_ref[x] = total
    half = rows // 2
    low = lax.broadcasted_iota(jnp.int32, (8, fine), 0) < 4
    for x in range(half):
        last = jnp.where(low, pltpu.roll(first_ref[x, 8:16], 4, 0), first_ref[x + half, 8:16])
        begin = jnp.where(low, first_ref[x, 0:8], pltpu.roll(first_ref[x + half, 0:8], 4, 0))
        to_a = jnp.where(even_z, last, begin)
        to_a_ref[x] = to_a[:, : fine // 2]
        to_a_ref[half + x] = to_a[:, fine // 2 :]
        to_b_ref[x] = jnp.where(even_z, begin, last)
    to_a_ref[2 * half :] = edge_a_ref[...]


def second_body(
    first_ref, half_ref, got_a_ref, got_b_ref, pick_ref, cells_ref,
    own_ref, to_xa, to_xb, to_za, to_zb, wide, fine_hi, fine_lo,
):
    even = is_even("az")
    rows, cols, fine = first_ref.shape
    half = rows // 2
    for x in range(half):
        got_a, got_b = jnp.concatenate([got_a_ref[x], got_a_ref[half + x]], axis=1), got_b_ref[x]
        before = jnp.where(even, got_b, got_a)
        after = jnp.where(even, got_a, got_b)
        wide[x, 0:8] = pltpu.roll(before, 4, 0)
        wide[x + half, 0:8] = before
        wide[x, 24:32] = after
        wide[x + half, 24:32] = pltpu.roll(after, 4, 0)
    lane = lax.broadcasted_iota(jnp.int32, (cols, fine), 1)
    for x in range(rows):
        wide[x, 8:24] = first_ref[x]
    for x in range(rows):
        w = weights_of(half_ref[x])
        total = w[0] * first_ref[x]
        for k in range(1, HMAX + 1):
            total = total + w[k] * (wide[x, 8 - k : 24 - k] + wide[x, 8 + k : 24 + k])
        result = w[0] * total
        for k in range(1, HMAX + 1):
            up = jnp.where(lane < fine - k, pltpu.roll(total, fine - k, 1), 0.0)
            down = jnp.where(lane >= k, pltpu.roll(total, k, 1), 0.0)
            result = result + w[k] * (up + down)
        hi, lo = split(result)
        fine_hi[x * cols : (x + 1) * cols] = hi
        fine_lo[x * cols : (x + 1) * cols] = lo
    radial = own_ref.shape[1]
    above = lax.broadcasted_iota(jnp.int32, (fine, radial), 0) - lax.broadcasted_iota(
        jnp.int32, (fine, radial), 1
    ) * (fine // radial)
    bins = jnp.where((above >= 0) & (above < fine // radial), source_gain, 0.0).astype(BF16)
    binned = dot(fine_hi[...], bins) + dot(fine_lo[...], bins)
    own_ref[...] = binned
    hi, lo = split(binned)
    most = pick_ref.shape[0] // 4
    for d, out in enumerate((to_xa, to_xb, to_za, to_zb)):
        pick = pick_ref[d * most : (d + 1) * most]
        out[0:most] = dot(pick, hi) + dot(pick, lo)
        out[most : most + 8] = cells_ref[d]


def gather_body(
    binned_ref, own_ref, xa, xb, za, zb, k_mid, k_rim, p_mid, p_rim, to_xa, to_xb, to_za, to_zb
):
    mid, cols, radial = p_mid.shape
    cells = (mid + 2 * RIM) * cols
    most = xa.shape[0] - 8

    def onehot(row):
        at = lax.broadcasted_iota(jnp.int32, (cells, row.shape[1]), 0)
        return jnp.where(at == row, 1.0, 0.0).astype(BF16)

    mats = [onehot(own_ref[...])]
    packets = [binned_ref[...]]
    for got in (xa, xb, za, zb):
        mats.append(onehot(got[most : most + 1, 0:most].astype(jnp.int32)))
        packets.append(got[0:most])
    mat = jnp.concatenate(mats, axis=1)
    hi, lo = split(jnp.concatenate(packets, axis=0))
    q = (dot(mat, hi) + dot(mat, lo)).reshape(mid + 2 * RIM, cols, radial)
    p_rim[0:RIM] = k_rim[4, 0:RIM] + q[0:RIM]
    p_mid[...] = k_mid[4] + q[RIM : RIM + mid]
    p_rim[RIM:] = k_rim[4, RIM:] + q[RIM + mid :]
    level = Parts(k_mid, k_rim, p_mid, p_rim)
    write_x(level, to_xa, to_xb)
    write_z(level, to_za, to_zb)


class Whole:
    def __init__(self, ref):
        self.ref = ref
        self.rows = ref.shape[1]

    def row(self, f, x):
        return self.ref[f, x]

    def group(self, f, g):
        if g is None:
            return jnp.concatenate([self.ref[f, 0:RIM], self.ref[f, self.rows - RIM :]], axis=0)
        return self.ref[f, RIM + g * GROUP : RIM + (g + 1) * GROUP]


class Parts:
    def __init__(self, mid, rim, p_mid=None, p_rim=None):
        self.arrays = (mid, rim, p_mid, p_rim)
        self.rows = mid.shape[1] + 2 * RIM

    def pick(self, f):
        mid, rim, p_mid, p_rim = self.arrays
        if f == 4 and p_mid is not None:
            return p_mid, p_rim
        return mid.at[f], rim.at[f]

    def row(self, f, x):
        mid, rim = self.pick(f)
        if RIM <= x < self.rows - RIM:
            return mid[x - RIM]
        return rim[x if x < RIM else x - self.rows + 2 * RIM]

    def group(self, f, g):
        mid, rim = self.pick(f)
        return rim[...] if g is None else mid[g * GROUP : (g + 1) * GROUP]

    def store(self, f, x, value):
        mid, rim = self.pick(f)
        if RIM <= x < self.rows - RIM:
            mid[x - RIM] = value
        else:
            rim[x if x < RIM else x - self.rows + 2 * RIM] = value


def join_last(ut, p):
    low = lax.broadcasted_iota(jnp.int32, ut.shape, 0) < 4
    return jnp.where(low, pltpu.roll(ut, 3, 0), pltpu.roll(p, 7, 0))


def join_first(ut, p):
    low = lax.broadcasted_iota(jnp.int32, ut.shape, 0) < 4
    return jnp.where(low, ut, pltpu.roll(p, 4, 0))


def write_x(level, to_xa, to_xb):
    even = is_even("ax")
    for f in range(5):
        for i in range(3):
            first, last = level.row(f, i), level.row(f, level.rows - 3 + i)
            to_xa[3 * f + i] = jnp.where(even, last, first)
            to_xb[3 * f + i] = jnp.where(even, first, last)


def write_z(level, to_za, to_zb):
    even = is_even("az")
    row = None
    for x in range(0, level.rows, 4):
        first, last = [], []
        for y in range(x, x + 4):
            ut, p = level.row(2, y), level.row(4, y)
            first.append(join_first(ut[0:8], p[0:8]))
            last.append(join_last(ut[8:16], p[8:16]))
        if row is None:
            row = lax.broadcasted_iota(jnp.int32, first[0].shape, 0) % 4 == 3
        for t in range(3):
            shift = 3 - t
            one = jnp.where(row, pltpu.roll(first[3], shift, 0), first[t])
            two = jnp.where(row, pltpu.roll(last[3], shift, 0), last[t])
            to_za[x // 4 * 3 + t] = jnp.where(even, two, one)
            to_zb[x // 4 * 3 + t] = jnp.where(even, one, two)


def edges_body(state, to_xa, to_xb, to_za, to_zb):
    level = Whole(state)
    write_x(level, to_xa, to_xb)
    write_z(level, to_za, to_zb)


def fill_halo(halo, xa, xb):
    n_ax, ax = lax.axis_size("ax"), lax.axis_index("ax")
    even = is_even("ax")
    for f in range(halo.shape[1]):
        a, b = xa[3 * f : 3 * f + 3], xb[3 * f : 3 * f + 3]
        halo[0, f] = jnp.where(ax > 0, jnp.where(even, b, a), 0.0)
        halo[1, f] = jnp.where(ax < n_ax - 1, jnp.where(even, a, b), 0.0)


def inverse_step(cols, radial):
    base = cols * lax.axis_size("az") / (2.0 * math.pi)
    at = lax.broadcasted_iota(jnp.int32, (1, radial), 1).astype(F32)
    return base / (base / hub_ratio + radial_step * (at + 0.5))


def along(row, x):
    total = drp_coeffs[0] * (row(x + 1) - row(x - 1))
    for s in (2, 3):
        total = total + drp_coeffs[s - 1] * (row(x + s) - row(x - s))
    return total


def apply_operator(level, groups, za, zb, tmat, rmat, finish, halo=None):
    even = is_even("az")
    tiles = level.rows // 4 * 3
    rim = RIM // 4 * 3

    def row(f, x):
        if x < 0:
            return halo[0, f, x + 3]
        if x >= level.rows:
            return halo[1, f, x - level.rows]
        return level.row(f, x)

    def beside(g):
        spans = [(0, rim), (tiles - rim, tiles)] if g is None else [(rim + 6 * g, rim + 6 * g + 6)]
        start = za.shape[0] - tiles
        sides = []
        for swap_ab in (False, True):
            for a, b in spans:
                got_a, got_b = za[start + a : start + b], zb[a:b]
                pair = (got_a, got_b) if swap_ab else (got_b, got_a)
                sides.append(jnp.where(even, *pair).reshape((b - a) * 8, za.shape[2]))
        return split(jnp.concatenate(sides, axis=0))

    for g in groups:
        if g is None:
            xs = [*range(RIM), *range(level.rows - RIM, level.rows)]
        else:
            xs = range(RIM + g * GROUP, RIM + (g + 1) * GROUP)
        ut, ur, p = [level.group(f, g) for f in (2, 3, 4)]
        _, cols, radial = ut.shape
        inv_h = inverse_step(cols, radial)
        side_hi, side_lo = beside(g)
        p_hi, p_lo = split(p.reshape(GROUP * cols, radial))
        ut_hi, ut_lo = split(ut.reshape(GROUP * cols, radial))
        ur_hi, ur_lo = split(ur.reshape(GROUP * cols, radial))

        def across(which, hi, lo):
            hi = jnp.concatenate([hi, side_hi], axis=0)
            lo = jnp.concatenate([lo, side_lo], axis=0)
            return dot(tmat[which, 0], hi) + dot(tmat[which, 0], lo) + dot(tmat[which, 1], hi)

        def outward(which, hi, lo):
            return dot(hi, rmat[which, 0]) + dot(lo, rmat[which, 0]) + dot(hi, rmat[which, 1])

        div_tr = across(0, ut_hi, ut_lo) * inv_h + outward(0, ur_hi, ur_lo)
        p_t = across(1, p_hi, p_lo) * inv_h
        p_r = outward(1, p_hi, p_lo)
        for i, x in enumerate(xs):
            part = slice(i * cols, (i + 1) * cols)
            d = [along(lambda y: row(f, y), x) for f in range(5)]
            div = d[1] + div_tr[part]
            finish(
                x,
                [
                    -mach_number * d[0] - div,
                    -mach_number * d[1] - d[4],
                    -mach_number * d[2] - p_t[part],
                    -mach_number * d[3] - p_r[part],
                    -mach_number * d[4] - div,
                ],
            )


def start_body(state, za, zb, xa, xb, tmat, rmat, k_mid, k_rim, halo):
    fill_halo(halo, xa, xb)
    level, out = Whole(state), Parts(k_mid, k_rim)

    def finish(x, tend):
        for f in range(5):
            out.store(f, x, tend[f])

    apply_operator(level, [*range(k_mid.shape[1] // GROUP), None], za, zb, tmat, rmat, finish, halo)


def inner_stage_body(factor, level, base, za, zb, tmat, rmat, out_mid):
    def finish(x, tend):
        for f in range(5):
            out_mid[f, x - RIM] = base.row(f, x) + factor * tend[f]

    apply_operator(level, range(out_mid.shape[1] // GROUP), za, zb, tmat, rmat, finish)


def rim_stage_body(factor, level, base, za, zb, xa, xb, tmat, rmat, out_mid, out_rim, to_xa, to_xb, to_za, to_zb, halo):
    fill_halo(halo, xa, xb)
    out = Parts(out_mid, out_rim)

    def finish(x, tend):
        for f in range(5):
            out.store(f, x, base.row(f, x) + factor * tend[f])

    apply_operator(level, [None], za, zb, tmat, rmat, finish, halo)
    write_x(out, to_xa, to_xb)
    write_z(out, to_za, to_zb)


def last_finish(fields, k, store):
    def finish(x, tend):
        for f in range(5):
            store(f, x, fields[f, x] + time_step * k.row(f, x) + (0.5 * time_step * time_step) * tend[f])

    return finish


def inner_last_body(level, k, fields, za, zb, tmat, rmat, out, result, sems):
    def store(f, x, value):
        result[f, x - RIM] = value

    def copy(g):
        at = g * GROUP
        return pltpu.make_async_copy(
            result.at[:, at : at + GROUP], out.at[:, RIM + at : RIM + at + GROUP], sems.at[g]
        )

    groups = range(result.shape[1] // GROUP)
    for g in groups:
        apply_operator(level, [g], za, zb, tmat, rmat, last_finish(fields, k, store))
        copy(g).start()
    for g in groups:
        copy(g).wait()


def rim_last_body(level, k, fields, za, zb, xa, xb, tmat, rmat, out, halo, result, sems):
    fill_halo(halo, xa, xb)
    rows = level.rows

    def store(f, x, value):
        result[f, x if x < RIM else x - rows + 2 * RIM] = value

    apply_operator(level, [None], za, zb, tmat, rmat, last_finish(fields, k, store), halo)
    copies = [
        pltpu.make_async_copy(result.at[:, 0:RIM], out.at[:, 0:RIM], sems.at[0]),
        pltpu.make_async_copy(result.at[:, RIM:], out.at[:, rows - RIM :], sems.at[1]),
    ]
    for copy in copies:
        copy.start()
    for copy in copies:
        copy.wait()


def local(noise, half_width, owner, target_cell, fields):
    px, pa, fine = noise.shape
    cx, ca, radial = fields.shape[1:]
    ncols = px * pa
    most = ncols // 2
    n_az = lax.axis_size("az")
    inner = cx - 2 * RIM

    block = ((px, pa, fine), F32)
    even = is_even("ax")
    to_a = jnp.where(even, noise[px - HMAX :], noise[:HMAX])
    to_b = jnp.where(even, noise[:HMAX], noise[px - HMAX :])
    noise_a, noise_b = swap(to_a, to_b, "ax")
    send_x, send_z = ((15, ca, radial), F32), ((cx // 4 * 3, 8, radial), F32)
    sends = [send_x, send_x, send_z, send_z]
    xa, xb, za, zb = full_specs(edges_body, sends, [fields], name="edges", after=[to_a])
    uxa, uxb = swap(xa, xb, "ax")
    partial, half_width = full_specs(
        inner_body, [block, ((px, pa, fine), jnp.int32)], [noise, half_width], name="filter_inner", after=[za]
    )
    filtered, to_a, to_b = full_specs(
        first_body,
        [block, ((px + send_z[0][0], 8, fine // 2), F32), ((px // 2, 8, fine), F32)],
        [partial, half_width, noise_a, noise_b, za],
        [((2, HMAX, pa, fine), F32)],
        name="filter_axial",
    )
    got_a, got_b = swap(to_a, to_b, "az")
    (uzb,) = swap_b(zb, "az")
    pick, cells, own = full_specs(
        route_body,
        [((4 * most, ncols), BF16), ((4, 8, radial), F32), ((1, ncols), jnp.int32)],
        [owner.reshape(1, ncols), target_cell.reshape(1, ncols)],
        name="route",
        after=[filtered],
    )
    packet = ((most + 8, radial), F32)
    binned, xa, xb, za, zb = full_specs(
        second_body,
        [((ncols, radial), F32), packet, packet, packet, packet],
        [filtered, half_width, got_a, got_b, pick, cells],
        [((px, 32, fine), F32), ((ncols, fine), BF16), ((ncols, fine), BF16)],
        name="filter_rest",
        cost=COST,
    )
    packets = (*swap(xa, xb, "ax"), *swap(za, zb, "az"))

    tmat = jnp.asarray(azimuth_matrices(ca))
    rmat = jnp.asarray(radial_matrices(float(ca * n_az), radial))
    mid, rim = ((5, inner, ca, radial), F32), ((5, 2 * RIM, ca, radial), F32)
    halo = ((2, 5, 3, ca, radial), F32)
    k_mid, k_rim = full_specs(
        start_body, [mid, rim], [fields, got_a, uzb, uxa, uxb, tmat, rmat], [halo], name="operator", after=[binned]
    )
    p_mid, p_rim, *edges = full_specs(
        gather_body,
        [((inner, ca, radial), F32), ((2 * RIM, ca, radial), F32), *sends],
        [binned, own, *packets, k_mid, k_rim],
        name="gather",
    )
    k = [k_mid, k_rim, p_mid, p_rim]
    level = k
    for factor in (time_step / 4.0, time_step / 3.0):
        size = len(level)
        xa, xb = swap(edges[0], edges[1], "ax")
        za, zb = swap(edges[2], edges[3], "az")

        def body(*refs, factor=factor, size=size):
            inner_stage_body(factor, Parts(*refs[:size]), Parts(*refs[size : size + 4]), *refs[size + 4 :])

        (new_mid,) = full_specs(body, [mid], [*level, *k, za, zb, tmat, rmat], name="stage_inner")

        def body(*refs, factor=factor, size=size):
            rim_stage_body(factor, Parts(*refs[:size]), Parts(*refs[size : size + 4]), *refs[size + 4 :])

        new_rim, *edges = full_specs(
            body, [rim, *sends], [*level, *k, za, zb, xa, xb, tmat, rmat, new_mid], [halo], name="stage_rim"
        )
        level = [new_mid, new_rim]
    xa, xb = swap(edges[0], edges[1], "ax")
    za, zb = swap(edges[2], edges[3], "az")

    def body(*refs):
        inner_last_body(Parts(*refs[:2]), Parts(*refs[2:6]), *refs[6:])

    whole = ((5, cx, ca, radial), F32)
    (out,) = full_specs(
        body,
        [whole],
        [*level, *k, fields, za, zb, tmat, rmat],
        [mid, pltpu.SemaphoreType.DMA((inner // GROUP,))],
        name="final_inner",
        out_specs=[ANY],
    )

    def body(out_in, *refs):
        rim_last_body(Parts(*refs[:2]), Parts(*refs[2:6]), *refs[6:])

    (out,) = full_specs(
        body,
        [whole],
        [out, *level, *k, fields, za, zb, xa, xb, tmat, rmat],
        [halo, rim, pltpu.SemaphoreType.DMA((2,))],
        name="final_rim",
        out_specs=[ANY],
        in_specs=[ANY] + [VM] * 13,
        alias={0: 0},
    )
    return out


def solution(mesh):
    return jax.shard_map(
        local,
        mesh=mesh,
        in_specs=(
            P("ax", "az", None),
            P("ax", "az", None),
            P(("ax", "az")),
            P(("ax", "az")),
            P(None, "ax", "az", None),
        ),
        out_specs=P(None, "ax", "az", None),
        check_vma=False,
    )
```

time: 77.2 us -> 78 us (1.010)
  waiting for transfers between devices: 23.5 us -> 35.6 us
  starting transfers between devices: 33.8 us -> 24.7 us
  local copies, waits for them, and re-layouts: 4.66 us -> 2.63 us
    ppermute x12 -> x11, waiting for transfers between devices: 8.95 us -> 31.6 us  [swap(): lax.ppermute(to_b, axis, pairs_b)]
    ppermute x12 -> x11, starting transfers between devices: 30.6 us -> 14.6 us  [swap(): lax.ppermute(to_b, axis, pairs_b)]
    ppermute x12 -> x11, waiting for transfers between devices: 14.6 us -> 3.97 us  [swap(): lax.ppermute(to_a, axis, pairs_a)]
    ppermute x0 -> x1, starting transfers between devices: none -> 5.99 us  [swap_b(): return (lax.ppermute(value, axis, pairs),)]
    unnamed x22 -> x16, local copies, waits for them, and re-layouts: 4.66 us -> 2.63 us
    ppermute x12 -> x11, starting transfers between devices: 3.24 us -> 4.08 us  [swap(): lax.ppermute(to_a, axis, pairs_a)]
    pallas_call x10 -> x13, Pallas kernels: 13.5 us -> 13.5 us  [full_specs(): pl.pallas_call(run, out_shape=[jax.ShapeDtypeStruct(s, d) for s, d in out...]
  transfers between devices with their start and end apart: 24 -> 23, of which waited for: 10 -> 11; matrix products, arithmetic and copies ran while one was open for 0% -> 0% of each run, Pallas kernels for 7% -> 13%
where the time goes in v3:
time: 78 us; the launch traced here: 77.8 us
  waiting for transfers between devices  35.6 us (46%)
  starting transfers between devices  24.7 us (32%)
  Pallas kernels  13.5 us (17%)
  local copies, waits for them, and re-layouts  2.63 us (3%)
  other arithmetic  1.05 us (1%)
    ppermute x11, waiting for transfers between devices, swap(): lax.ppermute(to_b, axis, pairs_b)  31.6 us
    ppermute x11, starting transfers between devices, swap(): lax.ppermute(to_b, axis, pairs_b)  14.6 us
    pallas_call x13, Pallas kernels, full_specs(): pl.pallas_call(run, out_shape=[jax.ShapeDtypeStruct(s, d) for s, d in out...  13.5 us
    ppermute x1, starting transfers between devices, swap_b(): return (lax.ppermute(value, axis, pairs),)  5.99 us
    ppermute x11, starting transfers between devices, swap(): lax.ppermute(to_a, axis, pairs_a)  4.08 us
    ppermute x11, waiting for transfers between devices, swap(): lax.ppermute(to_a, axis, pairs_a)  3.97 us
    unnamed x16, local copies, waits for them, and re-layouts  2.63 us
  transfers between devices with their start and end apart: 23, of which 11 were waited for; matrix products, arithmetic and copies ran while one was open for 0% of the time, Pallas kernels for 13%

profile of v3, /device:TPU:0, one launch (start us, length us, event | category | flops | bytes accessed | tf_op | source)
XLA Modules:
  0.0 77.8 jit_solution(14525137176250067222)
XLA Ops:
  0.0 1.0 %slice_select_fusion = (f32[4,16,512]{2,1,0:T(8,128)S(1)}, f32[4,16,512]{2,1,0:T(8,128)S(1)}) fusion(f32[16,16,512]{2,1,0:T(8,128)} %refs_0_.4, pred[]{:T(512)S(6)} %eq.3), kind=kLoop, calls=%fused_computation | loop fusion | flops 65536 | bytes 524289 | tf_op jit(solution)/shard_map/jit(_where)/select_n | solution.py:556
  1.1 3.2 %collective-permute-start.1 = (f32[4,16,512]{2,1,0:T(8,128)S(1)}, f32[4,16,512]{2,1,0:T(8,128)S(1)}, u32[]{:S(2)}, u32[]{:S(2)}) collective-permute-start(f32[4,16,512]{2,1,0:T(8,128)S(1)} %get-tuple-element.75), channel_id=1, source_target_pairs={{0,96},{32,64},{64,32},{96,0},{1,97},{33,65},{65,33},{97,1},{2,98}... | collective-permute-start | bytes 393224 | tf_op jit(solution)/shard_map/ppermute | solution.py:99
  4.2 0.1 collective-permute-start
  4.4 1.7 %copy-done = f32[5,32,16,256]{3,2,1,0:T(8,128)S(1)} copy-done((f32[5,32,16,256]{3,2,1,0:T(8,128)S(1)}, f32[5,32,16,256]{3,2,1,0:T(8,128)}, u32[]{:S(2)}) %copy-start) | copy-done | bytes 2621464
  6.1 0.1 edges.1
  6.2 0.0 copy-start.1
  6.3 0.0 copy-start.2
  6.3 0.0 copy-start.3
  6.3 0.9 %copy-done.5 = s32[16,16,512]{2,1,0:T(8,128)S(1)} copy-done((s32[16,16,512]{2,1,0:T(8,128)S(1)}, s32[16,16,512]{2,1,0:T(8,128)}, u32[]{:S(2)}) %copy-start.5) | copy-done | bytes 524312
  7.2 0.5 filter_inner.1
  7.6 0.1 collective-permute-done.1.refs_3_
  7.7 1.5 %collective-permute-done.refs_2_ = f32[4,16,512]{2,1,0:T(8,128)S(1)} collective-permute-done((f32[4,16,512]{2,1,0:T(8,128)S(1)}, f32[4,16,512]{2,1,0:T(8,128)S(1)}, u32[]{:S(2)}, u32[]{:S(2)}) %collective-permute-start) | collective-permute-done | bytes 131104 | tf_op jit(solution)/shard_map/ppermute | solution.py:99
  9.2 0.2 filter_axial.1
  9.4 0.1 collective-permute-start.2
  9.5 0.4 collective-permute-start.4
  9.9 6.0 %collective-permute-start.3 = (f32[24,8,256]{2,1,0:T(8,128)S(1)}, f32[24,8,256]{2,1,0:T(8,128)S(1)}, u32[]{:S(2)}, u32[]{:S(2)}) collective-permute-start(f32[24,8,256]{2,1,0:T(8,128)S(1)} %get-tuple-element.44), channel_id=1, source_target_pairs={{0,31},{1,2},{2,1},{3,4},{4,3},{5,6},{6,5},{7,8},{8,7},{9,10},{10,... | collective-permute-start | bytes 589832 | tf_op jit(solution)/shard_map/ppermute | solution.py:105
  15.9 0.0 collective-permute-start.6
  15.9 1.4 %collective-permute-start.5 = (f32[15,16,256]{2,1,0:T(8,128)S(1)}, f32[15,16,256]{2,1,0:T(8,128)S(1)}, u32[]{:S(2)}, u32[]{:S(2)}) collective-permute-start(f32[15,16,256]{2,1,0:T(8,128)S(1)} %get-tuple-element.46), channel_id=1, source_target_pairs={{0,96},{32,64},{64,32},{96,0},{1,97},{33,65},{65,33},{97,1},{2,98}... | collective-permute-start | bytes 737288 | tf_op jit(solution)/shard_map/ppermute | solution.py:99
  17.4 0.3 route.1
  17.7 6.0 %collective-permute-done.6.refs_3_ = f32[8,8,512]{2,1,0:T(8,128)S(1)} collective-permute-done((f32[8,8,512]{2,1,0:T(8,128)S(1)}, f32[8,8,512]{2,1,0:T(8,128)S(1)}, u32[]{:S(2)}, u32[]{:S(2)}) %collective-permute-start.6) | collective-permute-done | bytes 131104 | tf_op jit(solution)/shard_map/ppermute | solution.py:99
  23.6 0.0 collective-permute-done.2.refs_2_.refs_1_
  23.6 2.3 %filter_rest.1 = (f32[256,256]{1,0:T(8,128)S(1)}, f32[136,256]{1,0:T(8,128)S(1)}, f32[136,256]{1,0:T(8,128)S(1)}, f32[136,256]{1,0:T(8,128)S(1)}, f32[136,256]{1,0:T(8,128)S(1)}) custom-call(f32[16,16,512]{2,1,0:T(8,128)S(1)} %get-tuple-element.47.refs_2_.refs_0_, s32[16,16,512]{2,1,0:T(8,128)S(1)} %get-tuple-element.42.refs_1_, ...), custom_call_target="tpu_custom_call" | custom-call | bytes 134217728 | tf_op jit(solution)/shard_map/filter_rest/pallas_call | solution.py:114
  26.0 1.8 %collective-permute-start.7 = (f32[136,256]{1,0:T(8,128)S(1)}, f32[136,256]{1,0:T(8,128)S(1)}, u32[]{:S(2)}, u32[]{:S(2)}) collective-permute-start(f32[136,256]{1,0:T(8,128)S(1)} %get-tuple-element.55), channel_id=1, source_target_pairs={{0,32},{32,0},{64,96},{96,64},{1,33},{33,1},{65,97},{97,65},{2,34}... | collective-permute-start | bytes 417800 | tf_op jit(solution)/shard_map/ppermute | solution.py:99
  27.7 1.5 %collective-permute-start.8 = (f32[136,256]{1,0:T(8,128)S(1)}, f32[136,256]{1,0:T(8,128)S(1)}, u32[]{:S(2)}, u32[]{:S(2)}) collective-permute-start(f32[136,256]{1,0:T(8,128)S(1)} %get-tuple-element.56), channel_id=1, source_target_pairs={{0,96},{32,64},{64,32},{96,0},{1,97},{33,65},{65,33},{97,1},{2,98}... | collective-permute-start | bytes 417800 | tf_op jit(solution)/shard_map/ppermute | solution.py:99
  29.2 0.0 collective-permute-done.3.refs_2_
  29.2 0.0 collective-permute-start.9
  29.2 0.0 collective-permute-done.4.refs_3_
  29.2 1.6 %collective-permute-start.10 = (f32[136,256]{1,0:T(8,128)S(1)}, f32[136,256]{1,0:T(8,128)S(1)}, u32[]{:S(2)}, u32[]{:S(2)}) collective-permute-start(f32[136,256]{1,0:T(8,128)S(1)} %get-tuple-element.58), channel_id=1, source_target_pairs={{0,31},{1,2},{2,1},{3,4},{4,3},{5,6},{6,5},{7,8},{8,7},{9,10},{10,... | collective-permute-start | bytes 417800 | tf_op jit(solution)/shard_map/ppermute | solution.py:99
  30.8 0.0 collective-permute-done.5.refs_4_
  30.9 1.6 %operator.1 = (f32[5,24,16,256]{3,2,1,0:T(8,128)S(1)}, f32[5,8,16,256]{3,2,1,0:T(8,128)S(1)}) custom-call(f32[5,32,16,256]{3,2,1,0:T(8,128)S(1)} %copy-done.1, f32[40,8,256]{2,1,0:T(8,128)S(1)} %collective-permute-done.2.refs_2_.refs_1_, f32[24,8,256]{2,1,0:T(8,128)S(1)} %collective-permute-done.3.refs_2_, ...), custom_call_target="tpu_custom_call" | custom-call | tf_op jit(solution)/shard_map/operator/pallas_call | solution.py:114
  32.5 0.0 collective-permute-done.7.refs_2_
  32.5 1.5 %collective-permute-done.8.refs_3_ = f32[136,256]{1,0:T(8,128)S(1)} collective-permute-done((f32[136,256]{1,0:T(8,128)S(1)}, f32[136,256]{1,0:T(8,128)S(1)}, u32[]{:S(2)}, u32[]{:S(2)}) %collective-permute-start.8) | collective-permute-done | bytes 139296 | tf_op jit(solution)/shard_map/ppermute | solution.py:99
  34.0 0.0 collective-permute-done.9.refs_4_
  34.0 3.1 %collective-permute-done.10.refs_5_ = f32[136,256]{1,0:T(8,128)S(1)} collective-permute-done((f32[136,256]{1,0:T(8,128)S(1)}, f32[136,256]{1,0:T(8,128)S(1)}, u32[]{:S(2)}, u32[]{:S(2)}) %collective-permute-start.10) | collective-permute-done | bytes 139296 | tf_op jit(solution)/shard_map/ppermute | solution.py:99
  37.1 0.6 gather.1
  37.7 0.1 collective-permute-start.13
  37.8 1.8 %collective-permute-start.14 = (f32[15,16,256]{2,1,0:T(8,128)S(1)}, f32[15,16,256]{2,1,0:T(8,128)S(1)}, u32[]{:S(2)}, u32[]{:S(2)}) collective-permute-start(f32[15,16,256]{2,1,0:T(8,128)S(1)} %get-tuple-element.64), channel_id=1, source_target_pairs={{0,96},{32,64},{64,32},{96,0},{1,97},{33,65},{65,33},{97,1},{2,98}... | collective-permute-start | bytes 737288 | tf_op jit(solution)/shard_map/ppermute | solution.py:99
  39.6 0.0 collective-permute-start.11
  39.6 1.3 %collective-permute-start.12 = (f32[24,8,256]{2,1,0:T(8,128)S(1)}, f32[24,8,256]{2,1,0:T(8,128)S(1)}, u32[]{:S(2)}, u32[]{:S(2)}) collective-permute-start(f32[24,8,256]{2,1,0:T(8,128)S(1)} %get-tuple-element.62), channel_id=1, source_target_pairs={{0,31},{1,2},{2,1},{3,4},{4,3},{5,6},{6,5},{7,8},{8,7},{9,10},{10,... | collective-permute-start | bytes 589832 | tf_op jit(solution)/shard_map/ppermute | solution.py:99
  40.9 0.2 collective-permute-done.11.refs_8_
  41.1 7.0 %collective-permute-done.12.refs_9_ = f32[24,8,256]{2,1,0:T(8,128)S(1)} collective-permute-done((f32[24,8,256]{2,1,0:T(8,128)S(1)}, f32[24,8,256]{2,1,0:T(8,128)S(1)}, u32[]{:S(2)}, u32[]{:S(2)}) %collective-permute-start.12) | collective-permute-done | bytes 196640 | tf_op jit(solution)/shard_map/ppermute | solution.py:99
  48.0 1.4 %stage_inner.2.refs_14_.refs_0_ = f32[5,24,16,256]{3,2,1,0:T(8,128)S(1)} custom-call(f32[5,24,16,256]{3,2,1,0:T(8,128)S(1)} %get-tuple-element.52.refs_6_.refs_0_.refs_4_.refs_2_.refs_3_, f32[5,8,16,256]{3,2,1,0:T(8,128)S(1)} %get-tuple-element.53.refs_7_.refs_1_.refs_5_.refs_3_.refs_4_, ...), custom_call_target="tpu_custom_call" | custom-call | tf_op jit(solution)/shard_map/stage_inner/pallas_call | solution.py:114
  49.5 0.0 collective-permute-done.13.refs_10_
  49.5 0.0 collective-permute-done.14.refs_11_
  49.5 0.7 stage_rim.2
  50.1 1.4 %collective-permute-start.17 = (f32[15,16,256]{2,1,0:T(8,128)S(1)}, f32[15,16,256]{2,1,0:T(8,128)S(1)}, u32[]{:S(2)}, u32[]{:S(2)}) collective-permute-start(f32[15,16,256]{2,1,0:T(8,128)S(1)} %get-tuple-element.68), channel_id=1, source_target_pairs={{0,32},{32,0},{64,96},{96,64},{1,33},{33,1},{65,97},{97,65},{2,34}... | collective-permute-start | bytes 737288 | tf_op jit(solution)/shard_map/ppermute | solution.py:99
  51.6 1.5 %collective-permute-start.18 = (f32[15,16,256]{2,1,0:T(8,128)S(1)}, f32[15,16,256]{2,1,0:T(8,128)S(1)}, u32[]{:S(2)}, u32[]{:S(2)}) collective-permute-start(f32[15,16,256]{2,1,0:T(8,128)S(1)} %get-tuple-element.69), channel_id=1, source_target_pairs={{0,96},{32,64},{64,32},{96,0},{1,97},{33,65},{65,33},{97,1},{2,98}... | collective-permute-start | bytes 737288 | tf_op jit(solution)/shard_map/ppermute | solution.py:99
  53.0 0.0 collective-permute-start.15
  53.0 0.4 collective-permute-start.16
  53.5 1.0 %collective-permute-done.15.refs_6_ = f32[24,8,256]{2,1,0:T(8,128)S(1)} collective-permute-done((f32[24,8,256]{2,1,0:T(8,128)S(1)}, f32[24,8,256]{2,1,0:T(8,128)S(1)}, u32[]{:S(2)}, u32[]{:S(2)}) %collective-permute-start.15) | collective-permute-done | bytes 196640 | tf_op jit(solution)/shard_map/ppermute | solution.py:99
  54.5 7.0 %collective-permute-done.16.refs_7_ = f32[24,8,256]{2,1,0:T(8,128)S(1)} collective-permute-done((f32[24,8,256]{2,1,0:T(8,128)S(1)}, f32[24,8,256]{2,1,0:T(8,128)S(1)}, u32[]{:S(2)}, u32[]{:S(2)}) %collective-permute-start.16) | collective-permute-done | bytes 196640 | tf_op jit(solution)/shard_map/ppermute | solution.py:99
  61.5 1.3 %stage_inner.3.refs_12_.refs_0_.refs_1_ = f32[5,24,16,256]{3,2,1,0:T(8,128)S(1)} custom-call(f32[5,24,16,256]{3,2,1,0:T(8,128)S(1)} %stage_inner.2.refs_14_.refs_0_, f32[5,8,16,256]{3,2,1,0:T(8,128)S(1)} %get-tuple-element.65.refs_1_, f32[5,24,16,256]{3,2,1,0:T(8,128)S(1)} %get-tuple-element.52.refs_6_.refs_0_.refs_4_.refs_2_.refs_3_, ...), custom_call_target="tpu_custom_call" | custom-call | tf_op jit(solution)/shard_map/stage_inner/pallas_call | solution.py:114
  62.8 0.0 collective-permute-done.17.refs_8_
  62.8 0.0 collective-permute-done.18.refs_9_
  62.8 0.7 stage_rim.3
  63.5 0.2 collective-permute-start.21
  63.6 1.8 %collective-permute-start.22 = (f32[15,16,256]{2,1,0:T(8,128)S(1)}, f32[15,16,256]{2,1,0:T(8,128)S(1)}, u32[]{:S(2)}, u32[]{:S(2)}) collective-permute-start(f32[15,16,256]{2,1,0:T(8,128)S(1)} %get-tuple-element.74), channel_id=1, source_target_pairs={{0,96},{32,64},{64,32},{96,0},{1,97},{33,65},{65,33},{97,1},{2,98}... | collective-permute-start | bytes 737288 | tf_op jit(solution)/shard_map/ppermute | solution.py:99
  65.4 0.1 collective-permute-start.20
  65.5 1.3 %collective-permute-done.19.refs_7_.refs_8_ = f32[24,8,256]{2,1,0:T(8,128)S(1)} collective-permute-done((f32[24,8,256]{2,1,0:T(8,128)S(1)}, f32[24,8,256]{2,1,0:T(8,128)S(1)}, u32[]{:S(2)}, u32[]{:S(2)}) %collective-permute-start.19) | collective-permute-done | bytes 196640 | tf_op jit(solution)/shard_map/ppermute | solution.py:99
  66.8 7.0 %collective-permute-done.20.refs_8_.refs_9_ = f32[24,8,256]{2,1,0:T(8,128)S(1)} collective-permute-done((f32[24,8,256]{2,1,0:T(8,128)S(1)}, f32[24,8,256]{2,1,0:T(8,128)S(1)}, u32[]{:S(2)}, u32[]{:S(2)}) %collective-permute-start.20) | collective-permute-done | bytes 196640 | tf_op jit(solution)/shard_map/ppermute | solution.py:99
  73.8 2.4 %final_inner.1.refs_0_ = f32[5,32,16,256]{3,2,1,0:T(8,128)} custom-call(f32[5,24,16,256]{3,2,1,0:T(8,128)S(1)} %stage_inner.3.refs_12_.refs_0_.refs_1_, f32[5,8,16,256]{3,2,1,0:T(8,128)S(1)} %get-tuple-element.70.refs_1_.refs_2_, f32[5,24,16,256]{3,2,1,0:T(8,128)S(1)} %get-tuple-element.52.refs_6_.refs_0_.refs_4_.refs_2_.refs_3_, ...), custom_call_target="tpu_custom_call" | custom-call | tf_op jit(solution)/shard_map/final_inner/pallas_call | solution.py:114
  76.2 0.0 collective-permute-done.21.refs_10_
  76.2 0.0 collective-permute-done.22.refs_11_
  76.2 1.5 %final_rim.1 = f32[5,32,16,256]{3,2,1,0:T(8,128)} custom-call(f32[5,32,16,256]{3,2,1,0:T(8,128)} %final_inner.1.refs_0_, f32[5,24,16,256]{3,2,1,0:T(8,128)S(1)} %stage_inner.3.refs_12_.refs_0_.refs_1_, f32[5,8,16,256]{3,2,1,0:T(8,128)S(1)} %get-tuple-element.70.refs_1_.refs_2_, ...), custom_call_target="tpu_custom_call", output_to_operand_aliasing={{}: (0, {})} | custom-call | tf_op jit(solution)/shard_map/final_rim/pallas_call | solution.py:114
  (12 shorter events, 0.0 us)
Async XLA Ops:
  0.0 6.3 %copy-start.4 = (f32[16,16,512]{2,1,0:T(8,128)S(1)}, f32[16,16,512]{2,1,0:T(8,128)}, u32[]{:S(2)}) copy-start(f32[16,16,512]{2,1,0:T(8,128)} %refs_0_.4) | copy-start | bytes 1572868
  1.1 6.7 %collective-permute-start.1 = (f32[4,16,512]{2,1,0:T(8,128)S(1)}, f32[4,16,512]{2,1,0:T(8,128)S(1)}, u32[]{:S(2)}, u32[]{:S(2)}) collective-permute-start(f32[4,16,512]{2,1,0:T(8,128)S(1)} %get-tuple-element.75), channel_id=1, source_target_pairs={{0,96},{32,64},{64,32},{96,0},{1,97},{33,65},{65,33},{97,1},{2,98}... | collective-permute-start | bytes 393224 | tf_op jit(solution)/shard_map/ppermute | solution.py:99
  4.2 5.0 %collective-permute-start = (f32[4,16,512]{2,1,0:T(8,128)S(1)}, f32[4,16,512]{2,1,0:T(8,128)S(1)}, u32[]{:S(2)}, u32[]{:S(2)}) collective-permute-start(f32[4,16,512]{2,1,0:T(8,128)S(1)} %get-tuple-element.76.refs_1_), channel_id=1, source_target_pairs={{0,32},{32,0},{64,96},{96,64},{1,33},{33,1},{65,97},{97,65},{2,34}... | collective-permute-start | bytes 393224 | tf_op jit(solution)/shard_map/ppermute | solution.py:99
  4.4 1.7 %copy-start = (f32[5,32,16,256]{3,2,1,0:T(8,128)S(1)}, f32[5,32,16,256]{3,2,1,0:T(8,128)}, u32[]{:S(2)}) copy-start(f32[5,32,16,256]{3,2,1,0:T(8,128)} %refs_7_.1) | copy-start | bytes 7864324
  6.1 1.0 %copy-start.5 = (s32[16,16,512]{2,1,0:T(8,128)S(1)}, s32[16,16,512]{2,1,0:T(8,128)}, u32[]{:S(2)}) copy-start(s32[16,16,512]{2,1,0:T(8,128)} %refs_1_.1) | copy-start | bytes 1572868
  6.1 11.2 %copy-start.6 = (s32[256]{0:T(256)S(1)}, s32[256]{0:T(256)}, u32[]{:S(2)}) copy-start(s32[256]{0:T(256)} %param.9) | copy-start | bytes 3076
  6.1 11.2 %copy-start.7 = (s32[256]{0:T(256)S(1)}, s32[256]{0:T(256)}, u32[]{:S(2)}) copy-start(s32[256]{0:T(256)} %param.10) | copy-start | bytes 3076
  6.2 24.6 %copy-start.1 = (f32[5,32,16,256]{3,2,1,0:T(8,128)S(1)}, f32[5,32,16,256]{3,2,1,0:T(8,128)}, u32[]{:S(2)}) copy-start(f32[5,32,16,256]{3,2,1,0:T(8,128)} %refs_7_.1) | copy-start | bytes 7864324
  6.3 24.6 %copy-start.2 = (bf16[2,2,256,256]{3,2,1,0:T(8,128)(2,1)S(1)}, bf16[2,2,256,256]{3,2,1,0:T(8,128)(2,1)}, u32[]{:S(2)}) copy-start(bf16[2,2,256,256]{3,2,1,0:T(8,128)(2,1)} %constant.17.clone.refs_6_.refs_11_.refs_13_.refs_9_.refs_10_) | copy-start | bytes 1572868
  6.3 24.6 %copy-start.3 = (bf16[2,2,128,224]{3,2,1,0:T(8,128)(2,1)S(1)}, bf16[2,2,128,224]{3,2,1,0:T(8,128)(2,1)}, u32[]{:S(2)}) copy-start(bf16[2,2,128,224]{3,2,1,0:T(8,128)(2,1)} %constant.16.clone.refs_5_.refs_10_.refs_12_.refs_8_.refs_9_) | copy-start | bytes 688132
  9.4 14.2 %collective-permute-start.2 = (f32[40,8,256]{2,1,0:T(8,128)S(1)}, f32[40,8,256]{2,1,0:T(8,128)S(1)}, u32[]{:S(2)}, u32[]{:S(2)}) collective-permute-start(f32[40,8,256]{2,1,0:T(8,128)S(1)} %get-tuple-element.43), channel_id=1, source_target_pairs={{0,1},{1,0},{2,3},{3,2},{4,5},{5,4},{6,7},{7,6},{8,9},{9,8},{10,11... | collective-permute-start | bytes 983048 | tf_op jit(solution)/shard_map/ppermute | solution.py:99
  9.5 19.7 %collective-permute-start.4 = (f32[15,16,256]{2,1,0:T(8,128)S(1)}, f32[15,16,256]{2,1,0:T(8,128)S(1)}, u32[]{:S(2)}, u32[]{:S(2)}) collective-permute-start(f32[15,16,256]{2,1,0:T(8,128)S(1)} %get-tuple-element.45), channel_id=1, source_target_pairs={{0,32},{32,0},{64,96},{96,64},{1,33},{33,1},{65,97},{97,65},{2,34}... | collective-permute-start | bytes 737288 | tf_op jit(solution)/shard_map/ppermute | solution.py:99
  9.9 19.3 %collective-permute-start.3 = (f32[24,8,256]{2,1,0:T(8,128)S(1)}, f32[24,8,256]{2,1,0:T(8,128)S(1)}, u32[]{:S(2)}, u32[]{:S(2)}) collective-permute-start(f32[24,8,256]{2,1,0:T(8,128)S(1)} %get-tuple-element.44), channel_id=1, source_target_pairs={{0,31},{1,2},{2,1},{3,4},{4,3},{5,6},{6,5},{7,8},{8,7},{9,10},{10,... | collective-permute-start | bytes 589832 | tf_op jit(solution)/shard_map/ppermute | solution.py:105
  15.9 7.7 %collective-permute-start.6 = (f32[8,8,512]{2,1,0:T(8,128)S(1)}, f32[8,8,512]{2,1,0:T(8,128)S(1)}, u32[]{:S(2)}, u32[]{:S(2)}) collective-permute-start(f32[8,8,512]{2,1,0:T(8,128)S(1)} %get-tuple-element.48), channel_id=1, source_target_pairs={{0,31},{1,2},{2,1},{3,4},{4,3},{5,6},{6,5},{7,8},{8,7},{9,10},{10,... | collective-permute-start | bytes 393224 | tf_op jit(solution)/shard_map/ppermute | solution.py:99
  15.9 14.9 %collective-permute-start.5 = (f32[15,16,256]{2,1,0:T(8,128)S(1)}, f32[15,16,256]{2,1,0:T(8,128)S(1)}, u32[]{:S(2)}, u32[]{:S(2)}) collective-permute-start(f32[15,16,256]{2,1,0:T(8,128)S(1)} %get-tuple-element.46), channel_id=1, source_target_pairs={{0,96},{32,64},{64,32},{96,0},{1,97},{33,65},{65,33},{97,1},{2,98}... | collective-permute-start | bytes 737288 | tf_op jit(solution)/shard_map/ppermute | solution.py:99
  26.0 6.5 %collective-permute-start.7 = (f32[136,256]{1,0:T(8,128)S(1)}, f32[136,256]{1,0:T(8,128)S(1)}, u32[]{:S(2)}, u32[]{:S(2)}) collective-permute-start(f32[136,256]{1,0:T(8,128)S(1)} %get-tuple-element.55), channel_id=1, source_target_pairs={{0,32},{32,0},{64,96},{96,64},{1,33},{33,1},{65,97},{97,65},{2,34}... | collective-permute-start | bytes 417800 | tf_op jit(solution)/shard_map/ppermute | solution.py:99
  27.7 6.3 %collective-permute-start.8 = (f32[136,256]{1,0:T(8,128)S(1)}, f32[136,256]{1,0:T(8,128)S(1)}, u32[]{:S(2)}, u32[]{:S(2)}) collective-permute-start(f32[136,256]{1,0:T(8,128)S(1)} %get-tuple-element.56), channel_id=1, source_target_pairs={{0,96},{32,64},{64,32},{96,0},{1,97},{33,65},{65,33},{97,1},{2,98}... | collective-permute-start | bytes 417800 | tf_op jit(solution)/shard_map/ppermute | solution.py:99
  29.2 4.8 %collective-permute-start.9 = (f32[136,256]{1,0:T(8,128)S(1)}, f32[136,256]{1,0:T(8,128)S(1)}, u32[]{:S(2)}, u32[]{:S(2)}) collective-permute-start(f32[136,256]{1,0:T(8,128)S(1)} %get-tuple-element.57), channel_id=1, source_target_pairs={{0,1},{1,0},{2,3},{3,2},{4,5},{5,4},{6,7},{7,6},{8,9},{9,8},{10,11... | collective-permute-start | bytes 417800 | tf_op jit(solution)/shard_map/ppermute | solution.py:99
  29.2 7.9 %collective-permute-start.10 = (f32[136,256]{1,0:T(8,128)S(1)}, f32[136,256]{1,0:T(8,128)S(1)}, u32[]{:S(2)}, u32[]{:S(2)}) collective-permute-start(f32[136,256]{1,0:T(8,128)S(1)} %get-tuple-element.58), channel_id=1, source_target_pairs={{0,31},{1,2},{2,1},{3,4},{4,3},{5,6},{6,5},{7,8},{8,7},{9,10},{10,... | collective-permute-start | bytes 417800 | tf_op jit(solution)/shard_map/ppermute | solution.py:99
  37.7 11.8 %collective-permute-start.13 = (f32[15,16,256]{2,1,0:T(8,128)S(1)}, f32[15,16,256]{2,1,0:T(8,128)S(1)}, u32[]{:S(2)}, u32[]{:S(2)}) collective-permute-start(f32[15,16,256]{2,1,0:T(8,128)S(1)} %get-tuple-element.63), channel_id=1, source_target_pairs={{0,32},{32,0},{64,96},{96,64},{1,33},{33,1},{65,97},{97,65},{2,34}... | collective-permute-start | bytes 737288 | tf_op jit(solution)/shard_map/ppermute | solution.py:99
  37.8 11.7 %collective-permute-start.14 = (f32[15,16,256]{2,1,0:T(8,128)S(1)}, f32[15,16,256]{2,1,0:T(8,128)S(1)}, u32[]{:S(2)}, u32[]{:S(2)}) collective-permute-start(f32[15,16,256]{2,1,0:T(8,128)S(1)} %get-tuple-element.64), channel_id=1, source_target_pairs={{0,96},{32,64},{64,32},{96,0},{1,97},{33,65},{65,33},{97,1},{2,98}... | collective-permute-start | bytes 737288 | tf_op jit(solution)/shard_map/ppermute | solution.py:99
  39.6 1.4 %collective-permute-start.11 = (f32[24,8,256]{2,1,0:T(8,128)S(1)}, f32[24,8,256]{2,1,0:T(8,128)S(1)}, u32[]{:S(2)}, u32[]{:S(2)}) collective-permute-start(f32[24,8,256]{2,1,0:T(8,128)S(1)} %get-tuple-element.61), channel_id=1, source_target_pairs={{0,1},{1,0},{2,3},{3,2},{4,5},{5,4},{6,7},{7,6},{8,9},{9,8},{10,11... | collective-permute-start | bytes 589832 | tf_op jit(solution)/shard_map/ppermute | solution.py:99
  39.6 8.4 %collective-permute-start.12 = (f32[24,8,256]{2,1,0:T(8,128)S(1)}, f32[24,8,256]{2,1,0:T(8,128)S(1)}, u32[]{:S(2)}, u32[]{:S(2)}) collective-permute-start(f32[24,8,256]{2,1,0:T(8,128)S(1)} %get-tuple-element.62), channel_id=1, source_target_pairs={{0,31},{1,2},{2,1},{3,4},{4,3},{5,6},{6,5},{7,8},{8,7},{9,10},{10,... | collective-permute-start | bytes 589832 | tf_op jit(solution)/shard_map/ppermute | solution.py:99
  50.1 12.6 %collective-permute-start.17 = (f32[15,16,256]{2,1,0:T(8,128)S(1)}, f32[15,16,256]{2,1,0:T(8,128)S(1)}, u32[]{:S(2)}, u32[]{:S(2)}) collective-permute-start(f32[15,16,256]{2,1,0:T(8,128)S(1)} %get-tuple-element.68), channel_id=1, source_target_pairs={{0,32},{32,0},{64,96},{96,64},{1,33},{33,1},{65,97},{97,65},{2,34}... | collective-permute-start | bytes 737288 | tf_op jit(solution)/shard_map/ppermute | solution.py:99
  51.6 11.2 %collective-permute-start.18 = (f32[15,16,256]{2,1,0:T(8,128)S(1)}, f32[15,16,256]{2,1,0:T(8,128)S(1)}, u32[]{:S(2)}, u32[]{:S(2)}) collective-permute-start(f32[15,16,256]{2,1,0:T(8,128)S(1)} %get-tuple-element.69), channel_id=1, source_target_pairs={{0,96},{32,64},{64,32},{96,0},{1,97},{33,65},{65,33},{97,1},{2,98}... | collective-permute-start | bytes 737288 | tf_op jit(solution)/shard_map/ppermute | solution.py:99
  53.0 1.4 %collective-permute-start.15 = (f32[24,8,256]{2,1,0:T(8,128)S(1)}, f32[24,8,256]{2,1,0:T(8,128)S(1)}, u32[]{:S(2)}, u32[]{:S(2)}) collective-permute-start(f32[24,8,256]{2,1,0:T(8,128)S(1)} %get-tuple-element.66), channel_id=1, source_target_pairs={{0,1},{1,0},{2,3},{3,2},{4,5},{5,4},{6,7},{7,6},{8,9},{9,8},{10,11... | collective-permute-start | bytes 589832 | tf_op jit(solution)/shard_map/ppermute | solution.py:99
  53.0 8.4 %collective-permute-start.16 = (f32[24,8,256]{2,1,0:T(8,128)S(1)}, f32[24,8,256]{2,1,0:T(8,128)S(1)}, u32[]{:S(2)}, u32[]{:S(2)}) collective-permute-start(f32[24,8,256]{2,1,0:T(8,128)S(1)} %get-tuple-element.67), channel_id=1, source_target_pairs={{0,31},{1,2},{2,1},{3,4},{4,3},{5,6},{6,5},{7,8},{8,7},{9,10},{10,... | collective-permute-start | bytes 589832 | tf_op jit(solution)/shard_map/ppermute | solution.py:99
  63.5 12.7 %collective-permute-start.21 = (f32[15,16,256]{2,1,0:T(8,128)S(1)}, f32[15,16,256]{2,1,0:T(8,128)S(1)}, u32[]{:S(2)}, u32[]{:S(2)}) collective-permute-start(f32[15,16,256]{2,1,0:T(8,128)S(1)} %get-tuple-element.73), channel_id=1, source_target_pairs={{0,32},{32,0},{64,96},{96,64},{1,33},{33,1},{65,97},{97,65},{2,34}... | collective-permute-start | bytes 737288 | tf_op jit(solution)/shard_map/ppermute | solution.py:99
  63.6 12.5 %collective-permute-start.22 = (f32[15,16,256]{2,1,0:T(8,128)S(1)}, f32[15,16,256]{2,1,0:T(8,128)S(1)}, u32[]{:S(2)}, u32[]{:S(2)}) collective-permute-start(f32[15,16,256]{2,1,0:T(8,128)S(1)} %get-tuple-element.74), channel_id=1, source_target_pairs={{0,96},{32,64},{64,32},{96,0},{1,97},{33,65},{65,33},{97,1},{2,98}... | collective-permute-start | bytes 737288 | tf_op jit(solution)/shard_map/ppermute | solution.py:99
  65.4 1.4 %collective-permute-start.19 = (f32[24,8,256]{2,1,0:T(8,128)S(1)}, f32[24,8,256]{2,1,0:T(8,128)S(1)}, u32[]{:S(2)}, u32[]{:S(2)}) collective-permute-start(f32[24,8,256]{2,1,0:T(8,128)S(1)} %get-tuple-element.71), channel_id=1, source_target_pairs={{0,1},{1,0},{2,3},{3,2},{4,5},{5,4},{6,7},{7,6},{8,9},{9,8},{10,11... | collective-permute-start | bytes 589832 | tf_op jit(solution)/shard_map/ppermute | solution.py:99
  65.4 8.4 %collective-permute-start.20 = (f32[24,8,256]{2,1,0:T(8,128)S(1)}, f32[24,8,256]{2,1,0:T(8,128)S(1)}, u32[]{:S(2)}, u32[]{:S(2)}) collective-permute-start(f32[24,8,256]{2,1,0:T(8,128)S(1)} %get-tuple-element.72), channel_id=1, source_target_pairs={{0,31},{1,2},{2,1},{3,4},{4,3},{5,6},{6,5},{7,8},{8,7},{9,10},{10,... | collective-permute-start | bytes 589832 | tf_op jit(solution)/shard_map/ppermute | solution.py:99

commit v4 on v3

--- a/solution.py
+++ b/solution.py
@@ -105,7 +105,7 @@
     return (lax.ppermute(value, axis, pairs),)
 
 
-def full_specs(body, outs, args, scratch=(), name=None, in_specs=None, out_specs=None, after=(), cost=0, alias=None):
+def full_specs(body, outs, args, scratch=(), name=None, out_specs=None, after=(), cost=0):
     skip = len(args)
 
     def run(*refs):
@@ -114,8 +114,7 @@
     return pl.pallas_call(
         run,
         out_shape=[jax.ShapeDtypeStruct(s, d) for s, d in outs],
-        in_specs=(in_specs or [VM] * skip) + [ANY] * len(after),
-        input_output_aliases=alias or {},
+        in_specs=[VM] * skip + [ANY] * len(after),
         out_specs=out_specs or [VM] * len(outs),
         scratch_shapes=[pltpu.VMEM(*s) if isinstance(s, tuple) else s for s in scratch],
         compiler_params=PARAMS,
@@ -189,7 +188,7 @@
         first_ref[x] = total
 
 
-def first_body(inner_ref, half_ref, got_a_ref, got_b_ref, edge_a_ref, first_ref, to_a_ref, to_b_ref, halo):
+def first_body(inner_ref, half_ref, got_a_ref, got_b_ref, first_ref, to_a_ref, to_b_ref, halo):
     n_ax, ax = lax.axis_size("ax"), lax.axis_index("ax")
     even_x, even_z = is_even("ax"), is_even("az")
     rows, _, fine = half_ref.shape
@@ -214,22 +213,19 @@
     for x in range(half):
         last = jnp.where(low, pltpu.roll(first_ref[x, 8:16], 4, 0), first_ref[x + half, 8:16])
         begin = jnp.where(low, first_ref[x, 0:8], pltpu.roll(first_ref[x + half, 0:8], 4, 0))
-        to_a = jnp.where(even_z, last, begin)
-        to_a_ref[x] = to_a[:, : fine // 2]
-        to_a_ref[half + x] = to_a[:, fine // 2 :]
+        to_a_ref[x] = jnp.where(even_z, last, begin)
         to_b_ref[x] = jnp.where(even_z, begin, last)
-    to_a_ref[2 * half :] = edge_a_ref[...]
 
 
 def second_body(
-    first_ref, half_ref, got_a_ref, got_b_ref, pick_ref, cells_ref,
+    first_ref, half_ref, got_a_ref, got_b_ref, pick_ref, cells_ref, edge_a_ref,
     own_ref, to_xa, to_xb, to_za, to_zb, wide, fine_hi, fine_lo,
 ):
     even = is_even("az")
     rows, cols, fine = first_ref.shape
     half = rows // 2
     for x in range(half):
-        got_a, got_b = jnp.concatenate([got_a_ref[x], got_a_ref[half + x]], axis=1), got_b_ref[x]
+        got_a, got_b = got_a_ref[x], got_b_ref[x]
         before = jnp.where(even, got_b, got_a)
         after = jnp.where(even, got_a, got_b)
         wide[x, 0:8] = pltpu.roll(before, 4, 0)
@@ -263,8 +259,10 @@
     most = pick_ref.shape[0] // 4
     for d, out in enumerate((to_xa, to_xb, to_za, to_zb)):
         pick = pick_ref[d * most : (d + 1) * most]
-        out[0:most] = dot(pick, hi) + dot(pick, lo)
-        out[most : most + 8] = cells_ref[d]
+        tiles = most // 8
+        out[0:tiles] = (dot(pick, hi) + dot(pick, lo)).reshape(tiles, 8, radial)
+        out[tiles] = cells_ref[d]
+    to_za[most // 8 + 1 :] = edge_a_ref[...]
 
 
 def gather_body(
@@ -272,7 +270,7 @@
 ):
     mid, cols, radial = p_mid.shape
     cells = (mid + 2 * RIM) * cols
-    most = xa.shape[0] - 8
+    most = 8 * (xa.shape[0] - 1)
 
     def onehot(row):
         at = lax.broadcasted_iota(jnp.int32, (cells, row.shape[1]), 0)
@@ -281,8 +279,9 @@
     mats = [onehot(own_ref[...])]
     packets = [binned_ref[...]]
     for got in (xa, xb, za, zb):
-        mats.append(onehot(got[most : most + 1, 0:most].astype(jnp.int32)))
-        packets.append(got[0:most])
+        tiles = most // 8
+        mats.append(onehot(got[tiles, 0:1, 0:most].astype(jnp.int32)))
+        packets.append(got[0:tiles].reshape(most, radial))
     mat = jnp.concatenate(mats, axis=1)
     hi, lo = split(jnp.concatenate(packets, axis=0))
     q = (dot(mat, hi) + dot(mat, lo)).reshape(mid + 2 * RIM, cols, radial)
@@ -506,39 +505,31 @@
     return finish
 
 
-def inner_last_body(level, k, fields, za, zb, tmat, rmat, out, result, sems):
+def inner_last_body(level, k, fields, za, zb, tmat, rmat, out_mid):
     def store(f, x, value):
-        result[f, x - RIM] = value
-
-    def copy(g):
-        at = g * GROUP
-        return pltpu.make_async_copy(
-            result.at[:, at : at + GROUP], out.at[:, RIM + at : RIM + at + GROUP], sems.at[g]
-        )
-
-    groups = range(result.shape[1] // GROUP)
-    for g in groups:
-        apply_operator(level, [g], za, zb, tmat, rmat, last_finish(fields, k, store))
-        copy(g).start()
-    for g in groups:
-        copy(g).wait()
-
-
-def rim_last_body(level, k, fields, za, zb, xa, xb, tmat, rmat, out, halo, result, sems):
+        out_mid[f, x - RIM] = value
+
+    groups = range(out_mid.shape[1] // GROUP)
+    apply_operator(level, groups, za, zb, tmat, rmat, last_finish(fields, k, store))
+
+
+def rim_last_body(level, k, fields, za, zb, xa, xb, tmat, rmat, out_mid, out, halo, result, sems):
+    rows = level.rows
+    inner = pltpu.make_async_copy(out_mid, out.at[:, RIM : rows - RIM], sems.at[0])
+    inner.start()
     fill_halo(halo, xa, xb)
-    rows = level.rows
 
     def store(f, x, value):
         result[f, x if x < RIM else x - rows + 2 * RIM] = value
 
     apply_operator(level, [None], za, zb, tmat, rmat, last_finish(fields, k, store), halo)
     copies = [
-        pltpu.make_async_copy(result.at[:, 0:RIM], out.at[:, 0:RIM], sems.at[0]),
-        pltpu.make_async_copy(result.at[:, RIM:], out.at[:, rows - RIM :], sems.at[1]),
+        pltpu.make_async_copy(result.at[:, 0:RIM], out.at[:, 0:RIM], sems.at[1]),
+        pltpu.make_async_copy(result.at[:, RIM:], out.at[:, rows - RIM :], sems.at[2]),
     ]
     for copy in copies:
         copy.start()
-    for copy in copies:
+    for copy in (inner, *copies):
         copy.wait()
 
 
@@ -564,28 +555,29 @@
     )
     filtered, to_a, to_b = full_specs(
         first_body,
-        [block, ((px + send_z[0][0], 8, fine // 2), F32), ((px // 2, 8, fine), F32)],
-        [partial, half_width, noise_a, noise_b, za],
+        [block, ((px // 2, 8, fine), F32), ((px // 2, 8, fine), F32)],
+        [partial, half_width, noise_a, noise_b],
         [((2, HMAX, pa, fine), F32)],
         name="filter_axial",
     )
     got_a, got_b = swap(to_a, to_b, "az")
     (uzb,) = swap_b(zb, "az")
+    uza = za
     pick, cells, own = full_specs(
         route_body,
         [((4 * most, ncols), BF16), ((4, 8, radial), F32), ((1, ncols), jnp.int32)],
         [owner.reshape(1, ncols), target_cell.reshape(1, ncols)],
         name="route",
-        after=[filtered],
-    )
-    packet = ((most + 8, radial), F32)
+        after=[filtered, uxa, uxb, uzb],
+    )
+    tiles = most // 8 + 1
+    packet = ((tiles, 8, radial), F32)
     binned, xa, xb, za, zb = full_specs(
         second_body,
-        [((ncols, radial), F32), packet, packet, packet, packet],
-        [filtered, half_width, got_a, got_b, pick, cells],
+        [((ncols, radial), F32), packet, packet, ((tiles + send_z[0][0], 8, radial), F32), packet],
+        [filtered, half_width, got_a, got_b, pick, cells, uza],
         [((px, 32, fine), F32), ((ncols, fine), BF16), ((ncols, fine), BF16)],
         name="filter_rest",
-        cost=COST,
     )
     packets = (*swap(xa, xb, "ax"), *swap(za, zb, "az"))
 
@@ -594,7 +586,7 @@
     mid, rim = ((5, inner, ca, radial), F32), ((5, 2 * RIM, ca, radial), F32)
     halo = ((2, 5, 3, ca, radial), F32)
     k_mid, k_rim = full_specs(
-        start_body, [mid, rim], [fields, got_a, uzb, uxa, uxb, tmat, rmat], [halo], name="operator", after=[binned]
+        start_body, [mid, rim], [fields, packets[2], uzb, uxa, uxb, tmat, rmat], [halo], name="operator", after=[binned]
     )
     p_mid, p_rim, *edges = full_specs(
         gather_body,
@@ -612,7 +604,7 @@
         def body(*refs, factor=factor, size=size):
             inner_stage_body(factor, Parts(*refs[:size]), Parts(*refs[size : size + 4]), *refs[size + 4 :])
 
-        (new_mid,) = full_specs(body, [mid], [*level, *k, za, zb, tmat, rmat], name="stage_inner")
+        (new_mid,) = full_specs(body, [mid], [*level, *k, za, zb, tmat, rmat], name="stage_inner", cost=COST)
 
         def body(*refs, factor=factor, size=size):
             rim_stage_body(factor, Parts(*refs[:size]), Parts(*refs[size : size + 4]), *refs[size + 4 :])
@@ -627,28 +619,18 @@
     def body(*refs):
         inner_last_body(Parts(*refs[:2]), Parts(*refs[2:6]), *refs[6:])
 
-    whole = ((5, cx, ca, radial), F32)
+    (new_mid,) = full_specs(body, [mid], [*level, *k, fields, za, zb, tmat, rmat], name="final_inner", cost=COST)
+
+    def body(*refs):
+        rim_last_body(Parts(*refs[:2]), Parts(*refs[2:6]), *refs[6:])
+
     (out,) = full_specs(
         body,
-        [whole],
-        [*level, *k, fields, za, zb, tmat, rmat],
-        [mid, pltpu.SemaphoreType.DMA((inner // GROUP,))],
-        name="final_inner",
-        out_specs=[ANY],
-    )
-
-    def body(out_in, *refs):
-        rim_last_body(Parts(*refs[:2]), Parts(*refs[2:6]), *refs[6:])
-
-    (out,) = full_specs(
-        body,
-        [whole],
-        [out, *level, *k, fields, za, zb, xa, xb, tmat, rmat],
-        [halo, rim, pltpu.SemaphoreType.DMA((2,))],
+        [((5, cx, ca, radial), F32)],
+        [*level, *k, fields, za, zb, xa, xb, tmat, rmat, new_mid],
+        [halo, rim, pltpu.SemaphoreType.DMA((3,))],
         name="final_rim",
         out_specs=[ANY],
-        in_specs=[ANY] + [VM] * 13,
-        alias={0: 0},
     )
     return out
 

time: 78 us -> 75.9 us (0.973)
  waiting for transfers between devices: 35.6 us -> 32.8 us
  starting transfers between devices: 24.7 us -> 26.2 us
  local copies, waits for them, and re-layouts: 2.63 us -> 1.78 us
    ppermute x11, starting transfers between devices: 4.08 us -> 5.59 us  [swap(): lax.ppermute(to_a, axis, pairs_a)]
    ppermute x11, waiting for transfers between devices: 3.97 us -> 2.54 us  [swap(): lax.ppermute(to_a, axis, pairs_a)]
    ppermute x11, waiting for transfers between devices: 31.6 us -> 30.2 us  [swap(): lax.ppermute(to_b, axis, pairs_b)]
    ppermute x11, starting transfers between devices: 14.6 us -> 15.8 us  [swap(): lax.ppermute(to_b, axis, pairs_b)]
    ppermute x1, starting transfers between devices: 5.99 us -> 4.79 us  [swap_b(): return (lax.ppermute(value, axis, pairs),)]
    unnamed x16, local copies, waits for them, and re-layouts: 2.63 us -> 1.78 us
  transfers between devices with their start and end apart: 23 -> 23, of which waited for: 11 -> 10; matrix products, arithmetic and copies ran while one was open for 0% -> 0% of each run, Pallas kernels for 13% -> 10%
where the time goes in v4:
time: 75.9 us; the launch traced here: 75.7 us
  waiting for transfers between devices  32.8 us (43%)
  starting transfers between devices  26.2 us (35%)
  Pallas kernels  13.5 us (18%)
  local copies, waits for them, and re-layouts  1.78 us (2%)
  other arithmetic  1.05 us (1%)
    ppermute x11, waiting for transfers between devices, swap(): lax.ppermute(to_b, axis, pairs_b)  30.2 us
    ppermute x11, starting transfers between devices, swap(): lax.ppermute(to_b, axis, pairs_b)  15.8 us
    pallas_call x13, Pallas kernels, full_specs(): pl.pallas_call(run, out_shape=[jax.ShapeDtypeStruct(s, d) for s, d in out...  13.5 us
    ppermute x11, starting transfers between devices, swap(): lax.ppermute(to_a, axis, pairs_a)  5.59 us
    ppermute x1, starting transfers between devices, swap_b(): return (lax.ppermute(value, axis, pairs),)  4.79 us
    ppermute x11, waiting for transfers between devices, swap(): lax.ppermute(to_a, axis, pairs_a)  2.54 us
    unnamed x16, local copies, waits for them, and re-layouts  1.78 us
  transfers between devices with their start and end apart: 23, of which 10 were waited for; matrix products, arithmetic and copies ran while one was open for 0% of the time, Pallas kernels for 10%

profile of v4, /device:TPU:0, one launch (start us, length us, event | category | flops | bytes accessed | tf_op | source)
XLA Modules:
  0.0 75.7 jit_solution(15787344974370104560)
XLA Ops:
  0.0 1.0 %slice_select_fusion = (f32[4,16,512]{2,1,0:T(8,128)S(1)}, f32[4,16,512]{2,1,0:T(8,128)S(1)}) fusion(f32[16,16,512]{2,1,0:T(8,128)} %refs_0_.4, pred[]{:T(512)S(6)} %eq.3), kind=kLoop, calls=%fused_computation | loop fusion | flops 65536 | bytes 524289 | tf_op jit(solution)/shard_map/jit(_where)/select_n | solution.py:547
  1.1 3.2 %collective-permute-start.1 = (f32[4,16,512]{2,1,0:T(8,128)S(1)}, f32[4,16,512]{2,1,0:T(8,128)S(1)}, u32[]{:S(2)}, u32[]{:S(2)}) collective-permute-start(f32[4,16,512]{2,1,0:T(8,128)S(1)} %get-tuple-element.75), channel_id=1, source_target_pairs={{0,96},{32,64},{64,32},{96,0},{1,97},{33,65},{65,33},{97,1},{2,98}... | collective-permute-start | bytes 393224 | tf_op jit(solution)/shard_map/ppermute | solution.py:99
  4.2 0.1 collective-permute-start
  4.4 1.7 %copy-done = f32[5,32,16,256]{3,2,1,0:T(8,128)S(1)} copy-done((f32[5,32,16,256]{3,2,1,0:T(8,128)S(1)}, f32[5,32,16,256]{3,2,1,0:T(8,128)}, u32[]{:S(2)}) %copy-start) | copy-done | bytes 2621464
  6.1 0.1 edges.1
  6.2 0.0 copy-start.6
  6.2 0.0 copy-start.7
  6.3 2.0 %collective-permute-start.4 = (f32[15,16,256]{2,1,0:T(8,128)S(1)}, f32[15,16,256]{2,1,0:T(8,128)S(1)}, u32[]{:S(2)}, u32[]{:S(2)}) collective-permute-start(f32[15,16,256]{2,1,0:T(8,128)S(1)} %get-tuple-element.46), channel_id=1, source_target_pairs={{0,32},{32,0},{64,96},{96,64},{1,33},{33,1},{65,97},{97,65},{2,34}... | collective-permute-start | bytes 737288 | tf_op jit(solution)/shard_map/ppermute | solution.py:99
  8.2 0.1 collective-permute-start.5
  8.4 4.8 %collective-permute-start.6 = (f32[24,8,256]{2,1,0:T(8,128)S(1)}, f32[24,8,256]{2,1,0:T(8,128)S(1)}, u32[]{:S(2)}, u32[]{:S(2)}) collective-permute-start(f32[24,8,256]{2,1,0:T(8,128)S(1)} %get-tuple-element.48), channel_id=1, source_target_pairs={{0,31},{1,2},{2,1},{3,4},{4,3},{5,6},{6,5},{7,8},{8,7},{9,10},{10,... | collective-permute-start | bytes 589832 | tf_op jit(solution)/shard_map/ppermute | solution.py:105
  13.2 0.5 filter_inner.1
  13.6 0.0 collective-permute-done.1.refs_3_
  13.7 0.0 collective-permute-done.refs_2_
  13.7 0.0 copy-start.1
  13.7 0.0 copy-start.2
  13.7 0.0 copy-start.3
  13.7 0.2 filter_axial.1
  13.9 0.1 collective-permute-start.2
  14.0 2.7 %collective-permute-start.3 = (f32[8,8,512]{2,1,0:T(8,128)S(1)}, f32[8,8,512]{2,1,0:T(8,128)S(1)}, u32[]{:S(2)}, u32[]{:S(2)}) collective-permute-start(f32[8,8,512]{2,1,0:T(8,128)S(1)} %get-tuple-element.45), channel_id=1, source_target_pairs={{0,31},{1,2},{2,1},{3,4},{4,3},{5,6},{6,5},{7,8},{8,7},{9,10},{10,... | collective-permute-start | bytes 393224 | tf_op jit(solution)/shard_map/ppermute | solution.py:99
  16.7 0.1 collective-permute-done.6.refs_5_.refs_2_
  16.8 0.0 collective-permute-done.4.refs_3_
  16.8 0.0 collective-permute-done.5.refs_4_
  16.8 0.3 route.1
  17.1 0.0 collective-permute-done.2.refs_2_
  17.1 4.7 %collective-permute-done.3.refs_3_ = f32[8,8,512]{2,1,0:T(8,128)S(1)} collective-permute-done((f32[8,8,512]{2,1,0:T(8,128)S(1)}, f32[8,8,512]{2,1,0:T(8,128)S(1)}, u32[]{:S(2)}, u32[]{:S(2)}) %collective-permute-start.3) | collective-permute-done | bytes 131104 | tf_op jit(solution)/shard_map/ppermute | solution.py:99
  21.8 2.3 %filter_rest.1 = (f32[256,256]{1,0:T(8,128)S(1)}, f32[17,8,256]{2,1,0:T(8,128)S(1)}, f32[17,8,256]{2,1,0:T(8,128)S(1)}, f32[41,8,256]{2,1,0:T(8,128)S(1)}, f32[17,8,256]{2,1,0:T(8,128)S(1)}) custom-call(f32[16,16,512]{2,1,0:T(8,128)S(1)} %get-tuple-element.43.refs_2_.refs_0_, s32[16,16,512]{2,1,0:T(8,128)S(1)} %get-tuple-element.42.refs_1_, ...), custom_call_target="tpu_custom_call" | custom-call | tf_op jit(solution)/shard_map/filter_rest/pallas_call | solution.py:114
  24.1 0.1 collective-permute-start.7
  24.2 0.5 collective-permute-start.8
  24.7 2.6 %collective-permute-start.9 = (f32[17,8,256]{2,1,0:T(8,128)S(1)}, f32[17,8,256]{2,1,0:T(8,128)S(1)}, u32[]{:S(2)}, u32[]{:S(2)}) collective-permute-start(f32[17,8,256]{2,1,0:T(8,128)S(1)} %get-tuple-element.57), channel_id=1, source_target_pairs={{0,96},{32,64},{64,32},{96,0},{1,97},{33,65},{65,33},{97,1},{2,98}... | collective-permute-start | bytes 417800 | tf_op jit(solution)/shard_map/ppermute | solution.py:99
  27.3 1.4 %collective-permute-start.10 = (f32[17,8,256]{2,1,0:T(8,128)S(1)}, f32[17,8,256]{2,1,0:T(8,128)S(1)}, u32[]{:S(2)}, u32[]{:S(2)}) collective-permute-start(f32[17,8,256]{2,1,0:T(8,128)S(1)} %get-tuple-element.58), channel_id=1, source_target_pairs={{0,31},{1,2},{2,1},{3,4},{4,3},{5,6},{6,5},{7,8},{8,7},{9,10},{10,... | collective-permute-start | bytes 417800 | tf_op jit(solution)/shard_map/ppermute | solution.py:99
  28.7 0.0 collective-permute-done.7.refs_1_.refs_4_
  28.7 1.7 %operator.1 = (f32[5,24,16,256]{3,2,1,0:T(8,128)S(1)}, f32[5,8,16,256]{3,2,1,0:T(8,128)S(1)}) custom-call(f32[5,32,16,256]{3,2,1,0:T(8,128)S(1)} %copy-done.1, f32[41,8,256]{2,1,0:T(8,128)S(1)} %collective-permute-done.7.refs_1_.refs_4_, f32[24,8,256]{2,1,0:T(8,128)S(1)} %collective-permute-done.6.refs_5_.refs_2_, ...), custom_call_target="tpu_custom_call" | custom-call | tf_op jit(solution)/shard_map/operator/pallas_call | solution.py:114
  30.4 0.0 collective-permute-done.8.refs_2_
  30.4 1.2 %collective-permute-done.9.refs_3_ = f32[17,8,256]{2,1,0:T(8,128)S(1)} collective-permute-done((f32[17,8,256]{2,1,0:T(8,128)S(1)}, f32[17,8,256]{2,1,0:T(8,128)S(1)}, u32[]{:S(2)}, u32[]{:S(2)}) %collective-permute-start.9) | collective-permute-done | bytes 139296 | tf_op jit(solution)/shard_map/ppermute | solution.py:99
  31.6 3.4 %collective-permute-done.10.refs_5_ = f32[17,8,256]{2,1,0:T(8,128)S(1)} collective-permute-done((f32[17,8,256]{2,1,0:T(8,128)S(1)}, f32[17,8,256]{2,1,0:T(8,128)S(1)}, u32[]{:S(2)}, u32[]{:S(2)}) %collective-permute-start.10) | collective-permute-done | bytes 139296 | tf_op jit(solution)/shard_map/ppermute | solution.py:99
  35.1 0.6 gather.1
  35.7 1.4 %collective-permute-start.13 = (f32[15,16,256]{2,1,0:T(8,128)S(1)}, f32[15,16,256]{2,1,0:T(8,128)S(1)}, u32[]{:S(2)}, u32[]{:S(2)}) collective-permute-start(f32[15,16,256]{2,1,0:T(8,128)S(1)} %get-tuple-element.63), channel_id=1, source_target_pairs={{0,32},{32,0},{64,96},{96,64},{1,33},{33,1},{65,97},{97,65},{2,34}... | collective-permute-start | bytes 737288 | tf_op jit(solution)/shard_map/ppermute | solution.py:99
  37.1 0.6 collective-permute-start.14
  37.7 0.0 collective-permute-start.11
  37.7 1.3 %collective-permute-start.12 = (f32[24,8,256]{2,1,0:T(8,128)S(1)}, f32[24,8,256]{2,1,0:T(8,128)S(1)}, u32[]{:S(2)}, u32[]{:S(2)}) collective-permute-start(f32[24,8,256]{2,1,0:T(8,128)S(1)} %get-tuple-element.62), channel_id=1, source_target_pairs={{0,31},{1,2},{2,1},{3,4},{4,3},{5,6},{6,5},{7,8},{8,7},{9,10},{10,... | collective-permute-start | bytes 589832 | tf_op jit(solution)/shard_map/ppermute | solution.py:99
  39.0 0.1 collective-permute-done.11.refs_8_
  39.1 7.0 %collective-permute-done.12.refs_9_ = f32[24,8,256]{2,1,0:T(8,128)S(1)} collective-permute-done((f32[24,8,256]{2,1,0:T(8,128)S(1)}, f32[24,8,256]{2,1,0:T(8,128)S(1)}, u32[]{:S(2)}, u32[]{:S(2)}) %collective-permute-start.12) | collective-permute-done | bytes 196640 | tf_op jit(solution)/shard_map/ppermute | solution.py:99
  46.1 1.4 %stage_inner.2.refs_14_.refs_0_ = f32[5,24,16,256]{3,2,1,0:T(8,128)S(1)} custom-call(f32[5,24,16,256]{3,2,1,0:T(8,128)S(1)} %get-tuple-element.53.refs_6_.refs_0_.refs_4_.refs_2_, f32[5,8,16,256]{3,2,1,0:T(8,128)S(1)} %get-tuple-element.54.refs_7_.refs_1_.refs_5_.refs_3_, f32[24,16,256]{2,1,0:T(8,128)S(1)} %get-tuple-element.59.refs_2_.refs_6_.refs_4_, ...), custom_call_target="tpu_custom_call" | custom-call | bytes 134217728 | tf_op jit(solution)/shard_map/stage_inner/pallas_call | solution.py:114
  47.5 0.0 collective-permute-done.13.refs_10_
  47.5 0.0 collective-permute-done.14.refs_11_
  47.5 0.7 stage_rim.2
  48.2 0.2 collective-permute-start.17
  48.5 2.8 %collective-permute-start.18 = (f32[15,16,256]{2,1,0:T(8,128)S(1)}, f32[15,16,256]{2,1,0:T(8,128)S(1)}, u32[]{:S(2)}, u32[]{:S(2)}) collective-permute-start(f32[15,16,256]{2,1,0:T(8,128)S(1)} %get-tuple-element.69), channel_id=1, source_target_pairs={{0,96},{32,64},{64,32},{96,0},{1,97},{33,65},{65,33},{97,1},{2,98}... | collective-permute-start | bytes 737288 | tf_op jit(solution)/shard_map/ppermute | solution.py:99
  51.2 0.0 collective-permute-start.15
  51.2 0.3 collective-permute-start.16
  51.5 1.1 %collective-permute-done.15.refs_6_ = f32[24,8,256]{2,1,0:T(8,128)S(1)} collective-permute-done((f32[24,8,256]{2,1,0:T(8,128)S(1)}, f32[24,8,256]{2,1,0:T(8,128)S(1)}, u32[]{:S(2)}, u32[]{:S(2)}) %collective-permute-start.15) | collective-permute-done | bytes 196640 | tf_op jit(solution)/shard_map/ppermute | solution.py:99
  52.7 7.0 %collective-permute-done.16.refs_7_ = f32[24,8,256]{2,1,0:T(8,128)S(1)} collective-permute-done((f32[24,8,256]{2,1,0:T(8,128)S(1)}, f32[24,8,256]{2,1,0:T(8,128)S(1)}, u32[]{:S(2)}, u32[]{:S(2)}) %collective-permute-start.16) | collective-permute-done | bytes 196640 | tf_op jit(solution)/shard_map/ppermute | solution.py:99
  59.6 1.4 %stage_inner.3.refs_12_.refs_0_ = f32[5,24,16,256]{3,2,1,0:T(8,128)S(1)} custom-call(f32[5,24,16,256]{3,2,1,0:T(8,128)S(1)} %stage_inner.2.refs_14_.refs_0_, f32[5,8,16,256]{3,2,1,0:T(8,128)S(1)} %get-tuple-element.65.refs_1_, f32[5,24,16,256]{3,2,1,0:T(8,128)S(1)} %get-tuple-element.53.refs_6_.refs_0_.refs_4_.refs_2_, ...), custom_call_target="tpu_custom_call" | custom-call | bytes 134217728 | tf_op jit(solution)/shard_map/stage_inner/pallas_call | solution.py:114
  61.1 0.0 collective-permute-done.17.refs_8_
  61.1 0.0 collective-permute-done.18.refs_9_
  61.1 0.7 stage_rim.3
  61.8 1.2 %collective-permute-start.21 = (f32[15,16,256]{2,1,0:T(8,128)S(1)}, f32[15,16,256]{2,1,0:T(8,128)S(1)}, u32[]{:S(2)}, u32[]{:S(2)}) collective-permute-start(f32[15,16,256]{2,1,0:T(8,128)S(1)} %get-tuple-element.73), channel_id=1, source_target_pairs={{0,32},{32,0},{64,96},{96,64},{1,33},{33,1},{65,97},{97,65},{2,34}... | collective-permute-start | bytes 737288 | tf_op jit(solution)/shard_map/ppermute | solution.py:99
  63.0 0.6 collective-permute-start.22
  63.6 0.2 collective-permute-start.20
  63.8 1.3 %collective-permute-done.19.refs_7_ = f32[24,8,256]{2,1,0:T(8,128)S(1)} collective-permute-done((f32[24,8,256]{2,1,0:T(8,128)S(1)}, f32[24,8,256]{2,1,0:T(8,128)S(1)}, u32[]{:S(2)}, u32[]{:S(2)}) %collective-permute-start.19) | collective-permute-done | bytes 196640 | tf_op jit(solution)/shard_map/ppermute | solution.py:99
  65.1 7.0 %collective-permute-done.20.refs_8_ = f32[24,8,256]{2,1,0:T(8,128)S(1)} collective-permute-done((f32[24,8,256]{2,1,0:T(8,128)S(1)}, f32[24,8,256]{2,1,0:T(8,128)S(1)}, u32[]{:S(2)}, u32[]{:S(2)}) %collective-permute-start.20) | collective-permute-done | bytes 196640 | tf_op jit(solution)/shard_map/ppermute | solution.py:99
  72.0 1.6 %final_inner.1.refs_13_ = f32[5,24,16,256]{3,2,1,0:T(8,128)S(1)} custom-call(f32[5,24,16,256]{3,2,1,0:T(8,128)S(1)} %stage_inner.3.refs_12_.refs_0_, f32[5,8,16,256]{3,2,1,0:T(8,128)S(1)} %get-tuple-element.70.refs_1_, f32[5,24,16,256]{3,2,1,0:T(8,128)S(1)} %get-tuple-element.53.refs_6_.refs_0_.refs_4_.refs_2_, ...), custom_call_target="tpu_custom_call" | custom-call | bytes 134217728 | tf_op jit(solution)/shard_map/final_inner/pallas_call | solution.py:114
  73.6 0.0 collective-permute-done.22.refs_10_
  73.7 1.9 %final_rim.1 = f32[5,32,16,256]{3,2,1,0:T(8,128)} custom-call(f32[5,24,16,256]{3,2,1,0:T(8,128)S(1)} %stage_inner.3.refs_12_.refs_0_, f32[5,8,16,256]{3,2,1,0:T(8,128)S(1)} %get-tuple-element.70.refs_1_, f32[5,24,16,256]{3,2,1,0:T(8,128)S(1)} %get-tuple-element.53.refs_6_.refs_0_.refs_4_.refs_2_, ...), custom_call_target="tpu_custom_call" | custom-call | tf_op jit(solution)/shard_map/final_rim/pallas_call | solution.py:114
  (12 shorter events, 0.0 us)
Async XLA Ops:
  0.0 13.2 %copy-start.4 = (f32[16,16,512]{2,1,0:T(8,128)S(1)}, f32[16,16,512]{2,1,0:T(8,128)}, u32[]{:S(2)}) copy-start(f32[16,16,512]{2,1,0:T(8,128)} %refs_0_.4) | copy-start | bytes 1572868
  1.1 12.6 %collective-permute-start.1 = (f32[4,16,512]{2,1,0:T(8,128)S(1)}, f32[4,16,512]{2,1,0:T(8,128)S(1)}, u32[]{:S(2)}, u32[]{:S(2)}) collective-permute-start(f32[4,16,512]{2,1,0:T(8,128)S(1)} %get-tuple-element.75), channel_id=1, source_target_pairs={{0,96},{32,64},{64,32},{96,0},{1,97},{33,65},{65,33},{97,1},{2,98}... | collective-permute-start | bytes 393224 | tf_op jit(solution)/shard_map/ppermute | solution.py:99
  4.2 9.4 %collective-permute-start = (f32[4,16,512]{2,1,0:T(8,128)S(1)}, f32[4,16,512]{2,1,0:T(8,128)S(1)}, u32[]{:S(2)}, u32[]{:S(2)}) collective-permute-start(f32[4,16,512]{2,1,0:T(8,128)S(1)} %get-tuple-element.76.refs_1_), channel_id=1, source_target_pairs={{0,32},{32,0},{64,96},{96,64},{1,33},{33,1},{65,97},{97,65},{2,34}... | collective-permute-start | bytes 393224 | tf_op jit(solution)/shard_map/ppermute | solution.py:99
  4.4 1.7 %copy-start = (f32[5,32,16,256]{3,2,1,0:T(8,128)S(1)}, f32[5,32,16,256]{3,2,1,0:T(8,128)}, u32[]{:S(2)}) copy-start(f32[5,32,16,256]{3,2,1,0:T(8,128)} %refs_6_.4) | copy-start | bytes 7864324
  6.1 7.0 %copy-start.5 = (s32[16,16,512]{2,1,0:T(8,128)S(1)}, s32[16,16,512]{2,1,0:T(8,128)}, u32[]{:S(2)}) copy-start(s32[16,16,512]{2,1,0:T(8,128)} %refs_1_.1) | copy-start | bytes 1572868
  6.2 10.6 %copy-start.6 = (s32[256]{0:T(256)S(1)}, s32[256]{0:T(256)}, u32[]{:S(2)}) copy-start(s32[256]{0:T(256)} %param.9) | copy-start | bytes 3076
  6.2 10.5 %copy-start.7 = (s32[256]{0:T(256)S(1)}, s32[256]{0:T(256)}, u32[]{:S(2)}) copy-start(s32[256]{0:T(256)} %param.10) | copy-start | bytes 3076
  6.3 10.5 %collective-permute-start.4 = (f32[15,16,256]{2,1,0:T(8,128)S(1)}, f32[15,16,256]{2,1,0:T(8,128)S(1)}, u32[]{:S(2)}, u32[]{:S(2)}) collective-permute-start(f32[15,16,256]{2,1,0:T(8,128)S(1)} %get-tuple-element.46), channel_id=1, source_target_pairs={{0,32},{32,0},{64,96},{96,64},{1,33},{33,1},{65,97},{97,65},{2,34}... | collective-permute-start | bytes 737288 | tf_op jit(solution)/shard_map/ppermute | solution.py:99
  8.2 8.6 %collective-permute-start.5 = (f32[15,16,256]{2,1,0:T(8,128)S(1)}, f32[15,16,256]{2,1,0:T(8,128)S(1)}, u32[]{:S(2)}, u32[]{:S(2)}) collective-permute-start(f32[15,16,256]{2,1,0:T(8,128)S(1)} %get-tuple-element.47), channel_id=1, source_target_pairs={{0,96},{32,64},{64,32},{96,0},{1,97},{33,65},{65,33},{97,1},{2,98}... | collective-permute-start | bytes 737288 | tf_op jit(solution)/shard_map/ppermute | solution.py:99
  8.4 8.4 %collective-permute-start.6 = (f32[24,8,256]{2,1,0:T(8,128)S(1)}, f32[24,8,256]{2,1,0:T(8,128)S(1)}, u32[]{:S(2)}, u32[]{:S(2)}) collective-permute-start(f32[24,8,256]{2,1,0:T(8,128)S(1)} %get-tuple-element.48), channel_id=1, source_target_pairs={{0,31},{1,2},{2,1},{3,4},{4,3},{5,6},{6,5},{7,8},{8,7},{9,10},{10,... | collective-permute-start | bytes 589832 | tf_op jit(solution)/shard_map/ppermute | solution.py:105
  13.7 15.0 %copy-start.1 = (f32[5,32,16,256]{3,2,1,0:T(8,128)S(1)}, f32[5,32,16,256]{3,2,1,0:T(8,128)}, u32[]{:S(2)}) copy-start(f32[5,32,16,256]{3,2,1,0:T(8,128)} %refs_6_.4) | copy-start | bytes 7864324
  13.7 15.0 %copy-start.2 = (bf16[2,2,256,256]{3,2,1,0:T(8,128)(2,1)S(1)}, bf16[2,2,256,256]{3,2,1,0:T(8,128)(2,1)}, u32[]{:S(2)}) copy-start(bf16[2,2,256,256]{3,2,1,0:T(8,128)(2,1)} %constant.17.clone.refs_6_.refs_11_.refs_13_.refs_9_.refs_10_.refs_12_) | copy-start | bytes 1572868
  13.7 15.0 %copy-start.3 = (bf16[2,2,128,224]{3,2,1,0:T(8,128)(2,1)S(1)}, bf16[2,2,128,224]{3,2,1,0:T(8,128)(2,1)}, u32[]{:S(2)}) copy-start(bf16[2,2,128,224]{3,2,1,0:T(8,128)(2,1)} %constant.16.clone.refs_5_.refs_10_.refs_12_.refs_8_.refs_9_.refs_11_) | copy-start | bytes 688132
  13.9 3.2 %collective-permute-start.2 = (f32[8,8,512]{2,1,0:T(8,128)S(1)}, f32[8,8,512]{2,1,0:T(8,128)S(1)}, u32[]{:S(2)}, u32[]{:S(2)}) collective-permute-start(f32[8,8,512]{2,1,0:T(8,128)S(1)} %get-tuple-element.44), channel_id=1, source_target_pairs={{0,1},{1,0},{2,3},{3,2},{4,5},{5,4},{6,7},{7,6},{8,9},{9,8},{10,11... | collective-permute-start | bytes 393224 | tf_op jit(solution)/shard_map/ppermute | solution.py:99
  14.0 7.8 %collective-permute-start.3 = (f32[8,8,512]{2,1,0:T(8,128)S(1)}, f32[8,8,512]{2,1,0:T(8,128)S(1)}, u32[]{:S(2)}, u32[]{:S(2)}) collective-permute-start(f32[8,8,512]{2,1,0:T(8,128)S(1)} %get-tuple-element.45), channel_id=1, source_target_pairs={{0,31},{1,2},{2,1},{3,4},{4,3},{5,6},{6,5},{7,8},{8,7},{9,10},{10,... | collective-permute-start | bytes 393224 | tf_op jit(solution)/shard_map/ppermute | solution.py:99
  24.1 4.6 %collective-permute-start.7 = (f32[41,8,256]{2,1,0:T(8,128)S(1)}, f32[41,8,256]{2,1,0:T(8,128)S(1)}, u32[]{:S(2)}, u32[]{:S(2)}) collective-permute-start(f32[41,8,256]{2,1,0:T(8,128)S(1)} %get-tuple-element.51), channel_id=1, source_target_pairs={{0,1},{1,0},{2,3},{3,2},{4,5},{5,4},{6,7},{7,6},{8,9},{9,8},{10,11... | collective-permute-start | bytes 1007624 | tf_op jit(solution)/shard_map/ppermute | solution.py:99
  24.2 6.2 %collective-permute-start.8 = (f32[17,8,256]{2,1,0:T(8,128)S(1)}, f32[17,8,256]{2,1,0:T(8,128)S(1)}, u32[]{:S(2)}, u32[]{:S(2)}) collective-permute-start(f32[17,8,256]{2,1,0:T(8,128)S(1)} %get-tuple-element.56), channel_id=1, source_target_pairs={{0,32},{32,0},{64,96},{96,64},{1,33},{33,1},{65,97},{97,65},{2,34}... | collective-permute-start | bytes 417800 | tf_op jit(solution)/shard_map/ppermute | solution.py:99
  24.7 6.9 %collective-permute-start.9 = (f32[17,8,256]{2,1,0:T(8,128)S(1)}, f32[17,8,256]{2,1,0:T(8,128)S(1)}, u32[]{:S(2)}, u32[]{:S(2)}) collective-permute-start(f32[17,8,256]{2,1,0:T(8,128)S(1)} %get-tuple-element.57), channel_id=1, source_target_pairs={{0,96},{32,64},{64,32},{96,0},{1,97},{33,65},{65,33},{97,1},{2,98}... | collective-permute-start | bytes 417800 | tf_op jit(solution)/shard_map/ppermute | solution.py:99
  27.3 7.8 %collective-permute-start.10 = (f32[17,8,256]{2,1,0:T(8,128)S(1)}, f32[17,8,256]{2,1,0:T(8,128)S(1)}, u32[]{:S(2)}, u32[]{:S(2)}) collective-permute-start(f32[17,8,256]{2,1,0:T(8,128)S(1)} %get-tuple-element.58), channel_id=1, source_target_pairs={{0,31},{1,2},{2,1},{3,4},{4,3},{5,6},{6,5},{7,8},{8,7},{9,10},{10,... | collective-permute-start | bytes 417800 | tf_op jit(solution)/shard_map/ppermute | solution.py:99
  35.7 11.9 %collective-permute-start.13 = (f32[15,16,256]{2,1,0:T(8,128)S(1)}, f32[15,16,256]{2,1,0:T(8,128)S(1)}, u32[]{:S(2)}, u32[]{:S(2)}) collective-permute-start(f32[15,16,256]{2,1,0:T(8,128)S(1)} %get-tuple-element.63), channel_id=1, source_target_pairs={{0,32},{32,0},{64,96},{96,64},{1,33},{33,1},{65,97},{97,65},{2,34}... | collective-permute-start | bytes 737288 | tf_op jit(solution)/shard_map/ppermute | solution.py:99
  37.1 10.5 %collective-permute-start.14 = (f32[15,16,256]{2,1,0:T(8,128)S(1)}, f32[15,16,256]{2,1,0:T(8,128)S(1)}, u32[]{:S(2)}, u32[]{:S(2)}) collective-permute-start(f32[15,16,256]{2,1,0:T(8,128)S(1)} %get-tuple-element.64), channel_id=1, source_target_pairs={{0,96},{32,64},{64,32},{96,0},{1,97},{33,65},{65,33},{97,1},{2,98}... | collective-permute-start | bytes 737288 | tf_op jit(solution)/shard_map/ppermute | solution.py:99
  37.7 1.4 %collective-permute-start.11 = (f32[24,8,256]{2,1,0:T(8,128)S(1)}, f32[24,8,256]{2,1,0:T(8,128)S(1)}, u32[]{:S(2)}, u32[]{:S(2)}) collective-permute-start(f32[24,8,256]{2,1,0:T(8,128)S(1)} %get-tuple-element.61), channel_id=1, source_target_pairs={{0,1},{1,0},{2,3},{3,2},{4,5},{5,4},{6,7},{7,6},{8,9},{9,8},{10,11... | collective-permute-start | bytes 589832 | tf_op jit(solution)/shard_map/ppermute | solution.py:99
  37.7 8.4 %collective-permute-start.12 = (f32[24,8,256]{2,1,0:T(8,128)S(1)}, f32[24,8,256]{2,1,0:T(8,128)S(1)}, u32[]{:S(2)}, u32[]{:S(2)}) collective-permute-start(f32[24,8,256]{2,1,0:T(8,128)S(1)} %get-tuple-element.62), channel_id=1, source_target_pairs={{0,31},{1,2},{2,1},{3,4},{4,3},{5,6},{6,5},{7,8},{8,7},{9,10},{10,... | collective-permute-start | bytes 589832 | tf_op jit(solution)/shard_map/ppermute | solution.py:99
  48.2 12.8 %collective-permute-start.17 = (f32[15,16,256]{2,1,0:T(8,128)S(1)}, f32[15,16,256]{2,1,0:T(8,128)S(1)}, u32[]{:S(2)}, u32[]{:S(2)}) collective-permute-start(f32[15,16,256]{2,1,0:T(8,128)S(1)} %get-tuple-element.68), channel_id=1, source_target_pairs={{0,32},{32,0},{64,96},{96,64},{1,33},{33,1},{65,97},{97,65},{2,34}... | collective-permute-start | bytes 737288 | tf_op jit(solution)/shard_map/ppermute | solution.py:99
  48.5 12.6 %collective-permute-start.18 = (f32[15,16,256]{2,1,0:T(8,128)S(1)}, f32[15,16,256]{2,1,0:T(8,128)S(1)}, u32[]{:S(2)}, u32[]{:S(2)}) collective-permute-start(f32[15,16,256]{2,1,0:T(8,128)S(1)} %get-tuple-element.69), channel_id=1, source_target_pairs={{0,96},{32,64},{64,32},{96,0},{1,97},{33,65},{65,33},{97,1},{2,98}... | collective-permute-start | bytes 737288 | tf_op jit(solution)/shard_map/ppermute | solution.py:99
  51.2 1.4 %collective-permute-start.15 = (f32[24,8,256]{2,1,0:T(8,128)S(1)}, f32[24,8,256]{2,1,0:T(8,128)S(1)}, u32[]{:S(2)}, u32[]{:S(2)}) collective-permute-start(f32[24,8,256]{2,1,0:T(8,128)S(1)} %get-tuple-element.66), channel_id=1, source_target_pairs={{0,1},{1,0},{2,3},{3,2},{4,5},{5,4},{6,7},{7,6},{8,9},{9,8},{10,11... | collective-permute-start | bytes 589832 | tf_op jit(solution)/shard_map/ppermute | solution.py:99
  51.2 8.4 %collective-permute-start.16 = (f32[24,8,256]{2,1,0:T(8,128)S(1)}, f32[24,8,256]{2,1,0:T(8,128)S(1)}, u32[]{:S(2)}, u32[]{:S(2)}) collective-permute-start(f32[24,8,256]{2,1,0:T(8,128)S(1)} %get-tuple-element.67), channel_id=1, source_target_pairs={{0,31},{1,2},{2,1},{3,4},{4,3},{5,6},{6,5},{7,8},{8,7},{9,10},{10,... | collective-permute-start | bytes 589832 | tf_op jit(solution)/shard_map/ppermute | solution.py:99
  61.8 11.9 %collective-permute-start.21 = (f32[15,16,256]{2,1,0:T(8,128)S(1)}, f32[15,16,256]{2,1,0:T(8,128)S(1)}, u32[]{:S(2)}, u32[]{:S(2)}) collective-permute-start(f32[15,16,256]{2,1,0:T(8,128)S(1)} %get-tuple-element.73), channel_id=1, source_target_pairs={{0,32},{32,0},{64,96},{96,64},{1,33},{33,1},{65,97},{97,65},{2,34}... | collective-permute-start | bytes 737288 | tf_op jit(solution)/shard_map/ppermute | solution.py:99
  63.0 10.6 %collective-permute-start.22 = (f32[15,16,256]{2,1,0:T(8,128)S(1)}, f32[15,16,256]{2,1,0:T(8,128)S(1)}, u32[]{:S(2)}, u32[]{:S(2)}) collective-permute-start(f32[15,16,256]{2,1,0:T(8,128)S(1)} %get-tuple-element.74), channel_id=1, source_target_pairs={{0,96},{32,64},{64,32},{96,0},{1,97},{33,65},{65,33},{97,1},{2,98}... | collective-permute-start | bytes 737288 | tf_op jit(solution)/shard_map/ppermute | solution.py:99
  63.6 1.4 %collective-permute-start.19 = (f32[24,8,256]{2,1,0:T(8,128)S(1)}, f32[24,8,256]{2,1,0:T(8,128)S(1)}, u32[]{:S(2)}, u32[]{:S(2)}) collective-permute-start(f32[24,8,256]{2,1,0:T(8,128)S(1)} %get-tuple-element.71), channel_id=1, source_target_pairs={{0,1},{1,0},{2,3},{3,2},{4,5},{5,4},{6,7},{7,6},{8,9},{9,8},{10,11... | collective-permute-start | bytes 589832 | tf_op jit(solution)/shard_map/ppermute | solution.py:99
  63.6 8.4 %collective-permute-start.20 = (f32[24,8,256]{2,1,0:T(8,128)S(1)}, f32[24,8,256]{2,1,0:T(8,128)S(1)}, u32[]{:S(2)}, u32[]{:S(2)}) collective-permute-start(f32[24,8,256]{2,1,0:T(8,128)S(1)} %get-tuple-element.72), channel_id=1, source_target_pairs={{0,31},{1,2},{2,1},{3,4},{4,3},{5,6},{6,5},{7,8},{8,7},{9,10},{10,... | collective-permute-start | bytes 589832 | tf_op jit(solution)/shard_map/ppermute | solution.py:99

commit v5 on v4

--- a/solution.py
+++ b/solution.py
@@ -24,7 +24,7 @@
 PARAMS = pltpu.CompilerParams(vmem_limit_bytes=24 * 1024 * 1024)
 GROUP = 8
 RIM = 4
-COST = 1 << 27
+COST = 1 << 37
 
 
 def np_split(matrix):
@@ -96,6 +96,8 @@
     devices = lax.axis_size(axis)
     pairs_a = [(i, i ^ 1) for i in range(devices)]
     pairs_b = [(i, (i - 1) % devices if i % 2 == 0 else (i + 1) % devices) for i in range(devices)]
+    if axis == "ax":
+        pairs_b = [(i, j if abs(i - j) == 1 else i) for i, j in pairs_b]
     return lax.ppermute(to_a, axis, pairs_a), lax.ppermute(to_b, axis, pairs_b)
 
 
@@ -119,7 +121,7 @@
         scratch_shapes=[pltpu.VMEM(*s) if isinstance(s, tuple) else s for s in scratch],
         compiler_params=PARAMS,
         name=name,
-        cost_estimate=pl.CostEstimate(flops=0, bytes_accessed=cost, transcendentals=0),
+        cost_estimate=pl.CostEstimate(flops=cost, bytes_accessed=0, transcendentals=0),
     )(*args, *after)
 
 

time: 75.9 us -> 73.5 us (0.968)
  the two profiles are of different devices: /device:TPU:0 before, /device:TPU:8 now
where the time goes in v5:
time: 73.5 us; the launch traced here: 73.3 us
  starting transfers between devices  33.6 us (46%)
  waiting for transfers between devices  22.7 us (31%)
  Pallas kernels  13.6 us (19%)
  local copies, waits for them, and re-layouts  1.78 us (2%)
  other arithmetic  1.05 us (1%)
    ppermute x11, starting transfers between devices, swap(): lax.ppermute(to_b, axis, pairs_b)  26.3 us
    ppermute x11, waiting for transfers between devices, swap(): lax.ppermute(to_b, axis, pairs_b)  21.5 us
    pallas_call x13, Pallas kernels, full_specs(): pl.pallas_call(run, out_shape=[jax.ShapeDtypeStruct(s, d) for s, d in out...  13.6 us
    ppermute x1, starting transfers between devices, swap_b(): return (lax.ppermute(value, axis, pairs),)  4.63 us
    ppermute x11, starting transfers between devices, swap(): lax.ppermute(to_a, axis, pairs_a)  2.69 us
    unnamed x18, local copies, waits for them, and re-layouts  1.78 us
  transfers between devices with their start and end apart: 23, of which 10 were waited for; matrix products, arithmetic and copies ran while one was open for 0% of the time, Pallas kernels for 10%

profile of v5, /device:TPU:8, one launch (start us, length us, event | category | flops | bytes accessed | tf_op | source)
XLA Modules:
  0.0 73.3 jit_solution(13362592414866695745)
XLA Ops:
  0.0 1.0 %slice_select_fusion = (f32[4,16,512]{2,1,0:T(8,128)S(1)}, f32[4,16,512]{2,1,0:T(8,128)S(1)}) fusion(f32[16,16,512]{2,1,0:T(8,128)} %refs_0_.4, pred[]{:T(512)S(6)} %eq.3), kind=kLoop, calls=%fused_computation | loop fusion | flops 65536 | bytes 524289 | tf_op jit(solution)/shard_map/jit(_where)/select_n | solution.py:549
  1.1 3.5 %collective-permute-start.1 = (f32[4,16,512]{2,1,0:T(8,128)S(1)}, f32[4,16,512]{2,1,0:T(8,128)S(1)}, u32[]{:S(2)}, u32[]{:S(2)}) collective-permute-start(f32[4,16,512]{2,1,0:T(8,128)S(1)} %get-tuple-element.75), channel_id=1, source_target_pairs={{0,0},{32,64},{64,32},{96,96},{1,1},{33,65},{65,33},{97,97},{2,2},... | collective-permute-start | bytes 393224 | tf_op jit(solution)/shard_map/ppermute | solution.py:101
  4.5 0.1 collective-permute-start
  4.6 0.0 copy-start
  4.7 1.7 %copy-done = f32[5,32,16,256]{3,2,1,0:T(8,128)S(1)} copy-done((f32[5,32,16,256]{3,2,1,0:T(8,128)S(1)}, f32[5,32,16,256]{3,2,1,0:T(8,128)}, u32[]{:S(2)}) %copy-start) | copy-done | bytes 2621464
  6.4 0.1 edges.1
  6.5 0.0 copy-start.7
  6.5 0.0 copy-start.8
  6.5 2.1 %collective-permute-start.4 = (f32[15,16,256]{2,1,0:T(8,128)S(1)}, f32[15,16,256]{2,1,0:T(8,128)S(1)}, u32[]{:S(2)}, u32[]{:S(2)}) collective-permute-start(f32[15,16,256]{2,1,0:T(8,128)S(1)} %get-tuple-element.46), channel_id=1, source_target_pairs={{0,32},{32,0},{64,96},{96,64},{1,33},{33,1},{65,97},{97,65},{2,34}... | collective-permute-start | bytes 737288 | tf_op jit(solution)/shard_map/ppermute | solution.py:101
  8.6 2.3 %collective-permute-start.5 = (f32[15,16,256]{2,1,0:T(8,128)S(1)}, f32[15,16,256]{2,1,0:T(8,128)S(1)}, u32[]{:S(2)}, u32[]{:S(2)}) collective-permute-start(f32[15,16,256]{2,1,0:T(8,128)S(1)} %get-tuple-element.47), channel_id=1, source_target_pairs={{0,0},{32,64},{64,32},{96,96},{1,1},{33,65},{65,33},{97,97},{2,2},... | collective-permute-start | bytes 737288 | tf_op jit(solution)/shard_map/ppermute | solution.py:101
  11.0 4.6 %collective-permute-start.6 = (f32[24,8,256]{2,1,0:T(8,128)S(1)}, f32[24,8,256]{2,1,0:T(8,128)S(1)}, u32[]{:S(2)}, u32[]{:S(2)}) collective-permute-start(f32[24,8,256]{2,1,0:T(8,128)S(1)} %get-tuple-element.48), channel_id=1, source_target_pairs={{0,31},{1,2},{2,1},{3,4},{4,3},{5,6},{6,5},{7,8},{8,7},{9,10},{10,... | collective-permute-start | bytes 589832 | tf_op jit(solution)/shard_map/ppermute | solution.py:107
  15.6 0.5 filter_inner.1
  16.1 0.0 collective-permute-done.1.refs_3_
  16.1 0.0 collective-permute-done.refs_2_
  16.1 0.0 copy-start.1
  16.1 0.0 copy-start.3
  16.1 0.0 copy-start.4
  16.2 0.2 filter_axial.1
  16.4 0.1 collective-permute-start.2
  16.5 1.8 %collective-permute-start.3 = (f32[8,8,512]{2,1,0:T(8,128)S(1)}, f32[8,8,512]{2,1,0:T(8,128)S(1)}, u32[]{:S(2)}, u32[]{:S(2)}) collective-permute-start(f32[8,8,512]{2,1,0:T(8,128)S(1)} %get-tuple-element.45), channel_id=1, source_target_pairs={{0,31},{1,2},{2,1},{3,4},{4,3},{5,6},{6,5},{7,8},{8,7},{9,10},{10,... | collective-permute-start | bytes 393224 | tf_op jit(solution)/shard_map/ppermute | solution.py:101
  18.3 1.2 %collective-permute-done.6.refs_5_.refs_2_ = f32[24,8,256]{2,1,0:T(8,128)S(1)} collective-permute-done((f32[24,8,256]{2,1,0:T(8,128)S(1)}, f32[24,8,256]{2,1,0:T(8,128)S(1)}, u32[]{:S(2)}, u32[]{:S(2)}) %collective-permute-start.6) | collective-permute-done | bytes 196640 | tf_op jit(solution)/shard_map/ppermute | solution.py:107
  19.5 0.0 collective-permute-done.4.refs_3_
  19.5 0.0 collective-permute-done.5.refs_4_
  19.5 0.3 route.1
  19.8 0.0 collective-permute-done.2.refs_2_
  19.8 4.4 %collective-permute-done.3.refs_3_ = f32[8,8,512]{2,1,0:T(8,128)S(1)} collective-permute-done((f32[8,8,512]{2,1,0:T(8,128)S(1)}, f32[8,8,512]{2,1,0:T(8,128)S(1)}, u32[]{:S(2)}, u32[]{:S(2)}) %collective-permute-start.3) | collective-permute-done | bytes 131104 | tf_op jit(solution)/shard_map/ppermute | solution.py:101
  24.2 2.3 %filter_rest.1 = (f32[256,256]{1,0:T(8,128)S(1)}, f32[17,8,256]{2,1,0:T(8,128)S(1)}, f32[17,8,256]{2,1,0:T(8,128)S(1)}, f32[41,8,256]{2,1,0:T(8,128)S(1)}, f32[17,8,256]{2,1,0:T(8,128)S(1)}) custom-call(f32[16,16,512]{2,1,0:T(8,128)S(1)} %get-tuple-element.43.refs_2_.refs_0_, s32[16,16,512]{2,1,0:T(8,128)S(1)} %get-tuple-element.42.refs_1_, ...), custom_call_target="tpu_custom_call" | custom-call | tf_op jit(solution)/shard_map/filter_rest/pallas_call | solution.py:116
  26.6 0.1 collective-permute-start.7
  26.7 0.1 collective-permute-start.8
  26.8 3.5 %collective-permute-start.9 = (f32[17,8,256]{2,1,0:T(8,128)S(1)}, f32[17,8,256]{2,1,0:T(8,128)S(1)}, u32[]{:S(2)}, u32[]{:S(2)}) collective-permute-start(f32[17,8,256]{2,1,0:T(8,128)S(1)} %get-tuple-element.57), channel_id=1, source_target_pairs={{0,0},{32,64},{64,32},{96,96},{1,1},{33,65},{65,33},{97,97},{2,2},... | collective-permute-start | bytes 417800 | tf_op jit(solution)/shard_map/ppermute | solution.py:101
  30.3 1.5 %collective-permute-start.10 = (f32[17,8,256]{2,1,0:T(8,128)S(1)}, f32[17,8,256]{2,1,0:T(8,128)S(1)}, u32[]{:S(2)}, u32[]{:S(2)}) collective-permute-start(f32[17,8,256]{2,1,0:T(8,128)S(1)} %get-tuple-element.58), channel_id=1, source_target_pairs={{0,31},{1,2},{2,1},{3,4},{4,3},{5,6},{6,5},{7,8},{8,7},{9,10},{10,... | collective-permute-start | bytes 417800 | tf_op jit(solution)/shard_map/ppermute | solution.py:101
  31.8 0.0 collective-permute-done.7.refs_1_.refs_4_
  31.8 1.9 %operator.1 = (f32[5,24,16,256]{3,2,1,0:T(8,128)S(1)}, f32[5,8,16,256]{3,2,1,0:T(8,128)S(1)}) custom-call(f32[5,32,16,256]{3,2,1,0:T(8,128)S(1)} %copy-done.1, f32[41,8,256]{2,1,0:T(8,128)S(1)} %collective-permute-done.7.refs_1_.refs_4_, f32[24,8,256]{2,1,0:T(8,128)S(1)} %collective-permute-done.6.refs_5_.refs_2_, ...), custom_call_target="tpu_custom_call" | custom-call | tf_op jit(solution)/shard_map/operator/pallas_call | solution.py:116
  33.7 0.0 collective-permute-done.8.refs_2_
  33.7 1.0 %collective-permute-done.9.refs_3_ = f32[17,8,256]{2,1,0:T(8,128)S(1)} collective-permute-done((f32[17,8,256]{2,1,0:T(8,128)S(1)}, f32[17,8,256]{2,1,0:T(8,128)S(1)}, u32[]{:S(2)}, u32[]{:S(2)}) %collective-permute-start.9) | collective-permute-done | bytes 139296 | tf_op jit(solution)/shard_map/ppermute | solution.py:101
  34.7 3.5 %collective-permute-done.10.refs_5_ = f32[17,8,256]{2,1,0:T(8,128)S(1)} collective-permute-done((f32[17,8,256]{2,1,0:T(8,128)S(1)}, f32[17,8,256]{2,1,0:T(8,128)S(1)}, u32[]{:S(2)}, u32[]{:S(2)}) %collective-permute-start.10) | collective-permute-done | bytes 139296 | tf_op jit(solution)/shard_map/ppermute | solution.py:101
  38.2 0.6 gather.1
  38.8 0.1 collective-permute-start.11
  38.8 1.5 %collective-permute-start.12 = (f32[24,8,256]{2,1,0:T(8,128)S(1)}, f32[24,8,256]{2,1,0:T(8,128)S(1)}, u32[]{:S(2)}, u32[]{:S(2)}) collective-permute-start(f32[24,8,256]{2,1,0:T(8,128)S(1)} %get-tuple-element.62), channel_id=1, source_target_pairs={{0,31},{1,2},{2,1},{3,4},{4,3},{5,6},{6,5},{7,8},{8,7},{9,10},{10,... | collective-permute-start | bytes 589832 | tf_op jit(solution)/shard_map/ppermute | solution.py:101
  40.4 0.0 collective-permute-start.13
  40.4 2.7 %collective-permute-start.14 = (f32[15,16,256]{2,1,0:T(8,128)S(1)}, f32[15,16,256]{2,1,0:T(8,128)S(1)}, u32[]{:S(2)}, u32[]{:S(2)}) collective-permute-start(f32[15,16,256]{2,1,0:T(8,128)S(1)} %get-tuple-element.64), channel_id=1, source_target_pairs={{0,0},{32,64},{64,32},{96,96},{1,1},{33,65},{65,33},{97,97},{2,2},... | collective-permute-start | bytes 737288 | tf_op jit(solution)/shard_map/ppermute | solution.py:101
  43.0 0.0 collective-permute-done.11.refs_8_
  43.1 4.3 %collective-permute-done.12.refs_9_ = f32[24,8,256]{2,1,0:T(8,128)S(1)} collective-permute-done((f32[24,8,256]{2,1,0:T(8,128)S(1)}, f32[24,8,256]{2,1,0:T(8,128)S(1)}, u32[]{:S(2)}, u32[]{:S(2)}) %collective-permute-start.12) | collective-permute-done | bytes 196640 | tf_op jit(solution)/shard_map/ppermute | solution.py:101
  47.3 1.5 %stage_inner.2.refs_14_.refs_0_ = f32[5,24,16,256]{3,2,1,0:T(8,128)S(1)} custom-call(f32[5,24,16,256]{3,2,1,0:T(8,128)S(1)} %get-tuple-element.53.refs_6_.refs_0_.refs_4_.refs_2_, f32[5,8,16,256]{3,2,1,0:T(8,128)S(1)} %get-tuple-element.54.refs_7_.refs_1_.refs_5_.refs_3_, f32[24,16,256]{2,1,0:T(8,128)S(1)} %get-tuple-element.59.refs_2_.refs_6_.refs_4_, ...), custom_call_target="tpu_custom_call" | custom-call | flops 137438953472 | tf_op jit(solution)/shard_map/stage_inner/pallas_call | solution.py:116
  48.8 0.0 collective-permute-done.13.refs_10_
  48.8 0.3 collective-permute-done.14.refs_11_
  49.1 0.7 stage_rim.2
  49.8 0.1 collective-permute-start.15
  49.9 1.9 %collective-permute-start.16 = (f32[24,8,256]{2,1,0:T(8,128)S(1)}, f32[24,8,256]{2,1,0:T(8,128)S(1)}, u32[]{:S(2)}, u32[]{:S(2)}) collective-permute-start(f32[24,8,256]{2,1,0:T(8,128)S(1)} %get-tuple-element.67), channel_id=1, source_target_pairs={{0,31},{1,2},{2,1},{3,4},{4,3},{5,6},{6,5},{7,8},{8,7},{9,10},{10,... | collective-permute-start | bytes 589832 | tf_op jit(solution)/shard_map/ppermute | solution.py:101
  51.8 0.0 collective-permute-start.17
  51.8 2.7 %collective-permute-start.18 = (f32[15,16,256]{2,1,0:T(8,128)S(1)}, f32[15,16,256]{2,1,0:T(8,128)S(1)}, u32[]{:S(2)}, u32[]{:S(2)}) collective-permute-start(f32[15,16,256]{2,1,0:T(8,128)S(1)} %get-tuple-element.69), channel_id=1, source_target_pairs={{0,0},{32,64},{64,32},{96,96},{1,1},{33,65},{65,33},{97,97},{2,2},... | collective-permute-start | bytes 737288 | tf_op jit(solution)/shard_map/ppermute | solution.py:101
  54.6 3.8 %collective-permute-done.16.refs_7_ = f32[24,8,256]{2,1,0:T(8,128)S(1)} collective-permute-done((f32[24,8,256]{2,1,0:T(8,128)S(1)}, f32[24,8,256]{2,1,0:T(8,128)S(1)}, u32[]{:S(2)}, u32[]{:S(2)}) %collective-permute-start.16) | collective-permute-done | bytes 196640 | tf_op jit(solution)/shard_map/ppermute | solution.py:101
  58.4 1.4 %stage_inner.3.refs_12_.refs_0_ = f32[5,24,16,256]{3,2,1,0:T(8,128)S(1)} custom-call(f32[5,24,16,256]{3,2,1,0:T(8,128)S(1)} %stage_inner.2.refs_14_.refs_0_, f32[5,8,16,256]{3,2,1,0:T(8,128)S(1)} %get-tuple-element.65.refs_1_, f32[5,24,16,256]{3,2,1,0:T(8,128)S(1)} %get-tuple-element.53.refs_6_.refs_0_.refs_4_.refs_2_, ...), custom_call_target="tpu_custom_call" | custom-call | flops 137438953472 | tf_op jit(solution)/shard_map/stage_inner/pallas_call | solution.py:116
  59.8 0.0 copy-start.2
  59.8 0.0 collective-permute-done.17.refs_8_
  59.8 0.3 collective-permute-done.18.refs_9_
  60.1 0.7 stage_rim.3
  60.8 0.1 collective-permute-start.19
  60.9 2.2 %collective-permute-start.20 = (f32[24,8,256]{2,1,0:T(8,128)S(1)}, f32[24,8,256]{2,1,0:T(8,128)S(1)}, u32[]{:S(2)}, u32[]{:S(2)}) collective-permute-start(f32[24,8,256]{2,1,0:T(8,128)S(1)} %get-tuple-element.72), channel_id=1, source_target_pairs={{0,31},{1,2},{2,1},{3,4},{4,3},{5,6},{6,5},{7,8},{8,7},{9,10},{10,... | collective-permute-start | bytes 589832 | tf_op jit(solution)/shard_map/ppermute | solution.py:101
  63.1 2.6 %collective-permute-start.22 = (f32[15,16,256]{2,1,0:T(8,128)S(1)}, f32[15,16,256]{2,1,0:T(8,128)S(1)}, u32[]{:S(2)}, u32[]{:S(2)}) collective-permute-start(f32[15,16,256]{2,1,0:T(8,128)S(1)} %get-tuple-element.74), channel_id=1, source_target_pairs={{0,0},{32,64},{64,32},{96,96},{1,1},{33,65},{65,33},{97,97},{2,2},... | collective-permute-start | bytes 737288 | tf_op jit(solution)/shard_map/ppermute | solution.py:101
  65.7 3.7 %collective-permute-done.20.refs_8_ = f32[24,8,256]{2,1,0:T(8,128)S(1)} collective-permute-done((f32[24,8,256]{2,1,0:T(8,128)S(1)}, f32[24,8,256]{2,1,0:T(8,128)S(1)}, u32[]{:S(2)}, u32[]{:S(2)}) %collective-permute-start.20) | collective-permute-done | bytes 196640 | tf_op jit(solution)/shard_map/ppermute | solution.py:101
  69.4 1.5 %final_inner.1.refs_13_ = f32[5,24,16,256]{3,2,1,0:T(8,128)S(1)} custom-call(f32[5,24,16,256]{3,2,1,0:T(8,128)S(1)} %stage_inner.3.refs_12_.refs_0_, f32[5,8,16,256]{3,2,1,0:T(8,128)S(1)} %get-tuple-element.70.refs_1_, f32[5,24,16,256]{3,2,1,0:T(8,128)S(1)} %get-tuple-element.53.refs_6_.refs_0_.refs_4_.refs_2_, ...), custom_call_target="tpu_custom_call" | custom-call | flops 137438953472 | tf_op jit(solution)/shard_map/final_inner/pallas_call | solution.py:116
  71.0 0.2 collective-permute-done.22.refs_10_
  71.2 1.9 %final_rim.1 = f32[5,32,16,256]{3,2,1,0:T(8,128)} custom-call(f32[5,24,16,256]{3,2,1,0:T(8,128)S(1)} %stage_inner.3.refs_12_.refs_0_, f32[5,8,16,256]{3,2,1,0:T(8,128)S(1)} %get-tuple-element.70.refs_1_, f32[5,24,16,256]{3,2,1,0:T(8,128)S(1)} %get-tuple-element.53.refs_6_.refs_0_.refs_4_.refs_2_, ...), custom_call_target="tpu_custom_call" | custom-call | tf_op jit(solution)/shard_map/final_rim/pallas_call | solution.py:116
  (14 shorter events, 0.0 us)
Async XLA Ops:
  0.0 15.6 %copy-start.5 = (f32[16,16,512]{2,1,0:T(8,128)S(1)}, f32[16,16,512]{2,1,0:T(8,128)}, u32[]{:S(2)}) copy-start(f32[16,16,512]{2,1,0:T(8,128)} %refs_0_.4) | copy-start | bytes 1572868
  1.1 15.0 %collective-permute-start.1 = (f32[4,16,512]{2,1,0:T(8,128)S(1)}, f32[4,16,512]{2,1,0:T(8,128)S(1)}, u32[]{:S(2)}, u32[]{:S(2)}) collective-permute-start(f32[4,16,512]{2,1,0:T(8,128)S(1)} %get-tuple-element.75), channel_id=1, source_target_pairs={{0,0},{32,64},{64,32},{96,96},{1,1},{33,65},{65,33},{97,97},{2,2},... | collective-permute-start | bytes 393224 | tf_op jit(solution)/shard_map/ppermute | solution.py:101
  4.5 11.6 %collective-permute-start = (f32[4,16,512]{2,1,0:T(8,128)S(1)}, f32[4,16,512]{2,1,0:T(8,128)S(1)}, u32[]{:S(2)}, u32[]{:S(2)}) collective-permute-start(f32[4,16,512]{2,1,0:T(8,128)S(1)} %get-tuple-element.76.refs_1_), channel_id=1, source_target_pairs={{0,32},{32,0},{64,96},{96,64},{1,33},{33,1},{65,97},{97,65},{2,34}... | collective-permute-start | bytes 393224 | tf_op jit(solution)/shard_map/ppermute | solution.py:101
  4.6 1.7 %copy-start = (f32[5,32,16,256]{3,2,1,0:T(8,128)S(1)}, f32[5,32,16,256]{3,2,1,0:T(8,128)}, u32[]{:S(2)}) copy-start(f32[5,32,16,256]{3,2,1,0:T(8,128)} %refs_6_.4) | copy-start | bytes 7864324
  6.4 9.2 %copy-start.6 = (s32[16,16,512]{2,1,0:T(8,128)S(1)}, s32[16,16,512]{2,1,0:T(8,128)}, u32[]{:S(2)}) copy-start(s32[16,16,512]{2,1,0:T(8,128)} %refs_1_.1) | copy-start | bytes 1572868
  6.5 13.0 %copy-start.7 = (s32[256]{0:T(256)S(1)}, s32[256]{0:T(256)}, u32[]{:S(2)}) copy-start(s32[256]{0:T(256)} %param.9) | copy-start | bytes 3076
  6.5 13.0 %copy-start.8 = (s32[256]{0:T(256)S(1)}, s32[256]{0:T(256)}, u32[]{:S(2)}) copy-start(s32[256]{0:T(256)} %param.10) | copy-start | bytes 3076
  6.5 12.9 %collective-permute-start.4 = (f32[15,16,256]{2,1,0:T(8,128)S(1)}, f32[15,16,256]{2,1,0:T(8,128)S(1)}, u32[]{:S(2)}, u32[]{:S(2)}) collective-permute-start(f32[15,16,256]{2,1,0:T(8,128)S(1)} %get-tuple-element.46), channel_id=1, source_target_pairs={{0,32},{32,0},{64,96},{96,64},{1,33},{33,1},{65,97},{97,65},{2,34}... | collective-permute-start | bytes 737288 | tf_op jit(solution)/shard_map/ppermute | solution.py:101
  8.6 10.9 %collective-permute-start.5 = (f32[15,16,256]{2,1,0:T(8,128)S(1)}, f32[15,16,256]{2,1,0:T(8,128)S(1)}, u32[]{:S(2)}, u32[]{:S(2)}) collective-permute-start(f32[15,16,256]{2,1,0:T(8,128)S(1)} %get-tuple-element.47), channel_id=1, source_target_pairs={{0,0},{32,64},{64,32},{96,96},{1,1},{33,65},{65,33},{97,97},{2,2},... | collective-permute-start | bytes 737288 | tf_op jit(solution)/shard_map/ppermute | solution.py:101
  11.0 8.5 %collective-permute-start.6 = (f32[24,8,256]{2,1,0:T(8,128)S(1)}, f32[24,8,256]{2,1,0:T(8,128)S(1)}, u32[]{:S(2)}, u32[]{:S(2)}) collective-permute-start(f32[24,8,256]{2,1,0:T(8,128)S(1)} %get-tuple-element.48), channel_id=1, source_target_pairs={{0,31},{1,2},{2,1},{3,4},{4,3},{5,6},{6,5},{7,8},{8,7},{9,10},{10,... | collective-permute-start | bytes 589832 | tf_op jit(solution)/shard_map/ppermute | solution.py:107
  16.1 15.7 %copy-start.1 = (f32[5,32,16,256]{3,2,1,0:T(8,128)S(1)}, f32[5,32,16,256]{3,2,1,0:T(8,128)}, u32[]{:S(2)}) copy-start(f32[5,32,16,256]{3,2,1,0:T(8,128)} %refs_6_.4) | copy-start | bytes 7864324
  16.1 15.7 %copy-start.3 = (bf16[2,2,256,256]{3,2,1,0:T(8,128)(2,1)S(1)}, bf16[2,2,256,256]{3,2,1,0:T(8,128)(2,1)}, u32[]{:S(2)}) copy-start(bf16[2,2,256,256]{3,2,1,0:T(8,128)(2,1)} %constant.17.clone.refs_6_.refs_11_.refs_13_.refs_9_.refs_10_.refs_12_) | copy-start | bytes 1572868
  16.1 15.7 %copy-start.4 = (bf16[2,2,128,224]{3,2,1,0:T(8,128)(2,1)S(1)}, bf16[2,2,128,224]{3,2,1,0:T(8,128)(2,1)}, u32[]{:S(2)}) copy-start(bf16[2,2,128,224]{3,2,1,0:T(8,128)(2,1)} %constant.16.clone.refs_5_.refs_10_.refs_12_.refs_8_.refs_9_.refs_11_) | copy-start | bytes 688132
  16.4 3.5 %collective-permute-start.2 = (f32[8,8,512]{2,1,0:T(8,128)S(1)}, f32[8,8,512]{2,1,0:T(8,128)S(1)}, u32[]{:S(2)}, u32[]{:S(2)}) collective-permute-start(f32[8,8,512]{2,1,0:T(8,128)S(1)} %get-tuple-element.44), channel_id=1, source_target_pairs={{0,1},{1,0},{2,3},{3,2},{4,5},{5,4},{6,7},{7,6},{8,9},{9,8},{10,11... | collective-permute-start | bytes 393224 | tf_op jit(solution)/shard_map/ppermute | solution.py:101
  16.5 7.8 %collective-permute-start.3 = (f32[8,8,512]{2,1,0:T(8,128)S(1)}, f32[8,8,512]{2,1,0:T(8,128)S(1)}, u32[]{:S(2)}, u32[]{:S(2)}) collective-permute-start(f32[8,8,512]{2,1,0:T(8,128)S(1)} %get-tuple-element.45), channel_id=1, source_target_pairs={{0,31},{1,2},{2,1},{3,4},{4,3},{5,6},{6,5},{7,8},{8,7},{9,10},{10,... | collective-permute-start | bytes 393224 | tf_op jit(solution)/shard_map/ppermute | solution.py:101
  26.6 5.2 %collective-permute-start.7 = (f32[41,8,256]{2,1,0:T(8,128)S(1)}, f32[41,8,256]{2,1,0:T(8,128)S(1)}, u32[]{:S(2)}, u32[]{:S(2)}) collective-permute-start(f32[41,8,256]{2,1,0:T(8,128)S(1)} %get-tuple-element.51), channel_id=1, source_target_pairs={{0,1},{1,0},{2,3},{3,2},{4,5},{5,4},{6,7},{7,6},{8,9},{9,8},{10,11... | collective-permute-start | bytes 1007624 | tf_op jit(solution)/shard_map/ppermute | solution.py:101
  26.7 7.0 %collective-permute-start.8 = (f32[17,8,256]{2,1,0:T(8,128)S(1)}, f32[17,8,256]{2,1,0:T(8,128)S(1)}, u32[]{:S(2)}, u32[]{:S(2)}) collective-permute-start(f32[17,8,256]{2,1,0:T(8,128)S(1)} %get-tuple-element.56), channel_id=1, source_target_pairs={{0,32},{32,0},{64,96},{96,64},{1,33},{33,1},{65,97},{97,65},{2,34}... | collective-permute-start | bytes 417800 | tf_op jit(solution)/shard_map/ppermute | solution.py:101
  26.8 7.9 %collective-permute-start.9 = (f32[17,8,256]{2,1,0:T(8,128)S(1)}, f32[17,8,256]{2,1,0:T(8,128)S(1)}, u32[]{:S(2)}, u32[]{:S(2)}) collective-permute-start(f32[17,8,256]{2,1,0:T(8,128)S(1)} %get-tuple-element.57), channel_id=1, source_target_pairs={{0,0},{32,64},{64,32},{96,96},{1,1},{33,65},{65,33},{97,97},{2,2},... | collective-permute-start | bytes 417800 | tf_op jit(solution)/shard_map/ppermute | solution.py:101
  30.3 7.9 %collective-permute-start.10 = (f32[17,8,256]{2,1,0:T(8,128)S(1)}, f32[17,8,256]{2,1,0:T(8,128)S(1)}, u32[]{:S(2)}, u32[]{:S(2)}) collective-permute-start(f32[17,8,256]{2,1,0:T(8,128)S(1)} %get-tuple-element.58), channel_id=1, source_target_pairs={{0,31},{1,2},{2,1},{3,4},{4,3},{5,6},{6,5},{7,8},{8,7},{9,10},{10,... | collective-permute-start | bytes 417800 | tf_op jit(solution)/shard_map/ppermute | solution.py:101
  38.8 4.3 %collective-permute-start.11 = (f32[24,8,256]{2,1,0:T(8,128)S(1)}, f32[24,8,256]{2,1,0:T(8,128)S(1)}, u32[]{:S(2)}, u32[]{:S(2)}) collective-permute-start(f32[24,8,256]{2,1,0:T(8,128)S(1)} %get-tuple-element.61), channel_id=1, source_target_pairs={{0,1},{1,0},{2,3},{3,2},{4,5},{5,4},{6,7},{7,6},{8,9},{9,8},{10,11... | collective-permute-start | bytes 589832 | tf_op jit(solution)/shard_map/ppermute | solution.py:101
  38.8 8.5 %collective-permute-start.12 = (f32[24,8,256]{2,1,0:T(8,128)S(1)}, f32[24,8,256]{2,1,0:T(8,128)S(1)}, u32[]{:S(2)}, u32[]{:S(2)}) collective-permute-start(f32[24,8,256]{2,1,0:T(8,128)S(1)} %get-tuple-element.62), channel_id=1, source_target_pairs={{0,31},{1,2},{2,1},{3,4},{4,3},{5,6},{6,5},{7,8},{8,7},{9,10},{10,... | collective-permute-start | bytes 589832 | tf_op jit(solution)/shard_map/ppermute | solution.py:101
  40.4 8.4 %collective-permute-start.13 = (f32[15,16,256]{2,1,0:T(8,128)S(1)}, f32[15,16,256]{2,1,0:T(8,128)S(1)}, u32[]{:S(2)}, u32[]{:S(2)}) collective-permute-start(f32[15,16,256]{2,1,0:T(8,128)S(1)} %get-tuple-element.63), channel_id=1, source_target_pairs={{0,32},{32,0},{64,96},{96,64},{1,33},{33,1},{65,97},{97,65},{2,34}... | collective-permute-start | bytes 737288 | tf_op jit(solution)/shard_map/ppermute | solution.py:101
  40.4 8.7 %collective-permute-start.14 = (f32[15,16,256]{2,1,0:T(8,128)S(1)}, f32[15,16,256]{2,1,0:T(8,128)S(1)}, u32[]{:S(2)}, u32[]{:S(2)}) collective-permute-start(f32[15,16,256]{2,1,0:T(8,128)S(1)} %get-tuple-element.64), channel_id=1, source_target_pairs={{0,0},{32,64},{64,32},{96,96},{1,1},{33,65},{65,33},{97,97},{2,2},... | collective-permute-start | bytes 737288 | tf_op jit(solution)/shard_map/ppermute | solution.py:101
  49.8 4.8 %collective-permute-start.15 = (f32[24,8,256]{2,1,0:T(8,128)S(1)}, f32[24,8,256]{2,1,0:T(8,128)S(1)}, u32[]{:S(2)}, u32[]{:S(2)}) collective-permute-start(f32[24,8,256]{2,1,0:T(8,128)S(1)} %get-tuple-element.66), channel_id=1, source_target_pairs={{0,1},{1,0},{2,3},{3,2},{4,5},{5,4},{6,7},{7,6},{8,9},{9,8},{10,11... | collective-permute-start | bytes 589832 | tf_op jit(solution)/shard_map/ppermute | solution.py:101
  49.9 8.5 %collective-permute-start.16 = (f32[24,8,256]{2,1,0:T(8,128)S(1)}, f32[24,8,256]{2,1,0:T(8,128)S(1)}, u32[]{:S(2)}, u32[]{:S(2)}) collective-permute-start(f32[24,8,256]{2,1,0:T(8,128)S(1)} %get-tuple-element.67), channel_id=1, source_target_pairs={{0,31},{1,2},{2,1},{3,4},{4,3},{5,6},{6,5},{7,8},{8,7},{9,10},{10,... | collective-permute-start | bytes 589832 | tf_op jit(solution)/shard_map/ppermute | solution.py:101
  51.8 8.0 %collective-permute-start.17 = (f32[15,16,256]{2,1,0:T(8,128)S(1)}, f32[15,16,256]{2,1,0:T(8,128)S(1)}, u32[]{:S(2)}, u32[]{:S(2)}) collective-permute-start(f32[15,16,256]{2,1,0:T(8,128)S(1)} %get-tuple-element.68), channel_id=1, source_target_pairs={{0,32},{32,0},{64,96},{96,64},{1,33},{33,1},{65,97},{97,65},{2,34}... | collective-permute-start | bytes 737288 | tf_op jit(solution)/shard_map/ppermute | solution.py:101
  51.8 8.3 %collective-permute-start.18 = (f32[15,16,256]{2,1,0:T(8,128)S(1)}, f32[15,16,256]{2,1,0:T(8,128)S(1)}, u32[]{:S(2)}, u32[]{:S(2)}) collective-permute-start(f32[15,16,256]{2,1,0:T(8,128)S(1)} %get-tuple-element.69), channel_id=1, source_target_pairs={{0,0},{32,64},{64,32},{96,96},{1,1},{33,65},{65,33},{97,97},{2,2},... | collective-permute-start | bytes 737288 | tf_op jit(solution)/shard_map/ppermute | solution.py:101
  59.8 9.7 %copy-start.2 = (f32[5,32,16,256]{3,2,1,0:T(8,128)S(1)}, f32[5,32,16,256]{3,2,1,0:T(8,128)}, u32[]{:S(2)}) copy-start(f32[5,32,16,256]{3,2,1,0:T(8,128)} %refs_6_.4) | copy-start | bytes 7864324
  60.8 4.9 %collective-permute-start.19 = (f32[24,8,256]{2,1,0:T(8,128)S(1)}, f32[24,8,256]{2,1,0:T(8,128)S(1)}, u32[]{:S(2)}, u32[]{:S(2)}) collective-permute-start(f32[24,8,256]{2,1,0:T(8,128)S(1)} %get-tuple-element.71), channel_id=1, source_target_pairs={{0,1},{1,0},{2,3},{3,2},{4,5},{5,4},{6,7},{7,6},{8,9},{9,8},{10,11... | collective-permute-start | bytes 589832 | tf_op jit(solution)/shard_map/ppermute | solution.py:101
  60.9 8.5 %collective-permute-start.20 = (f32[24,8,256]{2,1,0:T(8,128)S(1)}, f32[24,8,256]{2,1,0:T(8,128)S(1)}, u32[]{:S(2)}, u32[]{:S(2)}) collective-permute-start(f32[24,8,256]{2,1,0:T(8,128)S(1)} %get-tuple-element.72), channel_id=1, source_target_pairs={{0,31},{1,2},{2,1},{3,4},{4,3},{5,6},{6,5},{7,8},{8,7},{9,10},{10,... | collective-permute-start | bytes 589832 | tf_op jit(solution)/shard_map/ppermute | solution.py:101
  63.1 7.9 %collective-permute-start.21 = (f32[15,16,256]{2,1,0:T(8,128)S(1)}, f32[15,16,256]{2,1,0:T(8,128)S(1)}, u32[]{:S(2)}, u32[]{:S(2)}) collective-permute-start(f32[15,16,256]{2,1,0:T(8,128)S(1)} %get-tuple-element.73), channel_id=1, source_target_pairs={{0,32},{32,0},{64,96},{96,64},{1,33},{33,1},{65,97},{97,65},{2,34}... | collective-permute-start | bytes 737288 | tf_op jit(solution)/shard_map/ppermute | solution.py:101
  63.1 8.1 %collective-permute-start.22 = (f32[15,16,256]{2,1,0:T(8,128)S(1)}, f32[15,16,256]{2,1,0:T(8,128)S(1)}, u32[]{:S(2)}, u32[]{:S(2)}) collective-permute-start(f32[15,16,256]{2,1,0:T(8,128)S(1)} %get-tuple-element.74), channel_id=1, source_target_pairs={{0,0},{32,64},{64,32},{96,96},{1,1},{33,65},{65,33},{97,97},{2,2},... | collective-permute-start | bytes 737288 | tf_op jit(solution)/shard_map/ppermute | solution.py:101

commit v6 on v5

--- a/solution.py
+++ b/solution.py
@@ -96,15 +96,7 @@
     devices = lax.axis_size(axis)
     pairs_a = [(i, i ^ 1) for i in range(devices)]
     pairs_b = [(i, (i - 1) % devices if i % 2 == 0 else (i + 1) % devices) for i in range(devices)]
-    if axis == "ax":
-        pairs_b = [(i, j if abs(i - j) == 1 else i) for i, j in pairs_b]
     return lax.ppermute(to_a, axis, pairs_a), lax.ppermute(to_b, axis, pairs_b)
-
-
-def swap_b(value, axis):
-    devices = lax.axis_size(axis)
-    pairs = [(i, (i - 1) % devices if i % 2 == 0 else (i + 1) % devices) for i in range(devices)]
-    return (lax.ppermute(value, axis, pairs),)
 
 
 def full_specs(body, outs, args, scratch=(), name=None, out_specs=None, after=(), cost=0):
@@ -190,7 +182,9 @@
         first_ref[x] = total
 
 
-def first_body(inner_ref, half_ref, got_a_ref, got_b_ref, first_ref, to_a_ref, to_b_ref, halo):
+def first_body(
+    inner_ref, half_ref, got_a_ref, got_b_ref, edge_a_ref, edge_b_ref, first_ref, to_a_ref, to_b_ref, halo
+):
     n_ax, ax = lax.axis_size("ax"), lax.axis_index("ax")
     even_x, even_z = is_even("ax"), is_even("az")
     rows, _, fine = half_ref.shape
@@ -215,19 +209,22 @@
     for x in range(half):
         last = jnp.where(low, pltpu.roll(first_ref[x, 8:16], 4, 0), first_ref[x + half, 8:16])
         begin = jnp.where(low, first_ref[x, 0:8], pltpu.roll(first_ref[x + half, 0:8], 4, 0))
-        to_a_ref[x] = jnp.where(even_z, last, begin)
-        to_b_ref[x] = jnp.where(even_z, begin, last)
+        for ref, value in ((to_a_ref, jnp.where(even_z, last, begin)), (to_b_ref, jnp.where(even_z, begin, last))):
+            ref[x] = value[:, : fine // 2]
+            ref[half + x] = value[:, fine // 2 :]
+    to_a_ref[rows:] = edge_a_ref[...]
+    to_b_ref[rows:] = edge_b_ref[...]
 
 
 def second_body(
-    first_ref, half_ref, got_a_ref, got_b_ref, pick_ref, cells_ref, edge_a_ref,
+    first_ref, half_ref, got_a_ref, got_b_ref, pick_ref, cells_ref,
     own_ref, to_xa, to_xb, to_za, to_zb, wide, fine_hi, fine_lo,
 ):
     even = is_even("az")
     rows, cols, fine = first_ref.shape
     half = rows // 2
     for x in range(half):
-        got_a, got_b = got_a_ref[x], got_b_ref[x]
+        got_a, got_b = [jnp.concatenate([got[x], got[half + x]], axis=1) for got in (got_a_ref, got_b_ref)]
         before = jnp.where(even, got_b, got_a)
         after = jnp.where(even, got_a, got_b)
         wide[x, 0:8] = pltpu.roll(before, 4, 0)
@@ -264,7 +261,8 @@
         tiles = most // 8
         out[0:tiles] = (dot(pick, hi) + dot(pick, lo)).reshape(tiles, 8, radial)
         out[tiles] = cells_ref[d]
-    to_za[most // 8 + 1 :] = edge_a_ref[...]
+    for out in (to_za, to_zb):
+        out[most // 8 + 1] = jnp.zeros(out.shape[1:], F32)
 
 
 def gather_body(
@@ -422,7 +420,7 @@
         sides = []
         for swap_ab in (False, True):
             for a, b in spans:
-                got_a, got_b = za[start + a : start + b], zb[a:b]
+                got_a, got_b = za[start + a : start + b], zb[start + a : start + b]
                 pair = (got_a, got_b) if swap_ab else (got_b, got_a)
                 sides.append(jnp.where(even, *pair).reshape((b - a) * 8, za.shape[2]))
         return split(jnp.concatenate(sides, axis=0))
@@ -555,29 +553,28 @@
     partial, half_width = full_specs(
         inner_body, [block, ((px, pa, fine), jnp.int32)], [noise, half_width], name="filter_inner", after=[za]
     )
+    long_z = ((px + send_z[0][0], 8, fine // 2), F32)
     filtered, to_a, to_b = full_specs(
         first_body,
-        [block, ((px // 2, 8, fine), F32), ((px // 2, 8, fine), F32)],
-        [partial, half_width, noise_a, noise_b],
+        [block, long_z, long_z],
+        [partial, half_width, noise_a, noise_b, za, zb],
         [((2, HMAX, pa, fine), F32)],
         name="filter_axial",
     )
     got_a, got_b = swap(to_a, to_b, "az")
-    (uzb,) = swap_b(zb, "az")
-    uza = za
     pick, cells, own = full_specs(
         route_body,
         [((4 * most, ncols), BF16), ((4, 8, radial), F32), ((1, ncols), jnp.int32)],
         [owner.reshape(1, ncols), target_cell.reshape(1, ncols)],
         name="route",
-        after=[filtered, uxa, uxb, uzb],
+        after=[filtered],
     )
     tiles = most // 8 + 1
-    packet = ((tiles, 8, radial), F32)
+    packet, packet_z = ((tiles, 8, radial), F32), ((tiles + 1, 8, radial), F32)
     binned, xa, xb, za, zb = full_specs(
         second_body,
-        [((ncols, radial), F32), packet, packet, ((tiles + send_z[0][0], 8, radial), F32), packet],
-        [filtered, half_width, got_a, got_b, pick, cells, uza],
+        [((ncols, radial), F32), packet, packet, packet_z, packet_z],
+        [filtered, half_width, got_a, got_b, pick, cells],
         [((px, 32, fine), F32), ((ncols, fine), BF16), ((ncols, fine), BF16)],
         name="filter_rest",
     )
@@ -588,7 +585,7 @@
     mid, rim = ((5, inner, ca, radial), F32), ((5, 2 * RIM, ca, radial), F32)
     halo = ((2, 5, 3, ca, radial), F32)
     k_mid, k_rim = full_specs(
-        start_body, [mid, rim], [fields, packets[2], uzb, uxa, uxb, tmat, rmat], [halo], name="operator", after=[binned]
+        start_body, [mid, rim], [fields, got_a, got_b, uxa, uxb, tmat, rmat], [halo], name="operator", after=[binned]
     )
     p_mid, p_rim, *edges = full_specs(
         gather_body,

time: 73.5 us -> 69.3 us (0.943)
  the two profiles are of different devices: /device:TPU:8 before, /device:TPU:0 now
where the time goes in v6:
time: 69.3 us; the launch traced here: 69.1 us
  starting transfers between devices  28.4 us (41%)
  waiting for transfers between devices  23.3 us (34%)
  Pallas kernels  13.3 us (19%)
  local copies, waits for them, and re-layouts  2.65 us (4%)
  other arithmetic  1.05 us (2%)
    ppermute x11, starting transfers between devices, swap(): lax.ppermute(to_b, axis, pairs_b)  25.9 us
    ppermute x11, waiting for transfers between devices, swap(): lax.ppermute(to_b, axis, pairs_b)  19.9 us
    pallas_call x13, Pallas kernels, full_specs(): pl.pallas_call(run, out_shape=[jax.ShapeDtypeStruct(s, d) for s, d in out...  13.3 us
    ppermute x11, waiting for transfers between devices, swap(): lax.ppermute(to_a, axis, pairs_a)  3.42 us
    unnamed x18, local copies, waits for them, and re-layouts  2.65 us
    ppermute x11, starting transfers between devices, swap(): lax.ppermute(to_a, axis, pairs_a)  2.53 us
  transfers between devices with their start and end apart: 22, of which 8 were waited for; matrix products, arithmetic and copies ran while one was open for 0% of the time, Pallas kernels for 13%

profile of v6, /device:TPU:0, one launch (start us, length us, event | category | flops | bytes accessed | tf_op | source)
XLA Modules:
  0.0 69.1 jit_solution(2232237524199580165)
XLA Ops:
  0.0 1.0 %slice_select_fusion = (f32[4,16,512]{2,1,0:T(8,128)S(1)}, f32[4,16,512]{2,1,0:T(8,128)S(1)}) fusion(f32[16,16,512]{2,1,0:T(8,128)} %refs_0_.4, pred[]{:T(512)S(6)} %eq.3), kind=kLoop, calls=%fused_computation | loop fusion | flops 65536 | bytes 524289 | tf_op jit(solution)/shard_map/jit(_where)/select_n | solution.py:547
  1.1 3.2 %collective-permute-start.1 = (f32[4,16,512]{2,1,0:T(8,128)S(1)}, f32[4,16,512]{2,1,0:T(8,128)S(1)}, u32[]{:S(2)}, u32[]{:S(2)}) collective-permute-start(f32[4,16,512]{2,1,0:T(8,128)S(1)} %get-tuple-element.75), channel_id=1, source_target_pairs={{0,96},{32,64},{64,32},{96,0},{1,97},{33,65},{65,33},{97,1},{2,98}... | collective-permute-start | bytes 393224 | tf_op jit(solution)/shard_map/ppermute | solution.py:99
  4.2 0.1 collective-permute-start
  4.4 1.7 %copy-done = f32[5,32,16,256]{3,2,1,0:T(8,128)S(1)} copy-done((f32[5,32,16,256]{3,2,1,0:T(8,128)S(1)}, f32[5,32,16,256]{3,2,1,0:T(8,128)}, u32[]{:S(2)}) %copy-start) | copy-done | bytes 2621464
  6.1 0.1 edges.1
  6.2 0.0 copy-start.7
  6.2 0.0 copy-start.8
  6.3 0.0 copy-done.5
  6.3 0.9 %copy-done.6 = s32[16,16,512]{2,1,0:T(8,128)S(1)} copy-done((s32[16,16,512]{2,1,0:T(8,128)S(1)}, s32[16,16,512]{2,1,0:T(8,128)}, u32[]{:S(2)}) %copy-start.6) | copy-done | bytes 524312
  7.2 0.5 filter_inner.1
  7.6 0.1 collective-permute-done.1.refs_3_
  7.7 1.5 %collective-permute-done.refs_2_ = f32[4,16,512]{2,1,0:T(8,128)S(1)} collective-permute-done((f32[4,16,512]{2,1,0:T(8,128)S(1)}, f32[4,16,512]{2,1,0:T(8,128)S(1)}, u32[]{:S(2)}, u32[]{:S(2)}) %collective-permute-start) | collective-permute-done | bytes 131104 | tf_op jit(solution)/shard_map/ppermute | solution.py:99
  9.2 0.2 filter_axial.1
  9.4 0.1 collective-permute-start.2
  9.5 6.3 %collective-permute-start.3 = (f32[40,8,256]{2,1,0:T(8,128)S(1)}, f32[40,8,256]{2,1,0:T(8,128)S(1)}, u32[]{:S(2)}, u32[]{:S(2)}) collective-permute-start(f32[40,8,256]{2,1,0:T(8,128)S(1)} %get-tuple-element.45), channel_id=1, source_target_pairs={{0,31},{1,2},{2,1},{3,4},{4,3},{5,6},{6,5},{7,8},{8,7},{9,10},{10,... | collective-permute-start | bytes 983048 | tf_op jit(solution)/shard_map/ppermute | solution.py:99
  15.8 0.4 collective-permute-start.4
  16.2 1.1 %collective-permute-start.5 = (f32[15,16,256]{2,1,0:T(8,128)S(1)}, f32[15,16,256]{2,1,0:T(8,128)S(1)}, u32[]{:S(2)}, u32[]{:S(2)}) collective-permute-start(f32[15,16,256]{2,1,0:T(8,128)S(1)} %get-tuple-element.47), channel_id=1, source_target_pairs={{0,96},{32,64},{64,32},{96,0},{1,97},{33,65},{65,33},{97,1},{2,98}... | collective-permute-start | bytes 737288 | tf_op jit(solution)/shard_map/ppermute | solution.py:99
  17.3 0.3 route.1
  17.7 0.0 collective-permute-done.2.refs_2_.refs_1_
  17.7 2.9 %collective-permute-done.3.refs_3_.refs_2_ = f32[40,8,256]{2,1,0:T(8,128)S(1)} collective-permute-done((f32[40,8,256]{2,1,0:T(8,128)S(1)}, f32[40,8,256]{2,1,0:T(8,128)S(1)}, u32[]{:S(2)}, u32[]{:S(2)}) %collective-permute-start.3) | collective-permute-done | bytes 327712 | tf_op jit(solution)/shard_map/ppermute | solution.py:99
  20.6 2.3 %filter_rest.1 = (f32[256,256]{1,0:T(8,128)S(1)}, f32[17,8,256]{2,1,0:T(8,128)S(1)}, f32[17,8,256]{2,1,0:T(8,128)S(1)}, f32[18,8,256]{2,1,0:T(8,128)S(1)}, f32[18,8,256]{2,1,0:T(8,128)S(1)}) custom-call(f32[16,16,512]{2,1,0:T(8,128)S(1)} %get-tuple-element.48.refs_2_.refs_0_, s32[16,16,512]{2,1,0:T(8,128)S(1)} %get-tuple-element.42.refs_1_, ...), custom_call_target="tpu_custom_call" | custom-call | tf_op jit(solution)/shard_map/filter_rest/pallas_call | solution.py:108
  22.9 0.1 collective-permute-start.8
  23.0 5.1 %collective-permute-start.9 = (f32[18,8,256]{2,1,0:T(8,128)S(1)}, f32[18,8,256]{2,1,0:T(8,128)S(1)}, u32[]{:S(2)}, u32[]{:S(2)}) collective-permute-start(f32[18,8,256]{2,1,0:T(8,128)S(1)} %get-tuple-element.58), channel_id=1, source_target_pairs={{0,31},{1,2},{2,1},{3,4},{4,3},{5,6},{6,5},{7,8},{8,7},{9,10},{10,... | collective-permute-start | bytes 442376 | tf_op jit(solution)/shard_map/ppermute | solution.py:99
  28.2 0.4 collective-permute-start.6
  28.6 0.0 collective-permute-done.4.refs_3_
  28.6 1.1 %collective-permute-start.7 = (f32[17,8,256]{2,1,0:T(8,128)S(1)}, f32[17,8,256]{2,1,0:T(8,128)S(1)}, u32[]{:S(2)}, u32[]{:S(2)}) collective-permute-start(f32[17,8,256]{2,1,0:T(8,128)S(1)} %get-tuple-element.56), channel_id=1, source_target_pairs={{0,96},{32,64},{64,32},{96,0},{1,97},{33,65},{65,33},{97,1},{2,98}... | collective-permute-start | bytes 417800 | tf_op jit(solution)/shard_map/ppermute | solution.py:99
  29.7 0.0 collective-permute-done.5.refs_4_
  29.7 1.6 %operator.1 = (f32[5,24,16,256]{3,2,1,0:T(8,128)S(1)}, f32[5,8,16,256]{3,2,1,0:T(8,128)S(1)}) custom-call(f32[5,32,16,256]{3,2,1,0:T(8,128)S(1)} %copy-done.1, f32[40,8,256]{2,1,0:T(8,128)S(1)} %collective-permute-done.2.refs_2_.refs_1_, f32[40,8,256]{2,1,0:T(8,128)S(1)} %collective-permute-done.3.refs_3_.refs_2_, ...), custom_call_target="tpu_custom_call" | custom-call | tf_op jit(solution)/shard_map/operator/pallas_call | solution.py:108
  31.3 1.9 %collective-permute-done.6.refs_2_ = f32[17,8,256]{2,1,0:T(8,128)S(1)} collective-permute-done((f32[17,8,256]{2,1,0:T(8,128)S(1)}, f32[17,8,256]{2,1,0:T(8,128)S(1)}, u32[]{:S(2)}, u32[]{:S(2)}) %collective-permute-start.6) | collective-permute-done | bytes 139296 | tf_op jit(solution)/shard_map/ppermute | solution.py:99
  33.2 1.6 %collective-permute-done.7.refs_3_ = f32[17,8,256]{2,1,0:T(8,128)S(1)} collective-permute-done((f32[17,8,256]{2,1,0:T(8,128)S(1)}, f32[17,8,256]{2,1,0:T(8,128)S(1)}, u32[]{:S(2)}, u32[]{:S(2)}) %collective-permute-start.7) | collective-permute-done | bytes 139296 | tf_op jit(solution)/shard_map/ppermute | solution.py:99
  34.8 0.0 collective-permute-done.8.refs_4_
  34.8 0.0 collective-permute-done.9.refs_5_
  34.8 0.6 gather.1
  35.4 0.1 collective-permute-start.10
  35.5 1.3 %collective-permute-start.11 = (f32[24,8,256]{2,1,0:T(8,128)S(1)}, f32[24,8,256]{2,1,0:T(8,128)S(1)}, u32[]{:S(2)}, u32[]{:S(2)}) collective-permute-start(f32[24,8,256]{2,1,0:T(8,128)S(1)} %get-tuple-element.62), channel_id=1, source_target_pairs={{0,31},{1,2},{2,1},{3,4},{4,3},{5,6},{6,5},{7,8},{8,7},{9,10},{10,... | collective-permute-start | bytes 589832 | tf_op jit(solution)/shard_map/ppermute | solution.py:99
  36.8 0.4 collective-permute-start.12
  37.2 1.1 %collective-permute-start.13 = (f32[15,16,256]{2,1,0:T(8,128)S(1)}, f32[15,16,256]{2,1,0:T(8,128)S(1)}, u32[]{:S(2)}, u32[]{:S(2)}) collective-permute-start(f32[15,16,256]{2,1,0:T(8,128)S(1)} %get-tuple-element.64), channel_id=1, source_target_pairs={{0,96},{32,64},{64,32},{96,0},{1,97},{33,65},{65,33},{97,1},{2,98}... | collective-permute-start | bytes 737288 | tf_op jit(solution)/shard_map/ppermute | solution.py:99
  38.3 0.0 collective-permute-done.10.refs_8_
  38.3 5.7 %collective-permute-done.11.refs_9_ = f32[24,8,256]{2,1,0:T(8,128)S(1)} collective-permute-done((f32[24,8,256]{2,1,0:T(8,128)S(1)}, f32[24,8,256]{2,1,0:T(8,128)S(1)}, u32[]{:S(2)}, u32[]{:S(2)}) %collective-permute-start.11) | collective-permute-done | bytes 196640 | tf_op jit(solution)/shard_map/ppermute | solution.py:99
  44.0 1.5 %stage_inner.2.refs_14_.refs_0_ = f32[5,24,16,256]{3,2,1,0:T(8,128)S(1)} custom-call(f32[5,24,16,256]{3,2,1,0:T(8,128)S(1)} %get-tuple-element.52.refs_6_.refs_0_.refs_4_.refs_2_, f32[5,8,16,256]{3,2,1,0:T(8,128)S(1)} %get-tuple-element.53.refs_7_.refs_1_.refs_5_.refs_3_, f32[24,16,256]{2,1,0:T(8,128)S(1)} %get-tuple-element.59.refs_2_.refs_6_.refs_4_, ...), custom_call_target="tpu_custom_call" | custom-call | flops 137438953472 | tf_op jit(solution)/shard_map/stage_inner/pallas_call | solution.py:108
  45.5 0.0 collective-permute-done.12.refs_10_
  45.5 0.0 collective-permute-done.13.refs_11_
  45.5 0.7 stage_rim.2
  46.2 0.1 collective-permute-start.14
  46.3 1.6 %collective-permute-start.15 = (f32[24,8,256]{2,1,0:T(8,128)S(1)}, f32[24,8,256]{2,1,0:T(8,128)S(1)}, u32[]{:S(2)}, u32[]{:S(2)}) collective-permute-start(f32[24,8,256]{2,1,0:T(8,128)S(1)} %get-tuple-element.67), channel_id=1, source_target_pairs={{0,31},{1,2},{2,1},{3,4},{4,3},{5,6},{6,5},{7,8},{8,7},{9,10},{10,... | collective-permute-start | bytes 589832 | tf_op jit(solution)/shard_map/ppermute | solution.py:99
  47.9 0.4 collective-permute-start.16
  48.3 1.4 %collective-permute-start.17 = (f32[15,16,256]{2,1,0:T(8,128)S(1)}, f32[15,16,256]{2,1,0:T(8,128)S(1)}, u32[]{:S(2)}, u32[]{:S(2)}) collective-permute-start(f32[15,16,256]{2,1,0:T(8,128)S(1)} %get-tuple-element.69), channel_id=1, source_target_pairs={{0,96},{32,64},{64,32},{96,0},{1,97},{33,65},{65,33},{97,1},{2,98}... | collective-permute-start | bytes 737288 | tf_op jit(solution)/shard_map/ppermute | solution.py:99
  49.8 0.0 collective-permute-done.14.refs_6_
  49.8 5.0 %collective-permute-done.15.refs_7_ = f32[24,8,256]{2,1,0:T(8,128)S(1)} collective-permute-done((f32[24,8,256]{2,1,0:T(8,128)S(1)}, f32[24,8,256]{2,1,0:T(8,128)S(1)}, u32[]{:S(2)}, u32[]{:S(2)}) %collective-permute-start.15) | collective-permute-done | bytes 196640 | tf_op jit(solution)/shard_map/ppermute | solution.py:99
  54.8 1.4 %stage_inner.3.refs_12_.refs_0_ = f32[5,24,16,256]{3,2,1,0:T(8,128)S(1)} custom-call(f32[5,24,16,256]{3,2,1,0:T(8,128)S(1)} %stage_inner.2.refs_14_.refs_0_, f32[5,8,16,256]{3,2,1,0:T(8,128)S(1)} %get-tuple-element.65.refs_1_, f32[5,24,16,256]{3,2,1,0:T(8,128)S(1)} %get-tuple-element.52.refs_6_.refs_0_.refs_4_.refs_2_, ...), custom_call_target="tpu_custom_call" | custom-call | flops 137438953472 | tf_op jit(solution)/shard_map/stage_inner/pallas_call | solution.py:108
  56.1 0.0 copy-start.2
  56.2 0.0 collective-permute-done.16.refs_8_
  56.2 0.0 collective-permute-done.17.refs_9_
  56.2 0.7 stage_rim.3
  56.9 0.1 collective-permute-start.18
  57.0 2.0 %collective-permute-start.19 = (f32[24,8,256]{2,1,0:T(8,128)S(1)}, f32[24,8,256]{2,1,0:T(8,128)S(1)}, u32[]{:S(2)}, u32[]{:S(2)}) collective-permute-start(f32[24,8,256]{2,1,0:T(8,128)S(1)} %get-tuple-element.72), channel_id=1, source_target_pairs={{0,31},{1,2},{2,1},{3,4},{4,3},{5,6},{6,5},{7,8},{8,7},{9,10},{10,... | collective-permute-start | bytes 589832 | tf_op jit(solution)/shard_map/ppermute | solution.py:99
  58.9 0.4 collective-permute-start.20
  59.4 1.5 %collective-permute-start.21 = (f32[15,16,256]{2,1,0:T(8,128)S(1)}, f32[15,16,256]{2,1,0:T(8,128)S(1)}, u32[]{:S(2)}, u32[]{:S(2)}) collective-permute-start(f32[15,16,256]{2,1,0:T(8,128)S(1)} %get-tuple-element.74), channel_id=1, source_target_pairs={{0,96},{32,64},{64,32},{96,0},{1,97},{33,65},{65,33},{97,1},{2,98}... | collective-permute-start | bytes 737288 | tf_op jit(solution)/shard_map/ppermute | solution.py:99
  60.9 0.0 collective-permute-done.18.refs_7_
  60.9 4.6 %collective-permute-done.19.refs_8_ = f32[24,8,256]{2,1,0:T(8,128)S(1)} collective-permute-done((f32[24,8,256]{2,1,0:T(8,128)S(1)}, f32[24,8,256]{2,1,0:T(8,128)S(1)}, u32[]{:S(2)}, u32[]{:S(2)}) %collective-permute-start.19) | collective-permute-done | bytes 196640 | tf_op jit(solution)/shard_map/ppermute | solution.py:99
  65.5 1.5 %final_inner.1.refs_13_ = f32[5,24,16,256]{3,2,1,0:T(8,128)S(1)} custom-call(f32[5,24,16,256]{3,2,1,0:T(8,128)S(1)} %stage_inner.3.refs_12_.refs_0_, f32[5,8,16,256]{3,2,1,0:T(8,128)S(1)} %get-tuple-element.70.refs_1_, f32[5,24,16,256]{3,2,1,0:T(8,128)S(1)} %get-tuple-element.52.refs_6_.refs_0_.refs_4_.refs_2_, ...), custom_call_target="tpu_custom_call" | custom-call | flops 137438953472 | tf_op jit(solution)/shard_map/final_inner/pallas_call | solution.py:108
  67.0 0.0 collective-permute-done.20.refs_9_
  67.0 0.0 collective-permute-done.21.refs_10_
  67.0 1.9 %final_rim.1 = f32[5,32,16,256]{3,2,1,0:T(8,128)} custom-call(f32[5,24,16,256]{3,2,1,0:T(8,128)S(1)} %stage_inner.3.refs_12_.refs_0_, f32[5,8,16,256]{3,2,1,0:T(8,128)S(1)} %get-tuple-element.70.refs_1_, f32[5,24,16,256]{3,2,1,0:T(8,128)S(1)} %get-tuple-element.52.refs_6_.refs_0_.refs_4_.refs_2_, ...), custom_call_target="tpu_custom_call" | custom-call | tf_op jit(solution)/shard_map/final_rim/pallas_call | solution.py:108
  (12 shorter events, 0.0 us)
Async XLA Ops:
  0.0 6.3 %copy-start.5 = (f32[16,16,512]{2,1,0:T(8,128)S(1)}, f32[16,16,512]{2,1,0:T(8,128)}, u32[]{:S(2)}) copy-start(f32[16,16,512]{2,1,0:T(8,128)} %refs_0_.4) | copy-start | bytes 1572868
  1.1 6.7 %collective-permute-start.1 = (f32[4,16,512]{2,1,0:T(8,128)S(1)}, f32[4,16,512]{2,1,0:T(8,128)S(1)}, u32[]{:S(2)}, u32[]{:S(2)}) collective-permute-start(f32[4,16,512]{2,1,0:T(8,128)S(1)} %get-tuple-element.75), channel_id=1, source_target_pairs={{0,96},{32,64},{64,32},{96,0},{1,97},{33,65},{65,33},{97,1},{2,98}... | collective-permute-start | bytes 393224 | tf_op jit(solution)/shard_map/ppermute | solution.py:99
  4.2 5.0 %collective-permute-start = (f32[4,16,512]{2,1,0:T(8,128)S(1)}, f32[4,16,512]{2,1,0:T(8,128)S(1)}, u32[]{:S(2)}, u32[]{:S(2)}) collective-permute-start(f32[4,16,512]{2,1,0:T(8,128)S(1)} %get-tuple-element.76.refs_1_), channel_id=1, source_target_pairs={{0,32},{32,0},{64,96},{96,64},{1,33},{33,1},{65,97},{97,65},{2,34}... | collective-permute-start | bytes 393224 | tf_op jit(solution)/shard_map/ppermute | solution.py:99
  4.4 1.7 %copy-start = (f32[5,32,16,256]{3,2,1,0:T(8,128)S(1)}, f32[5,32,16,256]{3,2,1,0:T(8,128)}, u32[]{:S(2)}) copy-start(f32[5,32,16,256]{3,2,1,0:T(8,128)} %refs_6_.4) | copy-start | bytes 7864324
  6.1 1.0 %copy-start.6 = (s32[16,16,512]{2,1,0:T(8,128)S(1)}, s32[16,16,512]{2,1,0:T(8,128)}, u32[]{:S(2)}) copy-start(s32[16,16,512]{2,1,0:T(8,128)} %refs_1_.1) | copy-start | bytes 1572868
  6.2 11.1 %copy-start.7 = (s32[256]{0:T(256)S(1)}, s32[256]{0:T(256)}, u32[]{:S(2)}) copy-start(s32[256]{0:T(256)} %param.9) | copy-start | bytes 3076
  6.2 11.1 %copy-start.8 = (s32[256]{0:T(256)S(1)}, s32[256]{0:T(256)}, u32[]{:S(2)}) copy-start(s32[256]{0:T(256)} %param.10) | copy-start | bytes 3076
  9.2 20.5 %copy-start.1 = (f32[5,32,16,256]{3,2,1,0:T(8,128)S(1)}, f32[5,32,16,256]{3,2,1,0:T(8,128)}, u32[]{:S(2)}) copy-start(f32[5,32,16,256]{3,2,1,0:T(8,128)} %refs_6_.4) | copy-start | bytes 7864324
  9.2 20.5 %copy-start.3 = (bf16[2,2,256,256]{3,2,1,0:T(8,128)(2,1)S(1)}, bf16[2,2,256,256]{3,2,1,0:T(8,128)(2,1)}, u32[]{:S(2)}) copy-start(bf16[2,2,256,256]{3,2,1,0:T(8,128)(2,1)} %constant.17.clone.refs_6_.refs_11_.refs_13_.refs_9_.refs_10_.refs_12_) | copy-start | bytes 1572868
  9.2 20.5 %copy-start.4 = (bf16[2,2,128,224]{3,2,1,0:T(8,128)(2,1)S(1)}, bf16[2,2,128,224]{3,2,1,0:T(8,128)(2,1)}, u32[]{:S(2)}) copy-start(bf16[2,2,128,224]{3,2,1,0:T(8,128)(2,1)} %constant.16.clone.refs_5_.refs_10_.refs_12_.refs_8_.refs_9_.refs_11_) | copy-start | bytes 688132
  9.4 8.3 %collective-permute-start.2 = (f32[40,8,256]{2,1,0:T(8,128)S(1)}, f32[40,8,256]{2,1,0:T(8,128)S(1)}, u32[]{:S(2)}, u32[]{:S(2)}) collective-permute-start(f32[40,8,256]{2,1,0:T(8,128)S(1)} %get-tuple-element.44), channel_id=1, source_target_pairs={{0,1},{1,0},{2,3},{3,2},{4,5},{5,4},{6,7},{7,6},{8,9},{9,8},{10,11... | collective-permute-start | bytes 983048 | tf_op jit(solution)/shard_map/ppermute | solution.py:99
  9.5 11.1 %collective-permute-start.3 = (f32[40,8,256]{2,1,0:T(8,128)S(1)}, f32[40,8,256]{2,1,0:T(8,128)S(1)}, u32[]{:S(2)}, u32[]{:S(2)}) collective-permute-start(f32[40,8,256]{2,1,0:T(8,128)S(1)} %get-tuple-element.45), channel_id=1, source_target_pairs={{0,31},{1,2},{2,1},{3,4},{4,3},{5,6},{6,5},{7,8},{8,7},{9,10},{10,... | collective-permute-start | bytes 983048 | tf_op jit(solution)/shard_map/ppermute | solution.py:99
  15.8 12.7 %collective-permute-start.4 = (f32[15,16,256]{2,1,0:T(8,128)S(1)}, f32[15,16,256]{2,1,0:T(8,128)S(1)}, u32[]{:S(2)}, u32[]{:S(2)}) collective-permute-start(f32[15,16,256]{2,1,0:T(8,128)S(1)} %get-tuple-element.46), channel_id=1, source_target_pairs={{0,32},{32,0},{64,96},{96,64},{1,33},{33,1},{65,97},{97,65},{2,34}... | collective-permute-start | bytes 737288 | tf_op jit(solution)/shard_map/ppermute | solution.py:99
  16.2 13.5 %collective-permute-start.5 = (f32[15,16,256]{2,1,0:T(8,128)S(1)}, f32[15,16,256]{2,1,0:T(8,128)S(1)}, u32[]{:S(2)}, u32[]{:S(2)}) collective-permute-start(f32[15,16,256]{2,1,0:T(8,128)S(1)} %get-tuple-element.47), channel_id=1, source_target_pairs={{0,96},{32,64},{64,32},{96,0},{1,97},{33,65},{65,33},{97,1},{2,98}... | collective-permute-start | bytes 737288 | tf_op jit(solution)/shard_map/ppermute | solution.py:99
  22.9 11.9 %collective-permute-start.8 = (f32[18,8,256]{2,1,0:T(8,128)S(1)}, f32[18,8,256]{2,1,0:T(8,128)S(1)}, u32[]{:S(2)}, u32[]{:S(2)}) collective-permute-start(f32[18,8,256]{2,1,0:T(8,128)S(1)} %get-tuple-element.57), channel_id=1, source_target_pairs={{0,1},{1,0},{2,3},{3,2},{4,5},{5,4},{6,7},{7,6},{8,9},{9,8},{10,11... | collective-permute-start | bytes 442376 | tf_op jit(solution)/shard_map/ppermute | solution.py:99
  23.0 11.8 %collective-permute-start.9 = (f32[18,8,256]{2,1,0:T(8,128)S(1)}, f32[18,8,256]{2,1,0:T(8,128)S(1)}, u32[]{:S(2)}, u32[]{:S(2)}) collective-permute-start(f32[18,8,256]{2,1,0:T(8,128)S(1)} %get-tuple-element.58), channel_id=1, source_target_pairs={{0,31},{1,2},{2,1},{3,4},{4,3},{5,6},{6,5},{7,8},{8,7},{9,10},{10,... | collective-permute-start | bytes 442376 | tf_op jit(solution)/shard_map/ppermute | solution.py:99
  28.2 5.1 %collective-permute-start.6 = (f32[17,8,256]{2,1,0:T(8,128)S(1)}, f32[17,8,256]{2,1,0:T(8,128)S(1)}, u32[]{:S(2)}, u32[]{:S(2)}) collective-permute-start(f32[17,8,256]{2,1,0:T(8,128)S(1)} %get-tuple-element.55), channel_id=1, source_target_pairs={{0,32},{32,0},{64,96},{96,64},{1,33},{33,1},{65,97},{97,65},{2,34}... | collective-permute-start | bytes 417800 | tf_op jit(solution)/shard_map/ppermute | solution.py:99
  28.6 6.3 %collective-permute-start.7 = (f32[17,8,256]{2,1,0:T(8,128)S(1)}, f32[17,8,256]{2,1,0:T(8,128)S(1)}, u32[]{:S(2)}, u32[]{:S(2)}) collective-permute-start(f32[17,8,256]{2,1,0:T(8,128)S(1)} %get-tuple-element.56), channel_id=1, source_target_pairs={{0,96},{32,64},{64,32},{96,0},{1,97},{33,65},{65,33},{97,1},{2,98}... | collective-permute-start | bytes 417800 | tf_op jit(solution)/shard_map/ppermute | solution.py:99
  35.4 2.9 %collective-permute-start.10 = (f32[24,8,256]{2,1,0:T(8,128)S(1)}, f32[24,8,256]{2,1,0:T(8,128)S(1)}, u32[]{:S(2)}, u32[]{:S(2)}) collective-permute-start(f32[24,8,256]{2,1,0:T(8,128)S(1)} %get-tuple-element.61), channel_id=1, source_target_pairs={{0,1},{1,0},{2,3},{3,2},{4,5},{5,4},{6,7},{7,6},{8,9},{9,8},{10,11... | collective-permute-start | bytes 589832 | tf_op jit(solution)/shard_map/ppermute | solution.py:99
  35.5 8.5 %collective-permute-start.11 = (f32[24,8,256]{2,1,0:T(8,128)S(1)}, f32[24,8,256]{2,1,0:T(8,128)S(1)}, u32[]{:S(2)}, u32[]{:S(2)}) collective-permute-start(f32[24,8,256]{2,1,0:T(8,128)S(1)} %get-tuple-element.62), channel_id=1, source_target_pairs={{0,31},{1,2},{2,1},{3,4},{4,3},{5,6},{6,5},{7,8},{8,7},{9,10},{10,... | collective-permute-start | bytes 589832 | tf_op jit(solution)/shard_map/ppermute | solution.py:99
  36.8 8.7 %collective-permute-start.12 = (f32[15,16,256]{2,1,0:T(8,128)S(1)}, f32[15,16,256]{2,1,0:T(8,128)S(1)}, u32[]{:S(2)}, u32[]{:S(2)}) collective-permute-start(f32[15,16,256]{2,1,0:T(8,128)S(1)} %get-tuple-element.63), channel_id=1, source_target_pairs={{0,32},{32,0},{64,96},{96,64},{1,33},{33,1},{65,97},{97,65},{2,34}... | collective-permute-start | bytes 737288 | tf_op jit(solution)/shard_map/ppermute | solution.py:99
  37.2 8.3 %collective-permute-start.13 = (f32[15,16,256]{2,1,0:T(8,128)S(1)}, f32[15,16,256]{2,1,0:T(8,128)S(1)}, u32[]{:S(2)}, u32[]{:S(2)}) collective-permute-start(f32[15,16,256]{2,1,0:T(8,128)S(1)} %get-tuple-element.64), channel_id=1, source_target_pairs={{0,96},{32,64},{64,32},{96,0},{1,97},{33,65},{65,33},{97,1},{2,98}... | collective-permute-start | bytes 737288 | tf_op jit(solution)/shard_map/ppermute | solution.py:99
  46.2 3.6 %collective-permute-start.14 = (f32[24,8,256]{2,1,0:T(8,128)S(1)}, f32[24,8,256]{2,1,0:T(8,128)S(1)}, u32[]{:S(2)}, u32[]{:S(2)}) collective-permute-start(f32[24,8,256]{2,1,0:T(8,128)S(1)} %get-tuple-element.66), channel_id=1, source_target_pairs={{0,1},{1,0},{2,3},{3,2},{4,5},{5,4},{6,7},{7,6},{8,9},{9,8},{10,11... | collective-permute-start | bytes 589832 | tf_op jit(solution)/shard_map/ppermute | solution.py:99
  46.3 8.5 %collective-permute-start.15 = (f32[24,8,256]{2,1,0:T(8,128)S(1)}, f32[24,8,256]{2,1,0:T(8,128)S(1)}, u32[]{:S(2)}, u32[]{:S(2)}) collective-permute-start(f32[24,8,256]{2,1,0:T(8,128)S(1)} %get-tuple-element.67), channel_id=1, source_target_pairs={{0,31},{1,2},{2,1},{3,4},{4,3},{5,6},{6,5},{7,8},{8,7},{9,10},{10,... | collective-permute-start | bytes 589832 | tf_op jit(solution)/shard_map/ppermute | solution.py:99
  47.9 8.2 %collective-permute-start.16 = (f32[15,16,256]{2,1,0:T(8,128)S(1)}, f32[15,16,256]{2,1,0:T(8,128)S(1)}, u32[]{:S(2)}, u32[]{:S(2)}) collective-permute-start(f32[15,16,256]{2,1,0:T(8,128)S(1)} %get-tuple-element.68), channel_id=1, source_target_pairs={{0,32},{32,0},{64,96},{96,64},{1,33},{33,1},{65,97},{97,65},{2,34}... | collective-permute-start | bytes 737288 | tf_op jit(solution)/shard_map/ppermute | solution.py:99
  48.3 7.9 %collective-permute-start.17 = (f32[15,16,256]{2,1,0:T(8,128)S(1)}, f32[15,16,256]{2,1,0:T(8,128)S(1)}, u32[]{:S(2)}, u32[]{:S(2)}) collective-permute-start(f32[15,16,256]{2,1,0:T(8,128)S(1)} %get-tuple-element.69), channel_id=1, source_target_pairs={{0,96},{32,64},{64,32},{96,0},{1,97},{33,65},{65,33},{97,1},{2,98}... | collective-permute-start | bytes 737288 | tf_op jit(solution)/shard_map/ppermute | solution.py:99
  56.1 9.3 %copy-start.2 = (f32[5,32,16,256]{3,2,1,0:T(8,128)S(1)}, f32[5,32,16,256]{3,2,1,0:T(8,128)}, u32[]{:S(2)}) copy-start(f32[5,32,16,256]{3,2,1,0:T(8,128)} %refs_6_.4) | copy-start | bytes 7864324
  56.9 4.0 %collective-permute-start.18 = (f32[24,8,256]{2,1,0:T(8,128)S(1)}, f32[24,8,256]{2,1,0:T(8,128)S(1)}, u32[]{:S(2)}, u32[]{:S(2)}) collective-permute-start(f32[24,8,256]{2,1,0:T(8,128)S(1)} %get-tuple-element.71), channel_id=1, source_target_pairs={{0,1},{1,0},{2,3},{3,2},{4,5},{5,4},{6,7},{7,6},{8,9},{9,8},{10,11... | collective-permute-start | bytes 589832 | tf_op jit(solution)/shard_map/ppermute | solution.py:99
  57.0 8.5 %collective-permute-start.19 = (f32[24,8,256]{2,1,0:T(8,128)S(1)}, f32[24,8,256]{2,1,0:T(8,128)S(1)}, u32[]{:S(2)}, u32[]{:S(2)}) collective-permute-start(f32[24,8,256]{2,1,0:T(8,128)S(1)} %get-tuple-element.72), channel_id=1, source_target_pairs={{0,31},{1,2},{2,1},{3,4},{4,3},{5,6},{6,5},{7,8},{8,7},{9,10},{10,... | collective-permute-start | bytes 589832 | tf_op jit(solution)/shard_map/ppermute | solution.py:99
  58.9 8.1 %collective-permute-start.20 = (f32[15,16,256]{2,1,0:T(8,128)S(1)}, f32[15,16,256]{2,1,0:T(8,128)S(1)}, u32[]{:S(2)}, u32[]{:S(2)}) collective-permute-start(f32[15,16,256]{2,1,0:T(8,128)S(1)} %get-tuple-element.73), channel_id=1, source_target_pairs={{0,32},{32,0},{64,96},{96,64},{1,33},{33,1},{65,97},{97,65},{2,34}... | collective-permute-start | bytes 737288 | tf_op jit(solution)/shard_map/ppermute | solution.py:99
  59.4 7.7 %collective-permute-start.21 = (f32[15,16,256]{2,1,0:T(8,128)S(1)}, f32[15,16,256]{2,1,0:T(8,128)S(1)}, u32[]{:S(2)}, u32[]{:S(2)}) collective-permute-start(f32[15,16,256]{2,1,0:T(8,128)S(1)} %get-tuple-element.74), channel_id=1, source_target_pairs={{0,96},{32,64},{64,32},{96,0},{1,97},{33,65},{65,33},{97,1},{2,98}... | collective-permute-start | bytes 737288 | tf_op jit(solution)/shard_map/ppermute | solution.py:99

commit v7 on v6

--- a/solution.py
+++ b/solution.py
@@ -99,7 +99,7 @@
     return lax.ppermute(to_a, axis, pairs_a), lax.ppermute(to_b, axis, pairs_b)
 
 
-def full_specs(body, outs, args, scratch=(), name=None, out_specs=None, after=(), cost=0):
+def full_specs(body, outs, args, scratch=(), name=None, in_specs=None, out_specs=None, after=(), cost=0, alias=None):
     skip = len(args)
 
     def run(*refs):
@@ -108,7 +108,8 @@
     return pl.pallas_call(
         run,
         out_shape=[jax.ShapeDtypeStruct(s, d) for s, d in outs],
-        in_specs=[VM] * skip + [ANY] * len(after),
+        in_specs=(in_specs or [VM] * skip) + [ANY] * len(after),
+        input_output_aliases=alias or {},
         out_specs=out_specs or [VM] * len(outs),
         scratch_shapes=[pltpu.VMEM(*s) if isinstance(s, tuple) else s for s in scratch],
         compiler_params=PARAMS,
@@ -290,7 +291,7 @@
     p_rim[RIM:] = k_rim[4, RIM:] + q[RIM + mid :]
     level = Parts(k_mid, k_rim, p_mid, p_rim)
     write_x(level, to_xa, to_xb)
-    write_z(level, to_za, to_zb)
+    write_z(level, range(0, level.rows, 4), to_za, to_zb)
 
 
 class Whole:
@@ -308,15 +309,15 @@
 
 
 class Parts:
-    def __init__(self, mid, rim, p_mid=None, p_rim=None):
+    def __init__(self, mid, rim, p_mid=None, p_rim=None, rows=None):
         self.arrays = (mid, rim, p_mid, p_rim)
-        self.rows = mid.shape[1] + 2 * RIM
+        self.rows = rows or mid.shape[1] + 2 * RIM
 
     def pick(self, f):
         mid, rim, p_mid, p_rim = self.arrays
         if f == 4 and p_mid is not None:
             return p_mid, p_rim
-        return mid.at[f], rim.at[f]
+        return mid if mid is None else mid.at[f], rim if rim is None else rim.at[f]
 
     def row(self, f, x):
         mid, rim = self.pick(f)
@@ -355,10 +356,10 @@
             to_xb[3 * f + i] = jnp.where(even, first, last)
 
 
-def write_z(level, to_za, to_zb):
+def write_z(level, starts, to_za, to_zb):
     even = is_even("az")
     row = None
-    for x in range(0, level.rows, 4):
+    for i, x in enumerate(starts):
         first, last = [], []
         for y in range(x, x + 4):
             ut, p = level.row(2, y), level.row(4, y)
@@ -370,14 +371,14 @@
             shift = 3 - t
             one = jnp.where(row, pltpu.roll(first[3], shift, 0), first[t])
             two = jnp.where(row, pltpu.roll(last[3], shift, 0), last[t])
-            to_za[x // 4 * 3 + t] = jnp.where(even, two, one)
-            to_zb[x // 4 * 3 + t] = jnp.where(even, one, two)
+            to_za[3 * i + t] = jnp.where(even, two, one)
+            to_zb[3 * i + t] = jnp.where(even, one, two)
 
 
 def edges_body(state, to_xa, to_xb, to_za, to_zb):
     level = Whole(state)
     write_x(level, to_xa, to_xb)
-    write_z(level, to_za, to_zb)
+    write_z(level, range(0, level.rows, 4), to_za, to_zb)
 
 
 def fill_halo(halo, xa, xb):
@@ -417,6 +418,10 @@
     def beside(g):
         spans = [(0, rim), (tiles - rim, tiles)] if g is None else [(rim + 6 * g, rim + 6 * g + 6)]
         start = za.shape[0] - tiles
+        if za.shape[0] == 2 * rim:
+            spans, start = [(0, rim), (rim, 2 * rim)], 0
+        elif za.shape[0] == tiles - 2 * rim:
+            start = -rim
         sides = []
         for swap_ab in (False, True):
             for a, b in spans:
@@ -476,17 +481,18 @@
     apply_operator(level, [*range(k_mid.shape[1] // GROUP), None], za, zb, tmat, rmat, finish, halo)
 
 
-def inner_stage_body(factor, level, base, za, zb, tmat, rmat, out_mid):
+def inner_stage_body(factor, level, base, za, zb, tmat, rmat, out_mid, to_za, to_zb):
     def finish(x, tend):
         for f in range(5):
             out_mid[f, x - RIM] = base.row(f, x) + factor * tend[f]
 
     apply_operator(level, range(out_mid.shape[1] // GROUP), za, zb, tmat, rmat, finish)
-
-
-def rim_stage_body(factor, level, base, za, zb, xa, xb, tmat, rmat, out_mid, out_rim, to_xa, to_xb, to_za, to_zb, halo):
+    write_z(Parts(out_mid, None, rows=level.rows), range(RIM, level.rows - RIM, 4), to_za, to_zb)
+
+
+def rim_stage_body(factor, level, base, za, zb, xa, xb, tmat, rmat, out_rim, to_xa, to_xb, to_za, to_zb, halo):
     fill_halo(halo, xa, xb)
-    out = Parts(out_mid, out_rim)
+    out = Parts(None, out_rim, rows=level.rows)
 
     def finish(x, tend):
         for f in range(5):
@@ -494,7 +500,7 @@
 
     apply_operator(level, [None], za, zb, tmat, rmat, finish, halo)
     write_x(out, to_xa, to_xb)
-    write_z(out, to_za, to_zb)
+    write_z(out, [0, level.rows - RIM], to_za, to_zb)
 
 
 def last_finish(fields, k, store):
@@ -505,18 +511,26 @@
     return finish
 
 
-def inner_last_body(level, k, fields, za, zb, tmat, rmat, out_mid):
+def inner_last_body(level, k, fields, za, zb, tmat, rmat, out, result, sems):
     def store(f, x, value):
-        out_mid[f, x - RIM] = value
-
-    groups = range(out_mid.shape[1] // GROUP)
-    apply_operator(level, groups, za, zb, tmat, rmat, last_finish(fields, k, store))
-
-
-def rim_last_body(level, k, fields, za, zb, xa, xb, tmat, rmat, out_mid, out, halo, result, sems):
+        result[f, x - RIM] = value
+
+    def copy(g):
+        at = g * GROUP
+        return pltpu.make_async_copy(
+            result.at[:, at : at + GROUP], out.at[:, RIM + at : RIM + at + GROUP], sems.at[g]
+        )
+
+    groups = range(result.shape[1] // GROUP)
+    for g in groups:
+        apply_operator(level, [g], za, zb, tmat, rmat, last_finish(fields, k, store))
+        copy(g).start()
+    for g in groups:
+        copy(g).wait()
+
+
+def rim_last_body(level, k, fields, za, zb, xa, xb, tmat, rmat, out, halo, result, sems):
     rows = level.rows
-    inner = pltpu.make_async_copy(out_mid, out.at[:, RIM : rows - RIM], sems.at[0])
-    inner.start()
     fill_halo(halo, xa, xb)
 
     def store(f, x, value):
@@ -524,12 +538,12 @@
 
     apply_operator(level, [None], za, zb, tmat, rmat, last_finish(fields, k, store), halo)
     copies = [
-        pltpu.make_async_copy(result.at[:, 0:RIM], out.at[:, 0:RIM], sems.at[1]),
-        pltpu.make_async_copy(result.at[:, RIM:], out.at[:, rows - RIM :], sems.at[2]),
+        pltpu.make_async_copy(result.at[:, 0:RIM], out.at[:, 0:RIM], sems.at[0]),
+        pltpu.make_async_copy(result.at[:, RIM:], out.at[:, rows - RIM :], sems.at[1]),
     ]
     for copy in copies:
         copy.start()
-    for copy in (inner, *copies):
+    for copy in copies:
         copy.wait()
 
 
@@ -594,42 +608,62 @@
         name="gather",
     )
     k = [k_mid, k_rim, p_mid, p_rim]
-    level = k
+    inner_z, rim_z = ((inner // 4 * 3, 8, radial), F32), ((RIM // 2 * 3, 8, radial), F32)
+    za, zb = swap(edges[2], edges[3], "az")
+    xa, xb = swap(edges[0], edges[1], "ax")
+    level, rim_a, rim_b = k, za, zb
     for factor in (time_step / 4.0, time_step / 3.0):
         size = len(level)
-        xa, xb = swap(edges[0], edges[1], "ax")
-        za, zb = swap(edges[2], edges[3], "az")
 
         def body(*refs, factor=factor, size=size):
             inner_stage_body(factor, Parts(*refs[:size]), Parts(*refs[size : size + 4]), *refs[size + 4 :])
 
-        (new_mid,) = full_specs(body, [mid], [*level, *k, za, zb, tmat, rmat], name="stage_inner", cost=COST)
+        new_mid, to_za, to_zb = full_specs(
+            body, [mid, inner_z, inner_z], [*level, *k, za, zb, tmat, rmat], name="stage_inner", cost=COST if level is k else 0
+        )
+        za, zb = swap(to_za, to_zb, "az")
 
         def body(*refs, factor=factor, size=size):
             rim_stage_body(factor, Parts(*refs[:size]), Parts(*refs[size : size + 4]), *refs[size + 4 :])
 
-        new_rim, *edges = full_specs(
-            body, [rim, *sends], [*level, *k, za, zb, xa, xb, tmat, rmat, new_mid], [halo], name="stage_rim"
+        new_rim, to_xa, to_xb, to_za, to_zb = full_specs(
+            body,
+            [rim, send_x, send_x, rim_z, rim_z],
+            [*level, *k, rim_a, rim_b, xa, xb, tmat, rmat],
+            [halo],
+            name="stage_rim",
+            after=[new_mid],
+            cost=COST,
         )
+        xa, xb = swap(to_xa, to_xb, "ax")
+        rim_a, rim_b = swap(to_za, to_zb, "az")
         level = [new_mid, new_rim]
-    xa, xb = swap(edges[0], edges[1], "ax")
-    za, zb = swap(edges[2], edges[3], "az")
 
     def body(*refs):
         inner_last_body(Parts(*refs[:2]), Parts(*refs[2:6]), *refs[6:])
 
-    (new_mid,) = full_specs(body, [mid], [*level, *k, fields, za, zb, tmat, rmat], name="final_inner", cost=COST)
-
-    def body(*refs):
-        rim_last_body(Parts(*refs[:2]), Parts(*refs[2:6]), *refs[6:])
-
+    whole = ((5, cx, ca, radial), F32)
     (out,) = full_specs(
         body,
-        [((5, cx, ca, radial), F32)],
-        [*level, *k, fields, za, zb, xa, xb, tmat, rmat, new_mid],
-        [halo, rim, pltpu.SemaphoreType.DMA((3,))],
+        [whole],
+        [*level, *k, fields, za, zb, tmat, rmat],
+        [mid, pltpu.SemaphoreType.DMA((inner // GROUP,))],
+        name="final_inner",
+        out_specs=[ANY],
+    )
+
+    def body(out_in, *refs):
+        rim_last_body(Parts(*refs[:2]), Parts(*refs[2:6]), *refs[6:])
+
+    (out,) = full_specs(
+        body,
+        [whole],
+        [out, *level, *k, fields, rim_a, rim_b, xa, xb, tmat, rmat],
+        [halo, rim, pltpu.SemaphoreType.DMA((2,))],
         name="final_rim",
+        in_specs=[ANY] + [VM] * 13,
         out_specs=[ANY],
+        alias={0: 0},
     )
     return out
 

time: 69.3 us -> 72.7 us (1.049)
  starting transfers between devices: 28.4 us -> 35.6 us
  waiting for transfers between devices: 23.3 us -> 19.6 us
    ppermute x11 -> x13, starting transfers between devices: 25.9 us -> 32.6 us  [swap(): lax.ppermute(to_b, axis, pairs_b)]
    ppermute x11 -> x13, waiting for transfers between devices: 19.9 us -> 15.9 us  [swap(): lax.ppermute(to_b, axis, pairs_b)]
    ppermute x11 -> x13, starting transfers between devices: 2.53 us -> 3.08 us  [swap(): lax.ppermute(to_a, axis, pairs_a)]
    ppermute x11 -> x13, waiting for transfers between devices: 3.42 us -> 3.63 us  [swap(): lax.ppermute(to_a, axis, pairs_a)]
  transfers between devices with their start and end apart: 22 -> 26, of which waited for: 8 -> 9; matrix products, arithmetic and copies ran while one was open for 0% -> 0% of each run, Pallas kernels for 13% -> 14%
where the time goes in v7:
time: 72.7 us; the launch traced here: 72.6 us
  starting transfers between devices  35.6 us (49%)
  waiting for transfers between devices  19.6 us (27%)
  Pallas kernels  13.3 us (18%)
  local copies, waits for them, and re-layouts  2.67 us (4%)
  other arithmetic  1.05 us (1%)
    ppermute x13, starting transfers between devices, swap(): lax.ppermute(to_b, axis, pairs_b)  32.6 us
    ppermute x13, waiting for transfers between devices, swap(): lax.ppermute(to_b, axis, pairs_b)  15.9 us
    pallas_call x13, Pallas kernels, full_specs(): pl.pallas_call(run, out_shape=[jax.ShapeDtypeStruct(s, d) for s, d in out...  13.3 us
    ppermute x13, waiting for transfers between devices, swap(): lax.ppermute(to_a, axis, pairs_a)  3.63 us
    ppermute x13, starting transfers between devices, swap(): lax.ppermute(to_a, axis, pairs_a)  3.08 us
    unnamed x18, local copies, waits for them, and re-layouts  2.67 us
  transfers between devices with their start and end apart: 26, of which 9 were waited for; matrix products, arithmetic and copies ran while one was open for 0% of the time, Pallas kernels for 14%

profile of v7, /device:TPU:0, one launch (start us, length us, event | category | flops | bytes accessed | tf_op | source)
XLA Modules:
  0.0 72.6 jit_solution(12993077558564750665)
XLA Ops:
  0.0 1.0 %slice_select_fusion = (f32[4,16,512]{2,1,0:T(8,128)S(1)}, f32[4,16,512]{2,1,0:T(8,128)S(1)}) fusion(f32[16,16,512]{2,1,0:T(8,128)} %refs_0_.4, pred[]{:T(512)S(6)} %eq.3), kind=kLoop, calls=%fused_computation | loop fusion | flops 65536 | bytes 524289 | tf_op jit(solution)/shard_map/jit(_where)/select_n | solution.py:561
  1.1 3.2 %collective-permute-start.1 = (f32[4,16,512]{2,1,0:T(8,128)S(1)}, f32[4,16,512]{2,1,0:T(8,128)S(1)}, u32[]{:S(2)}, u32[]{:S(2)}) collective-permute-start(f32[4,16,512]{2,1,0:T(8,128)S(1)} %get-tuple-element.87), channel_id=1, source_target_pairs={{0,96},{32,64},{64,32},{96,0},{1,97},{33,65},{65,33},{97,1},{2,98}... | collective-permute-start | bytes 393224 | tf_op jit(solution)/shard_map/ppermute | solution.py:99
  4.2 0.1 collective-permute-start
  4.4 1.7 %copy-done = f32[5,32,16,256]{3,2,1,0:T(8,128)S(1)} copy-done((f32[5,32,16,256]{3,2,1,0:T(8,128)S(1)}, f32[5,32,16,256]{3,2,1,0:T(8,128)}, u32[]{:S(2)}) %copy-start) | copy-done | bytes 2621464
  6.1 0.1 edges.1
  6.3 0.9 %copy-done.6 = s32[16,16,512]{2,1,0:T(8,128)S(1)} copy-done((s32[16,16,512]{2,1,0:T(8,128)S(1)}, s32[16,16,512]{2,1,0:T(8,128)}, u32[]{:S(2)}) %copy-start.6) | copy-done | bytes 524312
  7.2 0.5 filter_inner.1
  7.6 0.1 collective-permute-done.1.refs_3_
  7.7 1.5 %collective-permute-done.refs_2_ = f32[4,16,512]{2,1,0:T(8,128)S(1)} collective-permute-done((f32[4,16,512]{2,1,0:T(8,128)S(1)}, f32[4,16,512]{2,1,0:T(8,128)S(1)}, u32[]{:S(2)}, u32[]{:S(2)}) %collective-permute-start) | collective-permute-done | bytes 131104 | tf_op jit(solution)/shard_map/ppermute | solution.py:99
  9.2 0.2 filter_axial.1
  9.4 0.1 collective-permute-start.2
  9.5 6.3 %collective-permute-start.3 = (f32[40,8,256]{2,1,0:T(8,128)S(1)}, f32[40,8,256]{2,1,0:T(8,128)S(1)}, u32[]{:S(2)}, u32[]{:S(2)}) collective-permute-start(f32[40,8,256]{2,1,0:T(8,128)S(1)} %get-tuple-element.51), channel_id=1, source_target_pairs={{0,31},{1,2},{2,1},{3,4},{4,3},{5,6},{6,5},{7,8},{8,7},{9,10},{10,... | collective-permute-start | bytes 983048 | tf_op jit(solution)/shard_map/ppermute | solution.py:99
  15.8 0.4 collective-permute-start.4
  16.2 1.1 %collective-permute-start.5 = (f32[15,16,256]{2,1,0:T(8,128)S(1)}, f32[15,16,256]{2,1,0:T(8,128)S(1)}, u32[]{:S(2)}, u32[]{:S(2)}) collective-permute-start(f32[15,16,256]{2,1,0:T(8,128)S(1)} %get-tuple-element.53), channel_id=1, source_target_pairs={{0,96},{32,64},{64,32},{96,0},{1,97},{33,65},{65,33},{97,1},{2,98}... | collective-permute-start | bytes 737288 | tf_op jit(solution)/shard_map/ppermute | solution.py:99
  17.3 0.3 route.1
  17.6 0.0 collective-permute-done.2.refs_2_.refs_1_
  17.6 2.9 %collective-permute-done.3.refs_3_.refs_2_ = f32[40,8,256]{2,1,0:T(8,128)S(1)} collective-permute-done((f32[40,8,256]{2,1,0:T(8,128)S(1)}, f32[40,8,256]{2,1,0:T(8,128)S(1)}, u32[]{:S(2)}, u32[]{:S(2)}) %collective-permute-start.3) | collective-permute-done | bytes 327712 | tf_op jit(solution)/shard_map/ppermute | solution.py:99
  20.6 2.3 %filter_rest.1 = (f32[256,256]{1,0:T(8,128)S(1)}, f32[17,8,256]{2,1,0:T(8,128)S(1)}, f32[17,8,256]{2,1,0:T(8,128)S(1)}, f32[18,8,256]{2,1,0:T(8,128)S(1)}, f32[18,8,256]{2,1,0:T(8,128)S(1)}) custom-call(f32[16,16,512]{2,1,0:T(8,128)S(1)} %get-tuple-element.54.refs_2_.refs_0_, s32[16,16,512]{2,1,0:T(8,128)S(1)} %get-tuple-element.48.refs_1_, ...), custom_call_target="tpu_custom_call" | custom-call | tf_op jit(solution)/shard_map/filter_rest/pallas_call | solution.py:108
  22.9 0.1 collective-permute-start.8
  23.0 5.1 %collective-permute-start.9 = (f32[18,8,256]{2,1,0:T(8,128)S(1)}, f32[18,8,256]{2,1,0:T(8,128)S(1)}, u32[]{:S(2)}, u32[]{:S(2)}) collective-permute-start(f32[18,8,256]{2,1,0:T(8,128)S(1)} %get-tuple-element.64), channel_id=1, source_target_pairs={{0,31},{1,2},{2,1},{3,4},{4,3},{5,6},{6,5},{7,8},{8,7},{9,10},{10,... | collective-permute-start | bytes 442376 | tf_op jit(solution)/shard_map/ppermute | solution.py:99
  28.2 0.4 collective-permute-start.6
  28.5 0.0 collective-permute-done.4.refs_3_
  28.5 1.1 %collective-permute-start.7 = (f32[17,8,256]{2,1,0:T(8,128)S(1)}, f32[17,8,256]{2,1,0:T(8,128)S(1)}, u32[]{:S(2)}, u32[]{:S(2)}) collective-permute-start(f32[17,8,256]{2,1,0:T(8,128)S(1)} %get-tuple-element.62), channel_id=1, source_target_pairs={{0,96},{32,64},{64,32},{96,0},{1,97},{33,65},{65,33},{97,1},{2,98}... | collective-permute-start | bytes 417800 | tf_op jit(solution)/shard_map/ppermute | solution.py:99
  29.7 0.0 collective-permute-done.5.refs_4_
  29.7 1.6 %operator.1 = (f32[5,24,16,256]{3,2,1,0:T(8,128)S(1)}, f32[5,8,16,256]{3,2,1,0:T(8,128)S(1)}) custom-call(f32[5,32,16,256]{3,2,1,0:T(8,128)S(1)} %copy-done.1, f32[40,8,256]{2,1,0:T(8,128)S(1)} %collective-permute-done.2.refs_2_.refs_1_, f32[40,8,256]{2,1,0:T(8,128)S(1)} %collective-permute-done.3.refs_3_.refs_2_, ...), custom_call_target="tpu_custom_call" | custom-call | tf_op jit(solution)/shard_map/operator/pallas_call | solution.py:108
  31.2 2.0 %collective-permute-done.6.refs_2_ = f32[17,8,256]{2,1,0:T(8,128)S(1)} collective-permute-done((f32[17,8,256]{2,1,0:T(8,128)S(1)}, f32[17,8,256]{2,1,0:T(8,128)S(1)}, u32[]{:S(2)}, u32[]{:S(2)}) %collective-permute-start.6) | collective-permute-done | bytes 139296 | tf_op jit(solution)/shard_map/ppermute | solution.py:99
  33.2 1.6 %collective-permute-done.7.refs_3_ = f32[17,8,256]{2,1,0:T(8,128)S(1)} collective-permute-done((f32[17,8,256]{2,1,0:T(8,128)S(1)}, f32[17,8,256]{2,1,0:T(8,128)S(1)}, u32[]{:S(2)}, u32[]{:S(2)}) %collective-permute-start.7) | collective-permute-done | bytes 139296 | tf_op jit(solution)/shard_map/ppermute | solution.py:99
  34.8 0.0 collective-permute-done.8.refs_4_
  34.8 0.0 collective-permute-done.9.refs_5_
  34.8 0.6 gather.1
  35.4 0.1 collective-permute-start.10
  35.5 1.3 %collective-permute-start.11 = (f32[24,8,256]{2,1,0:T(8,128)S(1)}, f32[24,8,256]{2,1,0:T(8,128)S(1)}, u32[]{:S(2)}, u32[]{:S(2)}) collective-permute-start(f32[24,8,256]{2,1,0:T(8,128)S(1)} %get-tuple-element.68), channel_id=1, source_target_pairs={{0,31},{1,2},{2,1},{3,4},{4,3},{5,6},{6,5},{7,8},{8,7},{9,10},{10,... | collective-permute-start | bytes 589832 | tf_op jit(solution)/shard_map/ppermute | solution.py:99
  36.8 0.4 collective-permute-start.12
  37.2 1.1 %collective-permute-start.13 = (f32[15,16,256]{2,1,0:T(8,128)S(1)}, f32[15,16,256]{2,1,0:T(8,128)S(1)}, u32[]{:S(2)}, u32[]{:S(2)}) collective-permute-start(f32[15,16,256]{2,1,0:T(8,128)S(1)} %get-tuple-element.71), channel_id=1, source_target_pairs={{0,96},{32,64},{64,32},{96,0},{1,97},{33,65},{65,33},{97,1},{2,98}... | collective-permute-start | bytes 737288 | tf_op jit(solution)/shard_map/ppermute | solution.py:99
  38.3 0.0 collective-permute-done.10.refs_8_
  38.3 5.7 %collective-permute-done.11.refs_9_ = f32[24,8,256]{2,1,0:T(8,128)S(1)} collective-permute-done((f32[24,8,256]{2,1,0:T(8,128)S(1)}, f32[24,8,256]{2,1,0:T(8,128)S(1)}, u32[]{:S(2)}, u32[]{:S(2)}) %collective-permute-start.11) | collective-permute-done | bytes 196640 | tf_op jit(solution)/shard_map/ppermute | solution.py:99
  44.0 1.4 %stage_inner.2 = (f32[5,24,16,256]{3,2,1,0:T(8,128)S(1)}, f32[18,8,256]{2,1,0:T(8,128)S(1)}, f32[18,8,256]{2,1,0:T(8,128)S(1)}) custom-call(f32[5,24,16,256]{3,2,1,0:T(8,128)S(1)} %get-tuple-element.58.refs_6_.refs_0_.refs_4_.refs_2_.refs_3_, f32[5,8,16,256]{3,2,1,0:T(8,128)S(1)} %get-tuple-element.59.refs_7_.refs_1_.refs_5_.refs_3_.refs_4_, ...), custom_call_target="tpu_custom_call" | custom-call | flops 137438953472 | tf_op jit(solution)/shard_map/stage_inner/pallas_call | solution.py:108
  45.4 0.0 collective-permute-done.12.refs_10_
  45.4 0.0 collective-permute-done.13.refs_11_
  45.4 0.6 stage_rim.2
  46.0 0.5 collective-permute-start.18
  46.5 1.5 %collective-permute-start.19 = (f32[15,16,256]{2,1,0:T(8,128)S(1)}, f32[15,16,256]{2,1,0:T(8,128)S(1)}, u32[]{:S(2)}, u32[]{:S(2)}) collective-permute-start(f32[15,16,256]{2,1,0:T(8,128)S(1)} %get-tuple-element.79), channel_id=1, source_target_pairs={{0,96},{32,64},{64,32},{96,0},{1,97},{33,65},{65,33},{97,1},{2,98}... | collective-permute-start | bytes 737288 | tf_op jit(solution)/shard_map/ppermute | solution.py:99
  48.0 0.0 collective-permute-start.14
  48.0 1.1 %collective-permute-start.15 = (f32[18,8,256]{2,1,0:T(8,128)S(1)}, f32[18,8,256]{2,1,0:T(8,128)S(1)}, u32[]{:S(2)}, u32[]{:S(2)}) collective-permute-start(f32[18,8,256]{2,1,0:T(8,128)S(1)} %get-tuple-element.74), channel_id=1, source_target_pairs={{0,31},{1,2},{2,1},{3,4},{4,3},{5,6},{6,5},{7,8},{8,7},{9,10},{10,... | collective-permute-start | bytes 442376 | tf_op jit(solution)/shard_map/ppermute | solution.py:99
  49.0 0.2 collective-permute-start.16
  49.2 0.2 collective-permute-done.14.refs_6_
  49.4 3.7 %collective-permute-start.17 = (f32[6,8,256]{2,1,0:T(8,128)S(1)}, f32[6,8,256]{2,1,0:T(8,128)S(1)}, u32[]{:S(2)}, u32[]{:S(2)}) collective-permute-start(f32[6,8,256]{2,1,0:T(8,128)S(1)} %get-tuple-element.77), channel_id=1, source_target_pairs={{0,31},{1,2},{2,1},{3,4},{4,3},{5,6},{6,5},{7,8},{8,7},{9,10},{10,... | collective-permute-start | bytes 147464 | tf_op jit(solution)/shard_map/ppermute | solution.py:99
  53.1 2.8 %collective-permute-done.15.refs_7_ = f32[18,8,256]{2,1,0:T(8,128)S(1)} collective-permute-done((f32[18,8,256]{2,1,0:T(8,128)S(1)}, f32[18,8,256]{2,1,0:T(8,128)S(1)}, u32[]{:S(2)}, u32[]{:S(2)}) %collective-permute-start.15) | collective-permute-done | bytes 147488 | tf_op jit(solution)/shard_map/ppermute | solution.py:99
  55.9 1.4 %stage_inner.3 = (f32[5,24,16,256]{3,2,1,0:T(8,128)S(1)}, f32[18,8,256]{2,1,0:T(8,128)S(1)}, f32[18,8,256]{2,1,0:T(8,128)S(1)}) custom-call(f32[5,24,16,256]{3,2,1,0:T(8,128)S(1)} %get-tuple-element.69.refs_14_.refs_0_, f32[5,8,16,256]{3,2,1,0:T(8,128)S(1)} %get-tuple-element.72.refs_1_, ...), custom_call_target="tpu_custom_call" | custom-call | tf_op jit(solution)/shard_map/stage_inner/pallas_call | solution.py:108
  57.2 0.0 collective-permute-done.16.refs_6_
  57.3 0.0 collective-permute-done.18.refs_8_
  57.3 0.0 collective-permute-done.19.refs_9_
  57.3 0.0 copy-start.2
  57.3 0.6 stage_rim.3
  57.9 0.9 %collective-permute-start.24 = (f32[15,16,256]{2,1,0:T(8,128)S(1)}, f32[15,16,256]{2,1,0:T(8,128)S(1)}, u32[]{:S(2)}, u32[]{:S(2)}) collective-permute-start(f32[15,16,256]{2,1,0:T(8,128)S(1)} %get-tuple-element.85), channel_id=1, source_target_pairs={{0,32},{32,0},{64,96},{96,64},{1,33},{33,1},{65,97},{97,65},{2,34}... | collective-permute-start | bytes 737288 | tf_op jit(solution)/shard_map/ppermute | solution.py:99
  58.8 1.9 %collective-permute-start.25 = (f32[15,16,256]{2,1,0:T(8,128)S(1)}, f32[15,16,256]{2,1,0:T(8,128)S(1)}, u32[]{:S(2)}, u32[]{:S(2)}) collective-permute-start(f32[15,16,256]{2,1,0:T(8,128)S(1)} %get-tuple-element.86), channel_id=1, source_target_pairs={{0,96},{32,64},{64,32},{96,0},{1,97},{33,65},{65,33},{97,1},{2,98}... | collective-permute-start | bytes 737288 | tf_op jit(solution)/shard_map/ppermute | solution.py:99
  60.7 2.0 %collective-permute-start.21 = (f32[18,8,256]{2,1,0:T(8,128)S(1)}, f32[18,8,256]{2,1,0:T(8,128)S(1)}, u32[]{:S(2)}, u32[]{:S(2)}) collective-permute-start(f32[18,8,256]{2,1,0:T(8,128)S(1)} %get-tuple-element.82), channel_id=1, source_target_pairs={{0,31},{1,2},{2,1},{3,4},{4,3},{5,6},{6,5},{7,8},{8,7},{9,10},{10,... | collective-permute-start | bytes 442376 | tf_op jit(solution)/shard_map/ppermute | solution.py:99
  62.8 3.0 %collective-permute-start.23 = (f32[6,8,256]{2,1,0:T(8,128)S(1)}, f32[6,8,256]{2,1,0:T(8,128)S(1)}, u32[]{:S(2)}, u32[]{:S(2)}) collective-permute-start(f32[6,8,256]{2,1,0:T(8,128)S(1)} %get-tuple-element.84), channel_id=1, source_target_pairs={{0,31},{1,2},{2,1},{3,4},{4,3},{5,6},{6,5},{7,8},{8,7},{9,10},{10,... | collective-permute-start | bytes 147464 | tf_op jit(solution)/shard_map/ppermute | solution.py:99
  65.8 2.8 %collective-permute-done.21.refs_8_ = f32[18,8,256]{2,1,0:T(8,128)S(1)} collective-permute-done((f32[18,8,256]{2,1,0:T(8,128)S(1)}, f32[18,8,256]{2,1,0:T(8,128)S(1)}, u32[]{:S(2)}, u32[]{:S(2)}) %collective-permute-start.21) | collective-permute-done | bytes 147488 | tf_op jit(solution)/shard_map/ppermute | solution.py:99
  68.6 2.3 %final_inner.1.refs_0_ = f32[5,32,16,256]{3,2,1,0:T(8,128)} custom-call(f32[5,24,16,256]{3,2,1,0:T(8,128)S(1)} %get-tuple-element.75.refs_12_.refs_0_.refs_1_, f32[5,8,16,256]{3,2,1,0:T(8,128)S(1)} %get-tuple-element.80.refs_1_.refs_2_, f32[5,24,16,256]{3,2,1,0:T(8,128)S(1)} %get-tuple-element.58.refs_6_.refs_0_.refs_4_.refs_2_.refs_3_, ...), custom_call_target="tpu_custom_call" | custom-call | tf_op jit(solution)/shard_map/final_inner/pallas_call | solution.py:108
  70.9 0.0 collective-permute-done.22.refs_8_
  70.9 0.0 collective-permute-done.24.refs_10_
  71.0 0.0 collective-permute-done.25.refs_11_
  71.0 1.5 %final_rim.1 = f32[5,32,16,256]{3,2,1,0:T(8,128)} custom-call(f32[5,32,16,256]{3,2,1,0:T(8,128)} %final_inner.1.refs_0_, f32[5,24,16,256]{3,2,1,0:T(8,128)S(1)} %get-tuple-element.75.refs_12_.refs_0_.refs_1_, f32[5,8,16,256]{3,2,1,0:T(8,128)S(1)} %get-tuple-element.80.refs_1_.refs_2_, ...), custom_call_target="tpu_custom_call", output_to_operand_aliasing={{}: (0, {})} | custom-call | tf_op jit(solution)/shard_map/final_rim/pallas_call | solution.py:108
  (20 shorter events, 0.0 us)
Async XLA Ops:
  0.0 6.2 %copy-start.5 = (f32[16,16,512]{2,1,0:T(8,128)S(1)}, f32[16,16,512]{2,1,0:T(8,128)}, u32[]{:S(2)}) copy-start(f32[16,16,512]{2,1,0:T(8,128)} %refs_0_.4) | copy-start | bytes 1572868
  1.1 6.7 %collective-permute-start.1 = (f32[4,16,512]{2,1,0:T(8,128)S(1)}, f32[4,16,512]{2,1,0:T(8,128)S(1)}, u32[]{:S(2)}, u32[]{:S(2)}) collective-permute-start(f32[4,16,512]{2,1,0:T(8,128)S(1)} %get-tuple-element.87), channel_id=1, source_target_pairs={{0,96},{32,64},{64,32},{96,0},{1,97},{33,65},{65,33},{97,1},{2,98}... | collective-permute-start | bytes 393224 | tf_op jit(solution)/shard_map/ppermute | solution.py:99
  4.2 5.0 %collective-permute-start = (f32[4,16,512]{2,1,0:T(8,128)S(1)}, f32[4,16,512]{2,1,0:T(8,128)S(1)}, u32[]{:S(2)}, u32[]{:S(2)}) collective-permute-start(f32[4,16,512]{2,1,0:T(8,128)S(1)} %get-tuple-element.88.refs_1_), channel_id=1, source_target_pairs={{0,32},{32,0},{64,96},{96,64},{1,33},{33,1},{65,97},{97,65},{2,34}... | collective-permute-start | bytes 393224 | tf_op jit(solution)/shard_map/ppermute | solution.py:99
  4.4 1.7 %copy-start = (f32[5,32,16,256]{3,2,1,0:T(8,128)S(1)}, f32[5,32,16,256]{3,2,1,0:T(8,128)}, u32[]{:S(2)}) copy-start(f32[5,32,16,256]{3,2,1,0:T(8,128)} %refs_7_.1) | copy-start | bytes 7864324
  6.1 1.0 %copy-start.6 = (s32[16,16,512]{2,1,0:T(8,128)S(1)}, s32[16,16,512]{2,1,0:T(8,128)}, u32[]{:S(2)}) copy-start(s32[16,16,512]{2,1,0:T(8,128)} %refs_1_.1) | copy-start | bytes 1572868
  6.1 11.2 %copy-start.7 = (s32[256]{0:T(256)S(1)}, s32[256]{0:T(256)}, u32[]{:S(2)}) copy-start(s32[256]{0:T(256)} %param.9) | copy-start | bytes 3076
  6.1 11.2 %copy-start.8 = (s32[256]{0:T(256)S(1)}, s32[256]{0:T(256)}, u32[]{:S(2)}) copy-start(s32[256]{0:T(256)} %param.10) | copy-start | bytes 3076
  7.2 22.5 %copy-start.1 = (f32[5,32,16,256]{3,2,1,0:T(8,128)S(1)}, f32[5,32,16,256]{3,2,1,0:T(8,128)}, u32[]{:S(2)}) copy-start(f32[5,32,16,256]{3,2,1,0:T(8,128)} %refs_7_.1) | copy-start | bytes 7864324
  7.2 22.5 %copy-start.3 = (bf16[2,2,256,256]{3,2,1,0:T(8,128)(2,1)S(1)}, bf16[2,2,256,256]{3,2,1,0:T(8,128)(2,1)}, u32[]{:S(2)}) copy-start(bf16[2,2,256,256]{3,2,1,0:T(8,128)(2,1)} %constant.17.clone.refs_6_.refs_11_.refs_13_.refs_9_.refs_10_) | copy-start | bytes 1572868
  7.2 22.5 %copy-start.4 = (bf16[2,2,128,224]{3,2,1,0:T(8,128)(2,1)S(1)}, bf16[2,2,128,224]{3,2,1,0:T(8,128)(2,1)}, u32[]{:S(2)}) copy-start(bf16[2,2,128,224]{3,2,1,0:T(8,128)(2,1)} %constant.16.clone.refs_5_.refs_10_.refs_12_.refs_8_.refs_9_) | copy-start | bytes 688132
  9.4 8.2 %collective-permute-start.2 = (f32[40,8,256]{2,1,0:T(8,128)S(1)}, f32[40,8,256]{2,1,0:T(8,128)S(1)}, u32[]{:S(2)}, u32[]{:S(2)}) collective-permute-start(f32[40,8,256]{2,1,0:T(8,128)S(1)} %get-tuple-element.50), channel_id=1, source_target_pairs={{0,1},{1,0},{2,3},{3,2},{4,5},{5,4},{6,7},{7,6},{8,9},{9,8},{10,11... | collective-permute-start | bytes 983048 | tf_op jit(solution)/shard_map/ppermute | solution.py:99
  9.5 11.1 %collective-permute-start.3 = (f32[40,8,256]{2,1,0:T(8,128)S(1)}, f32[40,8,256]{2,1,0:T(8,128)S(1)}, u32[]{:S(2)}, u32[]{:S(2)}) collective-permute-start(f32[40,8,256]{2,1,0:T(8,128)S(1)} %get-tuple-element.51), channel_id=1, source_target_pairs={{0,31},{1,2},{2,1},{3,4},{4,3},{5,6},{6,5},{7,8},{8,7},{9,10},{10,... | collective-permute-start | bytes 983048 | tf_op jit(solution)/shard_map/ppermute | solution.py:99
  15.8 12.7 %collective-permute-start.4 = (f32[15,16,256]{2,1,0:T(8,128)S(1)}, f32[15,16,256]{2,1,0:T(8,128)S(1)}, u32[]{:S(2)}, u32[]{:S(2)}) collective-permute-start(f32[15,16,256]{2,1,0:T(8,128)S(1)} %get-tuple-element.52), channel_id=1, source_target_pairs={{0,32},{32,0},{64,96},{96,64},{1,33},{33,1},{65,97},{97,65},{2,34}... | collective-permute-start | bytes 737288 | tf_op jit(solution)/shard_map/ppermute | solution.py:99
  16.2 13.5 %collective-permute-start.5 = (f32[15,16,256]{2,1,0:T(8,128)S(1)}, f32[15,16,256]{2,1,0:T(8,128)S(1)}, u32[]{:S(2)}, u32[]{:S(2)}) collective-permute-start(f32[15,16,256]{2,1,0:T(8,128)S(1)} %get-tuple-element.53), channel_id=1, source_target_pairs={{0,96},{32,64},{64,32},{96,0},{1,97},{33,65},{65,33},{97,1},{2,98}... | collective-permute-start | bytes 737288 | tf_op jit(solution)/shard_map/ppermute | solution.py:99
  22.9 11.9 %collective-permute-start.8 = (f32[18,8,256]{2,1,0:T(8,128)S(1)}, f32[18,8,256]{2,1,0:T(8,128)S(1)}, u32[]{:S(2)}, u32[]{:S(2)}) collective-permute-start(f32[18,8,256]{2,1,0:T(8,128)S(1)} %get-tuple-element.63), channel_id=1, source_target_pairs={{0,1},{1,0},{2,3},{3,2},{4,5},{5,4},{6,7},{7,6},{8,9},{9,8},{10,11... | collective-permute-start | bytes 442376 | tf_op jit(solution)/shard_map/ppermute | solution.py:99
  23.0 11.8 %collective-permute-start.9 = (f32[18,8,256]{2,1,0:T(8,128)S(1)}, f32[18,8,256]{2,1,0:T(8,128)S(1)}, u32[]{:S(2)}, u32[]{:S(2)}) collective-permute-start(f32[18,8,256]{2,1,0:T(8,128)S(1)} %get-tuple-element.64), channel_id=1, source_target_pairs={{0,31},{1,2},{2,1},{3,4},{4,3},{5,6},{6,5},{7,8},{8,7},{9,10},{10,... | collective-permute-start | bytes 442376 | tf_op jit(solution)/shard_map/ppermute | solution.py:99
  28.2 5.1 %collective-permute-start.6 = (f32[17,8,256]{2,1,0:T(8,128)S(1)}, f32[17,8,256]{2,1,0:T(8,128)S(1)}, u32[]{:S(2)}, u32[]{:S(2)}) collective-permute-start(f32[17,8,256]{2,1,0:T(8,128)S(1)} %get-tuple-element.61), channel_id=1, source_target_pairs={{0,32},{32,0},{64,96},{96,64},{1,33},{33,1},{65,97},{97,65},{2,34}... | collective-permute-start | bytes 417800 | tf_op jit(solution)/shard_map/ppermute | solution.py:99
  28.5 6.3 %collective-permute-start.7 = (f32[17,8,256]{2,1,0:T(8,128)S(1)}, f32[17,8,256]{2,1,0:T(8,128)S(1)}, u32[]{:S(2)}, u32[]{:S(2)}) collective-permute-start(f32[17,8,256]{2,1,0:T(8,128)S(1)} %get-tuple-element.62), channel_id=1, source_target_pairs={{0,96},{32,64},{64,32},{96,0},{1,97},{33,65},{65,33},{97,1},{2,98}... | collective-permute-start | bytes 417800 | tf_op jit(solution)/shard_map/ppermute | solution.py:99
  35.4 2.9 %collective-permute-start.10 = (f32[24,8,256]{2,1,0:T(8,128)S(1)}, f32[24,8,256]{2,1,0:T(8,128)S(1)}, u32[]{:S(2)}, u32[]{:S(2)}) collective-permute-start(f32[24,8,256]{2,1,0:T(8,128)S(1)} %get-tuple-element.67), channel_id=1, source_target_pairs={{0,1},{1,0},{2,3},{3,2},{4,5},{5,4},{6,7},{7,6},{8,9},{9,8},{10,11... | collective-permute-start | bytes 589832 | tf_op jit(solution)/shard_map/ppermute | solution.py:99
  35.5 8.5 %collective-permute-start.11 = (f32[24,8,256]{2,1,0:T(8,128)S(1)}, f32[24,8,256]{2,1,0:T(8,128)S(1)}, u32[]{:S(2)}, u32[]{:S(2)}) collective-permute-start(f32[24,8,256]{2,1,0:T(8,128)S(1)} %get-tuple-element.68), channel_id=1, source_target_pairs={{0,31},{1,2},{2,1},{3,4},{4,3},{5,6},{6,5},{7,8},{8,7},{9,10},{10,... | collective-permute-start | bytes 589832 | tf_op jit(solution)/shard_map/ppermute | solution.py:99
  36.8 8.5 %collective-permute-start.12 = (f32[15,16,256]{2,1,0:T(8,128)S(1)}, f32[15,16,256]{2,1,0:T(8,128)S(1)}, u32[]{:S(2)}, u32[]{:S(2)}) collective-permute-start(f32[15,16,256]{2,1,0:T(8,128)S(1)} %get-tuple-element.70), channel_id=1, source_target_pairs={{0,32},{32,0},{64,96},{96,64},{1,33},{33,1},{65,97},{97,65},{2,34}... | collective-permute-start | bytes 737288 | tf_op jit(solution)/shard_map/ppermute | solution.py:99
  37.2 8.2 %collective-permute-start.13 = (f32[15,16,256]{2,1,0:T(8,128)S(1)}, f32[15,16,256]{2,1,0:T(8,128)S(1)}, u32[]{:S(2)}, u32[]{:S(2)}) collective-permute-start(f32[15,16,256]{2,1,0:T(8,128)S(1)} %get-tuple-element.71), channel_id=1, source_target_pairs={{0,96},{32,64},{64,32},{96,0},{1,97},{33,65},{65,33},{97,1},{2,98}... | collective-permute-start | bytes 737288 | tf_op jit(solution)/shard_map/ppermute | solution.py:99
  46.0 11.3 %collective-permute-start.18 = (f32[15,16,256]{2,1,0:T(8,128)S(1)}, f32[15,16,256]{2,1,0:T(8,128)S(1)}, u32[]{:S(2)}, u32[]{:S(2)}) collective-permute-start(f32[15,16,256]{2,1,0:T(8,128)S(1)} %get-tuple-element.78), channel_id=1, source_target_pairs={{0,32},{32,0},{64,96},{96,64},{1,33},{33,1},{65,97},{97,65},{2,34}... | collective-permute-start | bytes 737288 | tf_op jit(solution)/shard_map/ppermute | solution.py:99
  46.5 10.8 %collective-permute-start.19 = (f32[15,16,256]{2,1,0:T(8,128)S(1)}, f32[15,16,256]{2,1,0:T(8,128)S(1)}, u32[]{:S(2)}, u32[]{:S(2)}) collective-permute-start(f32[15,16,256]{2,1,0:T(8,128)S(1)} %get-tuple-element.79), channel_id=1, source_target_pairs={{0,96},{32,64},{64,32},{96,0},{1,97},{33,65},{65,33},{97,1},{2,98}... | collective-permute-start | bytes 737288 | tf_op jit(solution)/shard_map/ppermute | solution.py:99
  48.0 1.4 %collective-permute-start.14 = (f32[18,8,256]{2,1,0:T(8,128)S(1)}, f32[18,8,256]{2,1,0:T(8,128)S(1)}, u32[]{:S(2)}, u32[]{:S(2)}) collective-permute-start(f32[18,8,256]{2,1,0:T(8,128)S(1)} %get-tuple-element.73), channel_id=1, source_target_pairs={{0,1},{1,0},{2,3},{3,2},{4,5},{5,4},{6,7},{7,6},{8,9},{9,8},{10,11... | collective-permute-start | bytes 442376 | tf_op jit(solution)/shard_map/ppermute | solution.py:99
  48.0 7.9 %collective-permute-start.15 = (f32[18,8,256]{2,1,0:T(8,128)S(1)}, f32[18,8,256]{2,1,0:T(8,128)S(1)}, u32[]{:S(2)}, u32[]{:S(2)}) collective-permute-start(f32[18,8,256]{2,1,0:T(8,128)S(1)} %get-tuple-element.74), channel_id=1, source_target_pairs={{0,31},{1,2},{2,1},{3,4},{4,3},{5,6},{6,5},{7,8},{8,7},{9,10},{10,... | collective-permute-start | bytes 442376 | tf_op jit(solution)/shard_map/ppermute | solution.py:99
  49.0 8.2 %collective-permute-start.16 = (f32[6,8,256]{2,1,0:T(8,128)S(1)}, f32[6,8,256]{2,1,0:T(8,128)S(1)}, u32[]{:S(2)}, u32[]{:S(2)}) collective-permute-start(f32[6,8,256]{2,1,0:T(8,128)S(1)} %get-tuple-element.76), channel_id=1, source_target_pairs={{0,1},{1,0},{2,3},{3,2},{4,5},{5,4},{6,7},{7,6},{8,9},{9,8},{10,11... | collective-permute-start | bytes 147464 | tf_op jit(solution)/shard_map/ppermute | solution.py:99
  49.4 7.9 %collective-permute-start.17 = (f32[6,8,256]{2,1,0:T(8,128)S(1)}, f32[6,8,256]{2,1,0:T(8,128)S(1)}, u32[]{:S(2)}, u32[]{:S(2)}) collective-permute-start(f32[6,8,256]{2,1,0:T(8,128)S(1)} %get-tuple-element.77), channel_id=1, source_target_pairs={{0,31},{1,2},{2,1},{3,4},{4,3},{5,6},{6,5},{7,8},{8,7},{9,10},{10,... | collective-permute-start | bytes 147464 | tf_op jit(solution)/shard_map/ppermute | solution.py:99
  57.3 11.3 %copy-start.2 = (f32[5,32,16,256]{3,2,1,0:T(8,128)S(1)}, f32[5,32,16,256]{3,2,1,0:T(8,128)}, u32[]{:S(2)}) copy-start(f32[5,32,16,256]{3,2,1,0:T(8,128)} %refs_7_.1) | copy-start | bytes 7864324
  57.9 13.1 %collective-permute-start.24 = (f32[15,16,256]{2,1,0:T(8,128)S(1)}, f32[15,16,256]{2,1,0:T(8,128)S(1)}, u32[]{:S(2)}, u32[]{:S(2)}) collective-permute-start(f32[15,16,256]{2,1,0:T(8,128)S(1)} %get-tuple-element.85), channel_id=1, source_target_pairs={{0,32},{32,0},{64,96},{96,64},{1,33},{33,1},{65,97},{97,65},{2,34}... | collective-permute-start | bytes 737288 | tf_op jit(solution)/shard_map/ppermute | solution.py:99
  58.8 12.2 %collective-permute-start.25 = (f32[15,16,256]{2,1,0:T(8,128)S(1)}, f32[15,16,256]{2,1,0:T(8,128)S(1)}, u32[]{:S(2)}, u32[]{:S(2)}) collective-permute-start(f32[15,16,256]{2,1,0:T(8,128)S(1)} %get-tuple-element.86), channel_id=1, source_target_pairs={{0,96},{32,64},{64,32},{96,0},{1,97},{33,65},{65,33},{97,1},{2,98}... | collective-permute-start | bytes 737288 | tf_op jit(solution)/shard_map/ppermute | solution.py:99
  60.7 2.1 %collective-permute-start.20 = (f32[18,8,256]{2,1,0:T(8,128)S(1)}, f32[18,8,256]{2,1,0:T(8,128)S(1)}, u32[]{:S(2)}, u32[]{:S(2)}) collective-permute-start(f32[18,8,256]{2,1,0:T(8,128)S(1)} %get-tuple-element.81), channel_id=1, source_target_pairs={{0,1},{1,0},{2,3},{3,2},{4,5},{5,4},{6,7},{7,6},{8,9},{9,8},{10,11... | collective-permute-start | bytes 442376 | tf_op jit(solution)/shard_map/ppermute | solution.py:99
  60.7 7.9 %collective-permute-start.21 = (f32[18,8,256]{2,1,0:T(8,128)S(1)}, f32[18,8,256]{2,1,0:T(8,128)S(1)}, u32[]{:S(2)}, u32[]{:S(2)}) collective-permute-start(f32[18,8,256]{2,1,0:T(8,128)S(1)} %get-tuple-element.82), channel_id=1, source_target_pairs={{0,31},{1,2},{2,1},{3,4},{4,3},{5,6},{6,5},{7,8},{8,7},{9,10},{10,... | collective-permute-start | bytes 442376 | tf_op jit(solution)/shard_map/ppermute | solution.py:99
  62.7 8.2 %collective-permute-start.22 = (f32[6,8,256]{2,1,0:T(8,128)S(1)}, f32[6,8,256]{2,1,0:T(8,128)S(1)}, u32[]{:S(2)}, u32[]{:S(2)}) collective-permute-start(f32[6,8,256]{2,1,0:T(8,128)S(1)} %get-tuple-element.83), channel_id=1, source_target_pairs={{0,1},{1,0},{2,3},{3,2},{4,5},{5,4},{6,7},{7,6},{8,9},{9,8},{10,11... | collective-permute-start | bytes 147464 | tf_op jit(solution)/shard_map/ppermute | solution.py:99
  62.8 8.2 %collective-permute-start.23 = (f32[6,8,256]{2,1,0:T(8,128)S(1)}, f32[6,8,256]{2,1,0:T(8,128)S(1)}, u32[]{:S(2)}, u32[]{:S(2)}) collective-permute-start(f32[6,8,256]{2,1,0:T(8,128)S(1)} %get-tuple-element.84), channel_id=1, source_target_pairs={{0,31},{1,2},{2,1},{3,4},{4,3},{5,6},{6,5},{7,8},{8,7},{9,10},{10,... | collective-permute-start | bytes 147464 | tf_op jit(solution)/shard_map/ppermute | solution.py:99

commit v8 on v7

--- a/solution.py
+++ b/solution.py
@@ -24,6 +24,7 @@
 PARAMS = pltpu.CompilerParams(vmem_limit_bytes=24 * 1024 * 1024)
 GROUP = 8
 RIM = 4
+SOME = 2_000_000_000
 COST = 1 << 37
 
 
@@ -490,7 +491,7 @@
     write_z(Parts(out_mid, None, rows=level.rows), range(RIM, level.rows - RIM, 4), to_za, to_zb)
 
 
-def rim_stage_body(factor, level, base, za, zb, xa, xb, tmat, rmat, out_rim, to_xa, to_xb, to_za, to_zb, halo):
+def rim_stage_body(factor, level, base, xa, xb, za, zb, tmat, rmat, out_rim, to_xa, to_xb, to_za, to_zb, halo):
     fill_halo(halo, xa, xb)
     out = Parts(None, out_rim, rows=level.rows)
 
@@ -529,7 +530,7 @@
         copy(g).wait()
 
 
-def rim_last_body(level, k, fields, za, zb, xa, xb, tmat, rmat, out, halo, result, sems):
+def rim_last_body(level, k, fields, xa, xb, za, zb, tmat, rmat, out, halo, result, sems):
     rows = level.rows
     fill_halo(halo, xa, xb)
 
@@ -619,7 +620,7 @@
             inner_stage_body(factor, Parts(*refs[:size]), Parts(*refs[size : size + 4]), *refs[size + 4 :])
 
         new_mid, to_za, to_zb = full_specs(
-            body, [mid, inner_z, inner_z], [*level, *k, za, zb, tmat, rmat], name="stage_inner", cost=COST if level is k else 0
+            body, [mid, inner_z, inner_z], [*level, *k, za, zb, tmat, rmat], name="stage_inner", cost=COST if level is k else SOME
         )
         za, zb = swap(to_za, to_zb, "az")
 
@@ -629,7 +630,7 @@
         new_rim, to_xa, to_xb, to_za, to_zb = full_specs(
             body,
             [rim, send_x, send_x, rim_z, rim_z],
-            [*level, *k, rim_a, rim_b, xa, xb, tmat, rmat],
+            [*level, *k, xa, xb, rim_a, rim_b, tmat, rmat],
             [halo],
             name="stage_rim",
             after=[new_mid],
@@ -650,6 +651,7 @@
         [mid, pltpu.SemaphoreType.DMA((inner // GROUP,))],
         name="final_inner",
         out_specs=[ANY],
+        cost=SOME,
     )
 
     def body(out_in, *refs):
@@ -658,7 +660,7 @@
     (out,) = full_specs(
         body,
         [whole],
-        [out, *level, *k, fields, rim_a, rim_b, xa, xb, tmat, rmat],
+        [out, *level, *k, fields, xa, xb, rim_a, rim_b, tmat, rmat],
         [halo, rim, pltpu.SemaphoreType.DMA((2,))],
         name="final_rim",
         in_specs=[ANY] + [VM] * 13,

time: 72.7 us -> 68.5 us (0.942)
  waiting for transfers between devices: 19.6 us -> 16.1 us
  starting transfers between devices: 35.6 us -> 34.8 us
    ppermute x13, waiting for transfers between devices: 15.9 us -> 12.6 us  [swap(): lax.ppermute(to_b, axis, pairs_b)]
    ppermute x13, starting transfers between devices: 32.6 us -> 31.3 us  [swap(): lax.ppermute(to_b, axis, pairs_b)]
  transfers between devices with their start and end apart: 26 -> 26, of which waited for: 9 -> 9; matrix products, arithmetic and copies ran while one was open for 0% -> 0% of each run, Pallas kernels for 14% -> 16%
where the time goes in v8:
time: 68.5 us; the launch traced here: 68.3 us
  starting transfers between devices  34.8 us (51%)
  waiting for transfers between devices  16.1 us (24%)
  Pallas kernels  13.3 us (19%)
  local copies, waits for them, and re-layouts  2.67 us (4%)
  other arithmetic  1.05 us (2%)
    ppermute x13, starting transfers between devices, swap(): lax.ppermute(to_b, axis, pairs_b)  31.3 us
    pallas_call x13, Pallas kernels, full_specs(): pl.pallas_call(run, out_shape=[jax.ShapeDtypeStruct(s, d) for s, d in out...  13.3 us
    ppermute x13, waiting for transfers between devices, swap(): lax.ppermute(to_b, axis, pairs_b)  12.6 us
    ppermute x13, starting transfers between devices, swap(): lax.ppermute(to_a, axis, pairs_a)  3.51 us
    ppermute x13, waiting for transfers between devices, swap(): lax.ppermute(to_a, axis, pairs_a)  3.48 us
    unnamed x18, local copies, waits for them, and re-layouts  2.67 us
  transfers between devices with their start and end apart: 26, of which 9 were waited for; matrix products, arithmetic and copies ran while one was open for 0% of the time, Pallas kernels for 16%

profile of v8, /device:TPU:0, one launch (start us, length us, event | category | flops | bytes accessed | tf_op | source)
XLA Modules:
  0.0 68.3 jit_solution(1593802285119548250)
XLA Ops:
  0.0 1.0 %slice_select_fusion = (f32[4,16,512]{2,1,0:T(8,128)S(1)}, f32[4,16,512]{2,1,0:T(8,128)S(1)}) fusion(f32[16,16,512]{2,1,0:T(8,128)} %refs_0_.4, pred[]{:T(512)S(6)} %eq.3), kind=kLoop, calls=%fused_computation | loop fusion | flops 65536 | bytes 524289 | tf_op jit(solution)/shard_map/jit(_where)/select_n | solution.py:562
  1.1 3.2 %collective-permute-start.1 = (f32[4,16,512]{2,1,0:T(8,128)S(1)}, f32[4,16,512]{2,1,0:T(8,128)S(1)}, u32[]{:S(2)}, u32[]{:S(2)}) collective-permute-start(f32[4,16,512]{2,1,0:T(8,128)S(1)} %get-tuple-element.87), channel_id=1, source_target_pairs={{0,96},{32,64},{64,32},{96,0},{1,97},{33,65},{65,33},{97,1},{2,98}... | collective-permute-start | bytes 393224 | tf_op jit(solution)/shard_map/ppermute | solution.py:100
  4.2 0.1 collective-permute-start
  4.4 1.7 %copy-done = f32[5,32,16,256]{3,2,1,0:T(8,128)S(1)} copy-done((f32[5,32,16,256]{3,2,1,0:T(8,128)S(1)}, f32[5,32,16,256]{3,2,1,0:T(8,128)}, u32[]{:S(2)}) %copy-start) | copy-done | bytes 2621464
  6.1 0.1 edges.1
  6.3 0.9 %copy-done.6 = s32[16,16,512]{2,1,0:T(8,128)S(1)} copy-done((s32[16,16,512]{2,1,0:T(8,128)S(1)}, s32[16,16,512]{2,1,0:T(8,128)}, u32[]{:S(2)}) %copy-start.6) | copy-done | bytes 524312
  7.2 0.5 filter_inner.1
  7.6 0.1 collective-permute-done.1.refs_3_
  7.7 1.5 %collective-permute-done.refs_2_ = f32[4,16,512]{2,1,0:T(8,128)S(1)} collective-permute-done((f32[4,16,512]{2,1,0:T(8,128)S(1)}, f32[4,16,512]{2,1,0:T(8,128)S(1)}, u32[]{:S(2)}, u32[]{:S(2)}) %collective-permute-start) | collective-permute-done | bytes 131104 | tf_op jit(solution)/shard_map/ppermute | solution.py:100
  9.2 0.2 filter_axial.1
  9.4 0.1 collective-permute-start.2
  9.5 6.3 %collective-permute-start.3 = (f32[40,8,256]{2,1,0:T(8,128)S(1)}, f32[40,8,256]{2,1,0:T(8,128)S(1)}, u32[]{:S(2)}, u32[]{:S(2)}) collective-permute-start(f32[40,8,256]{2,1,0:T(8,128)S(1)} %get-tuple-element.51), channel_id=1, source_target_pairs={{0,31},{1,2},{2,1},{3,4},{4,3},{5,6},{6,5},{7,8},{8,7},{9,10},{10,... | collective-permute-start | bytes 983048 | tf_op jit(solution)/shard_map/ppermute | solution.py:100
  15.8 0.4 collective-permute-start.4
  16.2 1.1 %collective-permute-start.5 = (f32[15,16,256]{2,1,0:T(8,128)S(1)}, f32[15,16,256]{2,1,0:T(8,128)S(1)}, u32[]{:S(2)}, u32[]{:S(2)}) collective-permute-start(f32[15,16,256]{2,1,0:T(8,128)S(1)} %get-tuple-element.53), channel_id=1, source_target_pairs={{0,96},{32,64},{64,32},{96,0},{1,97},{33,65},{65,33},{97,1},{2,98}... | collective-permute-start | bytes 737288 | tf_op jit(solution)/shard_map/ppermute | solution.py:100
  17.3 0.3 route.1
  17.6 0.0 collective-permute-done.2.refs_2_.refs_1_
  17.6 2.9 %collective-permute-done.3.refs_3_.refs_2_ = f32[40,8,256]{2,1,0:T(8,128)S(1)} collective-permute-done((f32[40,8,256]{2,1,0:T(8,128)S(1)}, f32[40,8,256]{2,1,0:T(8,128)S(1)}, u32[]{:S(2)}, u32[]{:S(2)}) %collective-permute-start.3) | collective-permute-done | bytes 327712 | tf_op jit(solution)/shard_map/ppermute | solution.py:100
  20.6 2.3 %filter_rest.1 = (f32[256,256]{1,0:T(8,128)S(1)}, f32[17,8,256]{2,1,0:T(8,128)S(1)}, f32[17,8,256]{2,1,0:T(8,128)S(1)}, f32[18,8,256]{2,1,0:T(8,128)S(1)}, f32[18,8,256]{2,1,0:T(8,128)S(1)}) custom-call(f32[16,16,512]{2,1,0:T(8,128)S(1)} %get-tuple-element.54.refs_2_.refs_0_, s32[16,16,512]{2,1,0:T(8,128)S(1)} %get-tuple-element.48.refs_1_, ...), custom_call_target="tpu_custom_call" | custom-call | tf_op jit(solution)/shard_map/filter_rest/pallas_call | solution.py:109
  22.9 0.1 collective-permute-start.8
  23.0 5.1 %collective-permute-start.9 = (f32[18,8,256]{2,1,0:T(8,128)S(1)}, f32[18,8,256]{2,1,0:T(8,128)S(1)}, u32[]{:S(2)}, u32[]{:S(2)}) collective-permute-start(f32[18,8,256]{2,1,0:T(8,128)S(1)} %get-tuple-element.64), channel_id=1, source_target_pairs={{0,31},{1,2},{2,1},{3,4},{4,3},{5,6},{6,5},{7,8},{8,7},{9,10},{10,... | collective-permute-start | bytes 442376 | tf_op jit(solution)/shard_map/ppermute | solution.py:100
  28.2 0.4 collective-permute-start.6
  28.5 0.0 collective-permute-done.4.refs_3_
  28.5 1.1 %collective-permute-start.7 = (f32[17,8,256]{2,1,0:T(8,128)S(1)}, f32[17,8,256]{2,1,0:T(8,128)S(1)}, u32[]{:S(2)}, u32[]{:S(2)}) collective-permute-start(f32[17,8,256]{2,1,0:T(8,128)S(1)} %get-tuple-element.62), channel_id=1, source_target_pairs={{0,96},{32,64},{64,32},{96,0},{1,97},{33,65},{65,33},{97,1},{2,98}... | collective-permute-start | bytes 417800 | tf_op jit(solution)/shard_map/ppermute | solution.py:100
  29.7 0.0 collective-permute-done.5.refs_4_
  29.7 1.6 %operator.1 = (f32[5,24,16,256]{3,2,1,0:T(8,128)S(1)}, f32[5,8,16,256]{3,2,1,0:T(8,128)S(1)}) custom-call(f32[5,32,16,256]{3,2,1,0:T(8,128)S(1)} %copy-done.1, f32[40,8,256]{2,1,0:T(8,128)S(1)} %collective-permute-done.2.refs_2_.refs_1_, f32[40,8,256]{2,1,0:T(8,128)S(1)} %collective-permute-done.3.refs_3_.refs_2_, ...), custom_call_target="tpu_custom_call" | custom-call | tf_op jit(solution)/shard_map/operator/pallas_call | solution.py:109
  31.2 2.0 %collective-permute-done.6.refs_2_ = f32[17,8,256]{2,1,0:T(8,128)S(1)} collective-permute-done((f32[17,8,256]{2,1,0:T(8,128)S(1)}, f32[17,8,256]{2,1,0:T(8,128)S(1)}, u32[]{:S(2)}, u32[]{:S(2)}) %collective-permute-start.6) | collective-permute-done | bytes 139296 | tf_op jit(solution)/shard_map/ppermute | solution.py:100
  33.2 1.6 %collective-permute-done.7.refs_3_ = f32[17,8,256]{2,1,0:T(8,128)S(1)} collective-permute-done((f32[17,8,256]{2,1,0:T(8,128)S(1)}, f32[17,8,256]{2,1,0:T(8,128)S(1)}, u32[]{:S(2)}, u32[]{:S(2)}) %collective-permute-start.7) | collective-permute-done | bytes 139296 | tf_op jit(solution)/shard_map/ppermute | solution.py:100
  34.8 0.0 collective-permute-done.8.refs_4_
  34.8 0.0 collective-permute-done.9.refs_5_
  34.8 0.6 gather.1
  35.4 0.1 collective-permute-start.10
  35.5 1.3 %collective-permute-start.11 = (f32[24,8,256]{2,1,0:T(8,128)S(1)}, f32[24,8,256]{2,1,0:T(8,128)S(1)}, u32[]{:S(2)}, u32[]{:S(2)}) collective-permute-start(f32[24,8,256]{2,1,0:T(8,128)S(1)} %get-tuple-element.68), channel_id=1, source_target_pairs={{0,31},{1,2},{2,1},{3,4},{4,3},{5,6},{6,5},{7,8},{8,7},{9,10},{10,... | collective-permute-start | bytes 589832 | tf_op jit(solution)/shard_map/ppermute | solution.py:100
  36.8 0.4 collective-permute-start.12
  37.2 1.1 %collective-permute-start.13 = (f32[15,16,256]{2,1,0:T(8,128)S(1)}, f32[15,16,256]{2,1,0:T(8,128)S(1)}, u32[]{:S(2)}, u32[]{:S(2)}) collective-permute-start(f32[15,16,256]{2,1,0:T(8,128)S(1)} %get-tuple-element.71), channel_id=1, source_target_pairs={{0,96},{32,64},{64,32},{96,0},{1,97},{33,65},{65,33},{97,1},{2,98}... | collective-permute-start | bytes 737288 | tf_op jit(solution)/shard_map/ppermute | solution.py:100
  38.3 0.0 collective-permute-done.10.refs_8_.refs_10_
  38.3 5.7 %collective-permute-done.11.refs_9_.refs_11_ = f32[24,8,256]{2,1,0:T(8,128)S(1)} collective-permute-done((f32[24,8,256]{2,1,0:T(8,128)S(1)}, f32[24,8,256]{2,1,0:T(8,128)S(1)}, u32[]{:S(2)}, u32[]{:S(2)}) %collective-permute-start.11) | collective-permute-done | bytes 196640 | tf_op jit(solution)/shard_map/ppermute | solution.py:100
  44.0 1.4 %stage_inner.2 = (f32[5,24,16,256]{3,2,1,0:T(8,128)S(1)}, f32[18,8,256]{2,1,0:T(8,128)S(1)}, f32[18,8,256]{2,1,0:T(8,128)S(1)}) custom-call(f32[5,24,16,256]{3,2,1,0:T(8,128)S(1)} %get-tuple-element.58.refs_6_.refs_0_.refs_4_.refs_2_.refs_3_, f32[5,8,16,256]{3,2,1,0:T(8,128)S(1)} %get-tuple-element.59.refs_7_.refs_1_.refs_5_.refs_3_.refs_4_, ...), custom_call_target="tpu_custom_call" | custom-call | flops 137438953472 | tf_op jit(solution)/shard_map/stage_inner/pallas_call | solution.py:109
  45.4 0.1 collective-permute-start.14
  45.5 1.3 %collective-permute-start.15 = (f32[18,8,256]{2,1,0:T(8,128)S(1)}, f32[18,8,256]{2,1,0:T(8,128)S(1)}, u32[]{:S(2)}, u32[]{:S(2)}) collective-permute-start(f32[18,8,256]{2,1,0:T(8,128)S(1)} %get-tuple-element.74), channel_id=1, source_target_pairs={{0,31},{1,2},{2,1},{3,4},{4,3},{5,6},{6,5},{7,8},{8,7},{9,10},{10,... | collective-permute-start | bytes 442376 | tf_op jit(solution)/shard_map/ppermute | solution.py:100
  46.8 0.0 collective-permute-done.12.refs_8_
  46.8 0.0 collective-permute-done.13.refs_9_
  46.8 0.6 stage_rim.2
  47.4 0.6 collective-permute-start.16
  48.0 1.2 %collective-permute-start.17 = (f32[15,16,256]{2,1,0:T(8,128)S(1)}, f32[15,16,256]{2,1,0:T(8,128)S(1)}, u32[]{:S(2)}, u32[]{:S(2)}) collective-permute-start(f32[15,16,256]{2,1,0:T(8,128)S(1)} %get-tuple-element.77), channel_id=1, source_target_pairs={{0,96},{32,64},{64,32},{96,0},{1,97},{33,65},{65,33},{97,1},{2,98}... | collective-permute-start | bytes 737288 | tf_op jit(solution)/shard_map/ppermute | solution.py:100
  49.2 0.0 collective-permute-start.18
  49.2 0.0 collective-permute-done.14.refs_6_
  49.2 3.6 %collective-permute-start.19 = (f32[6,8,256]{2,1,0:T(8,128)S(1)}, f32[6,8,256]{2,1,0:T(8,128)S(1)}, u32[]{:S(2)}, u32[]{:S(2)}) collective-permute-start(f32[6,8,256]{2,1,0:T(8,128)S(1)} %get-tuple-element.79), channel_id=1, source_target_pairs={{0,31},{1,2},{2,1},{3,4},{4,3},{5,6},{6,5},{7,8},{8,7},{9,10},{10,... | collective-permute-start | bytes 147464 | tf_op jit(solution)/shard_map/ppermute | solution.py:100
  52.9 0.6 collective-permute-done.15.refs_7_
  53.4 1.4 %stage_inner.3 = (f32[5,24,16,256]{3,2,1,0:T(8,128)S(1)}, f32[18,8,256]{2,1,0:T(8,128)S(1)}, f32[18,8,256]{2,1,0:T(8,128)S(1)}) custom-call(f32[5,24,16,256]{3,2,1,0:T(8,128)S(1)} %get-tuple-element.69.refs_14_.refs_0_, f32[5,8,16,256]{3,2,1,0:T(8,128)S(1)} %get-tuple-element.72.refs_1_, ...), custom_call_target="tpu_custom_call" | custom-call | flops 2000000000 | tf_op jit(solution)/shard_map/stage_inner/pallas_call | solution.py:109
  54.8 0.1 collective-permute-start.20
  54.9 0.0 collective-permute-done.18.refs_8_
  54.9 1.3 %collective-permute-start.21 = (f32[18,8,256]{2,1,0:T(8,128)S(1)}, f32[18,8,256]{2,1,0:T(8,128)S(1)}, u32[]{:S(2)}, u32[]{:S(2)}) collective-permute-start(f32[18,8,256]{2,1,0:T(8,128)S(1)} %get-tuple-element.82), channel_id=1, source_target_pairs={{0,31},{1,2},{2,1},{3,4},{4,3},{5,6},{6,5},{7,8},{8,7},{9,10},{10,... | collective-permute-start | bytes 442376 | tf_op jit(solution)/shard_map/ppermute | solution.py:100
  56.2 0.0 collective-permute-done.19.refs_9_
  56.2 0.0 collective-permute-done.16.refs_6_
  56.2 0.0 copy-start.2
  56.3 0.6 stage_rim.3
  56.8 1.2 %collective-permute-start.22 = (f32[15,16,256]{2,1,0:T(8,128)S(1)}, f32[15,16,256]{2,1,0:T(8,128)S(1)}, u32[]{:S(2)}, u32[]{:S(2)}) collective-permute-start(f32[15,16,256]{2,1,0:T(8,128)S(1)} %get-tuple-element.83), channel_id=1, source_target_pairs={{0,32},{32,0},{64,96},{96,64},{1,33},{33,1},{65,97},{97,65},{2,34}... | collective-permute-start | bytes 737288 | tf_op jit(solution)/shard_map/ppermute | solution.py:100
  58.1 1.8 %collective-permute-start.23 = (f32[15,16,256]{2,1,0:T(8,128)S(1)}, f32[15,16,256]{2,1,0:T(8,128)S(1)}, u32[]{:S(2)}, u32[]{:S(2)}) collective-permute-start(f32[15,16,256]{2,1,0:T(8,128)S(1)} %get-tuple-element.84), channel_id=1, source_target_pairs={{0,96},{32,64},{64,32},{96,0},{1,97},{33,65},{65,33},{97,1},{2,98}... | collective-permute-start | bytes 737288 | tf_op jit(solution)/shard_map/ppermute | solution.py:100
  59.8 2.7 %collective-permute-start.25 = (f32[6,8,256]{2,1,0:T(8,128)S(1)}, f32[6,8,256]{2,1,0:T(8,128)S(1)}, u32[]{:S(2)}, u32[]{:S(2)}) collective-permute-start(f32[6,8,256]{2,1,0:T(8,128)S(1)} %get-tuple-element.86), channel_id=1, source_target_pairs={{0,31},{1,2},{2,1},{3,4},{4,3},{5,6},{6,5},{7,8},{8,7},{9,10},{10,... | collective-permute-start | bytes 147464 | tf_op jit(solution)/shard_map/ppermute | solution.py:100
  62.5 0.3 collective-permute-done.21.refs_8_
  62.9 2.3 %final_inner.1.refs_0_ = f32[5,32,16,256]{3,2,1,0:T(8,128)} custom-call(f32[5,24,16,256]{3,2,1,0:T(8,128)S(1)} %get-tuple-element.75.refs_12_.refs_0_.refs_1_, f32[5,8,16,256]{3,2,1,0:T(8,128)S(1)} %get-tuple-element.80.refs_1_.refs_2_, f32[5,24,16,256]{3,2,1,0:T(8,128)S(1)} %get-tuple-element.58.refs_6_.refs_0_.refs_4_.refs_2_.refs_3_, ...), custom_call_target="tpu_custom_call" | custom-call | flops 2000000000 | tf_op jit(solution)/shard_map/final_inner/pallas_call | solution.py:109
  65.2 0.0 collective-permute-done.24.refs_10_
  65.2 1.5 %collective-permute-done.25.refs_11_ = f32[6,8,256]{2,1,0:T(8,128)S(1)} collective-permute-done((f32[6,8,256]{2,1,0:T(8,128)S(1)}, f32[6,8,256]{2,1,0:T(8,128)S(1)}, u32[]{:S(2)}, u32[]{:S(2)}) %collective-permute-start.25) | collective-permute-done | bytes 49184 | tf_op jit(solution)/shard_map/ppermute | solution.py:100
  66.7 1.4 %final_rim.1 = f32[5,32,16,256]{3,2,1,0:T(8,128)} custom-call(f32[5,32,16,256]{3,2,1,0:T(8,128)} %final_inner.1.refs_0_, f32[5,24,16,256]{3,2,1,0:T(8,128)S(1)} %get-tuple-element.75.refs_12_.refs_0_.refs_1_, f32[5,8,16,256]{3,2,1,0:T(8,128)S(1)} %get-tuple-element.80.refs_1_.refs_2_, ...), custom_call_target="tpu_custom_call", output_to_operand_aliasing={{}: (0, {})} | custom-call | tf_op jit(solution)/shard_map/final_rim/pallas_call | solution.py:109
  (20 shorter events, 0.0 us)
Async XLA Ops:
  0.0 6.2 %copy-start.5 = (f32[16,16,512]{2,1,0:T(8,128)S(1)}, f32[16,16,512]{2,1,0:T(8,128)}, u32[]{:S(2)}) copy-start(f32[16,16,512]{2,1,0:T(8,128)} %refs_0_.4) | copy-start | bytes 1572868
  1.1 6.7 %collective-permute-start.1 = (f32[4,16,512]{2,1,0:T(8,128)S(1)}, f32[4,16,512]{2,1,0:T(8,128)S(1)}, u32[]{:S(2)}, u32[]{:S(2)}) collective-permute-start(f32[4,16,512]{2,1,0:T(8,128)S(1)} %get-tuple-element.87), channel_id=1, source_target_pairs={{0,96},{32,64},{64,32},{96,0},{1,97},{33,65},{65,33},{97,1},{2,98}... | collective-permute-start | bytes 393224 | tf_op jit(solution)/shard_map/ppermute | solution.py:100
  4.2 5.0 %collective-permute-start = (f32[4,16,512]{2,1,0:T(8,128)S(1)}, f32[4,16,512]{2,1,0:T(8,128)S(1)}, u32[]{:S(2)}, u32[]{:S(2)}) collective-permute-start(f32[4,16,512]{2,1,0:T(8,128)S(1)} %get-tuple-element.88.refs_1_), channel_id=1, source_target_pairs={{0,32},{32,0},{64,96},{96,64},{1,33},{33,1},{65,97},{97,65},{2,34}... | collective-permute-start | bytes 393224 | tf_op jit(solution)/shard_map/ppermute | solution.py:100
  4.4 1.7 %copy-start = (f32[5,32,16,256]{3,2,1,0:T(8,128)S(1)}, f32[5,32,16,256]{3,2,1,0:T(8,128)}, u32[]{:S(2)}) copy-start(f32[5,32,16,256]{3,2,1,0:T(8,128)} %refs_7_.1) | copy-start | bytes 7864324
  6.1 1.0 %copy-start.6 = (s32[16,16,512]{2,1,0:T(8,128)S(1)}, s32[16,16,512]{2,1,0:T(8,128)}, u32[]{:S(2)}) copy-start(s32[16,16,512]{2,1,0:T(8,128)} %refs_1_.1) | copy-start | bytes 1572868
  6.1 11.2 %copy-start.7 = (s32[256]{0:T(256)S(1)}, s32[256]{0:T(256)}, u32[]{:S(2)}) copy-start(s32[256]{0:T(256)} %param.9) | copy-start | bytes 3076
  6.1 11.2 %copy-start.8 = (s32[256]{0:T(256)S(1)}, s32[256]{0:T(256)}, u32[]{:S(2)}) copy-start(s32[256]{0:T(256)} %param.10) | copy-start | bytes 3076
  7.2 22.5 %copy-start.1 = (f32[5,32,16,256]{3,2,1,0:T(8,128)S(1)}, f32[5,32,16,256]{3,2,1,0:T(8,128)}, u32[]{:S(2)}) copy-start(f32[5,32,16,256]{3,2,1,0:T(8,128)} %refs_7_.1) | copy-start | bytes 7864324
  7.2 22.5 %copy-start.3 = (bf16[2,2,256,256]{3,2,1,0:T(8,128)(2,1)S(1)}, bf16[2,2,256,256]{3,2,1,0:T(8,128)(2,1)}, u32[]{:S(2)}) copy-start(bf16[2,2,256,256]{3,2,1,0:T(8,128)(2,1)} %constant.17.clone.refs_6_.refs_11_.refs_13_.refs_9_.refs_10_) | copy-start | bytes 1572868
  7.2 22.5 %copy-start.4 = (bf16[2,2,128,224]{3,2,1,0:T(8,128)(2,1)S(1)}, bf16[2,2,128,224]{3,2,1,0:T(8,128)(2,1)}, u32[]{:S(2)}) copy-start(bf16[2,2,128,224]{3,2,1,0:T(8,128)(2,1)} %constant.16.clone.refs_5_.refs_10_.refs_12_.refs_8_.refs_9_) | copy-start | bytes 688132
  9.4 8.2 %collective-permute-start.2 = (f32[40,8,256]{2,1,0:T(8,128)S(1)}, f32[40,8,256]{2,1,0:T(8,128)S(1)}, u32[]{:S(2)}, u32[]{:S(2)}) collective-permute-start(f32[40,8,256]{2,1,0:T(8,128)S(1)} %get-tuple-element.50), channel_id=1, source_target_pairs={{0,1},{1,0},{2,3},{3,2},{4,5},{5,4},{6,7},{7,6},{8,9},{9,8},{10,11... | collective-permute-start | bytes 983048 | tf_op jit(solution)/shard_map/ppermute | solution.py:100
  9.5 11.1 %collective-permute-start.3 = (f32[40,8,256]{2,1,0:T(8,128)S(1)}, f32[40,8,256]{2,1,0:T(8,128)S(1)}, u32[]{:S(2)}, u32[]{:S(2)}) collective-permute-start(f32[40,8,256]{2,1,0:T(8,128)S(1)} %get-tuple-element.51), channel_id=1, source_target_pairs={{0,31},{1,2},{2,1},{3,4},{4,3},{5,6},{6,5},{7,8},{8,7},{9,10},{10,... | collective-permute-start | bytes 983048 | tf_op jit(solution)/shard_map/ppermute | solution.py:100
  15.8 12.7 %collective-permute-start.4 = (f32[15,16,256]{2,1,0:T(8,128)S(1)}, f32[15,16,256]{2,1,0:T(8,128)S(1)}, u32[]{:S(2)}, u32[]{:S(2)}) collective-permute-start(f32[15,16,256]{2,1,0:T(8,128)S(1)} %get-tuple-element.52), channel_id=1, source_target_pairs={{0,32},{32,0},{64,96},{96,64},{1,33},{33,1},{65,97},{97,65},{2,34}... | collective-permute-start | bytes 737288 | tf_op jit(solution)/shard_map/ppermute | solution.py:100
  16.2 13.5 %collective-permute-start.5 = (f32[15,16,256]{2,1,0:T(8,128)S(1)}, f32[15,16,256]{2,1,0:T(8,128)S(1)}, u32[]{:S(2)}, u32[]{:S(2)}) collective-permute-start(f32[15,16,256]{2,1,0:T(8,128)S(1)} %get-tuple-element.53), channel_id=1, source_target_pairs={{0,96},{32,64},{64,32},{96,0},{1,97},{33,65},{65,33},{97,1},{2,98}... | collective-permute-start | bytes 737288 | tf_op jit(solution)/shard_map/ppermute | solution.py:100
  22.9 11.9 %collective-permute-start.8 = (f32[18,8,256]{2,1,0:T(8,128)S(1)}, f32[18,8,256]{2,1,0:T(8,128)S(1)}, u32[]{:S(2)}, u32[]{:S(2)}) collective-permute-start(f32[18,8,256]{2,1,0:T(8,128)S(1)} %get-tuple-element.63), channel_id=1, source_target_pairs={{0,1},{1,0},{2,3},{3,2},{4,5},{5,4},{6,7},{7,6},{8,9},{9,8},{10,11... | collective-permute-start | bytes 442376 | tf_op jit(solution)/shard_map/ppermute | solution.py:100
  23.0 11.8 %collective-permute-start.9 = (f32[18,8,256]{2,1,0:T(8,128)S(1)}, f32[18,8,256]{2,1,0:T(8,128)S(1)}, u32[]{:S(2)}, u32[]{:S(2)}) collective-permute-start(f32[18,8,256]{2,1,0:T(8,128)S(1)} %get-tuple-element.64), channel_id=1, source_target_pairs={{0,31},{1,2},{2,1},{3,4},{4,3},{5,6},{6,5},{7,8},{8,7},{9,10},{10,... | collective-permute-start | bytes 442376 | tf_op jit(solution)/shard_map/ppermute | solution.py:100
  28.2 5.1 %collective-permute-start.6 = (f32[17,8,256]{2,1,0:T(8,128)S(1)}, f32[17,8,256]{2,1,0:T(8,128)S(1)}, u32[]{:S(2)}, u32[]{:S(2)}) collective-permute-start(f32[17,8,256]{2,1,0:T(8,128)S(1)} %get-tuple-element.61), channel_id=1, source_target_pairs={{0,32},{32,0},{64,96},{96,64},{1,33},{33,1},{65,97},{97,65},{2,34}... | collective-permute-start | bytes 417800 | tf_op jit(solution)/shard_map/ppermute | solution.py:100
  28.5 6.3 %collective-permute-start.7 = (f32[17,8,256]{2,1,0:T(8,128)S(1)}, f32[17,8,256]{2,1,0:T(8,128)S(1)}, u32[]{:S(2)}, u32[]{:S(2)}) collective-permute-start(f32[17,8,256]{2,1,0:T(8,128)S(1)} %get-tuple-element.62), channel_id=1, source_target_pairs={{0,96},{32,64},{64,32},{96,0},{1,97},{33,65},{65,33},{97,1},{2,98}... | collective-permute-start | bytes 417800 | tf_op jit(solution)/shard_map/ppermute | solution.py:100
  35.4 2.9 %collective-permute-start.10 = (f32[24,8,256]{2,1,0:T(8,128)S(1)}, f32[24,8,256]{2,1,0:T(8,128)S(1)}, u32[]{:S(2)}, u32[]{:S(2)}) collective-permute-start(f32[24,8,256]{2,1,0:T(8,128)S(1)} %get-tuple-element.67), channel_id=1, source_target_pairs={{0,1},{1,0},{2,3},{3,2},{4,5},{5,4},{6,7},{7,6},{8,9},{9,8},{10,11... | collective-permute-start | bytes 589832 | tf_op jit(solution)/shard_map/ppermute | solution.py:100
  35.5 8.5 %collective-permute-start.11 = (f32[24,8,256]{2,1,0:T(8,128)S(1)}, f32[24,8,256]{2,1,0:T(8,128)S(1)}, u32[]{:S(2)}, u32[]{:S(2)}) collective-permute-start(f32[24,8,256]{2,1,0:T(8,128)S(1)} %get-tuple-element.68), channel_id=1, source_target_pairs={{0,31},{1,2},{2,1},{3,4},{4,3},{5,6},{6,5},{7,8},{8,7},{9,10},{10,... | collective-permute-start | bytes 589832 | tf_op jit(solution)/shard_map/ppermute | solution.py:100
  36.8 10.0 %collective-permute-start.12 = (f32[15,16,256]{2,1,0:T(8,128)S(1)}, f32[15,16,256]{2,1,0:T(8,128)S(1)}, u32[]{:S(2)}, u32[]{:S(2)}) collective-permute-start(f32[15,16,256]{2,1,0:T(8,128)S(1)} %get-tuple-element.70), channel_id=1, source_target_pairs={{0,32},{32,0},{64,96},{96,64},{1,33},{33,1},{65,97},{97,65},{2,34}... | collective-permute-start | bytes 737288 | tf_op jit(solution)/shard_map/ppermute | solution.py:100
  37.2 9.6 %collective-permute-start.13 = (f32[15,16,256]{2,1,0:T(8,128)S(1)}, f32[15,16,256]{2,1,0:T(8,128)S(1)}, u32[]{:S(2)}, u32[]{:S(2)}) collective-permute-start(f32[15,16,256]{2,1,0:T(8,128)S(1)} %get-tuple-element.71), channel_id=1, source_target_pairs={{0,96},{32,64},{64,32},{96,0},{1,97},{33,65},{65,33},{97,1},{2,98}... | collective-permute-start | bytes 737288 | tf_op jit(solution)/shard_map/ppermute | solution.py:100
  45.4 3.9 %collective-permute-start.14 = (f32[18,8,256]{2,1,0:T(8,128)S(1)}, f32[18,8,256]{2,1,0:T(8,128)S(1)}, u32[]{:S(2)}, u32[]{:S(2)}) collective-permute-start(f32[18,8,256]{2,1,0:T(8,128)S(1)} %get-tuple-element.73), channel_id=1, source_target_pairs={{0,1},{1,0},{2,3},{3,2},{4,5},{5,4},{6,7},{7,6},{8,9},{9,8},{10,11... | collective-permute-start | bytes 442376 | tf_op jit(solution)/shard_map/ppermute | solution.py:100
  45.5 8.0 %collective-permute-start.15 = (f32[18,8,256]{2,1,0:T(8,128)S(1)}, f32[18,8,256]{2,1,0:T(8,128)S(1)}, u32[]{:S(2)}, u32[]{:S(2)}) collective-permute-start(f32[18,8,256]{2,1,0:T(8,128)S(1)} %get-tuple-element.74), channel_id=1, source_target_pairs={{0,31},{1,2},{2,1},{3,4},{4,3},{5,6},{6,5},{7,8},{8,7},{9,10},{10,... | collective-permute-start | bytes 442376 | tf_op jit(solution)/shard_map/ppermute | solution.py:100
  47.4 8.8 %collective-permute-start.16 = (f32[15,16,256]{2,1,0:T(8,128)S(1)}, f32[15,16,256]{2,1,0:T(8,128)S(1)}, u32[]{:S(2)}, u32[]{:S(2)}) collective-permute-start(f32[15,16,256]{2,1,0:T(8,128)S(1)} %get-tuple-element.76), channel_id=1, source_target_pairs={{0,32},{32,0},{64,96},{96,64},{1,33},{33,1},{65,97},{97,65},{2,34}... | collective-permute-start | bytes 737288 | tf_op jit(solution)/shard_map/ppermute | solution.py:100
  48.0 8.2 %collective-permute-start.17 = (f32[15,16,256]{2,1,0:T(8,128)S(1)}, f32[15,16,256]{2,1,0:T(8,128)S(1)}, u32[]{:S(2)}, u32[]{:S(2)}) collective-permute-start(f32[15,16,256]{2,1,0:T(8,128)S(1)} %get-tuple-element.77), channel_id=1, source_target_pairs={{0,96},{32,64},{64,32},{96,0},{1,97},{33,65},{65,33},{97,1},{2,98}... | collective-permute-start | bytes 737288 | tf_op jit(solution)/shard_map/ppermute | solution.py:100
  49.2 5.7 %collective-permute-start.18 = (f32[6,8,256]{2,1,0:T(8,128)S(1)}, f32[6,8,256]{2,1,0:T(8,128)S(1)}, u32[]{:S(2)}, u32[]{:S(2)}) collective-permute-start(f32[6,8,256]{2,1,0:T(8,128)S(1)} %get-tuple-element.78), channel_id=1, source_target_pairs={{0,1},{1,0},{2,3},{3,2},{4,5},{5,4},{6,7},{7,6},{8,9},{9,8},{10,11... | collective-permute-start | bytes 147464 | tf_op jit(solution)/shard_map/ppermute | solution.py:100
  49.2 7.0 %collective-permute-start.19 = (f32[6,8,256]{2,1,0:T(8,128)S(1)}, f32[6,8,256]{2,1,0:T(8,128)S(1)}, u32[]{:S(2)}, u32[]{:S(2)}) collective-permute-start(f32[6,8,256]{2,1,0:T(8,128)S(1)} %get-tuple-element.79), channel_id=1, source_target_pairs={{0,31},{1,2},{2,1},{3,4},{4,3},{5,6},{6,5},{7,8},{8,7},{9,10},{10,... | collective-permute-start | bytes 147464 | tf_op jit(solution)/shard_map/ppermute | solution.py:100
  54.8 5.0 %collective-permute-start.20 = (f32[18,8,256]{2,1,0:T(8,128)S(1)}, f32[18,8,256]{2,1,0:T(8,128)S(1)}, u32[]{:S(2)}, u32[]{:S(2)}) collective-permute-start(f32[18,8,256]{2,1,0:T(8,128)S(1)} %get-tuple-element.81), channel_id=1, source_target_pairs={{0,1},{1,0},{2,3},{3,2},{4,5},{5,4},{6,7},{7,6},{8,9},{9,8},{10,11... | collective-permute-start | bytes 442376 | tf_op jit(solution)/shard_map/ppermute | solution.py:100
  54.9 8.0 %collective-permute-start.21 = (f32[18,8,256]{2,1,0:T(8,128)S(1)}, f32[18,8,256]{2,1,0:T(8,128)S(1)}, u32[]{:S(2)}, u32[]{:S(2)}) collective-permute-start(f32[18,8,256]{2,1,0:T(8,128)S(1)} %get-tuple-element.82), channel_id=1, source_target_pairs={{0,31},{1,2},{2,1},{3,4},{4,3},{5,6},{6,5},{7,8},{8,7},{9,10},{10,... | collective-permute-start | bytes 442376 | tf_op jit(solution)/shard_map/ppermute | solution.py:100
  56.2 6.6 %copy-start.2 = (f32[5,32,16,256]{3,2,1,0:T(8,128)S(1)}, f32[5,32,16,256]{3,2,1,0:T(8,128)}, u32[]{:S(2)}) copy-start(f32[5,32,16,256]{3,2,1,0:T(8,128)} %refs_7_.1) | copy-start | bytes 7864324
  56.8 9.8 %collective-permute-start.22 = (f32[15,16,256]{2,1,0:T(8,128)S(1)}, f32[15,16,256]{2,1,0:T(8,128)S(1)}, u32[]{:S(2)}, u32[]{:S(2)}) collective-permute-start(f32[15,16,256]{2,1,0:T(8,128)S(1)} %get-tuple-element.83), channel_id=1, source_target_pairs={{0,32},{32,0},{64,96},{96,64},{1,33},{33,1},{65,97},{97,65},{2,34}... | collective-permute-start | bytes 737288 | tf_op jit(solution)/shard_map/ppermute | solution.py:100
  58.1 8.6 %collective-permute-start.23 = (f32[15,16,256]{2,1,0:T(8,128)S(1)}, f32[15,16,256]{2,1,0:T(8,128)S(1)}, u32[]{:S(2)}, u32[]{:S(2)}) collective-permute-start(f32[15,16,256]{2,1,0:T(8,128)S(1)} %get-tuple-element.84), channel_id=1, source_target_pairs={{0,96},{32,64},{64,32},{96,0},{1,97},{33,65},{65,33},{97,1},{2,98}... | collective-permute-start | bytes 737288 | tf_op jit(solution)/shard_map/ppermute | solution.py:100
  59.8 5.4 %collective-permute-start.24 = (f32[6,8,256]{2,1,0:T(8,128)S(1)}, f32[6,8,256]{2,1,0:T(8,128)S(1)}, u32[]{:S(2)}, u32[]{:S(2)}) collective-permute-start(f32[6,8,256]{2,1,0:T(8,128)S(1)} %get-tuple-element.85), channel_id=1, source_target_pairs={{0,1},{1,0},{2,3},{3,2},{4,5},{5,4},{6,7},{7,6},{8,9},{9,8},{10,11... | collective-permute-start | bytes 147464 | tf_op jit(solution)/shard_map/ppermute | solution.py:100
  59.8 6.8 %collective-permute-start.25 = (f32[6,8,256]{2,1,0:T(8,128)S(1)}, f32[6,8,256]{2,1,0:T(8,128)S(1)}, u32[]{:S(2)}, u32[]{:S(2)}) collective-permute-start(f32[6,8,256]{2,1,0:T(8,128)S(1)} %get-tuple-element.86), channel_id=1, source_target_pairs={{0,31},{1,2},{2,1},{3,4},{4,3},{5,6},{6,5},{7,8},{8,7},{9,10},{10,... | collective-permute-start | bytes 147464 | tf_op jit(solution)/shard_map/ppermute | solution.py:100

commit v9 on v8

--- a/solution.py
+++ b/solution.py
@@ -98,6 +98,12 @@
     pairs_a = [(i, i ^ 1) for i in range(devices)]
     pairs_b = [(i, (i - 1) % devices if i % 2 == 0 else (i + 1) % devices) for i in range(devices)]
     return lax.ppermute(to_a, axis, pairs_a), lax.ppermute(to_b, axis, pairs_b)
+
+
+def swap_b(value, axis):
+    devices = lax.axis_size(axis)
+    pairs = [(i, (i - 1) % devices if i % 2 == 0 else (i + 1) % devices) for i in range(devices)]
+    return (lax.ppermute(value, axis, pairs),)
 
 
 def full_specs(body, outs, args, scratch=(), name=None, in_specs=None, out_specs=None, after=(), cost=0, alias=None):
@@ -185,7 +191,7 @@
 
 
 def first_body(
-    inner_ref, half_ref, got_a_ref, got_b_ref, edge_a_ref, edge_b_ref, first_ref, to_a_ref, to_b_ref, halo
+    inner_ref, half_ref, got_a_ref, got_b_ref, edge_a_ref, first_ref, to_a_ref, to_b_ref, halo
 ):
     n_ax, ax = lax.axis_size("ax"), lax.axis_index("ax")
     even_x, even_z = is_even("ax"), is_even("az")
@@ -215,25 +221,13 @@
             ref[x] = value[:, : fine // 2]
             ref[half + x] = value[:, fine // 2 :]
     to_a_ref[rows:] = edge_a_ref[...]
-    to_b_ref[rows:] = edge_b_ref[...]
-
-
-def second_body(
-    first_ref, half_ref, got_a_ref, got_b_ref, pick_ref, cells_ref,
-    own_ref, to_xa, to_xb, to_za, to_zb, wide, fine_hi, fine_lo,
-):
-    even = is_even("az")
+
+
+def middle_body(first_ref, half_ref, partial_ref, weight_ref, wide):
     rows, cols, fine = first_ref.shape
-    half = rows // 2
-    for x in range(half):
-        got_a, got_b = [jnp.concatenate([got[x], got[half + x]], axis=1) for got in (got_a_ref, got_b_ref)]
-        before = jnp.where(even, got_b, got_a)
-        after = jnp.where(even, got_a, got_b)
-        wide[x, 0:8] = pltpu.roll(before, 4, 0)
-        wide[x + half, 0:8] = before
-        wide[x, 24:32] = after
-        wide[x + half, 24:32] = pltpu.roll(after, 4, 0)
-    lane = lax.broadcasted_iota(jnp.int32, (cols, fine), 1)
+    blank = jnp.zeros((rows, 8, fine), F32)
+    wide[:, 0:8] = blank
+    wide[:, 24:32] = blank
     for x in range(rows):
         wide[x, 8:24] = first_ref[x]
     for x in range(rows):
@@ -241,6 +235,34 @@
         total = w[0] * first_ref[x]
         for k in range(1, HMAX + 1):
             total = total + w[k] * (wide[x, 8 - k : 24 - k] + wide[x, 8 + k : 24 + k])
+        partial_ref[x] = total
+        for k in range(HMAX + 1):
+            weight_ref[k, x] = w[k]
+
+
+def second_body(
+    partial_ref, weight_ref, got_a_ref, got_b_ref, pick_ref, cells_ref,
+    own_ref, to_xa, to_xb, to_za, to_zb, fine_hi, fine_lo,
+):
+    even = is_even("az")
+    rows, cols, fine = partial_ref.shape
+    half = rows // 2
+    lane = lax.broadcasted_iota(jnp.int32, (cols, fine), 1)
+    row = lax.broadcasted_iota(jnp.int32, (8, fine), 0)
+    for x in range(rows):
+        y = x % half
+        got_a, got_b = [jnp.concatenate([got[y], got[half + y]], axis=1) for got in (got_a_ref, got_b_ref)]
+        before, after = jnp.where(even, got_b, got_a), jnp.where(even, got_a, got_b)
+        if x < half:
+            before = pltpu.roll(before, 4, 0)
+        else:
+            after = pltpu.roll(after, 4, 0)
+        w = [weight_ref[k, x] for k in range(HMAX + 1)]
+        total = partial_ref[x]
+        for k in range(1, HMAX + 1):
+            low = jnp.where(row < k, pltpu.roll(before, k, 0), 0.0)
+            high = jnp.where(row >= 8 - k, pltpu.roll(after, 8 - k, 0), 0.0)
+            total = total + w[k] * jnp.concatenate([low, high], axis=0)
         result = w[0] * total
         for k in range(1, HMAX + 1):
             up = jnp.where(lane < fine - k, pltpu.roll(total, fine - k, 1), 0.0)
@@ -426,7 +448,8 @@
         sides = []
         for swap_ab in (False, True):
             for a, b in spans:
-                got_a, got_b = za[start + a : start + b], zb[start + a : start + b]
+                last_b = zb.shape[0] - za.shape[0] + start
+                got_a, got_b = za[start + a : start + b], zb[last_b + a : last_b + b]
                 pair = (got_a, got_b) if swap_ab else (got_b, got_a)
                 sides.append(jnp.where(even, *pair).reshape((b - a) * 8, za.shape[2]))
         return split(jnp.concatenate(sides, axis=0))
@@ -571,12 +594,13 @@
     long_z = ((px + send_z[0][0], 8, fine // 2), F32)
     filtered, to_a, to_b = full_specs(
         first_body,
-        [block, long_z, long_z],
-        [partial, half_width, noise_a, noise_b, za, zb],
+        [block, long_z, ((px, 8, fine // 2), F32)],
+        [partial, half_width, noise_a, noise_b, za],
         [((2, HMAX, pa, fine), F32)],
         name="filter_axial",
     )
     got_a, got_b = swap(to_a, to_b, "az")
+    (uzb,) = swap_b(zb, "az")
     pick, cells, own = full_specs(
         route_body,
         [((4 * most, ncols), BF16), ((4, 8, radial), F32), ((1, ncols), jnp.int32)],
@@ -584,14 +608,23 @@
         name="route",
         after=[filtered],
     )
+    partial, weights = full_specs(
+        middle_body,
+        [block, ((HMAX + 1, px, pa, fine), F32)],
+        [filtered, half_width],
+        [((px, 32, fine), F32)],
+        name="filter_middle",
+        after=[pick],
+    )
     tiles = most // 8 + 1
     packet, packet_z = ((tiles, 8, radial), F32), ((tiles + 1, 8, radial), F32)
     binned, xa, xb, za, zb = full_specs(
         second_body,
         [((ncols, radial), F32), packet, packet, packet_z, packet_z],
-        [filtered, half_width, got_a, got_b, pick, cells],
-        [((px, 32, fine), F32), ((ncols, fine), BF16), ((ncols, fine), BF16)],
+        [partial, weights, got_a, got_b, pick, cells],
+        [((ncols, fine), BF16), ((ncols, fine), BF16)],
         name="filter_rest",
+        cost=COST,
     )
     packets = (*swap(xa, xb, "ax"), *swap(za, zb, "az"))
 
@@ -600,7 +633,7 @@
     mid, rim = ((5, inner, ca, radial), F32), ((5, 2 * RIM, ca, radial), F32)
     halo = ((2, 5, 3, ca, radial), F32)
     k_mid, k_rim = full_specs(
-        start_body, [mid, rim], [fields, got_a, got_b, uxa, uxb, tmat, rmat], [halo], name="operator", after=[binned]
+        start_body, [mid, rim], [fields, got_a, uzb, uxa, uxb, tmat, rmat], [halo], name="operator", after=[binned]
     )
     p_mid, p_rim, *edges = full_specs(
         gather_body,

time: 68.5 us -> 66.9 us (0.977)
  waiting for transfers between devices: 16.1 us -> 12.1 us
  starting transfers between devices: 34.8 us -> 36.4 us
  Pallas kernels: 13.3 us -> 14 us
    ppermute x13, waiting for transfers between devices: 12.6 us -> 10.1 us  [swap(): lax.ppermute(to_b, axis, pairs_b)]
    ppermute x13, waiting for transfers between devices: 3.48 us -> 2.08 us  [swap(): lax.ppermute(to_a, axis, pairs_a)]
    ppermute x13, starting transfers between devices: 31.3 us -> 32.4 us  [swap(): lax.ppermute(to_b, axis, pairs_b)]
    pallas_call x13 -> x14, Pallas kernels: 13.3 us -> 14 us  [full_specs(): pl.pallas_call(run, out_shape=[jax.ShapeDtypeStruct(s, d) for s, d in out...]
  transfers between devices with their start and end apart: 26 -> 27, of which waited for: 9 -> 9; matrix products, arithmetic and copies ran while one was open for 0% -> 0% of each run, Pallas kernels for 16% -> 18%
where the time goes in v9:
time: 66.9 us; the launch traced here: 66.7 us
  starting transfers between devices  36.4 us (54%)
  Pallas kernels  14 us (21%)
  waiting for transfers between devices  12.1 us (18%)
  local copies, waits for them, and re-layouts  2.68 us (4%)
  other arithmetic  1.05 us (2%)
    ppermute x13, starting transfers between devices, swap(): lax.ppermute(to_b, axis, pairs_b)  32.4 us
    pallas_call x14, Pallas kernels, full_specs(): pl.pallas_call(run, out_shape=[jax.ShapeDtypeStruct(s, d) for s, d in out...  14 us
    ppermute x13, waiting for transfers between devices, swap(): lax.ppermute(to_b, axis, pairs_b)  10.1 us
    ppermute x13, starting transfers between devices, swap(): lax.ppermute(to_a, axis, pairs_a)  3.96 us
    unnamed x18, local copies, waits for them, and re-layouts  2.68 us
    ppermute x13, waiting for transfers between devices, swap(): lax.ppermute(to_a, axis, pairs_a)  2.08 us
  transfers between devices with their start and end apart: 27, of which 9 were waited for; matrix products, arithmetic and copies ran while one was open for 0% of the time, Pallas kernels for 18%

profile of v9, /device:TPU:0, one launch (start us, length us, event | category | flops | bytes accessed | tf_op | source)
XLA Modules:
  0.0 66.7 jit_solution(8464144059946689812)
XLA Ops:
  0.0 1.0 %slice_select_fusion = (f32[4,16,512]{2,1,0:T(8,128)S(1)}, f32[4,16,512]{2,1,0:T(8,128)S(1)}) fusion(f32[16,16,512]{2,1,0:T(8,128)} %refs_0_.4, pred[]{:T(512)S(6)} %eq.3), kind=kLoop, calls=%fused_computation | loop fusion | flops 65536 | bytes 524289 | tf_op jit(solution)/shard_map/jit(_where)/select_n | solution.py:585
  1.1 3.2 %collective-permute-start.1 = (f32[4,16,512]{2,1,0:T(8,128)S(1)}, f32[4,16,512]{2,1,0:T(8,128)S(1)}, u32[]{:S(2)}, u32[]{:S(2)}) collective-permute-start(f32[4,16,512]{2,1,0:T(8,128)S(1)} %get-tuple-element.91), channel_id=1, source_target_pairs={{0,96},{32,64},{64,32},{96,0},{1,97},{33,65},{65,33},{97,1},{2,98}... | collective-permute-start | bytes 393224 | tf_op jit(solution)/shard_map/ppermute | solution.py:100
  4.2 0.1 collective-permute-start
  4.4 1.7 %copy-done = f32[5,32,16,256]{3,2,1,0:T(8,128)S(1)} copy-done((f32[5,32,16,256]{3,2,1,0:T(8,128)S(1)}, f32[5,32,16,256]{3,2,1,0:T(8,128)}, u32[]{:S(2)}) %copy-start) | copy-done | bytes 2621464
  6.1 0.1 edges.1
  6.3 0.9 %copy-done.6 = s32[16,16,512]{2,1,0:T(8,128)S(1)} copy-done((s32[16,16,512]{2,1,0:T(8,128)S(1)}, s32[16,16,512]{2,1,0:T(8,128)}, u32[]{:S(2)}) %copy-start.6) | copy-done | bytes 524312
  7.2 0.5 filter_inner.1
  7.6 0.1 collective-permute-done.1.refs_3_
  7.7 1.5 %collective-permute-done.refs_2_ = f32[4,16,512]{2,1,0:T(8,128)S(1)} collective-permute-done((f32[4,16,512]{2,1,0:T(8,128)S(1)}, f32[4,16,512]{2,1,0:T(8,128)S(1)}, u32[]{:S(2)}, u32[]{:S(2)}) %collective-permute-start) | collective-permute-done | bytes 131104 | tf_op jit(solution)/shard_map/ppermute | solution.py:100
  9.2 0.2 filter_axial.1
  9.4 0.1 collective-permute-start.2
  9.5 6.3 %collective-permute-start.6 = (f32[16,8,256]{2,1,0:T(8,128)S(1)}, f32[16,8,256]{2,1,0:T(8,128)S(1)}, u32[]{:S(2)}, u32[]{:S(2)}) collective-permute-start(f32[16,8,256]{2,1,0:T(8,128)S(1)} %get-tuple-element.59), channel_id=1, source_target_pairs={{0,31},{1,2},{2,1},{3,4},{4,3},{5,6},{6,5},{7,8},{8,7},{9,10},{10,... | collective-permute-start | bytes 393224 | tf_op jit(solution)/shard_map/ppermute | solution.py:100
  15.8 0.0 collective-permute-start.3
  15.9 0.4 collective-permute-start.4
  16.2 1.1 %collective-permute-start.5 = (f32[15,16,256]{2,1,0:T(8,128)S(1)}, f32[15,16,256]{2,1,0:T(8,128)S(1)}, u32[]{:S(2)}, u32[]{:S(2)}) collective-permute-start(f32[15,16,256]{2,1,0:T(8,128)S(1)} %get-tuple-element.54), channel_id=1, source_target_pairs={{0,96},{32,64},{64,32},{96,0},{1,97},{33,65},{65,33},{97,1},{2,98}... | collective-permute-start | bytes 737288 | tf_op jit(solution)/shard_map/ppermute | solution.py:100
  17.4 0.3 route.1
  17.7 1.1 %filter_middle.1 = (f32[16,16,512]{2,1,0:T(8,128)S(1)}, f32[5,16,16,512]{3,2,1,0:T(8,128)S(1)}) custom-call(f32[16,16,512]{2,1,0:T(8,128)S(1)} %get-tuple-element.55.refs_2_.refs_0_, s32[16,16,512]{2,1,0:T(8,128)S(1)} %get-tuple-element.50.refs_1_, bf16[512,256]{1,0:T(8,128)(2,1)S(1)} %get-tuple-element.56.refs_2_.refs_4_), custom_call_target="tpu_custom_call" | custom-call | tf_op jit(solution)/shard_map/filter_middle/pallas_call | solution.py:115
  18.8 0.0 collective-permute-done.6.refs_3_
  18.8 0.0 collective-permute-done.2.refs_2_.refs_1_
  18.8 0.0 copy-start.1
  18.8 0.0 copy-start.3
  18.9 0.0 copy-start.4
  18.9 1.9 %filter_rest.1 = (f32[256,256]{1,0:T(8,128)S(1)}, f32[17,8,256]{2,1,0:T(8,128)S(1)}, f32[17,8,256]{2,1,0:T(8,128)S(1)}, f32[18,8,256]{2,1,0:T(8,128)S(1)}, f32[18,8,256]{2,1,0:T(8,128)S(1)}) custom-call(f32[16,16,512]{2,1,0:T(8,128)S(1)} %get-tuple-element.57.refs_0_, f32[5,16,16,512]{3,2,1,0:T(8,128)S(1)} %get-tuple-element.58.refs_1_, ...), custom_call_target="tpu_custom_call" | custom-call | flops 137438953472 | tf_op jit(solution)/shard_map/filter_rest/pallas_call | solution.py:115
  20.7 0.1 collective-permute-start.9
  20.8 4.8 %collective-permute-start.10 = (f32[18,8,256]{2,1,0:T(8,128)S(1)}, f32[18,8,256]{2,1,0:T(8,128)S(1)}, u32[]{:S(2)}, u32[]{:S(2)}) collective-permute-start(f32[18,8,256]{2,1,0:T(8,128)S(1)} %get-tuple-element.68), channel_id=1, source_target_pairs={{0,31},{1,2},{2,1},{3,4},{4,3},{5,6},{6,5},{7,8},{8,7},{9,10},{10,... | collective-permute-start | bytes 442376 | tf_op jit(solution)/shard_map/ppermute | solution.py:100
  25.7 0.0 collective-permute-done.3.refs_2_
  25.7 1.1 %collective-permute-start.7 = (f32[17,8,256]{2,1,0:T(8,128)S(1)}, f32[17,8,256]{2,1,0:T(8,128)S(1)}, u32[]{:S(2)}, u32[]{:S(2)}) collective-permute-start(f32[17,8,256]{2,1,0:T(8,128)S(1)} %get-tuple-element.65), channel_id=1, source_target_pairs={{0,32},{32,0},{64,96},{96,64},{1,33},{33,1},{65,97},{97,65},{2,34}... | collective-permute-start | bytes 417800 | tf_op jit(solution)/shard_map/ppermute | solution.py:100
  26.8 0.0 collective-permute-done.4.refs_3_
  26.8 1.8 %collective-permute-start.8 = (f32[17,8,256]{2,1,0:T(8,128)S(1)}, f32[17,8,256]{2,1,0:T(8,128)S(1)}, u32[]{:S(2)}, u32[]{:S(2)}) collective-permute-start(f32[17,8,256]{2,1,0:T(8,128)S(1)} %get-tuple-element.66), channel_id=1, source_target_pairs={{0,96},{32,64},{64,32},{96,0},{1,97},{33,65},{65,33},{97,1},{2,98}... | collective-permute-start | bytes 417800 | tf_op jit(solution)/shard_map/ppermute | solution.py:100
  28.6 1.6 %operator.1 = (f32[5,24,16,256]{3,2,1,0:T(8,128)S(1)}, f32[5,8,16,256]{3,2,1,0:T(8,128)S(1)}) custom-call(f32[5,32,16,256]{3,2,1,0:T(8,128)S(1)} %copy-done.1, f32[40,8,256]{2,1,0:T(8,128)S(1)} %collective-permute-done.2.refs_2_.refs_1_, f32[24,8,256]{2,1,0:T(8,128)S(1)} %collective-permute-done.3.refs_2_, ...), custom_call_target="tpu_custom_call" | custom-call | tf_op jit(solution)/shard_map/operator/pallas_call | solution.py:115
  30.2 0.6 collective-permute-done.7.refs_2_
  30.7 2.4 %collective-permute-done.8.refs_3_ = f32[17,8,256]{2,1,0:T(8,128)S(1)} collective-permute-done((f32[17,8,256]{2,1,0:T(8,128)S(1)}, f32[17,8,256]{2,1,0:T(8,128)S(1)}, u32[]{:S(2)}, u32[]{:S(2)}) %collective-permute-start.8) | collective-permute-done | bytes 139296 | tf_op jit(solution)/shard_map/ppermute | solution.py:100
  33.1 0.0 collective-permute-done.9.refs_4_
  33.1 0.0 collective-permute-done.10.refs_5_
  33.1 0.6 gather.1
  33.7 0.1 collective-permute-start.11
  33.8 1.4 %collective-permute-start.12 = (f32[24,8,256]{2,1,0:T(8,128)S(1)}, f32[24,8,256]{2,1,0:T(8,128)S(1)}, u32[]{:S(2)}, u32[]{:S(2)}) collective-permute-start(f32[24,8,256]{2,1,0:T(8,128)S(1)} %get-tuple-element.72), channel_id=1, source_target_pairs={{0,31},{1,2},{2,1},{3,4},{4,3},{5,6},{6,5},{7,8},{8,7},{9,10},{10,... | collective-permute-start | bytes 589832 | tf_op jit(solution)/shard_map/ppermute | solution.py:100
  35.1 0.3 collective-permute-start.13
  35.5 1.8 %collective-permute-start.14 = (f32[15,16,256]{2,1,0:T(8,128)S(1)}, f32[15,16,256]{2,1,0:T(8,128)S(1)}, u32[]{:S(2)}, u32[]{:S(2)}) collective-permute-start(f32[15,16,256]{2,1,0:T(8,128)S(1)} %get-tuple-element.75), channel_id=1, source_target_pairs={{0,96},{32,64},{64,32},{96,0},{1,97},{33,65},{65,33},{97,1},{2,98}... | collective-permute-start | bytes 737288 | tf_op jit(solution)/shard_map/ppermute | solution.py:100
  37.2 5.1 %collective-permute-done.12.refs_9_.refs_11_ = f32[24,8,256]{2,1,0:T(8,128)S(1)} collective-permute-done((f32[24,8,256]{2,1,0:T(8,128)S(1)}, f32[24,8,256]{2,1,0:T(8,128)S(1)}, u32[]{:S(2)}, u32[]{:S(2)}) %collective-permute-start.12) | collective-permute-done | bytes 196640 | tf_op jit(solution)/shard_map/ppermute | solution.py:100
  42.3 1.4 %stage_inner.2 = (f32[5,24,16,256]{3,2,1,0:T(8,128)S(1)}, f32[18,8,256]{2,1,0:T(8,128)S(1)}, f32[18,8,256]{2,1,0:T(8,128)S(1)}) custom-call(f32[5,24,16,256]{3,2,1,0:T(8,128)S(1)} %get-tuple-element.62.refs_6_.refs_0_.refs_4_.refs_2_.refs_3_, f32[5,8,16,256]{3,2,1,0:T(8,128)S(1)} %get-tuple-element.63.refs_7_.refs_1_.refs_5_.refs_3_.refs_4_, ...), custom_call_target="tpu_custom_call" | custom-call | flops 137438953472 | tf_op jit(solution)/shard_map/stage_inner/pallas_call | solution.py:115
  43.7 0.1 collective-permute-start.15
  43.7 1.6 %collective-permute-start.16 = (f32[18,8,256]{2,1,0:T(8,128)S(1)}, f32[18,8,256]{2,1,0:T(8,128)S(1)}, u32[]{:S(2)}, u32[]{:S(2)}) collective-permute-start(f32[18,8,256]{2,1,0:T(8,128)S(1)} %get-tuple-element.78), channel_id=1, source_target_pairs={{0,31},{1,2},{2,1},{3,4},{4,3},{5,6},{6,5},{7,8},{8,7},{9,10},{10,... | collective-permute-start | bytes 442376 | tf_op jit(solution)/shard_map/ppermute | solution.py:100
  45.3 0.6 stage_rim.2
  45.9 0.4 collective-permute-start.17
  46.3 1.7 %collective-permute-start.18 = (f32[15,16,256]{2,1,0:T(8,128)S(1)}, f32[15,16,256]{2,1,0:T(8,128)S(1)}, u32[]{:S(2)}, u32[]{:S(2)}) collective-permute-start(f32[15,16,256]{2,1,0:T(8,128)S(1)} %get-tuple-element.81), channel_id=1, source_target_pairs={{0,96},{32,64},{64,32},{96,0},{1,97},{33,65},{65,33},{97,1},{2,98}... | collective-permute-start | bytes 737288 | tf_op jit(solution)/shard_map/ppermute | solution.py:100
  48.1 3.3 %collective-permute-start.20 = (f32[6,8,256]{2,1,0:T(8,128)S(1)}, f32[6,8,256]{2,1,0:T(8,128)S(1)}, u32[]{:S(2)}, u32[]{:S(2)}) collective-permute-start(f32[6,8,256]{2,1,0:T(8,128)S(1)} %get-tuple-element.83), channel_id=1, source_target_pairs={{0,31},{1,2},{2,1},{3,4},{4,3},{5,6},{6,5},{7,8},{8,7},{9,10},{10,... | collective-permute-start | bytes 147464 | tf_op jit(solution)/shard_map/ppermute | solution.py:100
  51.4 0.5 collective-permute-done.16.refs_7_
  51.9 1.4 %stage_inner.3 = (f32[5,24,16,256]{3,2,1,0:T(8,128)S(1)}, f32[18,8,256]{2,1,0:T(8,128)S(1)}, f32[18,8,256]{2,1,0:T(8,128)S(1)}) custom-call(f32[5,24,16,256]{3,2,1,0:T(8,128)S(1)} %get-tuple-element.73.refs_14_.refs_0_, f32[5,8,16,256]{3,2,1,0:T(8,128)S(1)} %get-tuple-element.76.refs_1_, ...), custom_call_target="tpu_custom_call" | custom-call | flops 2000000000 | tf_op jit(solution)/shard_map/stage_inner/pallas_call | solution.py:115
  53.3 0.1 collective-permute-start.21
  53.4 1.4 %collective-permute-start.22 = (f32[18,8,256]{2,1,0:T(8,128)S(1)}, f32[18,8,256]{2,1,0:T(8,128)S(1)}, u32[]{:S(2)}, u32[]{:S(2)}) collective-permute-start(f32[18,8,256]{2,1,0:T(8,128)S(1)} %get-tuple-element.86), channel_id=1, source_target_pairs={{0,31},{1,2},{2,1},{3,4},{4,3},{5,6},{6,5},{7,8},{8,7},{9,10},{10,... | collective-permute-start | bytes 442376 | tf_op jit(solution)/shard_map/ppermute | solution.py:100
  54.7 0.2 collective-permute-done.20.refs_9_
  54.9 0.6 stage_rim.3
  55.6 1.2 %collective-permute-start.23 = (f32[15,16,256]{2,1,0:T(8,128)S(1)}, f32[15,16,256]{2,1,0:T(8,128)S(1)}, u32[]{:S(2)}, u32[]{:S(2)}) collective-permute-start(f32[15,16,256]{2,1,0:T(8,128)S(1)} %get-tuple-element.87), channel_id=1, source_target_pairs={{0,32},{32,0},{64,96},{96,64},{1,33},{33,1},{65,97},{97,65},{2,34}... | collective-permute-start | bytes 737288 | tf_op jit(solution)/shard_map/ppermute | solution.py:100
  56.7 1.5 %collective-permute-start.24 = (f32[15,16,256]{2,1,0:T(8,128)S(1)}, f32[15,16,256]{2,1,0:T(8,128)S(1)}, u32[]{:S(2)}, u32[]{:S(2)}) collective-permute-start(f32[15,16,256]{2,1,0:T(8,128)S(1)} %get-tuple-element.88), channel_id=1, source_target_pairs={{0,96},{32,64},{64,32},{96,0},{1,97},{33,65},{65,33},{97,1},{2,98}... | collective-permute-start | bytes 737288 | tf_op jit(solution)/shard_map/ppermute | solution.py:100
  58.2 0.0 collective-permute-start.25
  58.2 0.0 collective-permute-done.21.refs_7_
  58.2 2.7 %collective-permute-start.26 = (f32[6,8,256]{2,1,0:T(8,128)S(1)}, f32[6,8,256]{2,1,0:T(8,128)S(1)}, u32[]{:S(2)}, u32[]{:S(2)}) collective-permute-start(f32[6,8,256]{2,1,0:T(8,128)S(1)} %get-tuple-element.90), channel_id=1, source_target_pairs={{0,31},{1,2},{2,1},{3,4},{4,3},{5,6},{6,5},{7,8},{8,7},{9,10},{10,... | collective-permute-start | bytes 147464 | tf_op jit(solution)/shard_map/ppermute | solution.py:100
  60.9 0.4 collective-permute-done.22.refs_8_
  61.3 2.3 %final_inner.1.refs_0_ = f32[5,32,16,256]{3,2,1,0:T(8,128)} custom-call(f32[5,24,16,256]{3,2,1,0:T(8,128)S(1)} %get-tuple-element.79.refs_12_.refs_0_.refs_1_, f32[5,8,16,256]{3,2,1,0:T(8,128)S(1)} %get-tuple-element.84.refs_1_.refs_2_, f32[5,24,16,256]{3,2,1,0:T(8,128)S(1)} %get-tuple-element.62.refs_6_.refs_0_.refs_4_.refs_2_.refs_3_, ...), custom_call_target="tpu_custom_call" | custom-call | flops 2000000000 | tf_op jit(solution)/shard_map/final_inner/pallas_call | solution.py:115
  63.7 1.4 %collective-permute-done.26.refs_11_ = f32[6,8,256]{2,1,0:T(8,128)S(1)} collective-permute-done((f32[6,8,256]{2,1,0:T(8,128)S(1)}, f32[6,8,256]{2,1,0:T(8,128)S(1)}, u32[]{:S(2)}, u32[]{:S(2)}) %collective-permute-start.26) | collective-permute-done | bytes 49184 | tf_op jit(solution)/shard_map/ppermute | solution.py:100
  65.1 0.0 collective-permute-done.23.refs_8_
  65.1 0.0 collective-permute-done.24.refs_9_
  65.1 1.5 %final_rim.1 = f32[5,32,16,256]{3,2,1,0:T(8,128)} custom-call(f32[5,32,16,256]{3,2,1,0:T(8,128)} %final_inner.1.refs_0_, f32[5,24,16,256]{3,2,1,0:T(8,128)S(1)} %get-tuple-element.79.refs_12_.refs_0_.refs_1_, f32[5,8,16,256]{3,2,1,0:T(8,128)S(1)} %get-tuple-element.84.refs_1_.refs_2_, ...), custom_call_target="tpu_custom_call", output_to_operand_aliasing={{}: (0, {})} | custom-call | tf_op jit(solution)/shard_map/final_rim/pallas_call | solution.py:115
  (23 shorter events, 0.1 us)
Async XLA Ops:
  0.0 6.2 %copy-start.5 = (f32[16,16,512]{2,1,0:T(8,128)S(1)}, f32[16,16,512]{2,1,0:T(8,128)}, u32[]{:S(2)}) copy-start(f32[16,16,512]{2,1,0:T(8,128)} %refs_0_.4) | copy-start | bytes 1572868
  1.1 6.7 %collective-permute-start.1 = (f32[4,16,512]{2,1,0:T(8,128)S(1)}, f32[4,16,512]{2,1,0:T(8,128)S(1)}, u32[]{:S(2)}, u32[]{:S(2)}) collective-permute-start(f32[4,16,512]{2,1,0:T(8,128)S(1)} %get-tuple-element.91), channel_id=1, source_target_pairs={{0,96},{32,64},{64,32},{96,0},{1,97},{33,65},{65,33},{97,1},{2,98}... | collective-permute-start | bytes 393224 | tf_op jit(solution)/shard_map/ppermute | solution.py:100
  4.2 5.0 %collective-permute-start = (f32[4,16,512]{2,1,0:T(8,128)S(1)}, f32[4,16,512]{2,1,0:T(8,128)S(1)}, u32[]{:S(2)}, u32[]{:S(2)}) collective-permute-start(f32[4,16,512]{2,1,0:T(8,128)S(1)} %get-tuple-element.92.refs_1_), channel_id=1, source_target_pairs={{0,32},{32,0},{64,96},{96,64},{1,33},{33,1},{65,97},{97,65},{2,34}... | collective-permute-start | bytes 393224 | tf_op jit(solution)/shard_map/ppermute | solution.py:100
  4.4 1.7 %copy-start = (f32[5,32,16,256]{3,2,1,0:T(8,128)S(1)}, f32[5,32,16,256]{3,2,1,0:T(8,128)}, u32[]{:S(2)}) copy-start(f32[5,32,16,256]{3,2,1,0:T(8,128)} %refs_7_.1) | copy-start | bytes 7864324
  6.1 1.0 %copy-start.6 = (s32[16,16,512]{2,1,0:T(8,128)S(1)}, s32[16,16,512]{2,1,0:T(8,128)}, u32[]{:S(2)}) copy-start(s32[16,16,512]{2,1,0:T(8,128)} %refs_1_.1) | copy-start | bytes 1572868
  6.1 11.2 %copy-start.7 = (s32[256]{0:T(256)S(1)}, s32[256]{0:T(256)}, u32[]{:S(2)}) copy-start(s32[256]{0:T(256)} %param.9) | copy-start | bytes 3076
  6.1 11.2 %copy-start.8 = (s32[256]{0:T(256)S(1)}, s32[256]{0:T(256)}, u32[]{:S(2)}) copy-start(s32[256]{0:T(256)} %param.10) | copy-start | bytes 3076
  9.4 9.4 %collective-permute-start.2 = (f32[40,8,256]{2,1,0:T(8,128)S(1)}, f32[40,8,256]{2,1,0:T(8,128)S(1)}, u32[]{:S(2)}, u32[]{:S(2)}) collective-permute-start(f32[40,8,256]{2,1,0:T(8,128)S(1)} %get-tuple-element.51), channel_id=1, source_target_pairs={{0,1},{1,0},{2,3},{3,2},{4,5},{5,4},{6,7},{7,6},{8,9},{9,8},{10,11... | collective-permute-start | bytes 983048 | tf_op jit(solution)/shard_map/ppermute | solution.py:100
  9.5 9.3 %collective-permute-start.6 = (f32[16,8,256]{2,1,0:T(8,128)S(1)}, f32[16,8,256]{2,1,0:T(8,128)S(1)}, u32[]{:S(2)}, u32[]{:S(2)}) collective-permute-start(f32[16,8,256]{2,1,0:T(8,128)S(1)} %get-tuple-element.59), channel_id=1, source_target_pairs={{0,31},{1,2},{2,1},{3,4},{4,3},{5,6},{6,5},{7,8},{8,7},{9,10},{10,... | collective-permute-start | bytes 393224 | tf_op jit(solution)/shard_map/ppermute | solution.py:100
  15.8 9.8 %collective-permute-start.3 = (f32[24,8,256]{2,1,0:T(8,128)S(1)}, f32[24,8,256]{2,1,0:T(8,128)S(1)}, u32[]{:S(2)}, u32[]{:S(2)}) collective-permute-start(f32[24,8,256]{2,1,0:T(8,128)S(1)} %get-tuple-element.52), channel_id=1, source_target_pairs={{0,31},{1,2},{2,1},{3,4},{4,3},{5,6},{6,5},{7,8},{8,7},{9,10},{10,... | collective-permute-start | bytes 589832 | tf_op jit(solution)/shard_map/ppermute | solution.py:106
  15.9 11.0 %collective-permute-start.4 = (f32[15,16,256]{2,1,0:T(8,128)S(1)}, f32[15,16,256]{2,1,0:T(8,128)S(1)}, u32[]{:S(2)}, u32[]{:S(2)}) collective-permute-start(f32[15,16,256]{2,1,0:T(8,128)S(1)} %get-tuple-element.53), channel_id=1, source_target_pairs={{0,32},{32,0},{64,96},{96,64},{1,33},{33,1},{65,97},{97,65},{2,34}... | collective-permute-start | bytes 737288 | tf_op jit(solution)/shard_map/ppermute | solution.py:100
  16.2 12.4 %collective-permute-start.5 = (f32[15,16,256]{2,1,0:T(8,128)S(1)}, f32[15,16,256]{2,1,0:T(8,128)S(1)}, u32[]{:S(2)}, u32[]{:S(2)}) collective-permute-start(f32[15,16,256]{2,1,0:T(8,128)S(1)} %get-tuple-element.54), channel_id=1, source_target_pairs={{0,96},{32,64},{64,32},{96,0},{1,97},{33,65},{65,33},{97,1},{2,98}... | collective-permute-start | bytes 737288 | tf_op jit(solution)/shard_map/ppermute | solution.py:100
  18.8 9.7 %copy-start.1 = (f32[5,32,16,256]{3,2,1,0:T(8,128)S(1)}, f32[5,32,16,256]{3,2,1,0:T(8,128)}, u32[]{:S(2)}) copy-start(f32[5,32,16,256]{3,2,1,0:T(8,128)} %refs_7_.1) | copy-start | bytes 7864324
  18.8 9.7 %copy-start.3 = (bf16[2,2,256,256]{3,2,1,0:T(8,128)(2,1)S(1)}, bf16[2,2,256,256]{3,2,1,0:T(8,128)(2,1)}, u32[]{:S(2)}) copy-start(bf16[2,2,256,256]{3,2,1,0:T(8,128)(2,1)} %constant.17.clone.refs_6_.refs_11_.refs_13_.refs_9_.refs_10_) | copy-start | bytes 1572868
  18.9 9.7 %copy-start.4 = (bf16[2,2,128,224]{3,2,1,0:T(8,128)(2,1)S(1)}, bf16[2,2,128,224]{3,2,1,0:T(8,128)(2,1)}, u32[]{:S(2)}) copy-start(bf16[2,2,128,224]{3,2,1,0:T(8,128)(2,1)} %constant.16.clone.refs_5_.refs_10_.refs_12_.refs_8_.refs_9_) | copy-start | bytes 688132
  20.7 12.3 %collective-permute-start.9 = (f32[18,8,256]{2,1,0:T(8,128)S(1)}, f32[18,8,256]{2,1,0:T(8,128)S(1)}, u32[]{:S(2)}, u32[]{:S(2)}) collective-permute-start(f32[18,8,256]{2,1,0:T(8,128)S(1)} %get-tuple-element.67), channel_id=1, source_target_pairs={{0,1},{1,0},{2,3},{3,2},{4,5},{5,4},{6,7},{7,6},{8,9},{9,8},{10,11... | collective-permute-start | bytes 442376 | tf_op jit(solution)/shard_map/ppermute | solution.py:100
  20.8 12.3 %collective-permute-start.10 = (f32[18,8,256]{2,1,0:T(8,128)S(1)}, f32[18,8,256]{2,1,0:T(8,128)S(1)}, u32[]{:S(2)}, u32[]{:S(2)}) collective-permute-start(f32[18,8,256]{2,1,0:T(8,128)S(1)} %get-tuple-element.68), channel_id=1, source_target_pairs={{0,31},{1,2},{2,1},{3,4},{4,3},{5,6},{6,5},{7,8},{8,7},{9,10},{10,... | collective-permute-start | bytes 442376 | tf_op jit(solution)/shard_map/ppermute | solution.py:100
  25.7 5.1 %collective-permute-start.7 = (f32[17,8,256]{2,1,0:T(8,128)S(1)}, f32[17,8,256]{2,1,0:T(8,128)S(1)}, u32[]{:S(2)}, u32[]{:S(2)}) collective-permute-start(f32[17,8,256]{2,1,0:T(8,128)S(1)} %get-tuple-element.65), channel_id=1, source_target_pairs={{0,32},{32,0},{64,96},{96,64},{1,33},{33,1},{65,97},{97,65},{2,34}... | collective-permute-start | bytes 417800 | tf_op jit(solution)/shard_map/ppermute | solution.py:100
  26.8 6.3 %collective-permute-start.8 = (f32[17,8,256]{2,1,0:T(8,128)S(1)}, f32[17,8,256]{2,1,0:T(8,128)S(1)}, u32[]{:S(2)}, u32[]{:S(2)}) collective-permute-start(f32[17,8,256]{2,1,0:T(8,128)S(1)} %get-tuple-element.66), channel_id=1, source_target_pairs={{0,96},{32,64},{64,32},{96,0},{1,97},{33,65},{65,33},{97,1},{2,98}... | collective-permute-start | bytes 417800 | tf_op jit(solution)/shard_map/ppermute | solution.py:100
  33.7 3.5 %collective-permute-start.11 = (f32[24,8,256]{2,1,0:T(8,128)S(1)}, f32[24,8,256]{2,1,0:T(8,128)S(1)}, u32[]{:S(2)}, u32[]{:S(2)}) collective-permute-start(f32[24,8,256]{2,1,0:T(8,128)S(1)} %get-tuple-element.71), channel_id=1, source_target_pairs={{0,1},{1,0},{2,3},{3,2},{4,5},{5,4},{6,7},{7,6},{8,9},{9,8},{10,11... | collective-permute-start | bytes 589832 | tf_op jit(solution)/shard_map/ppermute | solution.py:100
  33.8 8.5 %collective-permute-start.12 = (f32[24,8,256]{2,1,0:T(8,128)S(1)}, f32[24,8,256]{2,1,0:T(8,128)S(1)}, u32[]{:S(2)}, u32[]{:S(2)}) collective-permute-start(f32[24,8,256]{2,1,0:T(8,128)S(1)} %get-tuple-element.72), channel_id=1, source_target_pairs={{0,31},{1,2},{2,1},{3,4},{4,3},{5,6},{6,5},{7,8},{8,7},{9,10},{10,... | collective-permute-start | bytes 589832 | tf_op jit(solution)/shard_map/ppermute | solution.py:100
  35.1 10.2 %collective-permute-start.13 = (f32[15,16,256]{2,1,0:T(8,128)S(1)}, f32[15,16,256]{2,1,0:T(8,128)S(1)}, u32[]{:S(2)}, u32[]{:S(2)}) collective-permute-start(f32[15,16,256]{2,1,0:T(8,128)S(1)} %get-tuple-element.74), channel_id=1, source_target_pairs={{0,32},{32,0},{64,96},{96,64},{1,33},{33,1},{65,97},{97,65},{2,34}... | collective-permute-start | bytes 737288 | tf_op jit(solution)/shard_map/ppermute | solution.py:100
  35.5 9.8 %collective-permute-start.14 = (f32[15,16,256]{2,1,0:T(8,128)S(1)}, f32[15,16,256]{2,1,0:T(8,128)S(1)}, u32[]{:S(2)}, u32[]{:S(2)}) collective-permute-start(f32[15,16,256]{2,1,0:T(8,128)S(1)} %get-tuple-element.75), channel_id=1, source_target_pairs={{0,96},{32,64},{64,32},{96,0},{1,97},{33,65},{65,33},{97,1},{2,98}... | collective-permute-start | bytes 737288 | tf_op jit(solution)/shard_map/ppermute | solution.py:100
  43.7 4.4 %collective-permute-start.15 = (f32[18,8,256]{2,1,0:T(8,128)S(1)}, f32[18,8,256]{2,1,0:T(8,128)S(1)}, u32[]{:S(2)}, u32[]{:S(2)}) collective-permute-start(f32[18,8,256]{2,1,0:T(8,128)S(1)} %get-tuple-element.77), channel_id=1, source_target_pairs={{0,1},{1,0},{2,3},{3,2},{4,5},{5,4},{6,7},{7,6},{8,9},{9,8},{10,11... | collective-permute-start | bytes 442376 | tf_op jit(solution)/shard_map/ppermute | solution.py:100
  43.7 8.1 %collective-permute-start.16 = (f32[18,8,256]{2,1,0:T(8,128)S(1)}, f32[18,8,256]{2,1,0:T(8,128)S(1)}, u32[]{:S(2)}, u32[]{:S(2)}) collective-permute-start(f32[18,8,256]{2,1,0:T(8,128)S(1)} %get-tuple-element.78), channel_id=1, source_target_pairs={{0,31},{1,2},{2,1},{3,4},{4,3},{5,6},{6,5},{7,8},{8,7},{9,10},{10,... | collective-permute-start | bytes 442376 | tf_op jit(solution)/shard_map/ppermute | solution.py:100
  45.9 9.0 %collective-permute-start.17 = (f32[15,16,256]{2,1,0:T(8,128)S(1)}, f32[15,16,256]{2,1,0:T(8,128)S(1)}, u32[]{:S(2)}, u32[]{:S(2)}) collective-permute-start(f32[15,16,256]{2,1,0:T(8,128)S(1)} %get-tuple-element.80), channel_id=1, source_target_pairs={{0,32},{32,0},{64,96},{96,64},{1,33},{33,1},{65,97},{97,65},{2,34}... | collective-permute-start | bytes 737288 | tf_op jit(solution)/shard_map/ppermute | solution.py:100
  46.3 8.6 %collective-permute-start.18 = (f32[15,16,256]{2,1,0:T(8,128)S(1)}, f32[15,16,256]{2,1,0:T(8,128)S(1)}, u32[]{:S(2)}, u32[]{:S(2)}) collective-permute-start(f32[15,16,256]{2,1,0:T(8,128)S(1)} %get-tuple-element.81), channel_id=1, source_target_pairs={{0,96},{32,64},{64,32},{96,0},{1,97},{33,65},{65,33},{97,1},{2,98}... | collective-permute-start | bytes 737288 | tf_op jit(solution)/shard_map/ppermute | solution.py:100
  48.1 5.3 %collective-permute-start.19 = (f32[6,8,256]{2,1,0:T(8,128)S(1)}, f32[6,8,256]{2,1,0:T(8,128)S(1)}, u32[]{:S(2)}, u32[]{:S(2)}) collective-permute-start(f32[6,8,256]{2,1,0:T(8,128)S(1)} %get-tuple-element.82), channel_id=1, source_target_pairs={{0,1},{1,0},{2,3},{3,2},{4,5},{5,4},{6,7},{7,6},{8,9},{9,8},{10,11... | collective-permute-start | bytes 147464 | tf_op jit(solution)/shard_map/ppermute | solution.py:100
  48.1 6.8 %collective-permute-start.20 = (f32[6,8,256]{2,1,0:T(8,128)S(1)}, f32[6,8,256]{2,1,0:T(8,128)S(1)}, u32[]{:S(2)}, u32[]{:S(2)}) collective-permute-start(f32[6,8,256]{2,1,0:T(8,128)S(1)} %get-tuple-element.83), channel_id=1, source_target_pairs={{0,31},{1,2},{2,1},{3,4},{4,3},{5,6},{6,5},{7,8},{8,7},{9,10},{10,... | collective-permute-start | bytes 147464 | tf_op jit(solution)/shard_map/ppermute | solution.py:100
  53.3 5.0 %collective-permute-start.21 = (f32[18,8,256]{2,1,0:T(8,128)S(1)}, f32[18,8,256]{2,1,0:T(8,128)S(1)}, u32[]{:S(2)}, u32[]{:S(2)}) collective-permute-start(f32[18,8,256]{2,1,0:T(8,128)S(1)} %get-tuple-element.85), channel_id=1, source_target_pairs={{0,1},{1,0},{2,3},{3,2},{4,5},{5,4},{6,7},{7,6},{8,9},{9,8},{10,11... | collective-permute-start | bytes 442376 | tf_op jit(solution)/shard_map/ppermute | solution.py:100
  53.4 8.0 %collective-permute-start.22 = (f32[18,8,256]{2,1,0:T(8,128)S(1)}, f32[18,8,256]{2,1,0:T(8,128)S(1)}, u32[]{:S(2)}, u32[]{:S(2)}) collective-permute-start(f32[18,8,256]{2,1,0:T(8,128)S(1)} %get-tuple-element.86), channel_id=1, source_target_pairs={{0,31},{1,2},{2,1},{3,4},{4,3},{5,6},{6,5},{7,8},{8,7},{9,10},{10,... | collective-permute-start | bytes 442376 | tf_op jit(solution)/shard_map/ppermute | solution.py:100
  54.9 6.4 %copy-start.2 = (f32[5,32,16,256]{3,2,1,0:T(8,128)S(1)}, f32[5,32,16,256]{3,2,1,0:T(8,128)}, u32[]{:S(2)}) copy-start(f32[5,32,16,256]{3,2,1,0:T(8,128)} %refs_7_.1) | copy-start | bytes 7864324
  55.6 9.5 %collective-permute-start.23 = (f32[15,16,256]{2,1,0:T(8,128)S(1)}, f32[15,16,256]{2,1,0:T(8,128)S(1)}, u32[]{:S(2)}, u32[]{:S(2)}) collective-permute-start(f32[15,16,256]{2,1,0:T(8,128)S(1)} %get-tuple-element.87), channel_id=1, source_target_pairs={{0,32},{32,0},{64,96},{96,64},{1,33},{33,1},{65,97},{97,65},{2,34}... | collective-permute-start | bytes 737288 | tf_op jit(solution)/shard_map/ppermute | solution.py:100
  56.7 8.3 %collective-permute-start.24 = (f32[15,16,256]{2,1,0:T(8,128)S(1)}, f32[15,16,256]{2,1,0:T(8,128)S(1)}, u32[]{:S(2)}, u32[]{:S(2)}) collective-permute-start(f32[15,16,256]{2,1,0:T(8,128)S(1)} %get-tuple-element.88), channel_id=1, source_target_pairs={{0,96},{32,64},{64,32},{96,0},{1,97},{33,65},{65,33},{97,1},{2,98}... | collective-permute-start | bytes 737288 | tf_op jit(solution)/shard_map/ppermute | solution.py:100
  58.2 5.5 %collective-permute-start.25 = (f32[6,8,256]{2,1,0:T(8,128)S(1)}, f32[6,8,256]{2,1,0:T(8,128)S(1)}, u32[]{:S(2)}, u32[]{:S(2)}) collective-permute-start(f32[6,8,256]{2,1,0:T(8,128)S(1)} %get-tuple-element.89), channel_id=1, source_target_pairs={{0,1},{1,0},{2,3},{3,2},{4,5},{5,4},{6,7},{7,6},{8,9},{9,8},{10,11... | collective-permute-start | bytes 147464 | tf_op jit(solution)/shard_map/ppermute | solution.py:100
  58.2 6.8 %collective-permute-start.26 = (f32[6,8,256]{2,1,0:T(8,128)S(1)}, f32[6,8,256]{2,1,0:T(8,128)S(1)}, u32[]{:S(2)}, u32[]{:S(2)}) collective-permute-start(f32[6,8,256]{2,1,0:T(8,128)S(1)} %get-tuple-element.90), channel_id=1, source_target_pairs={{0,31},{1,2},{2,1},{3,4},{4,3},{5,6},{6,5},{7,8},{8,7},{9,10},{10,... | collective-permute-start | bytes 147464 | tf_op jit(solution)/shard_map/ppermute | solution.py:100

commit v10 on v9

--- a/solution.py
+++ b/solution.py
@@ -285,7 +285,7 @@
         tiles = most // 8
         out[0:tiles] = (dot(pick, hi) + dot(pick, lo)).reshape(tiles, 8, radial)
         out[tiles] = cells_ref[d]
-    for out in (to_za, to_zb):
+    for out in (to_xa, to_xb):
         out[most // 8 + 1] = jnp.zeros(out.shape[1:], F32)
 
 
@@ -294,7 +294,7 @@
 ):
     mid, cols, radial = p_mid.shape
     cells = (mid + 2 * RIM) * cols
-    most = 8 * (xa.shape[0] - 1)
+    most = 8 * (za.shape[0] - 1)
 
     def onehot(row):
         at = lax.broadcasted_iota(jnp.int32, (cells, row.shape[1]), 0)
@@ -617,10 +617,10 @@
         after=[pick],
     )
     tiles = most // 8 + 1
-    packet, packet_z = ((tiles, 8, radial), F32), ((tiles + 1, 8, radial), F32)
+    packet, packet_x = ((tiles, 8, radial), F32), ((tiles + 1, 8, radial), F32)
     binned, xa, xb, za, zb = full_specs(
         second_body,
-        [((ncols, radial), F32), packet, packet, packet_z, packet_z],
+        [((ncols, radial), F32), packet_x, packet_x, packet, packet],
         [partial, weights, got_a, got_b, pick, cells],
         [((ncols, fine), BF16), ((ncols, fine), BF16)],
         name="filter_rest",

time: 66.9 us -> 68.3 us (1.021)
  starting transfers between devices: 36.4 us -> 38.7 us
  waiting for transfers between devices: 12.1 us -> 11.3 us
    ppermute x13, starting transfers between devices: 32.4 us -> 34.4 us  [swap(): lax.ppermute(to_b, axis, pairs_b)]
  transfers between devices with their start and end apart: 27 -> 27, of which waited for: 9 -> 7; matrix products, arithmetic and copies ran while one was open for 0% -> 0% of each run, Pallas kernels for 18% -> 17%
where the time goes in v10:
time: 68.3 us; the launch traced here: 68.1 us
  starting transfers between devices  38.7 us (57%)
  Pallas kernels  14 us (20%)
  waiting for transfers between devices  11.3 us (17%)
  local copies, waits for them, and re-layouts  2.68 us (4%)
  other arithmetic  1.05 us (2%)
    ppermute x13, starting transfers between devices, swap(): lax.ppermute(to_b, axis, pairs_b)  34.4 us
    pallas_call x14, Pallas kernels, full_specs(): pl.pallas_call(run, out_shape=[jax.ShapeDtypeStruct(s, d) for s, d in out...  14 us
    ppermute x13, waiting for transfers between devices, swap(): lax.ppermute(to_b, axis, pairs_b)  9.57 us
    ppermute x13, starting transfers between devices, swap(): lax.ppermute(to_a, axis, pairs_a)  4.23 us
    unnamed x18, local copies, waits for them, and re-layouts  2.68 us
    ppermute x13, waiting for transfers between devices, swap(): lax.ppermute(to_a, axis, pairs_a)  1.5 us
  transfers between devices with their start and end apart: 27, of which 7 were waited for; matrix products, arithmetic and copies ran while one was open for 0% of the time, Pallas kernels for 17%

profile of v10, /device:TPU:0, one launch (start us, length us, event | category | flops | bytes accessed | tf_op | source)
XLA Modules:
  0.0 68.1 jit_solution(14447350641656895505)
XLA Ops:
  0.0 1.0 %slice_select_fusion = (f32[4,16,512]{2,1,0:T(8,128)S(1)}, f32[4,16,512]{2,1,0:T(8,128)S(1)}) fusion(f32[16,16,512]{2,1,0:T(8,128)} %refs_0_.4, pred[]{:T(512)S(6)} %eq.3), kind=kLoop, calls=%fused_computation | loop fusion | flops 65536 | bytes 524289 | tf_op jit(solution)/shard_map/jit(_where)/select_n | solution.py:585
  1.1 3.2 %collective-permute-start.1 = (f32[4,16,512]{2,1,0:T(8,128)S(1)}, f32[4,16,512]{2,1,0:T(8,128)S(1)}, u32[]{:S(2)}, u32[]{:S(2)}) collective-permute-start(f32[4,16,512]{2,1,0:T(8,128)S(1)} %get-tuple-element.91), channel_id=1, source_target_pairs={{0,96},{32,64},{64,32},{96,0},{1,97},{33,65},{65,33},{97,1},{2,98}... | collective-permute-start | bytes 393224 | tf_op jit(solution)/shard_map/ppermute | solution.py:100
  4.2 0.1 collective-permute-start
  4.4 1.7 %copy-done = f32[5,32,16,256]{3,2,1,0:T(8,128)S(1)} copy-done((f32[5,32,16,256]{3,2,1,0:T(8,128)S(1)}, f32[5,32,16,256]{3,2,1,0:T(8,128)}, u32[]{:S(2)}) %copy-start) | copy-done | bytes 2621464
  6.1 0.1 edges.1
  6.3 0.9 %copy-done.6 = s32[16,16,512]{2,1,0:T(8,128)S(1)} copy-done((s32[16,16,512]{2,1,0:T(8,128)S(1)}, s32[16,16,512]{2,1,0:T(8,128)}, u32[]{:S(2)}) %copy-start.6) | copy-done | bytes 524312
  7.2 0.5 filter_inner.1
  7.6 0.1 collective-permute-done.1.refs_3_
  7.7 1.5 %collective-permute-done.refs_2_ = f32[4,16,512]{2,1,0:T(8,128)S(1)} collective-permute-done((f32[4,16,512]{2,1,0:T(8,128)S(1)}, f32[4,16,512]{2,1,0:T(8,128)S(1)}, u32[]{:S(2)}, u32[]{:S(2)}) %collective-permute-start) | collective-permute-done | bytes 131104 | tf_op jit(solution)/shard_map/ppermute | solution.py:100
  9.2 0.2 filter_axial.1
  9.4 0.1 collective-permute-start.2
  9.5 6.3 %collective-permute-start.6 = (f32[16,8,256]{2,1,0:T(8,128)S(1)}, f32[16,8,256]{2,1,0:T(8,128)S(1)}, u32[]{:S(2)}, u32[]{:S(2)}) collective-permute-start(f32[16,8,256]{2,1,0:T(8,128)S(1)} %get-tuple-element.59), channel_id=1, source_target_pairs={{0,31},{1,2},{2,1},{3,4},{4,3},{5,6},{6,5},{7,8},{8,7},{9,10},{10,... | collective-permute-start | bytes 393224 | tf_op jit(solution)/shard_map/ppermute | solution.py:100
  15.8 0.0 collective-permute-start.3
  15.9 0.4 collective-permute-start.4
  16.2 1.1 %collective-permute-start.5 = (f32[15,16,256]{2,1,0:T(8,128)S(1)}, f32[15,16,256]{2,1,0:T(8,128)S(1)}, u32[]{:S(2)}, u32[]{:S(2)}) collective-permute-start(f32[15,16,256]{2,1,0:T(8,128)S(1)} %get-tuple-element.54), channel_id=1, source_target_pairs={{0,96},{32,64},{64,32},{96,0},{1,97},{33,65},{65,33},{97,1},{2,98}... | collective-permute-start | bytes 737288 | tf_op jit(solution)/shard_map/ppermute | solution.py:100
  17.4 0.3 route.1
  17.7 1.1 %filter_middle.1 = (f32[16,16,512]{2,1,0:T(8,128)S(1)}, f32[5,16,16,512]{3,2,1,0:T(8,128)S(1)}) custom-call(f32[16,16,512]{2,1,0:T(8,128)S(1)} %get-tuple-element.55.refs_2_.refs_0_, s32[16,16,512]{2,1,0:T(8,128)S(1)} %get-tuple-element.50.refs_1_, bf16[512,256]{1,0:T(8,128)(2,1)S(1)} %get-tuple-element.56.refs_2_.refs_4_), custom_call_target="tpu_custom_call" | custom-call | tf_op jit(solution)/shard_map/filter_middle/pallas_call | solution.py:115
  18.8 0.0 collective-permute-done.6.refs_3_
  18.8 0.0 collective-permute-done.2.refs_2_.refs_1_
  18.8 0.0 copy-start.1
  18.8 0.0 copy-start.3
  18.9 0.0 copy-start.4
  18.9 1.9 %filter_rest.1 = (f32[256,256]{1,0:T(8,128)S(1)}, f32[18,8,256]{2,1,0:T(8,128)S(1)}, f32[18,8,256]{2,1,0:T(8,128)S(1)}, f32[17,8,256]{2,1,0:T(8,128)S(1)}, f32[17,8,256]{2,1,0:T(8,128)S(1)}) custom-call(f32[16,16,512]{2,1,0:T(8,128)S(1)} %get-tuple-element.57.refs_0_, f32[5,16,16,512]{3,2,1,0:T(8,128)S(1)} %get-tuple-element.58.refs_1_, ...), custom_call_target="tpu_custom_call" | custom-call | flops 137438953472 | tf_op jit(solution)/shard_map/filter_rest/pallas_call | solution.py:115
  20.8 1.5 %collective-permute-start.7 = (f32[18,8,256]{2,1,0:T(8,128)S(1)}, f32[18,8,256]{2,1,0:T(8,128)S(1)}, u32[]{:S(2)}, u32[]{:S(2)}) collective-permute-start(f32[18,8,256]{2,1,0:T(8,128)S(1)} %get-tuple-element.65), channel_id=1, source_target_pairs={{0,32},{32,0},{64,96},{96,64},{1,33},{33,1},{65,97},{97,65},{2,34}... | collective-permute-start | bytes 442376 | tf_op jit(solution)/shard_map/ppermute | solution.py:100
  22.3 1.8 %collective-permute-start.8 = (f32[18,8,256]{2,1,0:T(8,128)S(1)}, f32[18,8,256]{2,1,0:T(8,128)S(1)}, u32[]{:S(2)}, u32[]{:S(2)}) collective-permute-start(f32[18,8,256]{2,1,0:T(8,128)S(1)} %get-tuple-element.66), channel_id=1, source_target_pairs={{0,96},{32,64},{64,32},{96,0},{1,97},{33,65},{65,33},{97,1},{2,98}... | collective-permute-start | bytes 442376 | tf_op jit(solution)/shard_map/ppermute | solution.py:100
  24.0 0.2 collective-permute-done.3.refs_2_
  24.2 3.8 %collective-permute-start.10 = (f32[17,8,256]{2,1,0:T(8,128)S(1)}, f32[17,8,256]{2,1,0:T(8,128)S(1)}, u32[]{:S(2)}, u32[]{:S(2)}) collective-permute-start(f32[17,8,256]{2,1,0:T(8,128)S(1)} %get-tuple-element.68), channel_id=1, source_target_pairs={{0,31},{1,2},{2,1},{3,4},{4,3},{5,6},{6,5},{7,8},{8,7},{9,10},{10,... | collective-permute-start | bytes 417800 | tf_op jit(solution)/shard_map/ppermute | solution.py:100
  28.0 1.6 %operator.1 = (f32[5,24,16,256]{3,2,1,0:T(8,128)S(1)}, f32[5,8,16,256]{3,2,1,0:T(8,128)S(1)}) custom-call(f32[5,32,16,256]{3,2,1,0:T(8,128)S(1)} %copy-done.1, f32[40,8,256]{2,1,0:T(8,128)S(1)} %collective-permute-done.2.refs_2_.refs_1_, f32[24,8,256]{2,1,0:T(8,128)S(1)} %collective-permute-done.3.refs_2_, ...), custom_call_target="tpu_custom_call" | custom-call | tf_op jit(solution)/shard_map/operator/pallas_call | solution.py:115
  29.6 0.0 collective-permute-done.9.refs_4_
  29.6 2.4 %collective-permute-done.10.refs_5_ = f32[17,8,256]{2,1,0:T(8,128)S(1)} collective-permute-done((f32[17,8,256]{2,1,0:T(8,128)S(1)}, f32[17,8,256]{2,1,0:T(8,128)S(1)}, u32[]{:S(2)}, u32[]{:S(2)}) %collective-permute-start.10) | collective-permute-done | bytes 139296 | tf_op jit(solution)/shard_map/ppermute | solution.py:100
  32.0 0.0 collective-permute-done.7.refs_2_
  32.1 0.0 collective-permute-done.8.refs_3_
  32.1 0.6 gather.1
  32.7 0.1 collective-permute-start.11
  32.7 3.8 %collective-permute-start.12 = (f32[24,8,256]{2,1,0:T(8,128)S(1)}, f32[24,8,256]{2,1,0:T(8,128)S(1)}, u32[]{:S(2)}, u32[]{:S(2)}) collective-permute-start(f32[24,8,256]{2,1,0:T(8,128)S(1)} %get-tuple-element.72), channel_id=1, source_target_pairs={{0,31},{1,2},{2,1},{3,4},{4,3},{5,6},{6,5},{7,8},{8,7},{9,10},{10,... | collective-permute-start | bytes 589832 | tf_op jit(solution)/shard_map/ppermute | solution.py:100
  36.6 0.4 collective-permute-start.13
  37.0 1.4 %collective-permute-start.14 = (f32[15,16,256]{2,1,0:T(8,128)S(1)}, f32[15,16,256]{2,1,0:T(8,128)S(1)}, u32[]{:S(2)}, u32[]{:S(2)}) collective-permute-start(f32[15,16,256]{2,1,0:T(8,128)S(1)} %get-tuple-element.75), channel_id=1, source_target_pairs={{0,96},{32,64},{64,32},{96,0},{1,97},{33,65},{65,33},{97,1},{2,98}... | collective-permute-start | bytes 737288 | tf_op jit(solution)/shard_map/ppermute | solution.py:100
  38.4 2.9 %collective-permute-done.12.refs_9_.refs_11_ = f32[24,8,256]{2,1,0:T(8,128)S(1)} collective-permute-done((f32[24,8,256]{2,1,0:T(8,128)S(1)}, f32[24,8,256]{2,1,0:T(8,128)S(1)}, u32[]{:S(2)}, u32[]{:S(2)}) %collective-permute-start.12) | collective-permute-done | bytes 196640 | tf_op jit(solution)/shard_map/ppermute | solution.py:100
  41.2 1.4 %stage_inner.2 = (f32[5,24,16,256]{3,2,1,0:T(8,128)S(1)}, f32[18,8,256]{2,1,0:T(8,128)S(1)}, f32[18,8,256]{2,1,0:T(8,128)S(1)}) custom-call(f32[5,24,16,256]{3,2,1,0:T(8,128)S(1)} %get-tuple-element.62.refs_6_.refs_0_.refs_4_.refs_2_.refs_3_, f32[5,8,16,256]{3,2,1,0:T(8,128)S(1)} %get-tuple-element.63.refs_7_.refs_1_.refs_5_.refs_3_.refs_4_, ...), custom_call_target="tpu_custom_call" | custom-call | flops 137438953472 | tf_op jit(solution)/shard_map/stage_inner/pallas_call | solution.py:115
  42.6 0.1 collective-permute-start.15
  42.7 4.0 %collective-permute-start.16 = (f32[18,8,256]{2,1,0:T(8,128)S(1)}, f32[18,8,256]{2,1,0:T(8,128)S(1)}, u32[]{:S(2)}, u32[]{:S(2)}) collective-permute-start(f32[18,8,256]{2,1,0:T(8,128)S(1)} %get-tuple-element.78), channel_id=1, source_target_pairs={{0,31},{1,2},{2,1},{3,4},{4,3},{5,6},{6,5},{7,8},{8,7},{9,10},{10,... | collective-permute-start | bytes 442376 | tf_op jit(solution)/shard_map/ppermute | solution.py:100
  46.7 0.6 stage_rim.2
  47.4 0.4 collective-permute-start.17
  47.8 1.4 %collective-permute-start.18 = (f32[15,16,256]{2,1,0:T(8,128)S(1)}, f32[15,16,256]{2,1,0:T(8,128)S(1)}, u32[]{:S(2)}, u32[]{:S(2)}) collective-permute-start(f32[15,16,256]{2,1,0:T(8,128)S(1)} %get-tuple-element.81), channel_id=1, source_target_pairs={{0,96},{32,64},{64,32},{96,0},{1,97},{33,65},{65,33},{97,1},{2,98}... | collective-permute-start | bytes 737288 | tf_op jit(solution)/shard_map/ppermute | solution.py:100
  49.2 0.0 collective-permute-start.19
  49.2 0.0 collective-permute-done.15.refs_6_
  49.2 0.8 %collective-permute-start.20 = (f32[6,8,256]{2,1,0:T(8,128)S(1)}, f32[6,8,256]{2,1,0:T(8,128)S(1)}, u32[]{:S(2)}, u32[]{:S(2)}) collective-permute-start(f32[6,8,256]{2,1,0:T(8,128)S(1)} %get-tuple-element.83), channel_id=1, source_target_pairs={{0,31},{1,2},{2,1},{3,4},{4,3},{5,6},{6,5},{7,8},{8,7},{9,10},{10,... | collective-permute-start | bytes 147464 | tf_op jit(solution)/shard_map/ppermute | solution.py:100
  50.1 0.8 %collective-permute-done.16.refs_7_ = f32[18,8,256]{2,1,0:T(8,128)S(1)} collective-permute-done((f32[18,8,256]{2,1,0:T(8,128)S(1)}, f32[18,8,256]{2,1,0:T(8,128)S(1)}, u32[]{:S(2)}, u32[]{:S(2)}) %collective-permute-start.16) | collective-permute-done | bytes 147488 | tf_op jit(solution)/shard_map/ppermute | solution.py:100
  50.9 1.4 %stage_inner.3 = (f32[5,24,16,256]{3,2,1,0:T(8,128)S(1)}, f32[18,8,256]{2,1,0:T(8,128)S(1)}, f32[18,8,256]{2,1,0:T(8,128)S(1)}) custom-call(f32[5,24,16,256]{3,2,1,0:T(8,128)S(1)} %get-tuple-element.73.refs_14_.refs_0_, f32[5,8,16,256]{3,2,1,0:T(8,128)S(1)} %get-tuple-element.76.refs_1_, ...), custom_call_target="tpu_custom_call" | custom-call | flops 2000000000 | tf_op jit(solution)/shard_map/stage_inner/pallas_call | solution.py:115
  52.2 0.1 collective-permute-start.21
  52.3 0.0 collective-permute-done.19.refs_8_
  52.3 3.8 %collective-permute-start.22 = (f32[18,8,256]{2,1,0:T(8,128)S(1)}, f32[18,8,256]{2,1,0:T(8,128)S(1)}, u32[]{:S(2)}, u32[]{:S(2)}) collective-permute-start(f32[18,8,256]{2,1,0:T(8,128)S(1)} %get-tuple-element.86), channel_id=1, source_target_pairs={{0,31},{1,2},{2,1},{3,4},{4,3},{5,6},{6,5},{7,8},{8,7},{9,10},{10,... | collective-permute-start | bytes 442376 | tf_op jit(solution)/shard_map/ppermute | solution.py:100
  56.2 0.0 collective-permute-done.20.refs_9_
  56.2 0.0 collective-permute-done.17.refs_6_
  56.2 0.0 collective-permute-done.18.refs_7_
  56.2 0.0 copy-start.2
  56.2 0.6 stage_rim.3
  56.8 1.1 %collective-permute-start.23 = (f32[15,16,256]{2,1,0:T(8,128)S(1)}, f32[15,16,256]{2,1,0:T(8,128)S(1)}, u32[]{:S(2)}, u32[]{:S(2)}) collective-permute-start(f32[15,16,256]{2,1,0:T(8,128)S(1)} %get-tuple-element.87), channel_id=1, source_target_pairs={{0,32},{32,0},{64,96},{96,64},{1,33},{33,1},{65,97},{97,65},{2,34}... | collective-permute-start | bytes 737288 | tf_op jit(solution)/shard_map/ppermute | solution.py:100
  57.9 1.7 %collective-permute-start.24 = (f32[15,16,256]{2,1,0:T(8,128)S(1)}, f32[15,16,256]{2,1,0:T(8,128)S(1)}, u32[]{:S(2)}, u32[]{:S(2)}) collective-permute-start(f32[15,16,256]{2,1,0:T(8,128)S(1)} %get-tuple-element.88), channel_id=1, source_target_pairs={{0,96},{32,64},{64,32},{96,0},{1,97},{33,65},{65,33},{97,1},{2,98}... | collective-permute-start | bytes 737288 | tf_op jit(solution)/shard_map/ppermute | solution.py:100
  59.7 0.0 collective-permute-start.25
  59.7 1.2 %collective-permute-start.26 = (f32[6,8,256]{2,1,0:T(8,128)S(1)}, f32[6,8,256]{2,1,0:T(8,128)S(1)}, u32[]{:S(2)}, u32[]{:S(2)}) collective-permute-start(f32[6,8,256]{2,1,0:T(8,128)S(1)} %get-tuple-element.90), channel_id=1, source_target_pairs={{0,31},{1,2},{2,1},{3,4},{4,3},{5,6},{6,5},{7,8},{8,7},{9,10},{10,... | collective-permute-start | bytes 147464 | tf_op jit(solution)/shard_map/ppermute | solution.py:100
  60.8 2.3 %final_inner.1.refs_0_ = f32[5,32,16,256]{3,2,1,0:T(8,128)} custom-call(f32[5,24,16,256]{3,2,1,0:T(8,128)S(1)} %get-tuple-element.79.refs_12_.refs_0_.refs_1_, f32[5,8,16,256]{3,2,1,0:T(8,128)S(1)} %get-tuple-element.84.refs_1_.refs_2_, f32[5,24,16,256]{3,2,1,0:T(8,128)S(1)} %get-tuple-element.62.refs_6_.refs_0_.refs_4_.refs_2_.refs_3_, ...), custom_call_target="tpu_custom_call" | custom-call | flops 2000000000 | tf_op jit(solution)/shard_map/final_inner/pallas_call | solution.py:115
  63.2 3.3 %collective-permute-done.26.refs_11_ = f32[6,8,256]{2,1,0:T(8,128)S(1)} collective-permute-done((f32[6,8,256]{2,1,0:T(8,128)S(1)}, f32[6,8,256]{2,1,0:T(8,128)S(1)}, u32[]{:S(2)}, u32[]{:S(2)}) %collective-permute-start.26) | collective-permute-done | bytes 49184 | tf_op jit(solution)/shard_map/ppermute | solution.py:100
  66.5 1.5 %final_rim.1 = f32[5,32,16,256]{3,2,1,0:T(8,128)} custom-call(f32[5,32,16,256]{3,2,1,0:T(8,128)} %final_inner.1.refs_0_, f32[5,24,16,256]{3,2,1,0:T(8,128)S(1)} %get-tuple-element.79.refs_12_.refs_0_.refs_1_, f32[5,8,16,256]{3,2,1,0:T(8,128)S(1)} %get-tuple-element.84.refs_1_.refs_2_, ...), custom_call_target="tpu_custom_call", output_to_operand_aliasing={{}: (0, {})} | custom-call | tf_op jit(solution)/shard_map/final_rim/pallas_call | solution.py:115
  (23 shorter events, 0.1 us)
Async XLA Ops:
  0.0 6.2 %copy-start.5 = (f32[16,16,512]{2,1,0:T(8,128)S(1)}, f32[16,16,512]{2,1,0:T(8,128)}, u32[]{:S(2)}) copy-start(f32[16,16,512]{2,1,0:T(8,128)} %refs_0_.4) | copy-start | bytes 1572868
  1.1 6.7 %collective-permute-start.1 = (f32[4,16,512]{2,1,0:T(8,128)S(1)}, f32[4,16,512]{2,1,0:T(8,128)S(1)}, u32[]{:S(2)}, u32[]{:S(2)}) collective-permute-start(f32[4,16,512]{2,1,0:T(8,128)S(1)} %get-tuple-element.91), channel_id=1, source_target_pairs={{0,96},{32,64},{64,32},{96,0},{1,97},{33,65},{65,33},{97,1},{2,98}... | collective-permute-start | bytes 393224 | tf_op jit(solution)/shard_map/ppermute | solution.py:100
  4.2 5.0 %collective-permute-start = (f32[4,16,512]{2,1,0:T(8,128)S(1)}, f32[4,16,512]{2,1,0:T(8,128)S(1)}, u32[]{:S(2)}, u32[]{:S(2)}) collective-permute-start(f32[4,16,512]{2,1,0:T(8,128)S(1)} %get-tuple-element.92.refs_1_), channel_id=1, source_target_pairs={{0,32},{32,0},{64,96},{96,64},{1,33},{33,1},{65,97},{97,65},{2,34}... | collective-permute-start | bytes 393224 | tf_op jit(solution)/shard_map/ppermute | solution.py:100
  4.4 1.7 %copy-start = (f32[5,32,16,256]{3,2,1,0:T(8,128)S(1)}, f32[5,32,16,256]{3,2,1,0:T(8,128)}, u32[]{:S(2)}) copy-start(f32[5,32,16,256]{3,2,1,0:T(8,128)} %refs_7_.1) | copy-start | bytes 7864324
  6.1 1.0 %copy-start.6 = (s32[16,16,512]{2,1,0:T(8,128)S(1)}, s32[16,16,512]{2,1,0:T(8,128)}, u32[]{:S(2)}) copy-start(s32[16,16,512]{2,1,0:T(8,128)} %refs_1_.1) | copy-start | bytes 1572868
  6.1 11.2 %copy-start.7 = (s32[256]{0:T(256)S(1)}, s32[256]{0:T(256)}, u32[]{:S(2)}) copy-start(s32[256]{0:T(256)} %param.9) | copy-start | bytes 3076
  6.1 11.2 %copy-start.8 = (s32[256]{0:T(256)S(1)}, s32[256]{0:T(256)}, u32[]{:S(2)}) copy-start(s32[256]{0:T(256)} %param.10) | copy-start | bytes 3076
  9.4 9.4 %collective-permute-start.2 = (f32[40,8,256]{2,1,0:T(8,128)S(1)}, f32[40,8,256]{2,1,0:T(8,128)S(1)}, u32[]{:S(2)}, u32[]{:S(2)}) collective-permute-start(f32[40,8,256]{2,1,0:T(8,128)S(1)} %get-tuple-element.51), channel_id=1, source_target_pairs={{0,1},{1,0},{2,3},{3,2},{4,5},{5,4},{6,7},{7,6},{8,9},{9,8},{10,11... | collective-permute-start | bytes 983048 | tf_op jit(solution)/shard_map/ppermute | solution.py:100
  9.5 9.3 %collective-permute-start.6 = (f32[16,8,256]{2,1,0:T(8,128)S(1)}, f32[16,8,256]{2,1,0:T(8,128)S(1)}, u32[]{:S(2)}, u32[]{:S(2)}) collective-permute-start(f32[16,8,256]{2,1,0:T(8,128)S(1)} %get-tuple-element.59), channel_id=1, source_target_pairs={{0,31},{1,2},{2,1},{3,4},{4,3},{5,6},{6,5},{7,8},{8,7},{9,10},{10,... | collective-permute-start | bytes 393224 | tf_op jit(solution)/shard_map/ppermute | solution.py:100
  15.8 8.4 %collective-permute-start.3 = (f32[24,8,256]{2,1,0:T(8,128)S(1)}, f32[24,8,256]{2,1,0:T(8,128)S(1)}, u32[]{:S(2)}, u32[]{:S(2)}) collective-permute-start(f32[24,8,256]{2,1,0:T(8,128)S(1)} %get-tuple-element.52), channel_id=1, source_target_pairs={{0,31},{1,2},{2,1},{3,4},{4,3},{5,6},{6,5},{7,8},{8,7},{9,10},{10,... | collective-permute-start | bytes 589832 | tf_op jit(solution)/shard_map/ppermute | solution.py:106
  15.9 8.4 %collective-permute-start.4 = (f32[15,16,256]{2,1,0:T(8,128)S(1)}, f32[15,16,256]{2,1,0:T(8,128)S(1)}, u32[]{:S(2)}, u32[]{:S(2)}) collective-permute-start(f32[15,16,256]{2,1,0:T(8,128)S(1)} %get-tuple-element.53), channel_id=1, source_target_pairs={{0,32},{32,0},{64,96},{96,64},{1,33},{33,1},{65,97},{97,65},{2,34}... | collective-permute-start | bytes 737288 | tf_op jit(solution)/shard_map/ppermute | solution.py:100
  16.2 11.8 %collective-permute-start.5 = (f32[15,16,256]{2,1,0:T(8,128)S(1)}, f32[15,16,256]{2,1,0:T(8,128)S(1)}, u32[]{:S(2)}, u32[]{:S(2)}) collective-permute-start(f32[15,16,256]{2,1,0:T(8,128)S(1)} %get-tuple-element.54), channel_id=1, source_target_pairs={{0,96},{32,64},{64,32},{96,0},{1,97},{33,65},{65,33},{97,1},{2,98}... | collective-permute-start | bytes 737288 | tf_op jit(solution)/shard_map/ppermute | solution.py:100
  18.8 9.2 %copy-start.1 = (f32[5,32,16,256]{3,2,1,0:T(8,128)S(1)}, f32[5,32,16,256]{3,2,1,0:T(8,128)}, u32[]{:S(2)}) copy-start(f32[5,32,16,256]{3,2,1,0:T(8,128)} %refs_7_.1) | copy-start | bytes 7864324
  18.8 9.2 %copy-start.3 = (bf16[2,2,256,256]{3,2,1,0:T(8,128)(2,1)S(1)}, bf16[2,2,256,256]{3,2,1,0:T(8,128)(2,1)}, u32[]{:S(2)}) copy-start(bf16[2,2,256,256]{3,2,1,0:T(8,128)(2,1)} %constant.17.clone.refs_6_.refs_11_.refs_13_.refs_9_.refs_10_) | copy-start | bytes 1572868
  18.9 9.2 %copy-start.4 = (bf16[2,2,128,224]{3,2,1,0:T(8,128)(2,1)S(1)}, bf16[2,2,128,224]{3,2,1,0:T(8,128)(2,1)}, u32[]{:S(2)}) copy-start(bf16[2,2,128,224]{3,2,1,0:T(8,128)(2,1)} %constant.16.clone.refs_5_.refs_10_.refs_12_.refs_8_.refs_9_) | copy-start | bytes 688132
  20.8 11.3 %collective-permute-start.7 = (f32[18,8,256]{2,1,0:T(8,128)S(1)}, f32[18,8,256]{2,1,0:T(8,128)S(1)}, u32[]{:S(2)}, u32[]{:S(2)}) collective-permute-start(f32[18,8,256]{2,1,0:T(8,128)S(1)} %get-tuple-element.65), channel_id=1, source_target_pairs={{0,32},{32,0},{64,96},{96,64},{1,33},{33,1},{65,97},{97,65},{2,34}... | collective-permute-start | bytes 442376 | tf_op jit(solution)/shard_map/ppermute | solution.py:100
  22.3 9.8 %collective-permute-start.8 = (f32[18,8,256]{2,1,0:T(8,128)S(1)}, f32[18,8,256]{2,1,0:T(8,128)S(1)}, u32[]{:S(2)}, u32[]{:S(2)}) collective-permute-start(f32[18,8,256]{2,1,0:T(8,128)S(1)} %get-tuple-element.66), channel_id=1, source_target_pairs={{0,96},{32,64},{64,32},{96,0},{1,97},{33,65},{65,33},{97,1},{2,98}... | collective-permute-start | bytes 442376 | tf_op jit(solution)/shard_map/ppermute | solution.py:100
  24.2 5.4 %collective-permute-start.9 = (f32[17,8,256]{2,1,0:T(8,128)S(1)}, f32[17,8,256]{2,1,0:T(8,128)S(1)}, u32[]{:S(2)}, u32[]{:S(2)}) collective-permute-start(f32[17,8,256]{2,1,0:T(8,128)S(1)} %get-tuple-element.67), channel_id=1, source_target_pairs={{0,1},{1,0},{2,3},{3,2},{4,5},{5,4},{6,7},{7,6},{8,9},{9,8},{10,11... | collective-permute-start | bytes 417800 | tf_op jit(solution)/shard_map/ppermute | solution.py:100
  24.2 7.8 %collective-permute-start.10 = (f32[17,8,256]{2,1,0:T(8,128)S(1)}, f32[17,8,256]{2,1,0:T(8,128)S(1)}, u32[]{:S(2)}, u32[]{:S(2)}) collective-permute-start(f32[17,8,256]{2,1,0:T(8,128)S(1)} %get-tuple-element.68), channel_id=1, source_target_pairs={{0,31},{1,2},{2,1},{3,4},{4,3},{5,6},{6,5},{7,8},{8,7},{9,10},{10,... | collective-permute-start | bytes 417800 | tf_op jit(solution)/shard_map/ppermute | solution.py:100
  32.7 5.7 %collective-permute-start.11 = (f32[24,8,256]{2,1,0:T(8,128)S(1)}, f32[24,8,256]{2,1,0:T(8,128)S(1)}, u32[]{:S(2)}, u32[]{:S(2)}) collective-permute-start(f32[24,8,256]{2,1,0:T(8,128)S(1)} %get-tuple-element.71), channel_id=1, source_target_pairs={{0,1},{1,0},{2,3},{3,2},{4,5},{5,4},{6,7},{7,6},{8,9},{9,8},{10,11... | collective-permute-start | bytes 589832 | tf_op jit(solution)/shard_map/ppermute | solution.py:100
  32.7 8.5 %collective-permute-start.12 = (f32[24,8,256]{2,1,0:T(8,128)S(1)}, f32[24,8,256]{2,1,0:T(8,128)S(1)}, u32[]{:S(2)}, u32[]{:S(2)}) collective-permute-start(f32[24,8,256]{2,1,0:T(8,128)S(1)} %get-tuple-element.72), channel_id=1, source_target_pairs={{0,31},{1,2},{2,1},{3,4},{4,3},{5,6},{6,5},{7,8},{8,7},{9,10},{10,... | collective-permute-start | bytes 589832 | tf_op jit(solution)/shard_map/ppermute | solution.py:100
  36.6 10.1 %collective-permute-start.13 = (f32[15,16,256]{2,1,0:T(8,128)S(1)}, f32[15,16,256]{2,1,0:T(8,128)S(1)}, u32[]{:S(2)}, u32[]{:S(2)}) collective-permute-start(f32[15,16,256]{2,1,0:T(8,128)S(1)} %get-tuple-element.74), channel_id=1, source_target_pairs={{0,32},{32,0},{64,96},{96,64},{1,33},{33,1},{65,97},{97,65},{2,34}... | collective-permute-start | bytes 737288 | tf_op jit(solution)/shard_map/ppermute | solution.py:100
  37.0 9.8 %collective-permute-start.14 = (f32[15,16,256]{2,1,0:T(8,128)S(1)}, f32[15,16,256]{2,1,0:T(8,128)S(1)}, u32[]{:S(2)}, u32[]{:S(2)}) collective-permute-start(f32[15,16,256]{2,1,0:T(8,128)S(1)} %get-tuple-element.75), channel_id=1, source_target_pairs={{0,96},{32,64},{64,32},{96,0},{1,97},{33,65},{65,33},{97,1},{2,98}... | collective-permute-start | bytes 737288 | tf_op jit(solution)/shard_map/ppermute | solution.py:100
  42.6 6.6 %collective-permute-start.15 = (f32[18,8,256]{2,1,0:T(8,128)S(1)}, f32[18,8,256]{2,1,0:T(8,128)S(1)}, u32[]{:S(2)}, u32[]{:S(2)}) collective-permute-start(f32[18,8,256]{2,1,0:T(8,128)S(1)} %get-tuple-element.77), channel_id=1, source_target_pairs={{0,1},{1,0},{2,3},{3,2},{4,5},{5,4},{6,7},{7,6},{8,9},{9,8},{10,11... | collective-permute-start | bytes 442376 | tf_op jit(solution)/shard_map/ppermute | solution.py:100
  42.7 8.1 %collective-permute-start.16 = (f32[18,8,256]{2,1,0:T(8,128)S(1)}, f32[18,8,256]{2,1,0:T(8,128)S(1)}, u32[]{:S(2)}, u32[]{:S(2)}) collective-permute-start(f32[18,8,256]{2,1,0:T(8,128)S(1)} %get-tuple-element.78), channel_id=1, source_target_pairs={{0,31},{1,2},{2,1},{3,4},{4,3},{5,6},{6,5},{7,8},{8,7},{9,10},{10,... | collective-permute-start | bytes 442376 | tf_op jit(solution)/shard_map/ppermute | solution.py:100
  47.4 8.8 %collective-permute-start.17 = (f32[15,16,256]{2,1,0:T(8,128)S(1)}, f32[15,16,256]{2,1,0:T(8,128)S(1)}, u32[]{:S(2)}, u32[]{:S(2)}) collective-permute-start(f32[15,16,256]{2,1,0:T(8,128)S(1)} %get-tuple-element.80), channel_id=1, source_target_pairs={{0,32},{32,0},{64,96},{96,64},{1,33},{33,1},{65,97},{97,65},{2,34}... | collective-permute-start | bytes 737288 | tf_op jit(solution)/shard_map/ppermute | solution.py:100
  47.8 8.4 %collective-permute-start.18 = (f32[15,16,256]{2,1,0:T(8,128)S(1)}, f32[15,16,256]{2,1,0:T(8,128)S(1)}, u32[]{:S(2)}, u32[]{:S(2)}) collective-permute-start(f32[15,16,256]{2,1,0:T(8,128)S(1)} %get-tuple-element.81), channel_id=1, source_target_pairs={{0,96},{32,64},{64,32},{96,0},{1,97},{33,65},{65,33},{97,1},{2,98}... | collective-permute-start | bytes 737288 | tf_op jit(solution)/shard_map/ppermute | solution.py:100
  49.2 3.1 %collective-permute-start.19 = (f32[6,8,256]{2,1,0:T(8,128)S(1)}, f32[6,8,256]{2,1,0:T(8,128)S(1)}, u32[]{:S(2)}, u32[]{:S(2)}) collective-permute-start(f32[6,8,256]{2,1,0:T(8,128)S(1)} %get-tuple-element.82), channel_id=1, source_target_pairs={{0,1},{1,0},{2,3},{3,2},{4,5},{5,4},{6,7},{7,6},{8,9},{9,8},{10,11... | collective-permute-start | bytes 147464 | tf_op jit(solution)/shard_map/ppermute | solution.py:100
  49.2 7.0 %collective-permute-start.20 = (f32[6,8,256]{2,1,0:T(8,128)S(1)}, f32[6,8,256]{2,1,0:T(8,128)S(1)}, u32[]{:S(2)}, u32[]{:S(2)}) collective-permute-start(f32[6,8,256]{2,1,0:T(8,128)S(1)} %get-tuple-element.83), channel_id=1, source_target_pairs={{0,31},{1,2},{2,1},{3,4},{4,3},{5,6},{6,5},{7,8},{8,7},{9,10},{10,... | collective-permute-start | bytes 147464 | tf_op jit(solution)/shard_map/ppermute | solution.py:100
  52.2 7.4 %collective-permute-start.21 = (f32[18,8,256]{2,1,0:T(8,128)S(1)}, f32[18,8,256]{2,1,0:T(8,128)S(1)}, u32[]{:S(2)}, u32[]{:S(2)}) collective-permute-start(f32[18,8,256]{2,1,0:T(8,128)S(1)} %get-tuple-element.85), channel_id=1, source_target_pairs={{0,1},{1,0},{2,3},{3,2},{4,5},{5,4},{6,7},{7,6},{8,9},{9,8},{10,11... | collective-permute-start | bytes 442376 | tf_op jit(solution)/shard_map/ppermute | solution.py:100
  52.3 8.5 %collective-permute-start.22 = (f32[18,8,256]{2,1,0:T(8,128)S(1)}, f32[18,8,256]{2,1,0:T(8,128)S(1)}, u32[]{:S(2)}, u32[]{:S(2)}) collective-permute-start(f32[18,8,256]{2,1,0:T(8,128)S(1)} %get-tuple-element.86), channel_id=1, source_target_pairs={{0,31},{1,2},{2,1},{3,4},{4,3},{5,6},{6,5},{7,8},{8,7},{9,10},{10,... | collective-permute-start | bytes 442376 | tf_op jit(solution)/shard_map/ppermute | solution.py:100
  56.2 4.6 %copy-start.2 = (f32[5,32,16,256]{3,2,1,0:T(8,128)S(1)}, f32[5,32,16,256]{3,2,1,0:T(8,128)}, u32[]{:S(2)}) copy-start(f32[5,32,16,256]{3,2,1,0:T(8,128)} %refs_7_.1) | copy-start | bytes 7864324
  56.8 9.7 %collective-permute-start.23 = (f32[15,16,256]{2,1,0:T(8,128)S(1)}, f32[15,16,256]{2,1,0:T(8,128)S(1)}, u32[]{:S(2)}, u32[]{:S(2)}) collective-permute-start(f32[15,16,256]{2,1,0:T(8,128)S(1)} %get-tuple-element.87), channel_id=1, source_target_pairs={{0,32},{32,0},{64,96},{96,64},{1,33},{33,1},{65,97},{97,65},{2,34}... | collective-permute-start | bytes 737288 | tf_op jit(solution)/shard_map/ppermute | solution.py:100
  57.9 8.6 %collective-permute-start.24 = (f32[15,16,256]{2,1,0:T(8,128)S(1)}, f32[15,16,256]{2,1,0:T(8,128)S(1)}, u32[]{:S(2)}, u32[]{:S(2)}) collective-permute-start(f32[15,16,256]{2,1,0:T(8,128)S(1)} %get-tuple-element.88), channel_id=1, source_target_pairs={{0,96},{32,64},{64,32},{96,0},{1,97},{33,65},{65,33},{97,1},{2,98}... | collective-permute-start | bytes 737288 | tf_op jit(solution)/shard_map/ppermute | solution.py:100
  59.7 3.5 %collective-permute-start.25 = (f32[6,8,256]{2,1,0:T(8,128)S(1)}, f32[6,8,256]{2,1,0:T(8,128)S(1)}, u32[]{:S(2)}, u32[]{:S(2)}) collective-permute-start(f32[6,8,256]{2,1,0:T(8,128)S(1)} %get-tuple-element.89), channel_id=1, source_target_pairs={{0,1},{1,0},{2,3},{3,2},{4,5},{5,4},{6,7},{7,6},{8,9},{9,8},{10,11... | collective-permute-start | bytes 147464 | tf_op jit(solution)/shard_map/ppermute | solution.py:100
  59.7 6.8 %collective-permute-start.26 = (f32[6,8,256]{2,1,0:T(8,128)S(1)}, f32[6,8,256]{2,1,0:T(8,128)S(1)}, u32[]{:S(2)}, u32[]{:S(2)}) collective-permute-start(f32[6,8,256]{2,1,0:T(8,128)S(1)} %get-tuple-element.90), channel_id=1, source_target_pairs={{0,31},{1,2},{2,1},{3,4},{4,3},{5,6},{6,5},{7,8},{8,7},{9,10},{10,... | collective-permute-start | bytes 147464 | tf_op jit(solution)/shard_map/ppermute | solution.py:100

commit v11 on v9

--- a/solution.py
+++ b/solution.py
@@ -24,6 +24,7 @@
 PARAMS = pltpu.CompilerParams(vmem_limit_bytes=24 * 1024 * 1024)
 GROUP = 8
 RIM = 4
+MORE = 2_500_000_000
 SOME = 2_000_000_000
 COST = 1 << 37
 
@@ -240,6 +241,12 @@
             weight_ref[k, x] = w[k]
 
 
+def unpack_body(got_ref, out_ref):
+    half = out_ref.shape[0]
+    for y in range(half):
+        out_ref[y] = jnp.concatenate([got_ref[y], got_ref[half + y]], axis=1)
+
+
 def second_body(
     partial_ref, weight_ref, got_a_ref, got_b_ref, pick_ref, cells_ref,
     own_ref, to_xa, to_xb, to_za, to_zb, fine_hi, fine_lo,
@@ -251,7 +258,7 @@
     row = lax.broadcasted_iota(jnp.int32, (8, fine), 0)
     for x in range(rows):
         y = x % half
-        got_a, got_b = [jnp.concatenate([got[y], got[half + y]], axis=1) for got in (got_a_ref, got_b_ref)]
+        got_a, got_b = jnp.concatenate([got_a_ref[y], got_a_ref[half + y]], axis=1), got_b_ref[y]
         before, after = jnp.where(even, got_b, got_a), jnp.where(even, got_a, got_b)
         if x < half:
             before = pltpu.roll(before, 4, 0)
@@ -290,7 +297,7 @@
 
 
 def gather_body(
-    binned_ref, own_ref, xa, xb, za, zb, k_mid, k_rim, p_mid, p_rim, to_xa, to_xb, to_za, to_zb
+    binned_ref, own_ref, xa, xb, zb, za, k_mid, k_rim, p_mid, p_rim, to_xa, to_xb, to_za, to_zb
 ):
     mid, cols, radial = p_mid.shape
     cells = (mid + 2 * RIM) * cols
@@ -505,7 +512,7 @@
     apply_operator(level, [*range(k_mid.shape[1] // GROUP), None], za, zb, tmat, rmat, finish, halo)
 
 
-def inner_stage_body(factor, level, base, za, zb, tmat, rmat, out_mid, to_za, to_zb):
+def inner_stage_body(factor, level, base, zb, za, tmat, rmat, out_mid, to_za, to_zb):
     def finish(x, tend):
         for f in range(5):
             out_mid[f, x - RIM] = base.row(f, x) + factor * tend[f]
@@ -514,7 +521,7 @@
     write_z(Parts(out_mid, None, rows=level.rows), range(RIM, level.rows - RIM, 4), to_za, to_zb)
 
 
-def rim_stage_body(factor, level, base, xa, xb, za, zb, tmat, rmat, out_rim, to_xa, to_xb, to_za, to_zb, halo):
+def rim_stage_body(factor, level, base, xa, xb, zb, za, tmat, rmat, out_rim, to_xa, to_xb, to_za, to_zb, halo):
     fill_halo(halo, xa, xb)
     out = Parts(None, out_rim, rows=level.rows)
 
@@ -535,7 +542,7 @@
     return finish
 
 
-def inner_last_body(level, k, fields, za, zb, tmat, rmat, out, result, sems):
+def inner_last_body(level, k, fields, zb, za, tmat, rmat, out, result, sems):
     def store(f, x, value):
         result[f, x - RIM] = value
 
@@ -553,7 +560,7 @@
         copy(g).wait()
 
 
-def rim_last_body(level, k, fields, xa, xb, za, zb, tmat, rmat, out, halo, result, sems):
+def rim_last_body(level, k, fields, xa, xb, zb, za, tmat, rmat, out, halo, result, sems):
     rows = level.rows
     fill_halo(halo, xa, xb)
 
@@ -616,6 +623,9 @@
         name="filter_middle",
         after=[pick],
     )
+    (got_b,) = full_specs(
+        unpack_body, [((px // 2, 8, fine), F32)], [got_b], name="unpack", after=[weights], cost=MORE
+    )
     tiles = most // 8 + 1
     packet, packet_z = ((tiles, 8, radial), F32), ((tiles + 1, 8, radial), F32)
     binned, xa, xb, za, zb = full_specs(
@@ -626,7 +636,8 @@
         name="filter_rest",
         cost=COST,
     )
-    packets = (*swap(xa, xb, "ax"), *swap(za, zb, "az"))
+    za, zb = swap(za, zb, "az")
+    packets = (*swap(xa, xb, "ax"), zb, za)
 
     tmat = jnp.asarray(azimuth_matrices(ca))
     rmat = jnp.asarray(radial_matrices(float(ca * n_az), radial))
@@ -653,7 +664,7 @@
             inner_stage_body(factor, Parts(*refs[:size]), Parts(*refs[size : size + 4]), *refs[size + 4 :])
 
         new_mid, to_za, to_zb = full_specs(
-            body, [mid, inner_z, inner_z], [*level, *k, za, zb, tmat, rmat], name="stage_inner", cost=COST if level is k else SOME
+            body, [mid, inner_z, inner_z], [*level, *k, zb, za, tmat, rmat], name="stage_inner", cost=COST if level is k else SOME
         )
         za, zb = swap(to_za, to_zb, "az")
 
@@ -663,7 +674,7 @@
         new_rim, to_xa, to_xb, to_za, to_zb = full_specs(
             body,
             [rim, send_x, send_x, rim_z, rim_z],
-            [*level, *k, xa, xb, rim_a, rim_b, tmat, rmat],
+            [*level, *k, xa, xb, rim_b, rim_a, tmat, rmat],
             [halo],
             name="stage_rim",
             after=[new_mid],
@@ -680,7 +691,7 @@
     (out,) = full_specs(
         body,
         [whole],
-        [*level, *k, fields, za, zb, tmat, rmat],
+        [*level, *k, fields, zb, za, tmat, rmat],
         [mid, pltpu.SemaphoreType.DMA((inner // GROUP,))],
         name="final_inner",
         out_specs=[ANY],
@@ -693,7 +704,7 @@
     (out,) = full_specs(
         body,
         [whole],
-        [out, *level, *k, fields, xa, xb, rim_a, rim_b, tmat, rmat],
+        [out, *level, *k, fields, xa, xb, rim_b, rim_a, tmat, rmat],
         [halo, rim, pltpu.SemaphoreType.DMA((2,))],
         name="final_rim",
         in_specs=[ANY] + [VM] * 13,

time: 66.9 us -> 66.1 us (0.988)
  starting transfers between devices: 36.4 us -> 32 us
  waiting for transfers between devices: 12.1 us -> 15.6 us
    ppermute x13, starting transfers between devices: 32.4 us -> 27.1 us  [swap(): lax.ppermute(to_b, axis, pairs_b)]
    ppermute x13, waiting for transfers between devices: 10.1 us -> 12.2 us  [swap(): lax.ppermute(to_b, axis, pairs_b)]
    ppermute x1, starting transfers between devices: 0.03 us -> 1.96 us  [swap_b(): return (lax.ppermute(value, axis, pairs),)]
    ppermute x13, waiting for transfers between devices: 2.08 us -> 3.42 us  [swap(): lax.ppermute(to_a, axis, pairs_a)]
    ppermute x13, starting transfers between devices: 3.96 us -> 2.92 us  [swap(): lax.ppermute(to_a, axis, pairs_a)]
    pallas_call x14 -> x15, Pallas kernels: 14 us -> 14 us  [full_specs(): pl.pallas_call(run, out_shape=[jax.ShapeDtypeStruct(s, d) for s, d in out...]
  transfers between devices with their start and end apart: 27 -> 27, of which waited for: 9 -> 11; matrix products, arithmetic and copies ran while one was open for 0% -> 0% of each run, Pallas kernels for 18% -> 18%
where the time goes in v11:
time: 66.1 us; the launch traced here: 65.7 us
  starting transfers between devices  32 us (48%)
  waiting for transfers between devices  15.6 us (24%)
  Pallas kernels  14 us (21%)
  local copies, waits for them, and re-layouts  2.68 us (4%)
  other arithmetic  1.05 us (2%)
    ppermute x13, starting transfers between devices, swap(): lax.ppermute(to_b, axis, pairs_b)  27.1 us
    pallas_call x15, Pallas kernels, full_specs(): pl.pallas_call(run, out_shape=[jax.ShapeDtypeStruct(s, d) for s, d in out...  14 us
    ppermute x13, waiting for transfers between devices, swap(): lax.ppermute(to_b, axis, pairs_b)  12.2 us
    ppermute x13, waiting for transfers between devices, swap(): lax.ppermute(to_a, axis, pairs_a)  3.42 us
    ppermute x13, starting transfers between devices, swap(): lax.ppermute(to_a, axis, pairs_a)  2.92 us
    unnamed x18, local copies, waits for them, and re-layouts  2.68 us
    ppermute x1, starting transfers between devices, swap_b(): return (lax.ppermute(value, axis, pairs),)  1.96 us
  transfers between devices with their start and end apart: 27, of which 11 were waited for; matrix products, arithmetic and copies ran while one was open for 0% of the time, Pallas kernels for 18%

profile of v11, /device:TPU:0, one launch (start us, length us, event | category | flops | bytes accessed | tf_op | source)
XLA Modules:
  0.0 65.7 jit_solution(9719472901719879057)
XLA Ops:
  0.0 1.0 %slice_select_fusion = (f32[4,16,512]{2,1,0:T(8,128)S(1)}, f32[4,16,512]{2,1,0:T(8,128)S(1)}) fusion(f32[16,16,512]{2,1,0:T(8,128)} %refs_0_.4, pred[]{:T(512)S(6)} %eq.3), kind=kLoop, calls=%fused_computation | loop fusion | flops 65536 | bytes 524289 | tf_op jit(solution)/shard_map/jit(_where)/select_n | solution.py:592
  1.1 3.2 %collective-permute-start.1 = (f32[4,16,512]{2,1,0:T(8,128)S(1)}, f32[4,16,512]{2,1,0:T(8,128)S(1)}, u32[]{:S(2)}, u32[]{:S(2)}) collective-permute-start(f32[4,16,512]{2,1,0:T(8,128)S(1)} %get-tuple-element.91), channel_id=1, source_target_pairs={{0,96},{32,64},{64,32},{96,0},{1,97},{33,65},{65,33},{97,1},{2,98}... | collective-permute-start | bytes 393224 | tf_op jit(solution)/shard_map/ppermute | solution.py:101
  4.2 0.1 collective-permute-start
  4.4 1.7 %copy-done = f32[5,32,16,256]{3,2,1,0:T(8,128)S(1)} copy-done((f32[5,32,16,256]{3,2,1,0:T(8,128)S(1)}, f32[5,32,16,256]{3,2,1,0:T(8,128)}, u32[]{:S(2)}) %copy-start) | copy-done | bytes 2621464
  6.1 0.1 edges.1
  6.3 0.9 %copy-done.6 = s32[16,16,512]{2,1,0:T(8,128)S(1)} copy-done((s32[16,16,512]{2,1,0:T(8,128)S(1)}, s32[16,16,512]{2,1,0:T(8,128)}, u32[]{:S(2)}) %copy-start.6) | copy-done | bytes 524312
  7.2 0.5 filter_inner.1
  7.6 0.1 collective-permute-done.1.refs_3_
  7.7 1.5 %collective-permute-done.refs_2_ = f32[4,16,512]{2,1,0:T(8,128)S(1)} collective-permute-done((f32[4,16,512]{2,1,0:T(8,128)S(1)}, f32[4,16,512]{2,1,0:T(8,128)S(1)}, u32[]{:S(2)}, u32[]{:S(2)}) %collective-permute-start) | collective-permute-done | bytes 131104 | tf_op jit(solution)/shard_map/ppermute | solution.py:101
  9.2 0.2 filter_axial.1
  9.4 4.6 %collective-permute-start.6 = (f32[16,8,256]{2,1,0:T(8,128)S(1)}, f32[16,8,256]{2,1,0:T(8,128)S(1)}, u32[]{:S(2)}, u32[]{:S(2)}) collective-permute-start(f32[16,8,256]{2,1,0:T(8,128)S(1)} %get-tuple-element.59), channel_id=1, source_target_pairs={{0,31},{1,2},{2,1},{3,4},{4,3},{5,6},{6,5},{7,8},{8,7},{9,10},{10,... | collective-permute-start | bytes 393224 | tf_op jit(solution)/shard_map/ppermute | solution.py:101
  14.0 0.0 collective-permute-start.2
  14.0 2.0 %collective-permute-start.3 = (f32[24,8,256]{2,1,0:T(8,128)S(1)}, f32[24,8,256]{2,1,0:T(8,128)S(1)}, u32[]{:S(2)}, u32[]{:S(2)}) collective-permute-start(f32[24,8,256]{2,1,0:T(8,128)S(1)} %get-tuple-element.52), channel_id=1, source_target_pairs={{0,31},{1,2},{2,1},{3,4},{4,3},{5,6},{6,5},{7,8},{8,7},{9,10},{10,... | collective-permute-start | bytes 589832 | tf_op jit(solution)/shard_map/ppermute | solution.py:107
  15.9 0.4 collective-permute-start.4
  16.3 1.1 %collective-permute-start.5 = (f32[15,16,256]{2,1,0:T(8,128)S(1)}, f32[15,16,256]{2,1,0:T(8,128)S(1)}, u32[]{:S(2)}, u32[]{:S(2)}) collective-permute-start(f32[15,16,256]{2,1,0:T(8,128)S(1)} %get-tuple-element.54), channel_id=1, source_target_pairs={{0,96},{32,64},{64,32},{96,0},{1,97},{33,65},{65,33},{97,1},{2,98}... | collective-permute-start | bytes 737288 | tf_op jit(solution)/shard_map/ppermute | solution.py:101
  17.4 0.3 route.1
  17.7 1.1 %filter_middle.1 = (f32[16,16,512]{2,1,0:T(8,128)S(1)}, f32[5,16,16,512]{3,2,1,0:T(8,128)S(1)}) custom-call(f32[16,16,512]{2,1,0:T(8,128)S(1)} %get-tuple-element.55.refs_2_.refs_0_, s32[16,16,512]{2,1,0:T(8,128)S(1)} %get-tuple-element.50.refs_1_, bf16[512,256]{1,0:T(8,128)(2,1)S(1)} %get-tuple-element.56.refs_2_.refs_4_), custom_call_target="tpu_custom_call" | custom-call | tf_op jit(solution)/shard_map/filter_middle/pallas_call | solution.py:116
  18.9 0.0 collective-permute-done.6.refs_0_
  18.9 0.0 copy-start.1
  18.9 0.0 copy-start.3
  18.9 0.0 copy-start.4
  18.9 1.9 %filter_rest.1 = (f32[256,256]{1,0:T(8,128)S(1)}, f32[17,8,256]{2,1,0:T(8,128)S(1)}, f32[17,8,256]{2,1,0:T(8,128)S(1)}, f32[18,8,256]{2,1,0:T(8,128)S(1)}, f32[18,8,256]{2,1,0:T(8,128)S(1)}) custom-call(f32[16,16,512]{2,1,0:T(8,128)S(1)} %get-tuple-element.57.refs_0_, f32[5,16,16,512]{3,2,1,0:T(8,128)S(1)} %get-tuple-element.58.refs_1_, ...), custom_call_target="tpu_custom_call" | custom-call | flops 137438953472 | tf_op jit(solution)/shard_map/filter_rest/pallas_call | solution.py:116
  20.8 3.2 %collective-permute-start.9 = (f32[18,8,256]{2,1,0:T(8,128)S(1)}, f32[18,8,256]{2,1,0:T(8,128)S(1)}, u32[]{:S(2)}, u32[]{:S(2)}) collective-permute-start(f32[18,8,256]{2,1,0:T(8,128)S(1)} %get-tuple-element.67), channel_id=1, source_target_pairs={{0,31},{1,2},{2,1},{3,4},{4,3},{5,6},{6,5},{7,8},{8,7},{9,10},{10,... | collective-permute-start | bytes 442376 | tf_op jit(solution)/shard_map/ppermute | solution.py:101
  24.1 0.0 collective-permute-start.10
  24.1 0.0 collective-permute-done.3.refs_2_
  24.1 1.1 %collective-permute-start.7 = (f32[17,8,256]{2,1,0:T(8,128)S(1)}, f32[17,8,256]{2,1,0:T(8,128)S(1)}, u32[]{:S(2)}, u32[]{:S(2)}) collective-permute-start(f32[17,8,256]{2,1,0:T(8,128)S(1)} %get-tuple-element.65), channel_id=1, source_target_pairs={{0,32},{32,0},{64,96},{96,64},{1,33},{33,1},{65,97},{97,65},{2,34}... | collective-permute-start | bytes 417800 | tf_op jit(solution)/shard_map/ppermute | solution.py:101
  25.2 0.0 collective-permute-done.4.refs_3_
  25.2 1.4 %collective-permute-start.8 = (f32[17,8,256]{2,1,0:T(8,128)S(1)}, f32[17,8,256]{2,1,0:T(8,128)S(1)}, u32[]{:S(2)}, u32[]{:S(2)}) collective-permute-start(f32[17,8,256]{2,1,0:T(8,128)S(1)} %get-tuple-element.66), channel_id=1, source_target_pairs={{0,96},{32,64},{64,32},{96,0},{1,97},{33,65},{65,33},{97,1},{2,98}... | collective-permute-start | bytes 417800 | tf_op jit(solution)/shard_map/ppermute | solution.py:101
  26.6 0.0 collective-permute-done.5.refs_4_
  26.7 1.6 %operator.1 = (f32[5,24,16,256]{3,2,1,0:T(8,128)S(1)}, f32[5,8,16,256]{3,2,1,0:T(8,128)S(1)}) custom-call(f32[5,32,16,256]{3,2,1,0:T(8,128)S(1)} %copy-done.1, f32[40,8,256]{2,1,0:T(8,128)S(1)} %collective-permute-done.2.refs_2_.refs_1_, f32[24,8,256]{2,1,0:T(8,128)S(1)} %collective-permute-done.3.refs_2_, ...), custom_call_target="tpu_custom_call" | custom-call | tf_op jit(solution)/shard_map/operator/pallas_call | solution.py:116
  28.2 1.9 %collective-permute-done.7.refs_2_ = f32[17,8,256]{2,1,0:T(8,128)S(1)} collective-permute-done((f32[17,8,256]{2,1,0:T(8,128)S(1)}, f32[17,8,256]{2,1,0:T(8,128)S(1)}, u32[]{:S(2)}, u32[]{:S(2)}) %collective-permute-start.7) | collective-permute-done | bytes 139296 | tf_op jit(solution)/shard_map/ppermute | solution.py:101
  30.1 2.1 %collective-permute-done.8.refs_3_ = f32[17,8,256]{2,1,0:T(8,128)S(1)} collective-permute-done((f32[17,8,256]{2,1,0:T(8,128)S(1)}, f32[17,8,256]{2,1,0:T(8,128)S(1)}, u32[]{:S(2)}, u32[]{:S(2)}) %collective-permute-start.8) | collective-permute-done | bytes 139296 | tf_op jit(solution)/shard_map/ppermute | solution.py:101
  32.2 0.6 gather.1
  32.8 0.6 collective-permute-start.11
  33.4 0.0 collective-permute-start.12
  33.4 0.3 collective-permute-start.13
  33.8 1.4 %collective-permute-start.14 = (f32[15,16,256]{2,1,0:T(8,128)S(1)}, f32[15,16,256]{2,1,0:T(8,128)S(1)}, u32[]{:S(2)}, u32[]{:S(2)}) collective-permute-start(f32[15,16,256]{2,1,0:T(8,128)S(1)} %get-tuple-element.75), channel_id=1, source_target_pairs={{0,96},{32,64},{64,32},{96,0},{1,97},{33,65},{65,33},{97,1},{2,98}... | collective-permute-start | bytes 737288 | tf_op jit(solution)/shard_map/ppermute | solution.py:101
  35.2 6.1 %collective-permute-done.11.refs_8_.refs_10_ = f32[24,8,256]{2,1,0:T(8,128)S(1)} collective-permute-done((f32[24,8,256]{2,1,0:T(8,128)S(1)}, f32[24,8,256]{2,1,0:T(8,128)S(1)}, u32[]{:S(2)}, u32[]{:S(2)}) %collective-permute-start.11) | collective-permute-done | bytes 196640 | tf_op jit(solution)/shard_map/ppermute | solution.py:101
  41.3 0.0 collective-permute-done.12.refs_9_.refs_11_
  41.3 1.4 %stage_inner.2 = (f32[5,24,16,256]{3,2,1,0:T(8,128)S(1)}, f32[18,8,256]{2,1,0:T(8,128)S(1)}, f32[18,8,256]{2,1,0:T(8,128)S(1)}) custom-call(f32[5,24,16,256]{3,2,1,0:T(8,128)S(1)} %get-tuple-element.62.refs_6_.refs_0_.refs_4_.refs_2_.refs_3_, f32[5,8,16,256]{3,2,1,0:T(8,128)S(1)} %get-tuple-element.63.refs_7_.refs_1_.refs_5_.refs_3_.refs_4_, ...), custom_call_target="tpu_custom_call" | custom-call | flops 137438953472 | tf_op jit(solution)/shard_map/stage_inner/pallas_call | solution.py:116
  42.7 0.6 collective-permute-start.15
  43.3 0.0 collective-permute-start.16
  43.3 0.6 stage_rim.2
  44.0 0.4 collective-permute-start.17
  44.4 1.7 %collective-permute-start.18 = (f32[15,16,256]{2,1,0:T(8,128)S(1)}, f32[15,16,256]{2,1,0:T(8,128)S(1)}, u32[]{:S(2)}, u32[]{:S(2)}) collective-permute-start(f32[15,16,256]{2,1,0:T(8,128)S(1)} %get-tuple-element.81), channel_id=1, source_target_pairs={{0,96},{32,64},{64,32},{96,0},{1,97},{33,65},{65,33},{97,1},{2,98}... | collective-permute-start | bytes 737288 | tf_op jit(solution)/shard_map/ppermute | solution.py:101
  46.0 3.8 %collective-permute-start.19 = (f32[6,8,256]{2,1,0:T(8,128)S(1)}, f32[6,8,256]{2,1,0:T(8,128)S(1)}, u32[]{:S(2)}, u32[]{:S(2)}) collective-permute-start(f32[6,8,256]{2,1,0:T(8,128)S(1)} %get-tuple-element.82), channel_id=1, source_target_pairs={{0,31},{1,2},{2,1},{3,4},{4,3},{5,6},{6,5},{7,8},{8,7},{9,10},{10,... | collective-permute-start | bytes 147464 | tf_op jit(solution)/shard_map/ppermute | solution.py:101
  49.8 0.8 %collective-permute-done.15.refs_6_ = f32[18,8,256]{2,1,0:T(8,128)S(1)} collective-permute-done((f32[18,8,256]{2,1,0:T(8,128)S(1)}, f32[18,8,256]{2,1,0:T(8,128)S(1)}, u32[]{:S(2)}, u32[]{:S(2)}) %collective-permute-start.15) | collective-permute-done | bytes 147488 | tf_op jit(solution)/shard_map/ppermute | solution.py:101
  50.7 1.4 %stage_inner.3 = (f32[5,24,16,256]{3,2,1,0:T(8,128)S(1)}, f32[18,8,256]{2,1,0:T(8,128)S(1)}, f32[18,8,256]{2,1,0:T(8,128)S(1)}) custom-call(f32[5,24,16,256]{3,2,1,0:T(8,128)S(1)} %get-tuple-element.73.refs_14_.refs_0_, f32[5,8,16,256]{3,2,1,0:T(8,128)S(1)} %get-tuple-element.76.refs_1_, ...), custom_call_target="tpu_custom_call" | custom-call | flops 2000000000 | tf_op jit(solution)/shard_map/stage_inner/pallas_call | solution.py:116
  52.0 0.6 collective-permute-start.21
  52.7 0.2 collective-permute-done.19.refs_8_
  52.9 0.0 collective-permute-start.22
  52.9 0.0 collective-permute-done.20.refs_9_
  52.9 0.8 %collective-permute-done.18.refs_7_ = f32[15,16,256]{2,1,0:T(8,128)S(1)} collective-permute-done((f32[15,16,256]{2,1,0:T(8,128)S(1)}, f32[15,16,256]{2,1,0:T(8,128)S(1)}, u32[]{:S(2)}, u32[]{:S(2)}) %collective-permute-start.18) | collective-permute-done | bytes 245792 | tf_op jit(solution)/shard_map/ppermute | solution.py:101
  53.7 0.6 stage_rim.3
  54.3 0.5 collective-permute-start.23
  54.8 1.7 %collective-permute-start.24 = (f32[15,16,256]{2,1,0:T(8,128)S(1)}, f32[15,16,256]{2,1,0:T(8,128)S(1)}, u32[]{:S(2)}, u32[]{:S(2)}) collective-permute-start(f32[15,16,256]{2,1,0:T(8,128)S(1)} %get-tuple-element.88), channel_id=1, source_target_pairs={{0,96},{32,64},{64,32},{96,0},{1,97},{33,65},{65,33},{97,1},{2,98}... | collective-permute-start | bytes 737288 | tf_op jit(solution)/shard_map/ppermute | solution.py:101
  56.6 3.1 %collective-permute-start.25 = (f32[6,8,256]{2,1,0:T(8,128)S(1)}, f32[6,8,256]{2,1,0:T(8,128)S(1)}, u32[]{:S(2)}, u32[]{:S(2)}) collective-permute-start(f32[6,8,256]{2,1,0:T(8,128)S(1)} %get-tuple-element.89), channel_id=1, source_target_pairs={{0,31},{1,2},{2,1},{3,4},{4,3},{5,6},{6,5},{7,8},{8,7},{9,10},{10,... | collective-permute-start | bytes 147464 | tf_op jit(solution)/shard_map/ppermute | solution.py:101
  59.7 0.3 collective-permute-done.21.refs_7_
  60.0 0.0 collective-permute-start.26
  60.0 0.0 collective-permute-done.22.refs_8_
  60.0 2.3 %final_inner.1.refs_0_ = f32[5,32,16,256]{3,2,1,0:T(8,128)} custom-call(f32[5,24,16,256]{3,2,1,0:T(8,128)S(1)} %get-tuple-element.79.refs_12_.refs_0_.refs_1_, f32[5,8,16,256]{3,2,1,0:T(8,128)S(1)} %get-tuple-element.84.refs_1_.refs_2_, f32[5,24,16,256]{3,2,1,0:T(8,128)S(1)} %get-tuple-element.62.refs_6_.refs_0_.refs_4_.refs_2_.refs_3_, ...), custom_call_target="tpu_custom_call" | custom-call | flops 2000000000 | tf_op jit(solution)/shard_map/final_inner/pallas_call | solution.py:116
  62.4 1.1 %collective-permute-done.25.refs_10_ = f32[6,8,256]{2,1,0:T(8,128)S(1)} collective-permute-done((f32[6,8,256]{2,1,0:T(8,128)S(1)}, f32[6,8,256]{2,1,0:T(8,128)S(1)}, u32[]{:S(2)}, u32[]{:S(2)}) %collective-permute-start.25) | collective-permute-done | bytes 49184 | tf_op jit(solution)/shard_map/ppermute | solution.py:101
  63.4 0.6 collective-permute-done.24.refs_9_
  64.1 1.5 %final_rim.1 = f32[5,32,16,256]{3,2,1,0:T(8,128)} custom-call(f32[5,32,16,256]{3,2,1,0:T(8,128)} %final_inner.1.refs_0_, f32[5,24,16,256]{3,2,1,0:T(8,128)S(1)} %get-tuple-element.79.refs_12_.refs_0_.refs_1_, f32[5,8,16,256]{3,2,1,0:T(8,128)S(1)} %get-tuple-element.84.refs_1_.refs_2_, ...), custom_call_target="tpu_custom_call", output_to_operand_aliasing={{}: (0, {})} | custom-call | tf_op jit(solution)/shard_map/final_rim/pallas_call | solution.py:116
  (24 shorter events, 0.1 us)
Async XLA Ops:
  0.0 6.2 %copy-start.5 = (f32[16,16,512]{2,1,0:T(8,128)S(1)}, f32[16,16,512]{2,1,0:T(8,128)}, u32[]{:S(2)}) copy-start(f32[16,16,512]{2,1,0:T(8,128)} %refs_0_.4) | copy-start | bytes 1572868
  1.1 6.7 %collective-permute-start.1 = (f32[4,16,512]{2,1,0:T(8,128)S(1)}, f32[4,16,512]{2,1,0:T(8,128)S(1)}, u32[]{:S(2)}, u32[]{:S(2)}) collective-permute-start(f32[4,16,512]{2,1,0:T(8,128)S(1)} %get-tuple-element.91), channel_id=1, source_target_pairs={{0,96},{32,64},{64,32},{96,0},{1,97},{33,65},{65,33},{97,1},{2,98}... | collective-permute-start | bytes 393224 | tf_op jit(solution)/shard_map/ppermute | solution.py:101
  4.2 5.0 %collective-permute-start = (f32[4,16,512]{2,1,0:T(8,128)S(1)}, f32[4,16,512]{2,1,0:T(8,128)S(1)}, u32[]{:S(2)}, u32[]{:S(2)}) collective-permute-start(f32[4,16,512]{2,1,0:T(8,128)S(1)} %get-tuple-element.92.refs_1_), channel_id=1, source_target_pairs={{0,32},{32,0},{64,96},{96,64},{1,33},{33,1},{65,97},{97,65},{2,34}... | collective-permute-start | bytes 393224 | tf_op jit(solution)/shard_map/ppermute | solution.py:101
  4.4 1.7 %copy-start = (f32[5,32,16,256]{3,2,1,0:T(8,128)S(1)}, f32[5,32,16,256]{3,2,1,0:T(8,128)}, u32[]{:S(2)}) copy-start(f32[5,32,16,256]{3,2,1,0:T(8,128)} %refs_7_.1) | copy-start | bytes 7864324
  6.1 1.0 %copy-start.6 = (s32[16,16,512]{2,1,0:T(8,128)S(1)}, s32[16,16,512]{2,1,0:T(8,128)}, u32[]{:S(2)}) copy-start(s32[16,16,512]{2,1,0:T(8,128)} %refs_1_.1) | copy-start | bytes 1572868
  6.1 11.3 %copy-start.7 = (s32[256]{0:T(256)S(1)}, s32[256]{0:T(256)}, u32[]{:S(2)}) copy-start(s32[256]{0:T(256)} %param.9) | copy-start | bytes 3076
  6.1 11.3 %copy-start.8 = (s32[256]{0:T(256)S(1)}, s32[256]{0:T(256)}, u32[]{:S(2)}) copy-start(s32[256]{0:T(256)} %param.10) | copy-start | bytes 3076
  9.4 9.5 %collective-permute-start.6 = (f32[16,8,256]{2,1,0:T(8,128)S(1)}, f32[16,8,256]{2,1,0:T(8,128)S(1)}, u32[]{:S(2)}, u32[]{:S(2)}) collective-permute-start(f32[16,8,256]{2,1,0:T(8,128)S(1)} %get-tuple-element.59), channel_id=1, source_target_pairs={{0,31},{1,2},{2,1},{3,4},{4,3},{5,6},{6,5},{7,8},{8,7},{9,10},{10,... | collective-permute-start | bytes 393224 | tf_op jit(solution)/shard_map/ppermute | solution.py:101
  14.0 4.9 %collective-permute-start.2 = (f32[40,8,256]{2,1,0:T(8,128)S(1)}, f32[40,8,256]{2,1,0:T(8,128)S(1)}, u32[]{:S(2)}, u32[]{:S(2)}) collective-permute-start(f32[40,8,256]{2,1,0:T(8,128)S(1)} %get-tuple-element.51), channel_id=1, source_target_pairs={{0,1},{1,0},{2,3},{3,2},{4,5},{5,4},{6,7},{7,6},{8,9},{9,8},{10,11... | collective-permute-start | bytes 983048 | tf_op jit(solution)/shard_map/ppermute | solution.py:101
  14.0 10.1 %collective-permute-start.3 = (f32[24,8,256]{2,1,0:T(8,128)S(1)}, f32[24,8,256]{2,1,0:T(8,128)S(1)}, u32[]{:S(2)}, u32[]{:S(2)}) collective-permute-start(f32[24,8,256]{2,1,0:T(8,128)S(1)} %get-tuple-element.52), channel_id=1, source_target_pairs={{0,31},{1,2},{2,1},{3,4},{4,3},{5,6},{6,5},{7,8},{8,7},{9,10},{10,... | collective-permute-start | bytes 589832 | tf_op jit(solution)/shard_map/ppermute | solution.py:107
  15.9 9.3 %collective-permute-start.4 = (f32[15,16,256]{2,1,0:T(8,128)S(1)}, f32[15,16,256]{2,1,0:T(8,128)S(1)}, u32[]{:S(2)}, u32[]{:S(2)}) collective-permute-start(f32[15,16,256]{2,1,0:T(8,128)S(1)} %get-tuple-element.53), channel_id=1, source_target_pairs={{0,32},{32,0},{64,96},{96,64},{1,33},{33,1},{65,97},{97,65},{2,34}... | collective-permute-start | bytes 737288 | tf_op jit(solution)/shard_map/ppermute | solution.py:101
  16.3 10.4 %collective-permute-start.5 = (f32[15,16,256]{2,1,0:T(8,128)S(1)}, f32[15,16,256]{2,1,0:T(8,128)S(1)}, u32[]{:S(2)}, u32[]{:S(2)}) collective-permute-start(f32[15,16,256]{2,1,0:T(8,128)S(1)} %get-tuple-element.54), channel_id=1, source_target_pairs={{0,96},{32,64},{64,32},{96,0},{1,97},{33,65},{65,33},{97,1},{2,98}... | collective-permute-start | bytes 737288 | tf_op jit(solution)/shard_map/ppermute | solution.py:101
  18.9 7.7 %copy-start.1 = (f32[5,32,16,256]{3,2,1,0:T(8,128)S(1)}, f32[5,32,16,256]{3,2,1,0:T(8,128)}, u32[]{:S(2)}) copy-start(f32[5,32,16,256]{3,2,1,0:T(8,128)} %refs_7_.1) | copy-start | bytes 7864324
  18.9 7.7 %copy-start.3 = (bf16[2,2,256,256]{3,2,1,0:T(8,128)(2,1)S(1)}, bf16[2,2,256,256]{3,2,1,0:T(8,128)(2,1)}, u32[]{:S(2)}) copy-start(bf16[2,2,256,256]{3,2,1,0:T(8,128)(2,1)} %constant.17.clone.refs_6_.refs_11_.refs_13_.refs_9_.refs_10_) | copy-start | bytes 1572868
  18.9 7.7 %copy-start.4 = (bf16[2,2,128,224]{3,2,1,0:T(8,128)(2,1)S(1)}, bf16[2,2,128,224]{3,2,1,0:T(8,128)(2,1)}, u32[]{:S(2)}) copy-start(bf16[2,2,128,224]{3,2,1,0:T(8,128)(2,1)} %constant.16.clone.refs_5_.refs_10_.refs_12_.refs_8_.refs_9_) | copy-start | bytes 688132
  20.8 11.4 %collective-permute-start.9 = (f32[18,8,256]{2,1,0:T(8,128)S(1)}, f32[18,8,256]{2,1,0:T(8,128)S(1)}, u32[]{:S(2)}, u32[]{:S(2)}) collective-permute-start(f32[18,8,256]{2,1,0:T(8,128)S(1)} %get-tuple-element.67), channel_id=1, source_target_pairs={{0,31},{1,2},{2,1},{3,4},{4,3},{5,6},{6,5},{7,8},{8,7},{9,10},{10,... | collective-permute-start | bytes 442376 | tf_op jit(solution)/shard_map/ppermute | solution.py:101
  24.1 8.2 %collective-permute-start.10 = (f32[18,8,256]{2,1,0:T(8,128)S(1)}, f32[18,8,256]{2,1,0:T(8,128)S(1)}, u32[]{:S(2)}, u32[]{:S(2)}) collective-permute-start(f32[18,8,256]{2,1,0:T(8,128)S(1)} %get-tuple-element.68), channel_id=1, source_target_pairs={{0,1},{1,0},{2,3},{3,2},{4,5},{5,4},{6,7},{7,6},{8,9},{9,8},{10,11... | collective-permute-start | bytes 442376 | tf_op jit(solution)/shard_map/ppermute | solution.py:101
  24.1 6.1 %collective-permute-start.7 = (f32[17,8,256]{2,1,0:T(8,128)S(1)}, f32[17,8,256]{2,1,0:T(8,128)S(1)}, u32[]{:S(2)}, u32[]{:S(2)}) collective-permute-start(f32[17,8,256]{2,1,0:T(8,128)S(1)} %get-tuple-element.65), channel_id=1, source_target_pairs={{0,32},{32,0},{64,96},{96,64},{1,33},{33,1},{65,97},{97,65},{2,34}... | collective-permute-start | bytes 417800 | tf_op jit(solution)/shard_map/ppermute | solution.py:101
  25.2 7.0 %collective-permute-start.8 = (f32[17,8,256]{2,1,0:T(8,128)S(1)}, f32[17,8,256]{2,1,0:T(8,128)S(1)}, u32[]{:S(2)}, u32[]{:S(2)}) collective-permute-start(f32[17,8,256]{2,1,0:T(8,128)S(1)} %get-tuple-element.66), channel_id=1, source_target_pairs={{0,96},{32,64},{64,32},{96,0},{1,97},{33,65},{65,33},{97,1},{2,98}... | collective-permute-start | bytes 417800 | tf_op jit(solution)/shard_map/ppermute | solution.py:101
  32.8 8.5 %collective-permute-start.11 = (f32[24,8,256]{2,1,0:T(8,128)S(1)}, f32[24,8,256]{2,1,0:T(8,128)S(1)}, u32[]{:S(2)}, u32[]{:S(2)}) collective-permute-start(f32[24,8,256]{2,1,0:T(8,128)S(1)} %get-tuple-element.71), channel_id=1, source_target_pairs={{0,31},{1,2},{2,1},{3,4},{4,3},{5,6},{6,5},{7,8},{8,7},{9,10},{10,... | collective-permute-start | bytes 589832 | tf_op jit(solution)/shard_map/ppermute | solution.py:101
  33.4 7.9 %collective-permute-start.12 = (f32[24,8,256]{2,1,0:T(8,128)S(1)}, f32[24,8,256]{2,1,0:T(8,128)S(1)}, u32[]{:S(2)}, u32[]{:S(2)}) collective-permute-start(f32[24,8,256]{2,1,0:T(8,128)S(1)} %get-tuple-element.72), channel_id=1, source_target_pairs={{0,1},{1,0},{2,3},{3,2},{4,5},{5,4},{6,7},{7,6},{8,9},{9,8},{10,11... | collective-permute-start | bytes 589832 | tf_op jit(solution)/shard_map/ppermute | solution.py:101
  33.4 9.9 %collective-permute-start.13 = (f32[15,16,256]{2,1,0:T(8,128)S(1)}, f32[15,16,256]{2,1,0:T(8,128)S(1)}, u32[]{:S(2)}, u32[]{:S(2)}) collective-permute-start(f32[15,16,256]{2,1,0:T(8,128)S(1)} %get-tuple-element.74), channel_id=1, source_target_pairs={{0,32},{32,0},{64,96},{96,64},{1,33},{33,1},{65,97},{97,65},{2,34}... | collective-permute-start | bytes 737288 | tf_op jit(solution)/shard_map/ppermute | solution.py:101
  33.8 9.6 %collective-permute-start.14 = (f32[15,16,256]{2,1,0:T(8,128)S(1)}, f32[15,16,256]{2,1,0:T(8,128)S(1)}, u32[]{:S(2)}, u32[]{:S(2)}) collective-permute-start(f32[15,16,256]{2,1,0:T(8,128)S(1)} %get-tuple-element.75), channel_id=1, source_target_pairs={{0,96},{32,64},{64,32},{96,0},{1,97},{33,65},{65,33},{97,1},{2,98}... | collective-permute-start | bytes 737288 | tf_op jit(solution)/shard_map/ppermute | solution.py:101
  42.7 8.0 %collective-permute-start.15 = (f32[18,8,256]{2,1,0:T(8,128)S(1)}, f32[18,8,256]{2,1,0:T(8,128)S(1)}, u32[]{:S(2)}, u32[]{:S(2)}) collective-permute-start(f32[18,8,256]{2,1,0:T(8,128)S(1)} %get-tuple-element.77), channel_id=1, source_target_pairs={{0,31},{1,2},{2,1},{3,4},{4,3},{5,6},{6,5},{7,8},{8,7},{9,10},{10,... | collective-permute-start | bytes 442376 | tf_op jit(solution)/shard_map/ppermute | solution.py:101
  43.3 7.4 %collective-permute-start.16 = (f32[18,8,256]{2,1,0:T(8,128)S(1)}, f32[18,8,256]{2,1,0:T(8,128)S(1)}, u32[]{:S(2)}, u32[]{:S(2)}) collective-permute-start(f32[18,8,256]{2,1,0:T(8,128)S(1)} %get-tuple-element.78), channel_id=1, source_target_pairs={{0,1},{1,0},{2,3},{3,2},{4,5},{5,4},{6,7},{7,6},{8,9},{9,8},{10,11... | collective-permute-start | bytes 442376 | tf_op jit(solution)/shard_map/ppermute | solution.py:101
  44.0 8.9 %collective-permute-start.17 = (f32[15,16,256]{2,1,0:T(8,128)S(1)}, f32[15,16,256]{2,1,0:T(8,128)S(1)}, u32[]{:S(2)}, u32[]{:S(2)}) collective-permute-start(f32[15,16,256]{2,1,0:T(8,128)S(1)} %get-tuple-element.80), channel_id=1, source_target_pairs={{0,32},{32,0},{64,96},{96,64},{1,33},{33,1},{65,97},{97,65},{2,34}... | collective-permute-start | bytes 737288 | tf_op jit(solution)/shard_map/ppermute | solution.py:101
  44.4 9.3 %collective-permute-start.18 = (f32[15,16,256]{2,1,0:T(8,128)S(1)}, f32[15,16,256]{2,1,0:T(8,128)S(1)}, u32[]{:S(2)}, u32[]{:S(2)}) collective-permute-start(f32[15,16,256]{2,1,0:T(8,128)S(1)} %get-tuple-element.81), channel_id=1, source_target_pairs={{0,96},{32,64},{64,32},{96,0},{1,97},{33,65},{65,33},{97,1},{2,98}... | collective-permute-start | bytes 737288 | tf_op jit(solution)/shard_map/ppermute | solution.py:101
  46.0 6.8 %collective-permute-start.19 = (f32[6,8,256]{2,1,0:T(8,128)S(1)}, f32[6,8,256]{2,1,0:T(8,128)S(1)}, u32[]{:S(2)}, u32[]{:S(2)}) collective-permute-start(f32[6,8,256]{2,1,0:T(8,128)S(1)} %get-tuple-element.82), channel_id=1, source_target_pairs={{0,31},{1,2},{2,1},{3,4},{4,3},{5,6},{6,5},{7,8},{8,7},{9,10},{10,... | collective-permute-start | bytes 147464 | tf_op jit(solution)/shard_map/ppermute | solution.py:101
  50.7 2.2 %collective-permute-start.20 = (f32[6,8,256]{2,1,0:T(8,128)S(1)}, f32[6,8,256]{2,1,0:T(8,128)S(1)}, u32[]{:S(2)}, u32[]{:S(2)}) collective-permute-start(f32[6,8,256]{2,1,0:T(8,128)S(1)} %get-tuple-element.83), channel_id=1, source_target_pairs={{0,1},{1,0},{2,3},{3,2},{4,5},{5,4},{6,7},{7,6},{8,9},{9,8},{10,11... | collective-permute-start | bytes 147464 | tf_op jit(solution)/shard_map/ppermute | solution.py:101
  52.0 8.0 %collective-permute-start.21 = (f32[18,8,256]{2,1,0:T(8,128)S(1)}, f32[18,8,256]{2,1,0:T(8,128)S(1)}, u32[]{:S(2)}, u32[]{:S(2)}) collective-permute-start(f32[18,8,256]{2,1,0:T(8,128)S(1)} %get-tuple-element.85), channel_id=1, source_target_pairs={{0,31},{1,2},{2,1},{3,4},{4,3},{5,6},{6,5},{7,8},{8,7},{9,10},{10,... | collective-permute-start | bytes 442376 | tf_op jit(solution)/shard_map/ppermute | solution.py:101
  52.9 7.2 %collective-permute-start.22 = (f32[18,8,256]{2,1,0:T(8,128)S(1)}, f32[18,8,256]{2,1,0:T(8,128)S(1)}, u32[]{:S(2)}, u32[]{:S(2)}) collective-permute-start(f32[18,8,256]{2,1,0:T(8,128)S(1)} %get-tuple-element.86), channel_id=1, source_target_pairs={{0,1},{1,0},{2,3},{3,2},{4,5},{5,4},{6,7},{7,6},{8,9},{9,8},{10,11... | collective-permute-start | bytes 442376 | tf_op jit(solution)/shard_map/ppermute | solution.py:101
  53.7 6.3 %copy-start.2 = (f32[5,32,16,256]{3,2,1,0:T(8,128)S(1)}, f32[5,32,16,256]{3,2,1,0:T(8,128)}, u32[]{:S(2)}) copy-start(f32[5,32,16,256]{3,2,1,0:T(8,128)} %refs_7_.1) | copy-start | bytes 7864324
  54.3 9.1 %collective-permute-start.23 = (f32[15,16,256]{2,1,0:T(8,128)S(1)}, f32[15,16,256]{2,1,0:T(8,128)S(1)}, u32[]{:S(2)}, u32[]{:S(2)}) collective-permute-start(f32[15,16,256]{2,1,0:T(8,128)S(1)} %get-tuple-element.87), channel_id=1, source_target_pairs={{0,32},{32,0},{64,96},{96,64},{1,33},{33,1},{65,97},{97,65},{2,34}... | collective-permute-start | bytes 737288 | tf_op jit(solution)/shard_map/ppermute | solution.py:101
  54.8 9.2 %collective-permute-start.24 = (f32[15,16,256]{2,1,0:T(8,128)S(1)}, f32[15,16,256]{2,1,0:T(8,128)S(1)}, u32[]{:S(2)}, u32[]{:S(2)}) collective-permute-start(f32[15,16,256]{2,1,0:T(8,128)S(1)} %get-tuple-element.88), channel_id=1, source_target_pairs={{0,96},{32,64},{64,32},{96,0},{1,97},{33,65},{65,33},{97,1},{2,98}... | collective-permute-start | bytes 737288 | tf_op jit(solution)/shard_map/ppermute | solution.py:101
  56.6 6.8 %collective-permute-start.25 = (f32[6,8,256]{2,1,0:T(8,128)S(1)}, f32[6,8,256]{2,1,0:T(8,128)S(1)}, u32[]{:S(2)}, u32[]{:S(2)}) collective-permute-start(f32[6,8,256]{2,1,0:T(8,128)S(1)} %get-tuple-element.89), channel_id=1, source_target_pairs={{0,31},{1,2},{2,1},{3,4},{4,3},{5,6},{6,5},{7,8},{8,7},{9,10},{10,... | collective-permute-start | bytes 147464 | tf_op jit(solution)/shard_map/ppermute | solution.py:101
  60.0 3.4 %collective-permute-start.26 = (f32[6,8,256]{2,1,0:T(8,128)S(1)}, f32[6,8,256]{2,1,0:T(8,128)S(1)}, u32[]{:S(2)}, u32[]{:S(2)}) collective-permute-start(f32[6,8,256]{2,1,0:T(8,128)S(1)} %get-tuple-element.90), channel_id=1, source_target_pairs={{0,1},{1,0},{2,3},{3,2},{4,5},{5,4},{6,7},{7,6},{8,9},{9,8},{10,11... | collective-permute-start | bytes 147464 | tf_op jit(solution)/shard_map/ppermute | solution.py:101

commit v12 on v11

--- a/solution.py
+++ b/solution.py
@@ -297,7 +297,7 @@
 
 
 def gather_body(
-    binned_ref, own_ref, xa, xb, zb, za, k_mid, k_rim, p_mid, p_rim, to_xa, to_xb, to_za, to_zb
+    binned_ref, own_ref, xa, xb, zb, za, k_mid, k_rim, p_mid, p_rim, to_xa, to_xb, to_za, to_zb, rim_za, rim_zb
 ):
     mid, cols, radial = p_mid.shape
     cells = (mid + 2 * RIM) * cols
@@ -321,7 +321,8 @@
     p_rim[RIM:] = k_rim[4, RIM:] + q[RIM + mid :]
     level = Parts(k_mid, k_rim, p_mid, p_rim)
     write_x(level, to_xa, to_xb)
-    write_z(level, range(0, level.rows, 4), to_za, to_zb)
+    write_z(level, range(RIM, level.rows - RIM, 4), to_za, to_zb)
+    write_z(level, [0, level.rows - RIM], rim_za, rim_zb)
 
 
 class Whole:
@@ -564,16 +565,17 @@
     rows = level.rows
     fill_halo(halo, xa, xb)
 
-    def store(f, x, value):
-        result[f, x if x < RIM else x - rows + 2 * RIM] = value
-
-    apply_operator(level, [None], za, zb, tmat, rmat, last_finish(fields, k, store), halo)
     copies = [
         pltpu.make_async_copy(result.at[:, 0:RIM], out.at[:, 0:RIM], sems.at[0]),
         pltpu.make_async_copy(result.at[:, RIM:], out.at[:, rows - RIM :], sems.at[1]),
     ]
-    for copy in copies:
-        copy.start()
+
+    def store(f, x, value):
+        result[f, x if x < RIM else x - rows + 2 * RIM] = value
+        if f == 4 and x in (RIM - 1, rows - 1):
+            copies[x // RIM > 0].start()
+
+    apply_operator(level, [None], za, zb, tmat, rmat, last_finish(fields, k, store), halo)
     for copy in copies:
         copy.wait()
 
@@ -646,17 +648,18 @@
     k_mid, k_rim = full_specs(
         start_body, [mid, rim], [fields, got_a, uzb, uxa, uxb, tmat, rmat], [halo], name="operator", after=[binned]
     )
+    inner_z, rim_z = ((inner // 4 * 3, 8, radial), F32), ((RIM // 2 * 3, 8, radial), F32)
     p_mid, p_rim, *edges = full_specs(
         gather_body,
-        [((inner, ca, radial), F32), ((2 * RIM, ca, radial), F32), *sends],
+        [((inner, ca, radial), F32), ((2 * RIM, ca, radial), F32), send_x, send_x, inner_z, inner_z, rim_z, rim_z],
         [binned, own, *packets, k_mid, k_rim],
         name="gather",
     )
     k = [k_mid, k_rim, p_mid, p_rim]
-    inner_z, rim_z = ((inner // 4 * 3, 8, radial), F32), ((RIM // 2 * 3, 8, radial), F32)
     za, zb = swap(edges[2], edges[3], "az")
     xa, xb = swap(edges[0], edges[1], "ax")
-    level, rim_a, rim_b = k, za, zb
+    rim_a, rim_b = swap(edges[4], edges[5], "az")
+    level = k
     for factor in (time_step / 4.0, time_step / 3.0):
         size = len(level)
 
@@ -664,7 +667,7 @@
             inner_stage_body(factor, Parts(*refs[:size]), Parts(*refs[size : size + 4]), *refs[size + 4 :])
 
         new_mid, to_za, to_zb = full_specs(
-            body, [mid, inner_z, inner_z], [*level, *k, zb, za, tmat, rmat], name="stage_inner", cost=COST if level is k else SOME
+            body, [mid, inner_z, inner_z], [*level, *k, zb, za, tmat, rmat], name="stage_inner", cost=SOME
         )
         za, zb = swap(to_za, to_zb, "az")
 

time: 66.1 us -> 65.8 us (level)
  waiting for transfers between devices: 15.6 us -> 11 us
  starting transfers between devices: 32 us -> 36.1 us
    ppermute x13 -> x14, waiting for transfers between devices: 12.2 us -> 7.59 us  [swap(): lax.ppermute(to_b, axis, pairs_b)]
    ppermute x13 -> x14, starting transfers between devices: 27.1 us -> 31.1 us  [swap(): lax.ppermute(to_b, axis, pairs_b)]
    ppermute x13 -> x14, starting transfers between devices: 2.92 us -> 2.99 us  [swap(): lax.ppermute(to_a, axis, pairs_a)]
    ppermute x13 -> x14, waiting for transfers between devices: 3.42 us -> 3.43 us  [swap(): lax.ppermute(to_a, axis, pairs_a)]
  transfers between devices with their start and end apart: 27 -> 29, of which waited for: 11 -> 12; matrix products, arithmetic and copies ran while one was open for 0% -> 0% of each run, Pallas kernels for 18% -> 18%
where the time goes in v12:
time: 65.8 us; the launch traced here: 65.3 us
  starting transfers between devices  36.1 us (55%)
  Pallas kernels  14.1 us (21%)
  waiting for transfers between devices  11 us (17%)
  local copies, waits for them, and re-layouts  2.68 us (4%)
  other arithmetic  1.05 us (2%)
    ppermute x14, starting transfers between devices, swap(): lax.ppermute(to_b, axis, pairs_b)  31.1 us
    pallas_call x15, Pallas kernels, full_specs(): pl.pallas_call(run, out_shape=[jax.ShapeDtypeStruct(s, d) for s, d in out...  14.1 us
    ppermute x14, waiting for transfers between devices, swap(): lax.ppermute(to_b, axis, pairs_b)  7.59 us
    ppermute x14, waiting for transfers between devices, swap(): lax.ppermute(to_a, axis, pairs_a)  3.43 us
    ppermute x14, starting transfers between devices, swap(): lax.ppermute(to_a, axis, pairs_a)  2.99 us
    unnamed x18, local copies, waits for them, and re-layouts  2.68 us
    ppermute x1, starting transfers between devices, swap_b(): return (lax.ppermute(value, axis, pairs),)  1.96 us
  transfers between devices with their start and end apart: 29, of which 12 were waited for; matrix products, arithmetic and copies ran while one was open for 0% of the time, Pallas kernels for 18%

profile of v12, /device:TPU:0, one launch (start us, length us, event | category | flops | bytes accessed | tf_op | source)
XLA Modules:
  0.0 65.3 jit_solution(14774061636918399075)
XLA Ops:
  0.0 1.0 %slice_select_fusion = (f32[4,16,512]{2,1,0:T(8,128)S(1)}, f32[4,16,512]{2,1,0:T(8,128)S(1)}) fusion(f32[16,16,512]{2,1,0:T(8,128)} %refs_0_.4, pred[]{:T(512)S(6)} %eq.3), kind=kLoop, calls=%fused_computation | loop fusion | flops 65536 | bytes 524289 | tf_op jit(solution)/shard_map/jit(_where)/select_n | solution.py:594
  1.1 3.2 %collective-permute-start.1 = (f32[4,16,512]{2,1,0:T(8,128)S(1)}, f32[4,16,512]{2,1,0:T(8,128)S(1)}, u32[]{:S(2)}, u32[]{:S(2)}) collective-permute-start(f32[4,16,512]{2,1,0:T(8,128)S(1)} %get-tuple-element.95), channel_id=1, source_target_pairs={{0,96},{32,64},{64,32},{96,0},{1,97},{33,65},{65,33},{97,1},{2,98}... | collective-permute-start | bytes 393224 | tf_op jit(solution)/shard_map/ppermute | solution.py:101
  4.2 0.1 collective-permute-start
  4.4 1.7 %copy-done = f32[5,32,16,256]{3,2,1,0:T(8,128)S(1)} copy-done((f32[5,32,16,256]{3,2,1,0:T(8,128)S(1)}, f32[5,32,16,256]{3,2,1,0:T(8,128)}, u32[]{:S(2)}) %copy-start) | copy-done | bytes 2621464
  6.1 0.1 edges.1
  6.3 0.9 %copy-done.6 = s32[16,16,512]{2,1,0:T(8,128)S(1)} copy-done((s32[16,16,512]{2,1,0:T(8,128)S(1)}, s32[16,16,512]{2,1,0:T(8,128)}, u32[]{:S(2)}) %copy-start.6) | copy-done | bytes 524312
  7.2 0.5 filter_inner.1
  7.6 0.1 collective-permute-done.1.refs_3_
  7.7 1.5 %collective-permute-done.refs_2_ = f32[4,16,512]{2,1,0:T(8,128)S(1)} collective-permute-done((f32[4,16,512]{2,1,0:T(8,128)S(1)}, f32[4,16,512]{2,1,0:T(8,128)S(1)}, u32[]{:S(2)}, u32[]{:S(2)}) %collective-permute-start) | collective-permute-done | bytes 131104 | tf_op jit(solution)/shard_map/ppermute | solution.py:101
  9.2 0.2 filter_axial.1
  9.4 4.6 %collective-permute-start.6 = (f32[16,8,256]{2,1,0:T(8,128)S(1)}, f32[16,8,256]{2,1,0:T(8,128)S(1)}, u32[]{:S(2)}, u32[]{:S(2)}) collective-permute-start(f32[16,8,256]{2,1,0:T(8,128)S(1)} %get-tuple-element.61), channel_id=1, source_target_pairs={{0,31},{1,2},{2,1},{3,4},{4,3},{5,6},{6,5},{7,8},{8,7},{9,10},{10,... | collective-permute-start | bytes 393224 | tf_op jit(solution)/shard_map/ppermute | solution.py:101
  14.0 0.0 collective-permute-start.2
  14.0 2.0 %collective-permute-start.3 = (f32[24,8,256]{2,1,0:T(8,128)S(1)}, f32[24,8,256]{2,1,0:T(8,128)S(1)}, u32[]{:S(2)}, u32[]{:S(2)}) collective-permute-start(f32[24,8,256]{2,1,0:T(8,128)S(1)} %get-tuple-element.54), channel_id=1, source_target_pairs={{0,31},{1,2},{2,1},{3,4},{4,3},{5,6},{6,5},{7,8},{8,7},{9,10},{10,... | collective-permute-start | bytes 589832 | tf_op jit(solution)/shard_map/ppermute | solution.py:107
  15.9 0.4 collective-permute-start.4
  16.3 1.1 %collective-permute-start.5 = (f32[15,16,256]{2,1,0:T(8,128)S(1)}, f32[15,16,256]{2,1,0:T(8,128)S(1)}, u32[]{:S(2)}, u32[]{:S(2)}) collective-permute-start(f32[15,16,256]{2,1,0:T(8,128)S(1)} %get-tuple-element.56), channel_id=1, source_target_pairs={{0,96},{32,64},{64,32},{96,0},{1,97},{33,65},{65,33},{97,1},{2,98}... | collective-permute-start | bytes 737288 | tf_op jit(solution)/shard_map/ppermute | solution.py:101
  17.4 0.3 route.1
  17.7 1.1 %filter_middle.1 = (f32[16,16,512]{2,1,0:T(8,128)S(1)}, f32[5,16,16,512]{3,2,1,0:T(8,128)S(1)}) custom-call(f32[16,16,512]{2,1,0:T(8,128)S(1)} %get-tuple-element.57.refs_2_.refs_0_, s32[16,16,512]{2,1,0:T(8,128)S(1)} %get-tuple-element.52.refs_1_, bf16[512,256]{1,0:T(8,128)(2,1)S(1)} %get-tuple-element.58.refs_2_.refs_4_), custom_call_target="tpu_custom_call" | custom-call | tf_op jit(solution)/shard_map/filter_middle/pallas_call | solution.py:116
  18.9 0.0 collective-permute-done.6.refs_0_
  18.9 0.0 copy-start.1
  18.9 0.0 copy-start.3
  18.9 0.0 copy-start.4
  18.9 1.9 %filter_rest.1 = (f32[256,256]{1,0:T(8,128)S(1)}, f32[17,8,256]{2,1,0:T(8,128)S(1)}, f32[17,8,256]{2,1,0:T(8,128)S(1)}, f32[18,8,256]{2,1,0:T(8,128)S(1)}, f32[18,8,256]{2,1,0:T(8,128)S(1)}) custom-call(f32[16,16,512]{2,1,0:T(8,128)S(1)} %get-tuple-element.59.refs_0_, f32[5,16,16,512]{3,2,1,0:T(8,128)S(1)} %get-tuple-element.60.refs_1_, ...), custom_call_target="tpu_custom_call" | custom-call | flops 137438953472 | tf_op jit(solution)/shard_map/filter_rest/pallas_call | solution.py:116
  20.8 3.2 %collective-permute-start.9 = (f32[18,8,256]{2,1,0:T(8,128)S(1)}, f32[18,8,256]{2,1,0:T(8,128)S(1)}, u32[]{:S(2)}, u32[]{:S(2)}) collective-permute-start(f32[18,8,256]{2,1,0:T(8,128)S(1)} %get-tuple-element.69), channel_id=1, source_target_pairs={{0,31},{1,2},{2,1},{3,4},{4,3},{5,6},{6,5},{7,8},{8,7},{9,10},{10,... | collective-permute-start | bytes 442376 | tf_op jit(solution)/shard_map/ppermute | solution.py:101
  24.1 0.0 collective-permute-start.10
  24.1 0.0 collective-permute-done.3.refs_2_
  24.1 1.1 %collective-permute-start.7 = (f32[17,8,256]{2,1,0:T(8,128)S(1)}, f32[17,8,256]{2,1,0:T(8,128)S(1)}, u32[]{:S(2)}, u32[]{:S(2)}) collective-permute-start(f32[17,8,256]{2,1,0:T(8,128)S(1)} %get-tuple-element.67), channel_id=1, source_target_pairs={{0,32},{32,0},{64,96},{96,64},{1,33},{33,1},{65,97},{97,65},{2,34}... | collective-permute-start | bytes 417800 | tf_op jit(solution)/shard_map/ppermute | solution.py:101
  25.2 0.0 collective-permute-done.4.refs_3_
  25.2 1.4 %collective-permute-start.8 = (f32[17,8,256]{2,1,0:T(8,128)S(1)}, f32[17,8,256]{2,1,0:T(8,128)S(1)}, u32[]{:S(2)}, u32[]{:S(2)}) collective-permute-start(f32[17,8,256]{2,1,0:T(8,128)S(1)} %get-tuple-element.68), channel_id=1, source_target_pairs={{0,96},{32,64},{64,32},{96,0},{1,97},{33,65},{65,33},{97,1},{2,98}... | collective-permute-start | bytes 417800 | tf_op jit(solution)/shard_map/ppermute | solution.py:101
  26.6 0.0 collective-permute-done.5.refs_4_
  26.7 1.6 %operator.1 = (f32[5,24,16,256]{3,2,1,0:T(8,128)S(1)}, f32[5,8,16,256]{3,2,1,0:T(8,128)S(1)}) custom-call(f32[5,32,16,256]{3,2,1,0:T(8,128)S(1)} %copy-done.1, f32[40,8,256]{2,1,0:T(8,128)S(1)} %collective-permute-done.2.refs_2_.refs_1_, f32[24,8,256]{2,1,0:T(8,128)S(1)} %collective-permute-done.3.refs_2_, ...), custom_call_target="tpu_custom_call" | custom-call | tf_op jit(solution)/shard_map/operator/pallas_call | solution.py:116
  28.2 1.9 %collective-permute-done.7.refs_2_ = f32[17,8,256]{2,1,0:T(8,128)S(1)} collective-permute-done((f32[17,8,256]{2,1,0:T(8,128)S(1)}, f32[17,8,256]{2,1,0:T(8,128)S(1)}, u32[]{:S(2)}, u32[]{:S(2)}) %collective-permute-start.7) | collective-permute-done | bytes 139296 | tf_op jit(solution)/shard_map/ppermute | solution.py:101
  30.1 2.1 %collective-permute-done.8.refs_3_ = f32[17,8,256]{2,1,0:T(8,128)S(1)} collective-permute-done((f32[17,8,256]{2,1,0:T(8,128)S(1)}, f32[17,8,256]{2,1,0:T(8,128)S(1)}, u32[]{:S(2)}, u32[]{:S(2)}) %collective-permute-start.8) | collective-permute-done | bytes 139296 | tf_op jit(solution)/shard_map/ppermute | solution.py:101
  32.2 0.6 gather.1
  32.8 0.6 collective-permute-start.11
  33.4 0.0 collective-permute-start.12
  33.4 0.3 collective-permute-start.13
  33.8 1.4 %collective-permute-start.14 = (f32[15,16,256]{2,1,0:T(8,128)S(1)}, f32[15,16,256]{2,1,0:T(8,128)S(1)}, u32[]{:S(2)}, u32[]{:S(2)}) collective-permute-start(f32[15,16,256]{2,1,0:T(8,128)S(1)} %get-tuple-element.77), channel_id=1, source_target_pairs={{0,96},{32,64},{64,32},{96,0},{1,97},{33,65},{65,33},{97,1},{2,98}... | collective-permute-start | bytes 737288 | tf_op jit(solution)/shard_map/ppermute | solution.py:101
  35.2 4.0 %collective-permute-start.15 = (f32[6,8,256]{2,1,0:T(8,128)S(1)}, f32[6,8,256]{2,1,0:T(8,128)S(1)}, u32[]{:S(2)}, u32[]{:S(2)}) collective-permute-start(f32[6,8,256]{2,1,0:T(8,128)S(1)} %get-tuple-element.78), channel_id=1, source_target_pairs={{0,31},{1,2},{2,1},{3,4},{4,3},{5,6},{6,5},{7,8},{8,7},{9,10},{10,... | collective-permute-start | bytes 147464 | tf_op jit(solution)/shard_map/ppermute | solution.py:101
  39.2 1.6 %collective-permute-done.11.refs_8_ = f32[18,8,256]{2,1,0:T(8,128)S(1)} collective-permute-done((f32[18,8,256]{2,1,0:T(8,128)S(1)}, f32[18,8,256]{2,1,0:T(8,128)S(1)}, u32[]{:S(2)}, u32[]{:S(2)}) %collective-permute-start.11) | collective-permute-done | bytes 147488 | tf_op jit(solution)/shard_map/ppermute | solution.py:101
  40.8 0.0 collective-permute-start.16
  40.8 0.0 collective-permute-done.12.refs_9_
  40.8 1.5 %stage_inner.2 = (f32[5,24,16,256]{3,2,1,0:T(8,128)S(1)}, f32[18,8,256]{2,1,0:T(8,128)S(1)}, f32[18,8,256]{2,1,0:T(8,128)S(1)}) custom-call(f32[5,24,16,256]{3,2,1,0:T(8,128)S(1)} %get-tuple-element.64.refs_6_.refs_0_.refs_4_.refs_2_.refs_3_, f32[5,8,16,256]{3,2,1,0:T(8,128)S(1)} %get-tuple-element.65.refs_7_.refs_1_.refs_5_.refs_3_.refs_4_, ...), custom_call_target="tpu_custom_call" | custom-call | flops 2000000000 | tf_op jit(solution)/shard_map/stage_inner/pallas_call | solution.py:116
  42.3 0.6 collective-permute-start.17
  42.9 0.1 collective-permute-start.18
  43.0 0.0 collective-permute-done.16.refs_11_
  43.0 0.1 collective-permute-done.14.refs_9_
  43.1 0.6 stage_rim.2
  43.7 0.6 collective-permute-start.19
  44.2 1.8 %collective-permute-start.20 = (f32[15,16,256]{2,1,0:T(8,128)S(1)}, f32[15,16,256]{2,1,0:T(8,128)S(1)}, u32[]{:S(2)}, u32[]{:S(2)}) collective-permute-start(f32[15,16,256]{2,1,0:T(8,128)S(1)} %get-tuple-element.85), channel_id=1, source_target_pairs={{0,96},{32,64},{64,32},{96,0},{1,97},{33,65},{65,33},{97,1},{2,98}... | collective-permute-start | bytes 737288 | tf_op jit(solution)/shard_map/ppermute | solution.py:101
  46.0 3.4 %collective-permute-start.21 = (f32[6,8,256]{2,1,0:T(8,128)S(1)}, f32[6,8,256]{2,1,0:T(8,128)S(1)}, u32[]{:S(2)}, u32[]{:S(2)}) collective-permute-start(f32[6,8,256]{2,1,0:T(8,128)S(1)} %get-tuple-element.86), channel_id=1, source_target_pairs={{0,31},{1,2},{2,1},{3,4},{4,3},{5,6},{6,5},{7,8},{8,7},{9,10},{10,... | collective-permute-start | bytes 147464 | tf_op jit(solution)/shard_map/ppermute | solution.py:101
  49.4 0.8 %collective-permute-done.17.refs_6_ = f32[18,8,256]{2,1,0:T(8,128)S(1)} collective-permute-done((f32[18,8,256]{2,1,0:T(8,128)S(1)}, f32[18,8,256]{2,1,0:T(8,128)S(1)}, u32[]{:S(2)}, u32[]{:S(2)}) %collective-permute-start.17) | collective-permute-done | bytes 147488 | tf_op jit(solution)/shard_map/ppermute | solution.py:101
  50.3 1.4 %stage_inner.3 = (f32[5,24,16,256]{3,2,1,0:T(8,128)S(1)}, f32[18,8,256]{2,1,0:T(8,128)S(1)}, f32[18,8,256]{2,1,0:T(8,128)S(1)}) custom-call(f32[5,24,16,256]{3,2,1,0:T(8,128)S(1)} %get-tuple-element.75.refs_14_.refs_0_, f32[5,8,16,256]{3,2,1,0:T(8,128)S(1)} %get-tuple-element.80.refs_1_, ...), custom_call_target="tpu_custom_call" | custom-call | flops 2000000000 | tf_op jit(solution)/shard_map/stage_inner/pallas_call | solution.py:116
  51.7 0.9 %collective-permute-start.23 = (f32[18,8,256]{2,1,0:T(8,128)S(1)}, f32[18,8,256]{2,1,0:T(8,128)S(1)}, u32[]{:S(2)}, u32[]{:S(2)}) collective-permute-start(f32[18,8,256]{2,1,0:T(8,128)S(1)} %get-tuple-element.89), channel_id=1, source_target_pairs={{0,31},{1,2},{2,1},{3,4},{4,3},{5,6},{6,5},{7,8},{8,7},{9,10},{10,... | collective-permute-start | bytes 442376 | tf_op jit(solution)/shard_map/ppermute | solution.py:101
  52.6 0.3 collective-permute-done.21.refs_8_
  52.8 0.6 collective-permute-done.20.refs_7_
  53.5 0.6 stage_rim.3
  54.1 0.4 collective-permute-start.25
  54.4 1.8 %collective-permute-start.26 = (f32[15,16,256]{2,1,0:T(8,128)S(1)}, f32[15,16,256]{2,1,0:T(8,128)S(1)}, u32[]{:S(2)}, u32[]{:S(2)}) collective-permute-start(f32[15,16,256]{2,1,0:T(8,128)S(1)} %get-tuple-element.92), channel_id=1, source_target_pairs={{0,96},{32,64},{64,32},{96,0},{1,97},{33,65},{65,33},{97,1},{2,98}... | collective-permute-start | bytes 737288 | tf_op jit(solution)/shard_map/ppermute | solution.py:101
  56.2 3.1 %collective-permute-start.27 = (f32[6,8,256]{2,1,0:T(8,128)S(1)}, f32[6,8,256]{2,1,0:T(8,128)S(1)}, u32[]{:S(2)}, u32[]{:S(2)}) collective-permute-start(f32[6,8,256]{2,1,0:T(8,128)S(1)} %get-tuple-element.93), channel_id=1, source_target_pairs={{0,31},{1,2},{2,1},{3,4},{4,3},{5,6},{6,5},{7,8},{8,7},{9,10},{10,... | collective-permute-start | bytes 147464 | tf_op jit(solution)/shard_map/ppermute | solution.py:101
  59.3 0.4 collective-permute-done.23.refs_7_
  59.7 2.4 %final_inner.1.refs_0_ = f32[5,32,16,256]{3,2,1,0:T(8,128)} custom-call(f32[5,24,16,256]{3,2,1,0:T(8,128)S(1)} %get-tuple-element.83.refs_12_.refs_0_.refs_1_, f32[5,8,16,256]{3,2,1,0:T(8,128)S(1)} %get-tuple-element.88.refs_1_.refs_2_, f32[5,24,16,256]{3,2,1,0:T(8,128)S(1)} %get-tuple-element.64.refs_6_.refs_0_.refs_4_.refs_2_.refs_3_, ...), custom_call_target="tpu_custom_call" | custom-call | flops 2000000000 | tf_op jit(solution)/shard_map/final_inner/pallas_call | solution.py:116
  62.0 1.0 %collective-permute-done.27.refs_10_ = f32[6,8,256]{2,1,0:T(8,128)S(1)} collective-permute-done((f32[6,8,256]{2,1,0:T(8,128)S(1)}, f32[6,8,256]{2,1,0:T(8,128)S(1)}, u32[]{:S(2)}, u32[]{:S(2)}) %collective-permute-start.27) | collective-permute-done | bytes 49184 | tf_op jit(solution)/shard_map/ppermute | solution.py:101
  63.0 0.7 %collective-permute-done.26.refs_9_ = f32[15,16,256]{2,1,0:T(8,128)S(1)} collective-permute-done((f32[15,16,256]{2,1,0:T(8,128)S(1)}, f32[15,16,256]{2,1,0:T(8,128)S(1)}, u32[]{:S(2)}, u32[]{:S(2)}) %collective-permute-start.26) | collective-permute-done | bytes 245792 | tf_op jit(solution)/shard_map/ppermute | solution.py:101
  63.7 1.4 %final_rim.1 = f32[5,32,16,256]{3,2,1,0:T(8,128)} custom-call(f32[5,32,16,256]{3,2,1,0:T(8,128)} %final_inner.1.refs_0_, f32[5,24,16,256]{3,2,1,0:T(8,128)S(1)} %get-tuple-element.83.refs_12_.refs_0_.refs_1_, f32[5,8,16,256]{3,2,1,0:T(8,128)S(1)} %get-tuple-element.88.refs_1_.refs_2_, ...), custom_call_target="tpu_custom_call", output_to_operand_aliasing={{}: (0, {})} | custom-call | tf_op jit(solution)/shard_map/final_rim/pallas_call | solution.py:116
  (28 shorter events, 0.1 us)
Async XLA Ops:
  0.0 6.2 %copy-start.5 = (f32[16,16,512]{2,1,0:T(8,128)S(1)}, f32[16,16,512]{2,1,0:T(8,128)}, u32[]{:S(2)}) copy-start(f32[16,16,512]{2,1,0:T(8,128)} %refs_0_.4) | copy-start | bytes 1572868
  1.1 6.7 %collective-permute-start.1 = (f32[4,16,512]{2,1,0:T(8,128)S(1)}, f32[4,16,512]{2,1,0:T(8,128)S(1)}, u32[]{:S(2)}, u32[]{:S(2)}) collective-permute-start(f32[4,16,512]{2,1,0:T(8,128)S(1)} %get-tuple-element.95), channel_id=1, source_target_pairs={{0,96},{32,64},{64,32},{96,0},{1,97},{33,65},{65,33},{97,1},{2,98}... | collective-permute-start | bytes 393224 | tf_op jit(solution)/shard_map/ppermute | solution.py:101
  4.2 5.0 %collective-permute-start = (f32[4,16,512]{2,1,0:T(8,128)S(1)}, f32[4,16,512]{2,1,0:T(8,128)S(1)}, u32[]{:S(2)}, u32[]{:S(2)}) collective-permute-start(f32[4,16,512]{2,1,0:T(8,128)S(1)} %get-tuple-element.96.refs_1_), channel_id=1, source_target_pairs={{0,32},{32,0},{64,96},{96,64},{1,33},{33,1},{65,97},{97,65},{2,34}... | collective-permute-start | bytes 393224 | tf_op jit(solution)/shard_map/ppermute | solution.py:101
  4.4 1.7 %copy-start = (f32[5,32,16,256]{3,2,1,0:T(8,128)S(1)}, f32[5,32,16,256]{3,2,1,0:T(8,128)}, u32[]{:S(2)}) copy-start(f32[5,32,16,256]{3,2,1,0:T(8,128)} %refs_7_.1) | copy-start | bytes 7864324
  6.1 1.0 %copy-start.6 = (s32[16,16,512]{2,1,0:T(8,128)S(1)}, s32[16,16,512]{2,1,0:T(8,128)}, u32[]{:S(2)}) copy-start(s32[16,16,512]{2,1,0:T(8,128)} %refs_1_.1) | copy-start | bytes 1572868
  6.1 11.3 %copy-start.7 = (s32[256]{0:T(256)S(1)}, s32[256]{0:T(256)}, u32[]{:S(2)}) copy-start(s32[256]{0:T(256)} %param.9) | copy-start | bytes 3076
  6.1 11.3 %copy-start.8 = (s32[256]{0:T(256)S(1)}, s32[256]{0:T(256)}, u32[]{:S(2)}) copy-start(s32[256]{0:T(256)} %param.10) | copy-start | bytes 3076
  9.4 9.5 %collective-permute-start.6 = (f32[16,8,256]{2,1,0:T(8,128)S(1)}, f32[16,8,256]{2,1,0:T(8,128)S(1)}, u32[]{:S(2)}, u32[]{:S(2)}) collective-permute-start(f32[16,8,256]{2,1,0:T(8,128)S(1)} %get-tuple-element.61), channel_id=1, source_target_pairs={{0,31},{1,2},{2,1},{3,4},{4,3},{5,6},{6,5},{7,8},{8,7},{9,10},{10,... | collective-permute-start | bytes 393224 | tf_op jit(solution)/shard_map/ppermute | solution.py:101
  14.0 4.9 %collective-permute-start.2 = (f32[40,8,256]{2,1,0:T(8,128)S(1)}, f32[40,8,256]{2,1,0:T(8,128)S(1)}, u32[]{:S(2)}, u32[]{:S(2)}) collective-permute-start(f32[40,8,256]{2,1,0:T(8,128)S(1)} %get-tuple-element.53), channel_id=1, source_target_pairs={{0,1},{1,0},{2,3},{3,2},{4,5},{5,4},{6,7},{7,6},{8,9},{9,8},{10,11... | collective-permute-start | bytes 983048 | tf_op jit(solution)/shard_map/ppermute | solution.py:101
  14.0 10.1 %collective-permute-start.3 = (f32[24,8,256]{2,1,0:T(8,128)S(1)}, f32[24,8,256]{2,1,0:T(8,128)S(1)}, u32[]{:S(2)}, u32[]{:S(2)}) collective-permute-start(f32[24,8,256]{2,1,0:T(8,128)S(1)} %get-tuple-element.54), channel_id=1, source_target_pairs={{0,31},{1,2},{2,1},{3,4},{4,3},{5,6},{6,5},{7,8},{8,7},{9,10},{10,... | collective-permute-start | bytes 589832 | tf_op jit(solution)/shard_map/ppermute | solution.py:107
  15.9 9.3 %collective-permute-start.4 = (f32[15,16,256]{2,1,0:T(8,128)S(1)}, f32[15,16,256]{2,1,0:T(8,128)S(1)}, u32[]{:S(2)}, u32[]{:S(2)}) collective-permute-start(f32[15,16,256]{2,1,0:T(8,128)S(1)} %get-tuple-element.55), channel_id=1, source_target_pairs={{0,32},{32,0},{64,96},{96,64},{1,33},{33,1},{65,97},{97,65},{2,34}... | collective-permute-start | bytes 737288 | tf_op jit(solution)/shard_map/ppermute | solution.py:101
  16.3 10.4 %collective-permute-start.5 = (f32[15,16,256]{2,1,0:T(8,128)S(1)}, f32[15,16,256]{2,1,0:T(8,128)S(1)}, u32[]{:S(2)}, u32[]{:S(2)}) collective-permute-start(f32[15,16,256]{2,1,0:T(8,128)S(1)} %get-tuple-element.56), channel_id=1, source_target_pairs={{0,96},{32,64},{64,32},{96,0},{1,97},{33,65},{65,33},{97,1},{2,98}... | collective-permute-start | bytes 737288 | tf_op jit(solution)/shard_map/ppermute | solution.py:101
  18.9 7.7 %copy-start.1 = (f32[5,32,16,256]{3,2,1,0:T(8,128)S(1)}, f32[5,32,16,256]{3,2,1,0:T(8,128)}, u32[]{:S(2)}) copy-start(f32[5,32,16,256]{3,2,1,0:T(8,128)} %refs_7_.1) | copy-start | bytes 7864324
  18.9 7.7 %copy-start.3 = (bf16[2,2,256,256]{3,2,1,0:T(8,128)(2,1)S(1)}, bf16[2,2,256,256]{3,2,1,0:T(8,128)(2,1)}, u32[]{:S(2)}) copy-start(bf16[2,2,256,256]{3,2,1,0:T(8,128)(2,1)} %constant.17.clone.refs_6_.refs_11_.refs_13_.refs_9_.refs_10_) | copy-start | bytes 1572868
  18.9 7.7 %copy-start.4 = (bf16[2,2,128,224]{3,2,1,0:T(8,128)(2,1)S(1)}, bf16[2,2,128,224]{3,2,1,0:T(8,128)(2,1)}, u32[]{:S(2)}) copy-start(bf16[2,2,128,224]{3,2,1,0:T(8,128)(2,1)} %constant.16.clone.refs_5_.refs_10_.refs_12_.refs_8_.refs_9_) | copy-start | bytes 688132
  20.8 11.4 %collective-permute-start.9 = (f32[18,8,256]{2,1,0:T(8,128)S(1)}, f32[18,8,256]{2,1,0:T(8,128)S(1)}, u32[]{:S(2)}, u32[]{:S(2)}) collective-permute-start(f32[18,8,256]{2,1,0:T(8,128)S(1)} %get-tuple-element.69), channel_id=1, source_target_pairs={{0,31},{1,2},{2,1},{3,4},{4,3},{5,6},{6,5},{7,8},{8,7},{9,10},{10,... | collective-permute-start | bytes 442376 | tf_op jit(solution)/shard_map/ppermute | solution.py:101
  24.1 8.2 %collective-permute-start.10 = (f32[18,8,256]{2,1,0:T(8,128)S(1)}, f32[18,8,256]{2,1,0:T(8,128)S(1)}, u32[]{:S(2)}, u32[]{:S(2)}) collective-permute-start(f32[18,8,256]{2,1,0:T(8,128)S(1)} %get-tuple-element.70), channel_id=1, source_target_pairs={{0,1},{1,0},{2,3},{3,2},{4,5},{5,4},{6,7},{7,6},{8,9},{9,8},{10,11... | collective-permute-start | bytes 442376 | tf_op jit(solution)/shard_map/ppermute | solution.py:101
  24.1 6.1 %collective-permute-start.7 = (f32[17,8,256]{2,1,0:T(8,128)S(1)}, f32[17,8,256]{2,1,0:T(8,128)S(1)}, u32[]{:S(2)}, u32[]{:S(2)}) collective-permute-start(f32[17,8,256]{2,1,0:T(8,128)S(1)} %get-tuple-element.67), channel_id=1, source_target_pairs={{0,32},{32,0},{64,96},{96,64},{1,33},{33,1},{65,97},{97,65},{2,34}... | collective-permute-start | bytes 417800 | tf_op jit(solution)/shard_map/ppermute | solution.py:101
  25.2 7.0 %collective-permute-start.8 = (f32[17,8,256]{2,1,0:T(8,128)S(1)}, f32[17,8,256]{2,1,0:T(8,128)S(1)}, u32[]{:S(2)}, u32[]{:S(2)}) collective-permute-start(f32[17,8,256]{2,1,0:T(8,128)S(1)} %get-tuple-element.68), channel_id=1, source_target_pairs={{0,96},{32,64},{64,32},{96,0},{1,97},{33,65},{65,33},{97,1},{2,98}... | collective-permute-start | bytes 417800 | tf_op jit(solution)/shard_map/ppermute | solution.py:101
  32.8 8.0 %collective-permute-start.11 = (f32[18,8,256]{2,1,0:T(8,128)S(1)}, f32[18,8,256]{2,1,0:T(8,128)S(1)}, u32[]{:S(2)}, u32[]{:S(2)}) collective-permute-start(f32[18,8,256]{2,1,0:T(8,128)S(1)} %get-tuple-element.73), channel_id=1, source_target_pairs={{0,31},{1,2},{2,1},{3,4},{4,3},{5,6},{6,5},{7,8},{8,7},{9,10},{10,... | collective-permute-start | bytes 442376 | tf_op jit(solution)/shard_map/ppermute | solution.py:101
  33.4 7.4 %collective-permute-start.12 = (f32[18,8,256]{2,1,0:T(8,128)S(1)}, f32[18,8,256]{2,1,0:T(8,128)S(1)}, u32[]{:S(2)}, u32[]{:S(2)}) collective-permute-start(f32[18,8,256]{2,1,0:T(8,128)S(1)} %get-tuple-element.74), channel_id=1, source_target_pairs={{0,1},{1,0},{2,3},{3,2},{4,5},{5,4},{6,7},{7,6},{8,9},{9,8},{10,11... | collective-permute-start | bytes 442376 | tf_op jit(solution)/shard_map/ppermute | solution.py:101
  33.4 9.6 %collective-permute-start.13 = (f32[15,16,256]{2,1,0:T(8,128)S(1)}, f32[15,16,256]{2,1,0:T(8,128)S(1)}, u32[]{:S(2)}, u32[]{:S(2)}) collective-permute-start(f32[15,16,256]{2,1,0:T(8,128)S(1)} %get-tuple-element.76), channel_id=1, source_target_pairs={{0,32},{32,0},{64,96},{96,64},{1,33},{33,1},{65,97},{97,65},{2,34}... | collective-permute-start | bytes 737288 | tf_op jit(solution)/shard_map/ppermute | solution.py:101
  33.8 9.3 %collective-permute-start.14 = (f32[15,16,256]{2,1,0:T(8,128)S(1)}, f32[15,16,256]{2,1,0:T(8,128)S(1)}, u32[]{:S(2)}, u32[]{:S(2)}) collective-permute-start(f32[15,16,256]{2,1,0:T(8,128)S(1)} %get-tuple-element.77), channel_id=1, source_target_pairs={{0,96},{32,64},{64,32},{96,0},{1,97},{33,65},{65,33},{97,1},{2,98}... | collective-permute-start | bytes 737288 | tf_op jit(solution)/shard_map/ppermute | solution.py:101
  35.2 7.7 %collective-permute-start.15 = (f32[6,8,256]{2,1,0:T(8,128)S(1)}, f32[6,8,256]{2,1,0:T(8,128)S(1)}, u32[]{:S(2)}, u32[]{:S(2)}) collective-permute-start(f32[6,8,256]{2,1,0:T(8,128)S(1)} %get-tuple-element.78), channel_id=1, source_target_pairs={{0,31},{1,2},{2,1},{3,4},{4,3},{5,6},{6,5},{7,8},{8,7},{9,10},{10,... | collective-permute-start | bytes 147464 | tf_op jit(solution)/shard_map/ppermute | solution.py:101
  40.8 2.2 %collective-permute-start.16 = (f32[6,8,256]{2,1,0:T(8,128)S(1)}, f32[6,8,256]{2,1,0:T(8,128)S(1)}, u32[]{:S(2)}, u32[]{:S(2)}) collective-permute-start(f32[6,8,256]{2,1,0:T(8,128)S(1)} %get-tuple-element.79), channel_id=1, source_target_pairs={{0,1},{1,0},{2,3},{3,2},{4,5},{5,4},{6,7},{7,6},{8,9},{9,8},{10,11... | collective-permute-start | bytes 147464 | tf_op jit(solution)/shard_map/ppermute | solution.py:101
  42.3 8.0 %collective-permute-start.17 = (f32[18,8,256]{2,1,0:T(8,128)S(1)}, f32[18,8,256]{2,1,0:T(8,128)S(1)}, u32[]{:S(2)}, u32[]{:S(2)}) collective-permute-start(f32[18,8,256]{2,1,0:T(8,128)S(1)} %get-tuple-element.81), channel_id=1, source_target_pairs={{0,31},{1,2},{2,1},{3,4},{4,3},{5,6},{6,5},{7,8},{8,7},{9,10},{10,... | collective-permute-start | bytes 442376 | tf_op jit(solution)/shard_map/ppermute | solution.py:101
  42.9 7.4 %collective-permute-start.18 = (f32[18,8,256]{2,1,0:T(8,128)S(1)}, f32[18,8,256]{2,1,0:T(8,128)S(1)}, u32[]{:S(2)}, u32[]{:S(2)}) collective-permute-start(f32[18,8,256]{2,1,0:T(8,128)S(1)} %get-tuple-element.82), channel_id=1, source_target_pairs={{0,1},{1,0},{2,3},{3,2},{4,5},{5,4},{6,7},{7,6},{8,9},{9,8},{10,11... | collective-permute-start | bytes 442376 | tf_op jit(solution)/shard_map/ppermute | solution.py:101
  43.7 9.2 %collective-permute-start.19 = (f32[15,16,256]{2,1,0:T(8,128)S(1)}, f32[15,16,256]{2,1,0:T(8,128)S(1)}, u32[]{:S(2)}, u32[]{:S(2)}) collective-permute-start(f32[15,16,256]{2,1,0:T(8,128)S(1)} %get-tuple-element.84), channel_id=1, source_target_pairs={{0,32},{32,0},{64,96},{96,64},{1,33},{33,1},{65,97},{97,65},{2,34}... | collective-permute-start | bytes 737288 | tf_op jit(solution)/shard_map/ppermute | solution.py:101
  44.2 9.2 %collective-permute-start.20 = (f32[15,16,256]{2,1,0:T(8,128)S(1)}, f32[15,16,256]{2,1,0:T(8,128)S(1)}, u32[]{:S(2)}, u32[]{:S(2)}) collective-permute-start(f32[15,16,256]{2,1,0:T(8,128)S(1)} %get-tuple-element.85), channel_id=1, source_target_pairs={{0,96},{32,64},{64,32},{96,0},{1,97},{33,65},{65,33},{97,1},{2,98}... | collective-permute-start | bytes 737288 | tf_op jit(solution)/shard_map/ppermute | solution.py:101
  46.0 6.8 %collective-permute-start.21 = (f32[6,8,256]{2,1,0:T(8,128)S(1)}, f32[6,8,256]{2,1,0:T(8,128)S(1)}, u32[]{:S(2)}, u32[]{:S(2)}) collective-permute-start(f32[6,8,256]{2,1,0:T(8,128)S(1)} %get-tuple-element.86), channel_id=1, source_target_pairs={{0,31},{1,2},{2,1},{3,4},{4,3},{5,6},{6,5},{7,8},{8,7},{9,10},{10,... | collective-permute-start | bytes 147464 | tf_op jit(solution)/shard_map/ppermute | solution.py:101
  50.3 2.6 %collective-permute-start.22 = (f32[6,8,256]{2,1,0:T(8,128)S(1)}, f32[6,8,256]{2,1,0:T(8,128)S(1)}, u32[]{:S(2)}, u32[]{:S(2)}) collective-permute-start(f32[6,8,256]{2,1,0:T(8,128)S(1)} %get-tuple-element.87), channel_id=1, source_target_pairs={{0,1},{1,0},{2,3},{3,2},{4,5},{5,4},{6,7},{7,6},{8,9},{9,8},{10,11... | collective-permute-start | bytes 147464 | tf_op jit(solution)/shard_map/ppermute | solution.py:101
  51.7 8.0 %collective-permute-start.23 = (f32[18,8,256]{2,1,0:T(8,128)S(1)}, f32[18,8,256]{2,1,0:T(8,128)S(1)}, u32[]{:S(2)}, u32[]{:S(2)}) collective-permute-start(f32[18,8,256]{2,1,0:T(8,128)S(1)} %get-tuple-element.89), channel_id=1, source_target_pairs={{0,31},{1,2},{2,1},{3,4},{4,3},{5,6},{6,5},{7,8},{8,7},{9,10},{10,... | collective-permute-start | bytes 442376 | tf_op jit(solution)/shard_map/ppermute | solution.py:101
  52.8 6.8 %collective-permute-start.24 = (f32[18,8,256]{2,1,0:T(8,128)S(1)}, f32[18,8,256]{2,1,0:T(8,128)S(1)}, u32[]{:S(2)}, u32[]{:S(2)}) collective-permute-start(f32[18,8,256]{2,1,0:T(8,128)S(1)} %get-tuple-element.90), channel_id=1, source_target_pairs={{0,1},{1,0},{2,3},{3,2},{4,5},{5,4},{6,7},{7,6},{8,9},{9,8},{10,11... | collective-permute-start | bytes 442376 | tf_op jit(solution)/shard_map/ppermute | solution.py:101
  53.5 6.2 %copy-start.2 = (f32[5,32,16,256]{3,2,1,0:T(8,128)S(1)}, f32[5,32,16,256]{3,2,1,0:T(8,128)}, u32[]{:S(2)}) copy-start(f32[5,32,16,256]{3,2,1,0:T(8,128)} %refs_7_.1) | copy-start | bytes 7864324
  54.1 9.0 %collective-permute-start.25 = (f32[15,16,256]{2,1,0:T(8,128)S(1)}, f32[15,16,256]{2,1,0:T(8,128)S(1)}, u32[]{:S(2)}, u32[]{:S(2)}) collective-permute-start(f32[15,16,256]{2,1,0:T(8,128)S(1)} %get-tuple-element.91), channel_id=1, source_target_pairs={{0,32},{32,0},{64,96},{96,64},{1,33},{33,1},{65,97},{97,65},{2,34}... | collective-permute-start | bytes 737288 | tf_op jit(solution)/shard_map/ppermute | solution.py:101
  54.4 9.3 %collective-permute-start.26 = (f32[15,16,256]{2,1,0:T(8,128)S(1)}, f32[15,16,256]{2,1,0:T(8,128)S(1)}, u32[]{:S(2)}, u32[]{:S(2)}) collective-permute-start(f32[15,16,256]{2,1,0:T(8,128)S(1)} %get-tuple-element.92), channel_id=1, source_target_pairs={{0,96},{32,64},{64,32},{96,0},{1,97},{33,65},{65,33},{97,1},{2,98}... | collective-permute-start | bytes 737288 | tf_op jit(solution)/shard_map/ppermute | solution.py:101
  56.2 6.8 %collective-permute-start.27 = (f32[6,8,256]{2,1,0:T(8,128)S(1)}, f32[6,8,256]{2,1,0:T(8,128)S(1)}, u32[]{:S(2)}, u32[]{:S(2)}) collective-permute-start(f32[6,8,256]{2,1,0:T(8,128)S(1)} %get-tuple-element.93), channel_id=1, source_target_pairs={{0,31},{1,2},{2,1},{3,4},{4,3},{5,6},{6,5},{7,8},{8,7},{9,10},{10,... | collective-permute-start | bytes 147464 | tf_op jit(solution)/shard_map/ppermute | solution.py:101
  59.6 3.4 %collective-permute-start.28 = (f32[6,8,256]{2,1,0:T(8,128)S(1)}, f32[6,8,256]{2,1,0:T(8,128)S(1)}, u32[]{:S(2)}, u32[]{:S(2)}) collective-permute-start(f32[6,8,256]{2,1,0:T(8,128)S(1)} %get-tuple-element.94), channel_id=1, source_target_pairs={{0,1},{1,0},{2,3},{3,2},{4,5},{5,4},{6,7},{7,6},{8,9},{9,8},{10,11... | collective-permute-start | bytes 147464 | tf_op jit(solution)/shard_map/ppermute | solution.py:101

commit v13 on v12

--- a/solution.py
+++ b/solution.py
@@ -292,26 +292,26 @@
         tiles = most // 8
         out[0:tiles] = (dot(pick, hi) + dot(pick, lo)).reshape(tiles, 8, radial)
         out[tiles] = cells_ref[d]
-    for out in (to_za, to_zb):
-        out[most // 8 + 1] = jnp.zeros(out.shape[1:], F32)
+    for out in (to_xa, to_xb, to_zb):
+        out[most // 8 + 1 :] = jnp.zeros((out.shape[0] - most // 8 - 1, *out.shape[1:]), F32)
+
+
+def onehot(cells, row):
+    at = lax.broadcasted_iota(jnp.int32, (cells, row.shape[1]), 0)
+    return jnp.where(at == row, 1.0, 0.0).astype(BF16)
 
 
 def gather_body(
-    binned_ref, own_ref, xa, xb, zb, za, k_mid, k_rim, p_mid, p_rim, to_xa, to_xb, to_za, to_zb, rim_za, rim_zb
+    xa, xb, zb, za, k_mid, k_rim, p_mid, p_rim, to_xa, to_xb, to_za, to_zb, rim_za, rim_zb
 ):
     mid, cols, radial = p_mid.shape
     cells = (mid + 2 * RIM) * cols
-    most = 8 * (xa.shape[0] - 1)
-
-    def onehot(row):
-        at = lax.broadcasted_iota(jnp.int32, (cells, row.shape[1]), 0)
-        return jnp.where(at == row, 1.0, 0.0).astype(BF16)
-
-    mats = [onehot(own_ref[...])]
-    packets = [binned_ref[...]]
+    most = 8 * (za.shape[0] - 1)
+
+    mats, packets = [], []
     for got in (xa, xb, za, zb):
         tiles = most // 8
-        mats.append(onehot(got[tiles, 0:1, 0:most].astype(jnp.int32)))
+        mats.append(onehot(cells, got[tiles, 0:1, 0:most].astype(jnp.int32)))
         packets.append(got[0:tiles].reshape(most, radial))
     mat = jnp.concatenate(mats, axis=1)
     hi, lo = split(jnp.concatenate(packets, axis=0))
@@ -502,13 +502,17 @@
             )
 
 
-def start_body(state, za, zb, xa, xb, tmat, rmat, k_mid, k_rim, halo):
+def start_body(state, za, zb, xa, xb, tmat, rmat, binned, own, k_mid, k_rim, halo, source):
+    rows, cols, radial = source.shape
+    hi, lo = split(binned[...])
+    mat = onehot(rows * cols, own[...])
+    source[...] = (dot(mat, hi) + dot(mat, lo)).reshape(rows, cols, radial)
     fill_halo(halo, xa, xb)
     level, out = Whole(state), Parts(k_mid, k_rim)
 
     def finish(x, tend):
         for f in range(5):
-            out.store(f, x, tend[f])
+            out.store(f, x, tend[f] + source[x] if f == 4 else tend[f])
 
     apply_operator(level, [*range(k_mid.shape[1] // GROUP), None], za, zb, tmat, rmat, finish, halo)
 
@@ -629,10 +633,10 @@
         unpack_body, [((px // 2, 8, fine), F32)], [got_b], name="unpack", after=[weights], cost=MORE
     )
     tiles = most // 8 + 1
-    packet, packet_z = ((tiles, 8, radial), F32), ((tiles + 1, 8, radial), F32)
+    packet, packet_x, packet_b = [((tiles + spare, 8, radial), F32) for spare in (0, 1, 2)]
     binned, xa, xb, za, zb = full_specs(
         second_body,
-        [((ncols, radial), F32), packet, packet, packet_z, packet_z],
+        [((ncols, radial), F32), packet_x, packet_x, packet, packet_b],
         [partial, weights, got_a, got_b, pick, cells],
         [((ncols, fine), BF16), ((ncols, fine), BF16)],
         name="filter_rest",
@@ -646,13 +650,13 @@
     mid, rim = ((5, inner, ca, radial), F32), ((5, 2 * RIM, ca, radial), F32)
     halo = ((2, 5, 3, ca, radial), F32)
     k_mid, k_rim = full_specs(
-        start_body, [mid, rim], [fields, got_a, uzb, uxa, uxb, tmat, rmat], [halo], name="operator", after=[binned]
+        start_body, [mid, rim], [fields, got_a, uzb, uxa, uxb, tmat, rmat, binned, own], [halo, ((cx, ca, radial), F32)], name="operator"
     )
     inner_z, rim_z = ((inner // 4 * 3, 8, radial), F32), ((RIM // 2 * 3, 8, radial), F32)
     p_mid, p_rim, *edges = full_specs(
         gather_body,
         [((inner, ca, radial), F32), ((2 * RIM, ca, radial), F32), send_x, send_x, inner_z, inner_z, rim_z, rim_z],
-        [binned, own, *packets, k_mid, k_rim],
+        [*packets, k_mid, k_rim],
         name="gather",
     )
     k = [k_mid, k_rim, p_mid, p_rim]

time: 65.8 us -> 65.5 us (level)
  starting transfers between devices: 36.1 us -> 35.2 us
    ppermute x14, waiting for transfers between devices: 7.59 us -> 9.42 us  [swap(): lax.ppermute(to_b, axis, pairs_b)]
    ppermute x14, waiting for transfers between devices: 3.43 us -> 1.97 us  [swap(): lax.ppermute(to_a, axis, pairs_a)]
    ppermute x14, starting transfers between devices: 31.1 us -> 30.2 us  [swap(): lax.ppermute(to_b, axis, pairs_b)]
  transfers between devices with their start and end apart: 29 -> 29, of which waited for: 12 -> 12; matrix products, arithmetic and copies ran while one was open for 0% -> 0% of each run, Pallas kernels for 18% -> 19%
where the time goes in v13:
time: 65.5 us; the launch traced here: 65 us
  starting transfers between devices  35.2 us (54%)
  Pallas kernels  14.3 us (22%)
  waiting for transfers between devices  11.4 us (17%)
  local copies, waits for them, and re-layouts  2.68 us (4%)
  other arithmetic  1.05 us (2%)
    ppermute x14, starting transfers between devices, swap(): lax.ppermute(to_b, axis, pairs_b)  30.2 us
    pallas_call x15, Pallas kernels, full_specs(): pl.pallas_call(run, out_shape=[jax.ShapeDtypeStruct(s, d) for s, d in out...  14.3 us
    ppermute x14, waiting for transfers between devices, swap(): lax.ppermute(to_b, axis, pairs_b)  9.42 us
    ppermute x14, starting transfers between devices, swap(): lax.ppermute(to_a, axis, pairs_a)  3.1 us
    unnamed x18, local copies, waits for them, and re-layouts  2.68 us
    ppermute x14, waiting for transfers between devices, swap(): lax.ppermute(to_a, axis, pairs_a)  1.97 us
    ppermute x1, starting transfers between devices, swap_b(): return (lax.ppermute(value, axis, pairs),)  1.96 us
  transfers between devices with their start and end apart: 29, of which 12 were waited for; matrix products, arithmetic and copies ran while one was open for 0% of the time, Pallas kernels for 19%

profile of v13, /device:TPU:0, one launch (start us, length us, event | category | flops | bytes accessed | tf_op | source)
XLA Modules:
  0.0 65.0 jit_solution(6937473578104766643)
XLA Ops:
  0.0 1.0 %slice_select_fusion = (f32[4,16,512]{2,1,0:T(8,128)S(1)}, f32[4,16,512]{2,1,0:T(8,128)S(1)}) fusion(f32[16,16,512]{2,1,0:T(8,128)} %refs_0_.4, pred[]{:T(512)S(6)} %eq.3), kind=kLoop, calls=%fused_computation | loop fusion | flops 65536 | bytes 524289 | tf_op jit(solution)/shard_map/jit(_where)/select_n | solution.py:598
  1.1 3.2 %collective-permute-start.1 = (f32[4,16,512]{2,1,0:T(8,128)S(1)}, f32[4,16,512]{2,1,0:T(8,128)S(1)}, u32[]{:S(2)}, u32[]{:S(2)}) collective-permute-start(f32[4,16,512]{2,1,0:T(8,128)S(1)} %get-tuple-element.95), channel_id=1, source_target_pairs={{0,96},{32,64},{64,32},{96,0},{1,97},{33,65},{65,33},{97,1},{2,98}... | collective-permute-start | bytes 393224 | tf_op jit(solution)/shard_map/ppermute | solution.py:101
  4.2 0.1 collective-permute-start
  4.4 1.7 %copy-done = f32[5,32,16,256]{3,2,1,0:T(8,128)S(1)} copy-done((f32[5,32,16,256]{3,2,1,0:T(8,128)S(1)}, f32[5,32,16,256]{3,2,1,0:T(8,128)}, u32[]{:S(2)}) %copy-start) | copy-done | bytes 2621464
  6.1 0.1 edges.1
  6.3 0.9 %copy-done.6 = s32[16,16,512]{2,1,0:T(8,128)S(1)} copy-done((s32[16,16,512]{2,1,0:T(8,128)S(1)}, s32[16,16,512]{2,1,0:T(8,128)}, u32[]{:S(2)}) %copy-start.6) | copy-done | bytes 524312
  7.2 0.5 filter_inner.1
  7.6 0.1 collective-permute-done.1.refs_3_
  7.7 1.5 %collective-permute-done.refs_2_ = f32[4,16,512]{2,1,0:T(8,128)S(1)} collective-permute-done((f32[4,16,512]{2,1,0:T(8,128)S(1)}, f32[4,16,512]{2,1,0:T(8,128)S(1)}, u32[]{:S(2)}, u32[]{:S(2)}) %collective-permute-start) | collective-permute-done | bytes 131104 | tf_op jit(solution)/shard_map/ppermute | solution.py:101
  9.2 0.2 filter_axial.1
  9.4 4.6 %collective-permute-start.6 = (f32[16,8,256]{2,1,0:T(8,128)S(1)}, f32[16,8,256]{2,1,0:T(8,128)S(1)}, u32[]{:S(2)}, u32[]{:S(2)}) collective-permute-start(f32[16,8,256]{2,1,0:T(8,128)S(1)} %get-tuple-element.61), channel_id=1, source_target_pairs={{0,31},{1,2},{2,1},{3,4},{4,3},{5,6},{6,5},{7,8},{8,7},{9,10},{10,... | collective-permute-start | bytes 393224 | tf_op jit(solution)/shard_map/ppermute | solution.py:101
  14.0 0.0 collective-permute-start.2
  14.0 2.0 %collective-permute-start.3 = (f32[24,8,256]{2,1,0:T(8,128)S(1)}, f32[24,8,256]{2,1,0:T(8,128)S(1)}, u32[]{:S(2)}, u32[]{:S(2)}) collective-permute-start(f32[24,8,256]{2,1,0:T(8,128)S(1)} %get-tuple-element.54), channel_id=1, source_target_pairs={{0,31},{1,2},{2,1},{3,4},{4,3},{5,6},{6,5},{7,8},{8,7},{9,10},{10,... | collective-permute-start | bytes 589832 | tf_op jit(solution)/shard_map/ppermute | solution.py:107
  15.9 0.4 collective-permute-start.4
  16.3 1.1 %collective-permute-start.5 = (f32[15,16,256]{2,1,0:T(8,128)S(1)}, f32[15,16,256]{2,1,0:T(8,128)S(1)}, u32[]{:S(2)}, u32[]{:S(2)}) collective-permute-start(f32[15,16,256]{2,1,0:T(8,128)S(1)} %get-tuple-element.56), channel_id=1, source_target_pairs={{0,96},{32,64},{64,32},{96,0},{1,97},{33,65},{65,33},{97,1},{2,98}... | collective-permute-start | bytes 737288 | tf_op jit(solution)/shard_map/ppermute | solution.py:101
  17.4 0.3 route.1
  17.7 1.1 %filter_middle.1 = (f32[16,16,512]{2,1,0:T(8,128)S(1)}, f32[5,16,16,512]{3,2,1,0:T(8,128)S(1)}) custom-call(f32[16,16,512]{2,1,0:T(8,128)S(1)} %get-tuple-element.57.refs_2_.refs_0_, s32[16,16,512]{2,1,0:T(8,128)S(1)} %get-tuple-element.52.refs_1_, bf16[512,256]{1,0:T(8,128)(2,1)S(1)} %get-tuple-element.58.refs_2_.refs_4_), custom_call_target="tpu_custom_call" | custom-call | tf_op jit(solution)/shard_map/filter_middle/pallas_call | solution.py:116
  18.9 0.0 collective-permute-done.6.refs_0_
  18.9 0.0 copy-start.1
  18.9 0.0 copy-start.3
  18.9 0.0 copy-start.4
  18.9 1.9 %filter_rest.1 = (f32[256,256]{1,0:T(8,128)S(1)}, f32[18,8,256]{2,1,0:T(8,128)S(1)}, f32[18,8,256]{2,1,0:T(8,128)S(1)}, f32[17,8,256]{2,1,0:T(8,128)S(1)}, f32[19,8,256]{2,1,0:T(8,128)S(1)}) custom-call(f32[16,16,512]{2,1,0:T(8,128)S(1)} %get-tuple-element.59.refs_0_, f32[5,16,16,512]{3,2,1,0:T(8,128)S(1)} %get-tuple-element.60.refs_1_, ...), custom_call_target="tpu_custom_call" | custom-call | flops 137438953472 | tf_op jit(solution)/shard_map/filter_rest/pallas_call | solution.py:116
  20.9 3.2 %collective-permute-start.9 = (f32[19,8,256]{2,1,0:T(8,128)S(1)}, f32[19,8,256]{2,1,0:T(8,128)S(1)}, u32[]{:S(2)}, u32[]{:S(2)}) collective-permute-start(f32[19,8,256]{2,1,0:T(8,128)S(1)} %get-tuple-element.69), channel_id=1, source_target_pairs={{0,31},{1,2},{2,1},{3,4},{4,3},{5,6},{6,5},{7,8},{8,7},{9,10},{10,... | collective-permute-start | bytes 466952 | tf_op jit(solution)/shard_map/ppermute | solution.py:101
  24.1 1.1 %collective-permute-start.7 = (f32[18,8,256]{2,1,0:T(8,128)S(1)}, f32[18,8,256]{2,1,0:T(8,128)S(1)}, u32[]{:S(2)}, u32[]{:S(2)}) collective-permute-start(f32[18,8,256]{2,1,0:T(8,128)S(1)} %get-tuple-element.67), channel_id=1, source_target_pairs={{0,32},{32,0},{64,96},{96,64},{1,33},{33,1},{65,97},{97,65},{2,34}... | collective-permute-start | bytes 442376 | tf_op jit(solution)/shard_map/ppermute | solution.py:101
  25.3 1.4 %collective-permute-start.8 = (f32[18,8,256]{2,1,0:T(8,128)S(1)}, f32[18,8,256]{2,1,0:T(8,128)S(1)}, u32[]{:S(2)}, u32[]{:S(2)}) collective-permute-start(f32[18,8,256]{2,1,0:T(8,128)S(1)} %get-tuple-element.68), channel_id=1, source_target_pairs={{0,96},{32,64},{64,32},{96,0},{1,97},{33,65},{65,33},{97,1},{2,98}... | collective-permute-start | bytes 442376 | tf_op jit(solution)/shard_map/ppermute | solution.py:101
  26.7 0.0 collective-permute-done.5.refs_4_
  26.7 2.0 %operator.1 = (f32[5,24,16,256]{3,2,1,0:T(8,128)S(1)}, f32[5,8,16,256]{3,2,1,0:T(8,128)S(1)}) custom-call(f32[5,32,16,256]{3,2,1,0:T(8,128)S(1)} %copy-done.1, f32[40,8,256]{2,1,0:T(8,128)S(1)} %collective-permute-done.2.refs_2_.refs_1_, f32[24,8,256]{2,1,0:T(8,128)S(1)} %collective-permute-done.3.refs_2_, ...), custom_call_target="tpu_custom_call" | custom-call | tf_op jit(solution)/shard_map/operator/pallas_call | solution.py:116
  28.8 0.0 collective-permute-done.10.refs_3_
  28.8 0.5 collective-permute-done.7.refs_0_
  29.3 2.4 %collective-permute-done.8.refs_1_ = f32[18,8,256]{2,1,0:T(8,128)S(1)} collective-permute-done((f32[18,8,256]{2,1,0:T(8,128)S(1)}, f32[18,8,256]{2,1,0:T(8,128)S(1)}, u32[]{:S(2)}, u32[]{:S(2)}) %collective-permute-start.8) | collective-permute-done | bytes 147488 | tf_op jit(solution)/shard_map/ppermute | solution.py:101
  31.6 0.0 collective-permute-done.9.refs_2_
  31.6 0.5 gather.1
  32.1 0.8 %collective-permute-start.11 = (f32[18,8,256]{2,1,0:T(8,128)S(1)}, f32[18,8,256]{2,1,0:T(8,128)S(1)}, u32[]{:S(2)}, u32[]{:S(2)}) collective-permute-start(f32[18,8,256]{2,1,0:T(8,128)S(1)} %get-tuple-element.73), channel_id=1, source_target_pairs={{0,31},{1,2},{2,1},{3,4},{4,3},{5,6},{6,5},{7,8},{8,7},{9,10},{10,... | collective-permute-start | bytes 442376 | tf_op jit(solution)/shard_map/ppermute | solution.py:101
  32.9 0.0 collective-permute-start.12
  32.9 0.8 %collective-permute-start.13 = (f32[15,16,256]{2,1,0:T(8,128)S(1)}, f32[15,16,256]{2,1,0:T(8,128)S(1)}, u32[]{:S(2)}, u32[]{:S(2)}) collective-permute-start(f32[15,16,256]{2,1,0:T(8,128)S(1)} %get-tuple-element.76), channel_id=1, source_target_pairs={{0,32},{32,0},{64,96},{96,64},{1,33},{33,1},{65,97},{97,65},{2,34}... | collective-permute-start | bytes 737288 | tf_op jit(solution)/shard_map/ppermute | solution.py:101
  33.8 1.4 %collective-permute-start.14 = (f32[15,16,256]{2,1,0:T(8,128)S(1)}, f32[15,16,256]{2,1,0:T(8,128)S(1)}, u32[]{:S(2)}, u32[]{:S(2)}) collective-permute-start(f32[15,16,256]{2,1,0:T(8,128)S(1)} %get-tuple-element.77), channel_id=1, source_target_pairs={{0,96},{32,64},{64,32},{96,0},{1,97},{33,65},{65,33},{97,1},{2,98}... | collective-permute-start | bytes 737288 | tf_op jit(solution)/shard_map/ppermute | solution.py:101
  35.2 3.3 %collective-permute-start.15 = (f32[6,8,256]{2,1,0:T(8,128)S(1)}, f32[6,8,256]{2,1,0:T(8,128)S(1)}, u32[]{:S(2)}, u32[]{:S(2)}) collective-permute-start(f32[6,8,256]{2,1,0:T(8,128)S(1)} %get-tuple-element.78), channel_id=1, source_target_pairs={{0,31},{1,2},{2,1},{3,4},{4,3},{5,6},{6,5},{7,8},{8,7},{9,10},{10,... | collective-permute-start | bytes 147464 | tf_op jit(solution)/shard_map/ppermute | solution.py:101
  38.5 1.6 %collective-permute-done.11.refs_8_ = f32[18,8,256]{2,1,0:T(8,128)S(1)} collective-permute-done((f32[18,8,256]{2,1,0:T(8,128)S(1)}, f32[18,8,256]{2,1,0:T(8,128)S(1)}, u32[]{:S(2)}, u32[]{:S(2)}) %collective-permute-start.11) | collective-permute-done | bytes 147488 | tf_op jit(solution)/shard_map/ppermute | solution.py:101
  40.1 0.0 collective-permute-start.16
  40.1 0.0 collective-permute-done.12.refs_9_
  40.1 1.4 %stage_inner.2 = (f32[5,24,16,256]{3,2,1,0:T(8,128)S(1)}, f32[18,8,256]{2,1,0:T(8,128)S(1)}, f32[18,8,256]{2,1,0:T(8,128)S(1)}) custom-call(f32[5,24,16,256]{3,2,1,0:T(8,128)S(1)} %get-tuple-element.65.refs_4_.refs_0_.refs_2_.refs_3_, f32[5,8,16,256]{3,2,1,0:T(8,128)S(1)} %get-tuple-element.66.refs_5_.refs_1_.refs_3_.refs_4_, ...), custom_call_target="tpu_custom_call" | custom-call | flops 2000000000 | tf_op jit(solution)/shard_map/stage_inner/pallas_call | solution.py:116
  41.4 0.9 %collective-permute-start.17 = (f32[18,8,256]{2,1,0:T(8,128)S(1)}, f32[18,8,256]{2,1,0:T(8,128)S(1)}, u32[]{:S(2)}, u32[]{:S(2)}) collective-permute-start(f32[18,8,256]{2,1,0:T(8,128)S(1)} %get-tuple-element.81), channel_id=1, source_target_pairs={{0,31},{1,2},{2,1},{3,4},{4,3},{5,6},{6,5},{7,8},{8,7},{9,10},{10,... | collective-permute-start | bytes 442376 | tf_op jit(solution)/shard_map/ppermute | solution.py:101
  42.3 0.0 collective-permute-done.15.refs_10_
  42.3 0.0 collective-permute-done.13.refs_8_
  42.3 0.8 %collective-permute-done.14.refs_9_ = f32[15,16,256]{2,1,0:T(8,128)S(1)} collective-permute-done((f32[15,16,256]{2,1,0:T(8,128)S(1)}, f32[15,16,256]{2,1,0:T(8,128)S(1)}, u32[]{:S(2)}, u32[]{:S(2)}) %collective-permute-start.14) | collective-permute-done | bytes 245792 | tf_op jit(solution)/shard_map/ppermute | solution.py:101
  43.1 0.6 stage_rim.2
  43.7 0.2 collective-permute-start.19
  43.8 1.7 %collective-permute-start.20 = (f32[15,16,256]{2,1,0:T(8,128)S(1)}, f32[15,16,256]{2,1,0:T(8,128)S(1)}, u32[]{:S(2)}, u32[]{:S(2)}) collective-permute-start(f32[15,16,256]{2,1,0:T(8,128)S(1)} %get-tuple-element.85), channel_id=1, source_target_pairs={{0,96},{32,64},{64,32},{96,0},{1,97},{33,65},{65,33},{97,1},{2,98}... | collective-permute-start | bytes 737288 | tf_op jit(solution)/shard_map/ppermute | solution.py:101
  45.6 3.0 %collective-permute-start.21 = (f32[6,8,256]{2,1,0:T(8,128)S(1)}, f32[6,8,256]{2,1,0:T(8,128)S(1)}, u32[]{:S(2)}, u32[]{:S(2)}) collective-permute-start(f32[6,8,256]{2,1,0:T(8,128)S(1)} %get-tuple-element.86), channel_id=1, source_target_pairs={{0,31},{1,2},{2,1},{3,4},{4,3},{5,6},{6,5},{7,8},{8,7},{9,10},{10,... | collective-permute-start | bytes 147464 | tf_op jit(solution)/shard_map/ppermute | solution.py:101
  48.5 0.9 %collective-permute-done.17.refs_6_ = f32[18,8,256]{2,1,0:T(8,128)S(1)} collective-permute-done((f32[18,8,256]{2,1,0:T(8,128)S(1)}, f32[18,8,256]{2,1,0:T(8,128)S(1)}, u32[]{:S(2)}, u32[]{:S(2)}) %collective-permute-start.17) | collective-permute-done | bytes 147488 | tf_op jit(solution)/shard_map/ppermute | solution.py:101
  49.4 1.4 %stage_inner.3 = (f32[5,24,16,256]{3,2,1,0:T(8,128)S(1)}, f32[18,8,256]{2,1,0:T(8,128)S(1)}, f32[18,8,256]{2,1,0:T(8,128)S(1)}) custom-call(f32[5,24,16,256]{3,2,1,0:T(8,128)S(1)} %get-tuple-element.75.refs_14_.refs_0_, f32[5,8,16,256]{3,2,1,0:T(8,128)S(1)} %get-tuple-element.80.refs_1_, ...), custom_call_target="tpu_custom_call" | custom-call | flops 2000000000 | tf_op jit(solution)/shard_map/stage_inner/pallas_call | solution.py:116
  50.8 1.3 %collective-permute-start.23 = (f32[18,8,256]{2,1,0:T(8,128)S(1)}, f32[18,8,256]{2,1,0:T(8,128)S(1)}, u32[]{:S(2)}, u32[]{:S(2)}) collective-permute-start(f32[18,8,256]{2,1,0:T(8,128)S(1)} %get-tuple-element.89), channel_id=1, source_target_pairs={{0,31},{1,2},{2,1},{3,4},{4,3},{5,6},{6,5},{7,8},{8,7},{9,10},{10,... | collective-permute-start | bytes 442376 | tf_op jit(solution)/shard_map/ppermute | solution.py:101
  52.1 0.3 collective-permute-done.21.refs_8_
  52.4 0.0 collective-permute-start.24
  52.4 0.7 %collective-permute-done.20.refs_7_ = f32[15,16,256]{2,1,0:T(8,128)S(1)} collective-permute-done((f32[15,16,256]{2,1,0:T(8,128)S(1)}, f32[15,16,256]{2,1,0:T(8,128)S(1)}, u32[]{:S(2)}, u32[]{:S(2)}) %collective-permute-start.20) | collective-permute-done | bytes 245792 | tf_op jit(solution)/shard_map/ppermute | solution.py:101
  53.1 0.6 stage_rim.3
  53.7 0.4 collective-permute-start.25
  54.2 1.8 %collective-permute-start.26 = (f32[15,16,256]{2,1,0:T(8,128)S(1)}, f32[15,16,256]{2,1,0:T(8,128)S(1)}, u32[]{:S(2)}, u32[]{:S(2)}) collective-permute-start(f32[15,16,256]{2,1,0:T(8,128)S(1)} %get-tuple-element.92), channel_id=1, source_target_pairs={{0,96},{32,64},{64,32},{96,0},{1,97},{33,65},{65,33},{97,1},{2,98}... | collective-permute-start | bytes 737288 | tf_op jit(solution)/shard_map/ppermute | solution.py:101
  56.0 2.4 %collective-permute-start.27 = (f32[6,8,256]{2,1,0:T(8,128)S(1)}, f32[6,8,256]{2,1,0:T(8,128)S(1)}, u32[]{:S(2)}, u32[]{:S(2)}) collective-permute-start(f32[6,8,256]{2,1,0:T(8,128)S(1)} %get-tuple-element.93), channel_id=1, source_target_pairs={{0,31},{1,2},{2,1},{3,4},{4,3},{5,6},{6,5},{7,8},{8,7},{9,10},{10,... | collective-permute-start | bytes 147464 | tf_op jit(solution)/shard_map/ppermute | solution.py:101
  58.4 0.4 collective-permute-done.23.refs_7_
  58.8 2.3 %final_inner.1.refs_0_ = f32[5,32,16,256]{3,2,1,0:T(8,128)} custom-call(f32[5,24,16,256]{3,2,1,0:T(8,128)S(1)} %get-tuple-element.83.refs_12_.refs_0_.refs_1_, f32[5,8,16,256]{3,2,1,0:T(8,128)S(1)} %get-tuple-element.88.refs_1_.refs_2_, f32[5,24,16,256]{3,2,1,0:T(8,128)S(1)} %get-tuple-element.65.refs_4_.refs_0_.refs_2_.refs_3_, ...), custom_call_target="tpu_custom_call" | custom-call | flops 2000000000 | tf_op jit(solution)/shard_map/final_inner/pallas_call | solution.py:116
  61.1 1.7 %collective-permute-done.27.refs_10_ = f32[6,8,256]{2,1,0:T(8,128)S(1)} collective-permute-done((f32[6,8,256]{2,1,0:T(8,128)S(1)}, f32[6,8,256]{2,1,0:T(8,128)S(1)}, u32[]{:S(2)}, u32[]{:S(2)}) %collective-permute-start.27) | collective-permute-done | bytes 49184 | tf_op jit(solution)/shard_map/ppermute | solution.py:101
  62.8 0.6 collective-permute-done.26.refs_9_
  63.4 1.4 %final_rim.1 = f32[5,32,16,256]{3,2,1,0:T(8,128)} custom-call(f32[5,32,16,256]{3,2,1,0:T(8,128)} %final_inner.1.refs_0_, f32[5,24,16,256]{3,2,1,0:T(8,128)S(1)} %get-tuple-element.83.refs_12_.refs_0_.refs_1_, f32[5,8,16,256]{3,2,1,0:T(8,128)S(1)} %get-tuple-element.88.refs_1_.refs_2_, ...), custom_call_target="tpu_custom_call", output_to_operand_aliasing={{}: (0, {})} | custom-call | tf_op jit(solution)/shard_map/final_rim/pallas_call | solution.py:116
  (28 shorter events, 0.1 us)
Async XLA Ops:
  0.0 6.2 %copy-start.5 = (f32[16,16,512]{2,1,0:T(8,128)S(1)}, f32[16,16,512]{2,1,0:T(8,128)}, u32[]{:S(2)}) copy-start(f32[16,16,512]{2,1,0:T(8,128)} %refs_0_.4) | copy-start | bytes 1572868
  1.1 6.7 %collective-permute-start.1 = (f32[4,16,512]{2,1,0:T(8,128)S(1)}, f32[4,16,512]{2,1,0:T(8,128)S(1)}, u32[]{:S(2)}, u32[]{:S(2)}) collective-permute-start(f32[4,16,512]{2,1,0:T(8,128)S(1)} %get-tuple-element.95), channel_id=1, source_target_pairs={{0,96},{32,64},{64,32},{96,0},{1,97},{33,65},{65,33},{97,1},{2,98}... | collective-permute-start | bytes 393224 | tf_op jit(solution)/shard_map/ppermute | solution.py:101
  4.2 5.0 %collective-permute-start = (f32[4,16,512]{2,1,0:T(8,128)S(1)}, f32[4,16,512]{2,1,0:T(8,128)S(1)}, u32[]{:S(2)}, u32[]{:S(2)}) collective-permute-start(f32[4,16,512]{2,1,0:T(8,128)S(1)} %get-tuple-element.96.refs_1_), channel_id=1, source_target_pairs={{0,32},{32,0},{64,96},{96,64},{1,33},{33,1},{65,97},{97,65},{2,34}... | collective-permute-start | bytes 393224 | tf_op jit(solution)/shard_map/ppermute | solution.py:101
  4.4 1.7 %copy-start = (f32[5,32,16,256]{3,2,1,0:T(8,128)S(1)}, f32[5,32,16,256]{3,2,1,0:T(8,128)}, u32[]{:S(2)}) copy-start(f32[5,32,16,256]{3,2,1,0:T(8,128)} %refs_7_.1) | copy-start | bytes 7864324
  6.1 1.0 %copy-start.6 = (s32[16,16,512]{2,1,0:T(8,128)S(1)}, s32[16,16,512]{2,1,0:T(8,128)}, u32[]{:S(2)}) copy-start(s32[16,16,512]{2,1,0:T(8,128)} %refs_1_.1) | copy-start | bytes 1572868
  6.1 11.3 %copy-start.7 = (s32[256]{0:T(256)S(1)}, s32[256]{0:T(256)}, u32[]{:S(2)}) copy-start(s32[256]{0:T(256)} %param.9) | copy-start | bytes 3076
  6.1 11.3 %copy-start.8 = (s32[256]{0:T(256)S(1)}, s32[256]{0:T(256)}, u32[]{:S(2)}) copy-start(s32[256]{0:T(256)} %param.10) | copy-start | bytes 3076
  9.4 9.5 %collective-permute-start.6 = (f32[16,8,256]{2,1,0:T(8,128)S(1)}, f32[16,8,256]{2,1,0:T(8,128)S(1)}, u32[]{:S(2)}, u32[]{:S(2)}) collective-permute-start(f32[16,8,256]{2,1,0:T(8,128)S(1)} %get-tuple-element.61), channel_id=1, source_target_pairs={{0,31},{1,2},{2,1},{3,4},{4,3},{5,6},{6,5},{7,8},{8,7},{9,10},{10,... | collective-permute-start | bytes 393224 | tf_op jit(solution)/shard_map/ppermute | solution.py:101
  14.0 4.9 %collective-permute-start.2 = (f32[40,8,256]{2,1,0:T(8,128)S(1)}, f32[40,8,256]{2,1,0:T(8,128)S(1)}, u32[]{:S(2)}, u32[]{:S(2)}) collective-permute-start(f32[40,8,256]{2,1,0:T(8,128)S(1)} %get-tuple-element.53), channel_id=1, source_target_pairs={{0,1},{1,0},{2,3},{3,2},{4,5},{5,4},{6,7},{7,6},{8,9},{9,8},{10,11... | collective-permute-start | bytes 983048 | tf_op jit(solution)/shard_map/ppermute | solution.py:101
  14.0 11.3 %collective-permute-start.3 = (f32[24,8,256]{2,1,0:T(8,128)S(1)}, f32[24,8,256]{2,1,0:T(8,128)S(1)}, u32[]{:S(2)}, u32[]{:S(2)}) collective-permute-start(f32[24,8,256]{2,1,0:T(8,128)S(1)} %get-tuple-element.54), channel_id=1, source_target_pairs={{0,31},{1,2},{2,1},{3,4},{4,3},{5,6},{6,5},{7,8},{8,7},{9,10},{10,... | collective-permute-start | bytes 589832 | tf_op jit(solution)/shard_map/ppermute | solution.py:107
  15.9 10.8 %collective-permute-start.4 = (f32[15,16,256]{2,1,0:T(8,128)S(1)}, f32[15,16,256]{2,1,0:T(8,128)S(1)}, u32[]{:S(2)}, u32[]{:S(2)}) collective-permute-start(f32[15,16,256]{2,1,0:T(8,128)S(1)} %get-tuple-element.55), channel_id=1, source_target_pairs={{0,32},{32,0},{64,96},{96,64},{1,33},{33,1},{65,97},{97,65},{2,34}... | collective-permute-start | bytes 737288 | tf_op jit(solution)/shard_map/ppermute | solution.py:101
  16.3 10.4 %collective-permute-start.5 = (f32[15,16,256]{2,1,0:T(8,128)S(1)}, f32[15,16,256]{2,1,0:T(8,128)S(1)}, u32[]{:S(2)}, u32[]{:S(2)}) collective-permute-start(f32[15,16,256]{2,1,0:T(8,128)S(1)} %get-tuple-element.56), channel_id=1, source_target_pairs={{0,96},{32,64},{64,32},{96,0},{1,97},{33,65},{65,33},{97,1},{2,98}... | collective-permute-start | bytes 737288 | tf_op jit(solution)/shard_map/ppermute | solution.py:101
  18.9 7.8 %copy-start.1 = (f32[5,32,16,256]{3,2,1,0:T(8,128)S(1)}, f32[5,32,16,256]{3,2,1,0:T(8,128)}, u32[]{:S(2)}) copy-start(f32[5,32,16,256]{3,2,1,0:T(8,128)} %refs_7_.1) | copy-start | bytes 7864324
  18.9 7.8 %copy-start.3 = (bf16[2,2,256,256]{3,2,1,0:T(8,128)(2,1)S(1)}, bf16[2,2,256,256]{3,2,1,0:T(8,128)(2,1)}, u32[]{:S(2)}) copy-start(bf16[2,2,256,256]{3,2,1,0:T(8,128)(2,1)} %constant.17.clone.refs_6_.refs_11_.refs_13_.refs_9_.refs_10_) | copy-start | bytes 1572868
  18.9 7.8 %copy-start.4 = (bf16[2,2,128,224]{3,2,1,0:T(8,128)(2,1)S(1)}, bf16[2,2,128,224]{3,2,1,0:T(8,128)(2,1)}, u32[]{:S(2)}) copy-start(bf16[2,2,128,224]{3,2,1,0:T(8,128)(2,1)} %constant.16.clone.refs_5_.refs_10_.refs_12_.refs_8_.refs_9_) | copy-start | bytes 688132
  20.9 10.7 %collective-permute-start.9 = (f32[19,8,256]{2,1,0:T(8,128)S(1)}, f32[19,8,256]{2,1,0:T(8,128)S(1)}, u32[]{:S(2)}, u32[]{:S(2)}) collective-permute-start(f32[19,8,256]{2,1,0:T(8,128)S(1)} %get-tuple-element.69), channel_id=1, source_target_pairs={{0,31},{1,2},{2,1},{3,4},{4,3},{5,6},{6,5},{7,8},{8,7},{9,10},{10,... | collective-permute-start | bytes 466952 | tf_op jit(solution)/shard_map/ppermute | solution.py:101
  24.1 5.1 %collective-permute-start.7 = (f32[18,8,256]{2,1,0:T(8,128)S(1)}, f32[18,8,256]{2,1,0:T(8,128)S(1)}, u32[]{:S(2)}, u32[]{:S(2)}) collective-permute-start(f32[18,8,256]{2,1,0:T(8,128)S(1)} %get-tuple-element.67), channel_id=1, source_target_pairs={{0,32},{32,0},{64,96},{96,64},{1,33},{33,1},{65,97},{97,65},{2,34}... | collective-permute-start | bytes 442376 | tf_op jit(solution)/shard_map/ppermute | solution.py:101
  25.3 6.4 %collective-permute-start.8 = (f32[18,8,256]{2,1,0:T(8,128)S(1)}, f32[18,8,256]{2,1,0:T(8,128)S(1)}, u32[]{:S(2)}, u32[]{:S(2)}) collective-permute-start(f32[18,8,256]{2,1,0:T(8,128)S(1)} %get-tuple-element.68), channel_id=1, source_target_pairs={{0,96},{32,64},{64,32},{96,0},{1,97},{33,65},{65,33},{97,1},{2,98}... | collective-permute-start | bytes 442376 | tf_op jit(solution)/shard_map/ppermute | solution.py:101
  26.7 2.1 %collective-permute-start.10 = (f32[17,8,256]{2,1,0:T(8,128)S(1)}, f32[17,8,256]{2,1,0:T(8,128)S(1)}, u32[]{:S(2)}, u32[]{:S(2)}) collective-permute-start(f32[17,8,256]{2,1,0:T(8,128)S(1)} %get-tuple-element.70), channel_id=1, source_target_pairs={{0,1},{1,0},{2,3},{3,2},{4,5},{5,4},{6,7},{7,6},{8,9},{9,8},{10,11... | collective-permute-start | bytes 417800 | tf_op jit(solution)/shard_map/ppermute | solution.py:101
  32.1 8.0 %collective-permute-start.11 = (f32[18,8,256]{2,1,0:T(8,128)S(1)}, f32[18,8,256]{2,1,0:T(8,128)S(1)}, u32[]{:S(2)}, u32[]{:S(2)}) collective-permute-start(f32[18,8,256]{2,1,0:T(8,128)S(1)} %get-tuple-element.73), channel_id=1, source_target_pairs={{0,31},{1,2},{2,1},{3,4},{4,3},{5,6},{6,5},{7,8},{8,7},{9,10},{10,... | collective-permute-start | bytes 442376 | tf_op jit(solution)/shard_map/ppermute | solution.py:101
  32.9 7.1 %collective-permute-start.12 = (f32[18,8,256]{2,1,0:T(8,128)S(1)}, f32[18,8,256]{2,1,0:T(8,128)S(1)}, u32[]{:S(2)}, u32[]{:S(2)}) collective-permute-start(f32[18,8,256]{2,1,0:T(8,128)S(1)} %get-tuple-element.74), channel_id=1, source_target_pairs={{0,1},{1,0},{2,3},{3,2},{4,5},{5,4},{6,7},{7,6},{8,9},{9,8},{10,11... | collective-permute-start | bytes 442376 | tf_op jit(solution)/shard_map/ppermute | solution.py:101
  32.9 9.4 %collective-permute-start.13 = (f32[15,16,256]{2,1,0:T(8,128)S(1)}, f32[15,16,256]{2,1,0:T(8,128)S(1)}, u32[]{:S(2)}, u32[]{:S(2)}) collective-permute-start(f32[15,16,256]{2,1,0:T(8,128)S(1)} %get-tuple-element.76), channel_id=1, source_target_pairs={{0,32},{32,0},{64,96},{96,64},{1,33},{33,1},{65,97},{97,65},{2,34}... | collective-permute-start | bytes 737288 | tf_op jit(solution)/shard_map/ppermute | solution.py:101
  33.8 9.3 %collective-permute-start.14 = (f32[15,16,256]{2,1,0:T(8,128)S(1)}, f32[15,16,256]{2,1,0:T(8,128)S(1)}, u32[]{:S(2)}, u32[]{:S(2)}) collective-permute-start(f32[15,16,256]{2,1,0:T(8,128)S(1)} %get-tuple-element.77), channel_id=1, source_target_pairs={{0,96},{32,64},{64,32},{96,0},{1,97},{33,65},{65,33},{97,1},{2,98}... | collective-permute-start | bytes 737288 | tf_op jit(solution)/shard_map/ppermute | solution.py:101
  35.2 7.1 %collective-permute-start.15 = (f32[6,8,256]{2,1,0:T(8,128)S(1)}, f32[6,8,256]{2,1,0:T(8,128)S(1)}, u32[]{:S(2)}, u32[]{:S(2)}) collective-permute-start(f32[6,8,256]{2,1,0:T(8,128)S(1)} %get-tuple-element.78), channel_id=1, source_target_pairs={{0,31},{1,2},{2,1},{3,4},{4,3},{5,6},{6,5},{7,8},{8,7},{9,10},{10,... | collective-permute-start | bytes 147464 | tf_op jit(solution)/shard_map/ppermute | solution.py:101
  40.1 2.2 %collective-permute-start.16 = (f32[6,8,256]{2,1,0:T(8,128)S(1)}, f32[6,8,256]{2,1,0:T(8,128)S(1)}, u32[]{:S(2)}, u32[]{:S(2)}) collective-permute-start(f32[6,8,256]{2,1,0:T(8,128)S(1)} %get-tuple-element.79), channel_id=1, source_target_pairs={{0,1},{1,0},{2,3},{3,2},{4,5},{5,4},{6,7},{7,6},{8,9},{9,8},{10,11... | collective-permute-start | bytes 147464 | tf_op jit(solution)/shard_map/ppermute | solution.py:101
  41.4 8.0 %collective-permute-start.17 = (f32[18,8,256]{2,1,0:T(8,128)S(1)}, f32[18,8,256]{2,1,0:T(8,128)S(1)}, u32[]{:S(2)}, u32[]{:S(2)}) collective-permute-start(f32[18,8,256]{2,1,0:T(8,128)S(1)} %get-tuple-element.81), channel_id=1, source_target_pairs={{0,31},{1,2},{2,1},{3,4},{4,3},{5,6},{6,5},{7,8},{8,7},{9,10},{10,... | collective-permute-start | bytes 442376 | tf_op jit(solution)/shard_map/ppermute | solution.py:101
  42.3 7.1 %collective-permute-start.18 = (f32[18,8,256]{2,1,0:T(8,128)S(1)}, f32[18,8,256]{2,1,0:T(8,128)S(1)}, u32[]{:S(2)}, u32[]{:S(2)}) collective-permute-start(f32[18,8,256]{2,1,0:T(8,128)S(1)} %get-tuple-element.82), channel_id=1, source_target_pairs={{0,1},{1,0},{2,3},{3,2},{4,5},{5,4},{6,7},{7,6},{8,9},{9,8},{10,11... | collective-permute-start | bytes 442376 | tf_op jit(solution)/shard_map/ppermute | solution.py:101
  43.7 8.7 %collective-permute-start.19 = (f32[15,16,256]{2,1,0:T(8,128)S(1)}, f32[15,16,256]{2,1,0:T(8,128)S(1)}, u32[]{:S(2)}, u32[]{:S(2)}) collective-permute-start(f32[15,16,256]{2,1,0:T(8,128)S(1)} %get-tuple-element.84), channel_id=1, source_target_pairs={{0,32},{32,0},{64,96},{96,64},{1,33},{33,1},{65,97},{97,65},{2,34}... | collective-permute-start | bytes 737288 | tf_op jit(solution)/shard_map/ppermute | solution.py:101
  43.8 9.3 %collective-permute-start.20 = (f32[15,16,256]{2,1,0:T(8,128)S(1)}, f32[15,16,256]{2,1,0:T(8,128)S(1)}, u32[]{:S(2)}, u32[]{:S(2)}) collective-permute-start(f32[15,16,256]{2,1,0:T(8,128)S(1)} %get-tuple-element.85), channel_id=1, source_target_pairs={{0,96},{32,64},{64,32},{96,0},{1,97},{33,65},{65,33},{97,1},{2,98}... | collective-permute-start | bytes 737288 | tf_op jit(solution)/shard_map/ppermute | solution.py:101
  45.6 6.8 %collective-permute-start.21 = (f32[6,8,256]{2,1,0:T(8,128)S(1)}, f32[6,8,256]{2,1,0:T(8,128)S(1)}, u32[]{:S(2)}, u32[]{:S(2)}) collective-permute-start(f32[6,8,256]{2,1,0:T(8,128)S(1)} %get-tuple-element.86), channel_id=1, source_target_pairs={{0,31},{1,2},{2,1},{3,4},{4,3},{5,6},{6,5},{7,8},{8,7},{9,10},{10,... | collective-permute-start | bytes 147464 | tf_op jit(solution)/shard_map/ppermute | solution.py:101
  49.4 3.0 %collective-permute-start.22 = (f32[6,8,256]{2,1,0:T(8,128)S(1)}, f32[6,8,256]{2,1,0:T(8,128)S(1)}, u32[]{:S(2)}, u32[]{:S(2)}) collective-permute-start(f32[6,8,256]{2,1,0:T(8,128)S(1)} %get-tuple-element.87), channel_id=1, source_target_pairs={{0,1},{1,0},{2,3},{3,2},{4,5},{5,4},{6,7},{7,6},{8,9},{9,8},{10,11... | collective-permute-start | bytes 147464 | tf_op jit(solution)/shard_map/ppermute | solution.py:101
  50.8 8.0 %collective-permute-start.23 = (f32[18,8,256]{2,1,0:T(8,128)S(1)}, f32[18,8,256]{2,1,0:T(8,128)S(1)}, u32[]{:S(2)}, u32[]{:S(2)}) collective-permute-start(f32[18,8,256]{2,1,0:T(8,128)S(1)} %get-tuple-element.89), channel_id=1, source_target_pairs={{0,31},{1,2},{2,1},{3,4},{4,3},{5,6},{6,5},{7,8},{8,7},{9,10},{10,... | collective-permute-start | bytes 442376 | tf_op jit(solution)/shard_map/ppermute | solution.py:101
  52.4 6.4 %collective-permute-start.24 = (f32[18,8,256]{2,1,0:T(8,128)S(1)}, f32[18,8,256]{2,1,0:T(8,128)S(1)}, u32[]{:S(2)}, u32[]{:S(2)}) collective-permute-start(f32[18,8,256]{2,1,0:T(8,128)S(1)} %get-tuple-element.90), channel_id=1, source_target_pairs={{0,1},{1,0},{2,3},{3,2},{4,5},{5,4},{6,7},{7,6},{8,9},{9,8},{10,11... | collective-permute-start | bytes 442376 | tf_op jit(solution)/shard_map/ppermute | solution.py:101
  53.1 5.6 %copy-start.2 = (f32[5,32,16,256]{3,2,1,0:T(8,128)S(1)}, f32[5,32,16,256]{3,2,1,0:T(8,128)}, u32[]{:S(2)}) copy-start(f32[5,32,16,256]{3,2,1,0:T(8,128)} %refs_7_.1) | copy-start | bytes 7864324
  53.7 9.1 %collective-permute-start.25 = (f32[15,16,256]{2,1,0:T(8,128)S(1)}, f32[15,16,256]{2,1,0:T(8,128)S(1)}, u32[]{:S(2)}, u32[]{:S(2)}) collective-permute-start(f32[15,16,256]{2,1,0:T(8,128)S(1)} %get-tuple-element.91), channel_id=1, source_target_pairs={{0,32},{32,0},{64,96},{96,64},{1,33},{33,1},{65,97},{97,65},{2,34}... | collective-permute-start | bytes 737288 | tf_op jit(solution)/shard_map/ppermute | solution.py:101
  54.2 9.3 %collective-permute-start.26 = (f32[15,16,256]{2,1,0:T(8,128)S(1)}, f32[15,16,256]{2,1,0:T(8,128)S(1)}, u32[]{:S(2)}, u32[]{:S(2)}) collective-permute-start(f32[15,16,256]{2,1,0:T(8,128)S(1)} %get-tuple-element.92), channel_id=1, source_target_pairs={{0,96},{32,64},{64,32},{96,0},{1,97},{33,65},{65,33},{97,1},{2,98}... | collective-permute-start | bytes 737288 | tf_op jit(solution)/shard_map/ppermute | solution.py:101
  56.0 6.8 %collective-permute-start.27 = (f32[6,8,256]{2,1,0:T(8,128)S(1)}, f32[6,8,256]{2,1,0:T(8,128)S(1)}, u32[]{:S(2)}, u32[]{:S(2)}) collective-permute-start(f32[6,8,256]{2,1,0:T(8,128)S(1)} %get-tuple-element.93), channel_id=1, source_target_pairs={{0,31},{1,2},{2,1},{3,4},{4,3},{5,6},{6,5},{7,8},{8,7},{9,10},{10,... | collective-permute-start | bytes 147464 | tf_op jit(solution)/shard_map/ppermute | solution.py:101
  58.7 4.0 %collective-permute-start.28 = (f32[6,8,256]{2,1,0:T(8,128)S(1)}, f32[6,8,256]{2,1,0:T(8,128)S(1)}, u32[]{:S(2)}, u32[]{:S(2)}) collective-permute-start(f32[6,8,256]{2,1,0:T(8,128)S(1)} %get-tuple-element.94), channel_id=1, source_target_pairs={{0,1},{1,0},{2,3},{3,2},{4,5},{5,4},{6,7},{7,6},{8,9},{9,8},{10,11... | collective-permute-start | bytes 147464 | tf_op jit(solution)/shard_map/ppermute | solution.py:101

commit v14 on v13

--- a/solution.py
+++ b/solution.py
@@ -604,6 +604,13 @@
     partial, half_width = full_specs(
         inner_body, [block, ((px, pa, fine), jnp.int32)], [noise, half_width], name="filter_inner", after=[za]
     )
+    pick, cells, own = full_specs(
+        route_body,
+        [((4 * most, ncols), BF16), ((4, 8, radial), F32), ((1, ncols), jnp.int32)],
+        [owner.reshape(1, ncols), target_cell.reshape(1, ncols)],
+        name="route",
+        after=[partial],
+    )
     long_z = ((px + send_z[0][0], 8, fine // 2), F32)
     filtered, to_a, to_b = full_specs(
         first_body,
@@ -611,16 +618,10 @@
         [partial, half_width, noise_a, noise_b, za],
         [((2, HMAX, pa, fine), F32)],
         name="filter_axial",
+        after=[pick],
     )
     got_a, got_b = swap(to_a, to_b, "az")
     (uzb,) = swap_b(zb, "az")
-    pick, cells, own = full_specs(
-        route_body,
-        [((4 * most, ncols), BF16), ((4, 8, radial), F32), ((1, ncols), jnp.int32)],
-        [owner.reshape(1, ncols), target_cell.reshape(1, ncols)],
-        name="route",
-        after=[filtered],
-    )
     partial, weights = full_specs(
         middle_body,
         [block, ((HMAX + 1, px, pa, fine), F32)],

time: 65.5 us -> 65.4 us (level)
    ppermute x14, starting transfers between devices: 3.1 us -> 3.87 us  [swap(): lax.ppermute(to_a, axis, pairs_a)]
  transfers between devices with their start and end apart: 29 -> 29, of which waited for: 12 -> 11; matrix products, arithmetic and copies ran while one was open for 0% -> 0% of each run, Pallas kernels for 19% -> 19%
where the time goes in v14:
time: 65.4 us; the launch traced here: 64.9 us
  starting transfers between devices  35.5 us (54%)
  Pallas kernels  14.3 us (22%)
  waiting for transfers between devices  11 us (17%)
  local copies, waits for them, and re-layouts  2.68 us (4%)
  other arithmetic  1.04 us (2%)
    ppermute x14, starting transfers between devices, swap(): lax.ppermute(to_b, axis, pairs_b)  29.7 us
    pallas_call x15, Pallas kernels, full_specs(): pl.pallas_call(run, out_shape=[jax.ShapeDtypeStruct(s, d) for s, d in out...  14.3 us
    ppermute x14, waiting for transfers between devices, swap(): lax.ppermute(to_b, axis, pairs_b)  9.28 us
    ppermute x14, starting transfers between devices, swap(): lax.ppermute(to_a, axis, pairs_a)  3.87 us
    unnamed x18, local copies, waits for them, and re-layouts  2.68 us
    ppermute x1, starting transfers between devices, swap_b(): return (lax.ppermute(value, axis, pairs),)  1.96 us
    ppermute x14, waiting for transfers between devices, swap(): lax.ppermute(to_a, axis, pairs_a)  1.71 us
  transfers between devices with their start and end apart: 29, of which 11 were waited for; matrix products, arithmetic and copies ran while one was open for 0% of the time, Pallas kernels for 19%

profile of v14, /device:TPU:0, one launch (start us, length us, event | category | flops | bytes accessed | tf_op | source)
XLA Modules:
  0.0 64.9 jit_solution(15772578854115133105)
XLA Ops:
  0.0 1.0 %slice_select_fusion = (f32[4,16,512]{2,1,0:T(8,128)S(1)}, f32[4,16,512]{2,1,0:T(8,128)S(1)}) fusion(f32[16,16,512]{2,1,0:T(8,128)} %refs_0_.4, pred[]{:T(512)S(6)} %eq.3), kind=kLoop, calls=%fused_computation | loop fusion | flops 65536 | bytes 524289 | tf_op jit(solution)/shard_map/jit(_where)/select_n | solution.py:598
  1.1 3.2 %collective-permute-start.1 = (f32[4,16,512]{2,1,0:T(8,128)S(1)}, f32[4,16,512]{2,1,0:T(8,128)S(1)}, u32[]{:S(2)}, u32[]{:S(2)}) collective-permute-start(f32[4,16,512]{2,1,0:T(8,128)S(1)} %get-tuple-element.95), channel_id=1, source_target_pairs={{0,96},{32,64},{64,32},{96,0},{1,97},{33,65},{65,33},{97,1},{2,98}... | collective-permute-start | bytes 393224 | tf_op jit(solution)/shard_map/ppermute | solution.py:101
  4.2 0.1 collective-permute-start
  4.4 1.7 %copy-done = f32[5,32,16,256]{3,2,1,0:T(8,128)S(1)} copy-done((f32[5,32,16,256]{3,2,1,0:T(8,128)S(1)}, f32[5,32,16,256]{3,2,1,0:T(8,128)}, u32[]{:S(2)}) %copy-start) | copy-done | bytes 2621464
  6.1 0.1 edges.1
  6.3 0.9 %copy-done.6 = s32[16,16,512]{2,1,0:T(8,128)S(1)} copy-done((s32[16,16,512]{2,1,0:T(8,128)S(1)}, s32[16,16,512]{2,1,0:T(8,128)}, u32[]{:S(2)}) %copy-start.6) | copy-done | bytes 524312
  7.2 0.5 filter_inner.1
  7.7 0.3 route.1
  8.0 1.2 %collective-permute-done.refs_2_ = f32[4,16,512]{2,1,0:T(8,128)S(1)} collective-permute-done((f32[4,16,512]{2,1,0:T(8,128)S(1)}, f32[4,16,512]{2,1,0:T(8,128)S(1)}, u32[]{:S(2)}, u32[]{:S(2)}) %collective-permute-start) | collective-permute-done | bytes 131104 | tf_op jit(solution)/shard_map/ppermute | solution.py:101
  9.2 0.2 filter_axial.1
  9.4 4.6 %collective-permute-start.6 = (f32[16,8,256]{2,1,0:T(8,128)S(1)}, f32[16,8,256]{2,1,0:T(8,128)S(1)}, u32[]{:S(2)}, u32[]{:S(2)}) collective-permute-start(f32[16,8,256]{2,1,0:T(8,128)S(1)} %get-tuple-element.61), channel_id=1, source_target_pairs={{0,31},{1,2},{2,1},{3,4},{4,3},{5,6},{6,5},{7,8},{8,7},{9,10},{10,... | collective-permute-start | bytes 393224 | tf_op jit(solution)/shard_map/ppermute | solution.py:101
  14.0 0.0 collective-permute-start.2
  14.0 2.0 %collective-permute-start.3 = (f32[24,8,256]{2,1,0:T(8,128)S(1)}, f32[24,8,256]{2,1,0:T(8,128)S(1)}, u32[]{:S(2)}, u32[]{:S(2)}) collective-permute-start(f32[24,8,256]{2,1,0:T(8,128)S(1)} %get-tuple-element.55), channel_id=1, source_target_pairs={{0,31},{1,2},{2,1},{3,4},{4,3},{5,6},{6,5},{7,8},{8,7},{9,10},{10,... | collective-permute-start | bytes 589832 | tf_op jit(solution)/shard_map/ppermute | solution.py:107
  15.9 0.7 %collective-permute-start.4 = (f32[15,16,256]{2,1,0:T(8,128)S(1)}, f32[15,16,256]{2,1,0:T(8,128)S(1)}, u32[]{:S(2)}, u32[]{:S(2)}) collective-permute-start(f32[15,16,256]{2,1,0:T(8,128)S(1)} %get-tuple-element.56), channel_id=1, source_target_pairs={{0,32},{32,0},{64,96},{96,64},{1,33},{33,1},{65,97},{97,65},{2,34}... | collective-permute-start | bytes 737288 | tf_op jit(solution)/shard_map/ppermute | solution.py:101
  16.6 0.8 %collective-permute-start.5 = (f32[15,16,256]{2,1,0:T(8,128)S(1)}, f32[15,16,256]{2,1,0:T(8,128)S(1)}, u32[]{:S(2)}, u32[]{:S(2)}) collective-permute-start(f32[15,16,256]{2,1,0:T(8,128)S(1)} %get-tuple-element.57), channel_id=1, source_target_pairs={{0,96},{32,64},{64,32},{96,0},{1,97},{33,65},{65,33},{97,1},{2,98}... | collective-permute-start | bytes 737288 | tf_op jit(solution)/shard_map/ppermute | solution.py:101
  17.4 1.1 %filter_middle.1 = (f32[16,16,512]{2,1,0:T(8,128)S(1)}, f32[5,16,16,512]{3,2,1,0:T(8,128)S(1)}) custom-call(f32[16,16,512]{2,1,0:T(8,128)S(1)} %get-tuple-element.58.refs_0_, s32[16,16,512]{2,1,0:T(8,128)S(1)} %get-tuple-element.52.refs_1_, bf16[512,256]{1,0:T(8,128)(2,1)S(1)} %get-tuple-element.53.refs_5_.refs_2_.refs_4_), custom_call_target="tpu_custom_call" | custom-call | tf_op jit(solution)/shard_map/filter_middle/pallas_call | solution.py:116
  18.5 0.0 collective-permute-done.6.refs_0_
  18.6 0.0 collective-permute-done.2.refs_2_.refs_1_
  18.6 0.0 copy-start.1
  18.6 0.0 copy-start.3
  18.6 0.0 copy-start.4
  18.6 2.0 %filter_rest.1 = (f32[256,256]{1,0:T(8,128)S(1)}, f32[18,8,256]{2,1,0:T(8,128)S(1)}, f32[18,8,256]{2,1,0:T(8,128)S(1)}, f32[17,8,256]{2,1,0:T(8,128)S(1)}, f32[19,8,256]{2,1,0:T(8,128)S(1)}) custom-call(f32[16,16,512]{2,1,0:T(8,128)S(1)} %get-tuple-element.59.refs_0_, f32[5,16,16,512]{3,2,1,0:T(8,128)S(1)} %get-tuple-element.60.refs_1_, ...), custom_call_target="tpu_custom_call" | custom-call | flops 137438953472 | tf_op jit(solution)/shard_map/filter_rest/pallas_call | solution.py:116
  20.6 3.2 %collective-permute-start.9 = (f32[19,8,256]{2,1,0:T(8,128)S(1)}, f32[19,8,256]{2,1,0:T(8,128)S(1)}, u32[]{:S(2)}, u32[]{:S(2)}) collective-permute-start(f32[19,8,256]{2,1,0:T(8,128)S(1)} %get-tuple-element.69), channel_id=1, source_target_pairs={{0,31},{1,2},{2,1},{3,4},{4,3},{5,6},{6,5},{7,8},{8,7},{9,10},{10,... | collective-permute-start | bytes 466952 | tf_op jit(solution)/shard_map/ppermute | solution.py:101
  23.8 1.3 %collective-permute-start.7 = (f32[18,8,256]{2,1,0:T(8,128)S(1)}, f32[18,8,256]{2,1,0:T(8,128)S(1)}, u32[]{:S(2)}, u32[]{:S(2)}) collective-permute-start(f32[18,8,256]{2,1,0:T(8,128)S(1)} %get-tuple-element.67), channel_id=1, source_target_pairs={{0,32},{32,0},{64,96},{96,64},{1,33},{33,1},{65,97},{97,65},{2,34}... | collective-permute-start | bytes 442376 | tf_op jit(solution)/shard_map/ppermute | solution.py:101
  25.1 0.0 collective-permute-done.3.refs_2_
  25.1 1.2 %collective-permute-start.8 = (f32[18,8,256]{2,1,0:T(8,128)S(1)}, f32[18,8,256]{2,1,0:T(8,128)S(1)}, u32[]{:S(2)}, u32[]{:S(2)}) collective-permute-start(f32[18,8,256]{2,1,0:T(8,128)S(1)} %get-tuple-element.68), channel_id=1, source_target_pairs={{0,96},{32,64},{64,32},{96,0},{1,97},{33,65},{65,33},{97,1},{2,98}... | collective-permute-start | bytes 442376 | tf_op jit(solution)/shard_map/ppermute | solution.py:101
  26.4 0.0 collective-permute-done.4.refs_3_
  26.4 0.0 collective-permute-start.10
  26.4 0.0 collective-permute-done.5.refs_4_
  26.4 2.0 %operator.1 = (f32[5,24,16,256]{3,2,1,0:T(8,128)S(1)}, f32[5,8,16,256]{3,2,1,0:T(8,128)S(1)}) custom-call(f32[5,32,16,256]{3,2,1,0:T(8,128)S(1)} %copy-done.1, f32[40,8,256]{2,1,0:T(8,128)S(1)} %collective-permute-done.2.refs_2_.refs_1_, f32[24,8,256]{2,1,0:T(8,128)S(1)} %collective-permute-done.3.refs_2_, ...), custom_call_target="tpu_custom_call" | custom-call | tf_op jit(solution)/shard_map/operator/pallas_call | solution.py:116
  28.5 0.0 collective-permute-done.10.refs_3_
  28.5 0.5 collective-permute-done.7.refs_0_
  28.9 2.5 %collective-permute-done.8.refs_1_ = f32[18,8,256]{2,1,0:T(8,128)S(1)} collective-permute-done((f32[18,8,256]{2,1,0:T(8,128)S(1)}, f32[18,8,256]{2,1,0:T(8,128)S(1)}, u32[]{:S(2)}, u32[]{:S(2)}) %collective-permute-start.8) | collective-permute-done | bytes 147488 | tf_op jit(solution)/shard_map/ppermute | solution.py:101
  31.5 0.5 gather.1
  32.0 0.7 %collective-permute-start.11 = (f32[18,8,256]{2,1,0:T(8,128)S(1)}, f32[18,8,256]{2,1,0:T(8,128)S(1)}, u32[]{:S(2)}, u32[]{:S(2)}) collective-permute-start(f32[18,8,256]{2,1,0:T(8,128)S(1)} %get-tuple-element.73), channel_id=1, source_target_pairs={{0,31},{1,2},{2,1},{3,4},{4,3},{5,6},{6,5},{7,8},{8,7},{9,10},{10,... | collective-permute-start | bytes 442376 | tf_op jit(solution)/shard_map/ppermute | solution.py:101
  32.6 1.0 %collective-permute-start.13 = (f32[15,16,256]{2,1,0:T(8,128)S(1)}, f32[15,16,256]{2,1,0:T(8,128)S(1)}, u32[]{:S(2)}, u32[]{:S(2)}) collective-permute-start(f32[15,16,256]{2,1,0:T(8,128)S(1)} %get-tuple-element.76), channel_id=1, source_target_pairs={{0,32},{32,0},{64,96},{96,64},{1,33},{33,1},{65,97},{97,65},{2,34}... | collective-permute-start | bytes 737288 | tf_op jit(solution)/shard_map/ppermute | solution.py:101
  33.6 1.3 %collective-permute-start.14 = (f32[15,16,256]{2,1,0:T(8,128)S(1)}, f32[15,16,256]{2,1,0:T(8,128)S(1)}, u32[]{:S(2)}, u32[]{:S(2)}) collective-permute-start(f32[15,16,256]{2,1,0:T(8,128)S(1)} %get-tuple-element.77), channel_id=1, source_target_pairs={{0,96},{32,64},{64,32},{96,0},{1,97},{33,65},{65,33},{97,1},{2,98}... | collective-permute-start | bytes 737288 | tf_op jit(solution)/shard_map/ppermute | solution.py:101
  34.9 3.6 %collective-permute-start.15 = (f32[6,8,256]{2,1,0:T(8,128)S(1)}, f32[6,8,256]{2,1,0:T(8,128)S(1)}, u32[]{:S(2)}, u32[]{:S(2)}) collective-permute-start(f32[6,8,256]{2,1,0:T(8,128)S(1)} %get-tuple-element.78), channel_id=1, source_target_pairs={{0,31},{1,2},{2,1},{3,4},{4,3},{5,6},{6,5},{7,8},{8,7},{9,10},{10,... | collective-permute-start | bytes 147464 | tf_op jit(solution)/shard_map/ppermute | solution.py:101
  38.5 1.4 %collective-permute-done.11.refs_8_ = f32[18,8,256]{2,1,0:T(8,128)S(1)} collective-permute-done((f32[18,8,256]{2,1,0:T(8,128)S(1)}, f32[18,8,256]{2,1,0:T(8,128)S(1)}, u32[]{:S(2)}, u32[]{:S(2)}) %collective-permute-start.11) | collective-permute-done | bytes 147488 | tf_op jit(solution)/shard_map/ppermute | solution.py:101
  39.9 0.0 collective-permute-start.16
  39.9 1.4 %stage_inner.2 = (f32[5,24,16,256]{3,2,1,0:T(8,128)S(1)}, f32[18,8,256]{2,1,0:T(8,128)S(1)}, f32[18,8,256]{2,1,0:T(8,128)S(1)}) custom-call(f32[5,24,16,256]{3,2,1,0:T(8,128)S(1)} %get-tuple-element.65.refs_4_.refs_0_.refs_2_.refs_3_, f32[5,8,16,256]{3,2,1,0:T(8,128)S(1)} %get-tuple-element.66.refs_5_.refs_1_.refs_3_.refs_4_, ...), custom_call_target="tpu_custom_call" | custom-call | flops 2000000000 | tf_op jit(solution)/shard_map/stage_inner/pallas_call | solution.py:116
  41.3 0.7 %collective-permute-start.17 = (f32[18,8,256]{2,1,0:T(8,128)S(1)}, f32[18,8,256]{2,1,0:T(8,128)S(1)}, u32[]{:S(2)}, u32[]{:S(2)}) collective-permute-start(f32[18,8,256]{2,1,0:T(8,128)S(1)} %get-tuple-element.81), channel_id=1, source_target_pairs={{0,31},{1,2},{2,1},{3,4},{4,3},{5,6},{6,5},{7,8},{8,7},{9,10},{10,... | collective-permute-start | bytes 442376 | tf_op jit(solution)/shard_map/ppermute | solution.py:101
  42.0 0.0 collective-permute-done.15.refs_10_
  42.0 0.0 collective-permute-start.18
  42.0 1.0 %collective-permute-done.14.refs_9_ = f32[15,16,256]{2,1,0:T(8,128)S(1)} collective-permute-done((f32[15,16,256]{2,1,0:T(8,128)S(1)}, f32[15,16,256]{2,1,0:T(8,128)S(1)}, u32[]{:S(2)}, u32[]{:S(2)}) %collective-permute-start.14) | collective-permute-done | bytes 245792 | tf_op jit(solution)/shard_map/ppermute | solution.py:101
  42.9 0.6 stage_rim.2
  43.5 0.2 collective-permute-start.19
  43.8 1.8 %collective-permute-start.20 = (f32[15,16,256]{2,1,0:T(8,128)S(1)}, f32[15,16,256]{2,1,0:T(8,128)S(1)}, u32[]{:S(2)}, u32[]{:S(2)}) collective-permute-start(f32[15,16,256]{2,1,0:T(8,128)S(1)} %get-tuple-element.85), channel_id=1, source_target_pairs={{0,96},{32,64},{64,32},{96,0},{1,97},{33,65},{65,33},{97,1},{2,98}... | collective-permute-start | bytes 737288 | tf_op jit(solution)/shard_map/ppermute | solution.py:101
  45.6 3.0 %collective-permute-start.21 = (f32[6,8,256]{2,1,0:T(8,128)S(1)}, f32[6,8,256]{2,1,0:T(8,128)S(1)}, u32[]{:S(2)}, u32[]{:S(2)}) collective-permute-start(f32[6,8,256]{2,1,0:T(8,128)S(1)} %get-tuple-element.86), channel_id=1, source_target_pairs={{0,31},{1,2},{2,1},{3,4},{4,3},{5,6},{6,5},{7,8},{8,7},{9,10},{10,... | collective-permute-start | bytes 147464 | tf_op jit(solution)/shard_map/ppermute | solution.py:101
  48.6 0.7 %collective-permute-done.17.refs_6_ = f32[18,8,256]{2,1,0:T(8,128)S(1)} collective-permute-done((f32[18,8,256]{2,1,0:T(8,128)S(1)}, f32[18,8,256]{2,1,0:T(8,128)S(1)}, u32[]{:S(2)}, u32[]{:S(2)}) %collective-permute-start.17) | collective-permute-done | bytes 147488 | tf_op jit(solution)/shard_map/ppermute | solution.py:101
  49.3 1.4 %stage_inner.3 = (f32[5,24,16,256]{3,2,1,0:T(8,128)S(1)}, f32[18,8,256]{2,1,0:T(8,128)S(1)}, f32[18,8,256]{2,1,0:T(8,128)S(1)}) custom-call(f32[5,24,16,256]{3,2,1,0:T(8,128)S(1)} %get-tuple-element.75.refs_14_.refs_0_, f32[5,8,16,256]{3,2,1,0:T(8,128)S(1)} %get-tuple-element.80.refs_1_, ...), custom_call_target="tpu_custom_call" | custom-call | flops 2000000000 | tf_op jit(solution)/shard_map/stage_inner/pallas_call | solution.py:116
  50.6 1.5 %collective-permute-start.23 = (f32[18,8,256]{2,1,0:T(8,128)S(1)}, f32[18,8,256]{2,1,0:T(8,128)S(1)}, u32[]{:S(2)}, u32[]{:S(2)}) collective-permute-start(f32[18,8,256]{2,1,0:T(8,128)S(1)} %get-tuple-element.89), channel_id=1, source_target_pairs={{0,31},{1,2},{2,1},{3,4},{4,3},{5,6},{6,5},{7,8},{8,7},{9,10},{10,... | collective-permute-start | bytes 442376 | tf_op jit(solution)/shard_map/ppermute | solution.py:101
  52.1 0.3 collective-permute-done.21.refs_8_
  52.4 0.6 collective-permute-done.20.refs_7_
  53.1 0.6 stage_rim.3
  53.6 0.4 collective-permute-start.25
  54.0 1.8 %collective-permute-start.26 = (f32[15,16,256]{2,1,0:T(8,128)S(1)}, f32[15,16,256]{2,1,0:T(8,128)S(1)}, u32[]{:S(2)}, u32[]{:S(2)}) collective-permute-start(f32[15,16,256]{2,1,0:T(8,128)S(1)} %get-tuple-element.92), channel_id=1, source_target_pairs={{0,96},{32,64},{64,32},{96,0},{1,97},{33,65},{65,33},{97,1},{2,98}... | collective-permute-start | bytes 737288 | tf_op jit(solution)/shard_map/ppermute | solution.py:101
  55.8 2.4 %collective-permute-start.27 = (f32[6,8,256]{2,1,0:T(8,128)S(1)}, f32[6,8,256]{2,1,0:T(8,128)S(1)}, u32[]{:S(2)}, u32[]{:S(2)}) collective-permute-start(f32[6,8,256]{2,1,0:T(8,128)S(1)} %get-tuple-element.93), channel_id=1, source_target_pairs={{0,31},{1,2},{2,1},{3,4},{4,3},{5,6},{6,5},{7,8},{8,7},{9,10},{10,... | collective-permute-start | bytes 147464 | tf_op jit(solution)/shard_map/ppermute | solution.py:101
  58.2 0.4 collective-permute-done.23.refs_7_
  58.6 2.3 %final_inner.1.refs_0_ = f32[5,32,16,256]{3,2,1,0:T(8,128)} custom-call(f32[5,24,16,256]{3,2,1,0:T(8,128)S(1)} %get-tuple-element.83.refs_12_.refs_0_.refs_1_, f32[5,8,16,256]{3,2,1,0:T(8,128)S(1)} %get-tuple-element.88.refs_1_.refs_2_, f32[5,24,16,256]{3,2,1,0:T(8,128)S(1)} %get-tuple-element.65.refs_4_.refs_0_.refs_2_.refs_3_, ...), custom_call_target="tpu_custom_call" | custom-call | flops 2000000000 | tf_op jit(solution)/shard_map/final_inner/pallas_call | solution.py:116
  60.9 1.7 %collective-permute-done.27.refs_10_ = f32[6,8,256]{2,1,0:T(8,128)S(1)} collective-permute-done((f32[6,8,256]{2,1,0:T(8,128)S(1)}, f32[6,8,256]{2,1,0:T(8,128)S(1)}, u32[]{:S(2)}, u32[]{:S(2)}) %collective-permute-start.27) | collective-permute-done | bytes 49184 | tf_op jit(solution)/shard_map/ppermute | solution.py:101
  62.6 0.0 collective-permute-done.28.refs_11_
  62.7 0.7 %collective-permute-done.26.refs_9_ = f32[15,16,256]{2,1,0:T(8,128)S(1)} collective-permute-done((f32[15,16,256]{2,1,0:T(8,128)S(1)}, f32[15,16,256]{2,1,0:T(8,128)S(1)}, u32[]{:S(2)}, u32[]{:S(2)}) %collective-permute-start.26) | collective-permute-done | bytes 245792 | tf_op jit(solution)/shard_map/ppermute | solution.py:101
  63.3 1.4 %final_rim.1 = f32[5,32,16,256]{3,2,1,0:T(8,128)} custom-call(f32[5,32,16,256]{3,2,1,0:T(8,128)} %final_inner.1.refs_0_, f32[5,24,16,256]{3,2,1,0:T(8,128)S(1)} %get-tuple-element.83.refs_12_.refs_0_.refs_1_, f32[5,8,16,256]{3,2,1,0:T(8,128)S(1)} %get-tuple-element.88.refs_1_.refs_2_, ...), custom_call_target="tpu_custom_call", output_to_operand_aliasing={{}: (0, {})} | custom-call | tf_op jit(solution)/shard_map/final_rim/pallas_call | solution.py:116
  (28 shorter events, 0.1 us)
Async XLA Ops:
  0.0 6.2 %copy-start.5 = (f32[16,16,512]{2,1,0:T(8,128)S(1)}, f32[16,16,512]{2,1,0:T(8,128)}, u32[]{:S(2)}) copy-start(f32[16,16,512]{2,1,0:T(8,128)} %refs_0_.4) | copy-start | bytes 1572868
  0.0 7.6 %copy-start.8 = (s32[256]{0:T(256)S(1)}, s32[256]{0:T(256)}, u32[]{:S(2)}) copy-start(s32[256]{0:T(256)} %param.10) | copy-start | bytes 3076
  0.0 7.7 %copy-start.7 = (s32[256]{0:T(256)S(1)}, s32[256]{0:T(256)}, u32[]{:S(2)}) copy-start(s32[256]{0:T(256)} %param.9) | copy-start | bytes 3076
  1.1 6.9 %collective-permute-start.1 = (f32[4,16,512]{2,1,0:T(8,128)S(1)}, f32[4,16,512]{2,1,0:T(8,128)S(1)}, u32[]{:S(2)}, u32[]{:S(2)}) collective-permute-start(f32[4,16,512]{2,1,0:T(8,128)S(1)} %get-tuple-element.95), channel_id=1, source_target_pairs={{0,96},{32,64},{64,32},{96,0},{1,97},{33,65},{65,33},{97,1},{2,98}... | collective-permute-start | bytes 393224 | tf_op jit(solution)/shard_map/ppermute | solution.py:101
  4.2 5.0 %collective-permute-start = (f32[4,16,512]{2,1,0:T(8,128)S(1)}, f32[4,16,512]{2,1,0:T(8,128)S(1)}, u32[]{:S(2)}, u32[]{:S(2)}) collective-permute-start(f32[4,16,512]{2,1,0:T(8,128)S(1)} %get-tuple-element.96.refs_1_), channel_id=1, source_target_pairs={{0,32},{32,0},{64,96},{96,64},{1,33},{33,1},{65,97},{97,65},{2,34}... | collective-permute-start | bytes 393224 | tf_op jit(solution)/shard_map/ppermute | solution.py:101
  4.4 1.7 %copy-start = (f32[5,32,16,256]{3,2,1,0:T(8,128)S(1)}, f32[5,32,16,256]{3,2,1,0:T(8,128)}, u32[]{:S(2)}) copy-start(f32[5,32,16,256]{3,2,1,0:T(8,128)} %refs_7_.1) | copy-start | bytes 7864324
  6.1 1.0 %copy-start.6 = (s32[16,16,512]{2,1,0:T(8,128)S(1)}, s32[16,16,512]{2,1,0:T(8,128)}, u32[]{:S(2)}) copy-start(s32[16,16,512]{2,1,0:T(8,128)} %refs_1_.1) | copy-start | bytes 1572868
  9.4 9.1 %collective-permute-start.6 = (f32[16,8,256]{2,1,0:T(8,128)S(1)}, f32[16,8,256]{2,1,0:T(8,128)S(1)}, u32[]{:S(2)}, u32[]{:S(2)}) collective-permute-start(f32[16,8,256]{2,1,0:T(8,128)S(1)} %get-tuple-element.61), channel_id=1, source_target_pairs={{0,31},{1,2},{2,1},{3,4},{4,3},{5,6},{6,5},{7,8},{8,7},{9,10},{10,... | collective-permute-start | bytes 393224 | tf_op jit(solution)/shard_map/ppermute | solution.py:101
  14.0 4.6 %collective-permute-start.2 = (f32[40,8,256]{2,1,0:T(8,128)S(1)}, f32[40,8,256]{2,1,0:T(8,128)S(1)}, u32[]{:S(2)}, u32[]{:S(2)}) collective-permute-start(f32[40,8,256]{2,1,0:T(8,128)S(1)} %get-tuple-element.54), channel_id=1, source_target_pairs={{0,1},{1,0},{2,3},{3,2},{4,5},{5,4},{6,7},{7,6},{8,9},{9,8},{10,11... | collective-permute-start | bytes 983048 | tf_op jit(solution)/shard_map/ppermute | solution.py:101
  14.0 11.2 %collective-permute-start.3 = (f32[24,8,256]{2,1,0:T(8,128)S(1)}, f32[24,8,256]{2,1,0:T(8,128)S(1)}, u32[]{:S(2)}, u32[]{:S(2)}) collective-permute-start(f32[24,8,256]{2,1,0:T(8,128)S(1)} %get-tuple-element.55), channel_id=1, source_target_pairs={{0,31},{1,2},{2,1},{3,4},{4,3},{5,6},{6,5},{7,8},{8,7},{9,10},{10,... | collective-permute-start | bytes 589832 | tf_op jit(solution)/shard_map/ppermute | solution.py:107
  15.9 10.4 %collective-permute-start.4 = (f32[15,16,256]{2,1,0:T(8,128)S(1)}, f32[15,16,256]{2,1,0:T(8,128)S(1)}, u32[]{:S(2)}, u32[]{:S(2)}) collective-permute-start(f32[15,16,256]{2,1,0:T(8,128)S(1)} %get-tuple-element.56), channel_id=1, source_target_pairs={{0,32},{32,0},{64,96},{96,64},{1,33},{33,1},{65,97},{97,65},{2,34}... | collective-permute-start | bytes 737288 | tf_op jit(solution)/shard_map/ppermute | solution.py:101
  16.6 9.7 %collective-permute-start.5 = (f32[15,16,256]{2,1,0:T(8,128)S(1)}, f32[15,16,256]{2,1,0:T(8,128)S(1)}, u32[]{:S(2)}, u32[]{:S(2)}) collective-permute-start(f32[15,16,256]{2,1,0:T(8,128)S(1)} %get-tuple-element.57), channel_id=1, source_target_pairs={{0,96},{32,64},{64,32},{96,0},{1,97},{33,65},{65,33},{97,1},{2,98}... | collective-permute-start | bytes 737288 | tf_op jit(solution)/shard_map/ppermute | solution.py:101
  18.6 7.8 %copy-start.1 = (f32[5,32,16,256]{3,2,1,0:T(8,128)S(1)}, f32[5,32,16,256]{3,2,1,0:T(8,128)}, u32[]{:S(2)}) copy-start(f32[5,32,16,256]{3,2,1,0:T(8,128)} %refs_7_.1) | copy-start | bytes 7864324
  18.6 7.8 %copy-start.3 = (bf16[2,2,256,256]{3,2,1,0:T(8,128)(2,1)S(1)}, bf16[2,2,256,256]{3,2,1,0:T(8,128)(2,1)}, u32[]{:S(2)}) copy-start(bf16[2,2,256,256]{3,2,1,0:T(8,128)(2,1)} %constant.17.clone.refs_6_.refs_11_.refs_13_.refs_9_.refs_10_) | copy-start | bytes 1572868
  18.6 7.8 %copy-start.4 = (bf16[2,2,128,224]{3,2,1,0:T(8,128)(2,1)S(1)}, bf16[2,2,128,224]{3,2,1,0:T(8,128)(2,1)}, u32[]{:S(2)}) copy-start(bf16[2,2,128,224]{3,2,1,0:T(8,128)(2,1)} %constant.16.clone.refs_5_.refs_10_.refs_12_.refs_8_.refs_9_) | copy-start | bytes 688132
  20.6 10.9 %collective-permute-start.9 = (f32[19,8,256]{2,1,0:T(8,128)S(1)}, f32[19,8,256]{2,1,0:T(8,128)S(1)}, u32[]{:S(2)}, u32[]{:S(2)}) collective-permute-start(f32[19,8,256]{2,1,0:T(8,128)S(1)} %get-tuple-element.69), channel_id=1, source_target_pairs={{0,31},{1,2},{2,1},{3,4},{4,3},{5,6},{6,5},{7,8},{8,7},{9,10},{10,... | collective-permute-start | bytes 466952 | tf_op jit(solution)/shard_map/ppermute | solution.py:101
  23.8 5.1 %collective-permute-start.7 = (f32[18,8,256]{2,1,0:T(8,128)S(1)}, f32[18,8,256]{2,1,0:T(8,128)S(1)}, u32[]{:S(2)}, u32[]{:S(2)}) collective-permute-start(f32[18,8,256]{2,1,0:T(8,128)S(1)} %get-tuple-element.67), channel_id=1, source_target_pairs={{0,32},{32,0},{64,96},{96,64},{1,33},{33,1},{65,97},{97,65},{2,34}... | collective-permute-start | bytes 442376 | tf_op jit(solution)/shard_map/ppermute | solution.py:101
  25.1 6.4 %collective-permute-start.8 = (f32[18,8,256]{2,1,0:T(8,128)S(1)}, f32[18,8,256]{2,1,0:T(8,128)S(1)}, u32[]{:S(2)}, u32[]{:S(2)}) collective-permute-start(f32[18,8,256]{2,1,0:T(8,128)S(1)} %get-tuple-element.68), channel_id=1, source_target_pairs={{0,96},{32,64},{64,32},{96,0},{1,97},{33,65},{65,33},{97,1},{2,98}... | collective-permute-start | bytes 442376 | tf_op jit(solution)/shard_map/ppermute | solution.py:101
  26.4 2.1 %collective-permute-start.10 = (f32[17,8,256]{2,1,0:T(8,128)S(1)}, f32[17,8,256]{2,1,0:T(8,128)S(1)}, u32[]{:S(2)}, u32[]{:S(2)}) collective-permute-start(f32[17,8,256]{2,1,0:T(8,128)S(1)} %get-tuple-element.70), channel_id=1, source_target_pairs={{0,1},{1,0},{2,3},{3,2},{4,5},{5,4},{6,7},{7,6},{8,9},{9,8},{10,11... | collective-permute-start | bytes 417800 | tf_op jit(solution)/shard_map/ppermute | solution.py:101
  32.0 8.0 %collective-permute-start.11 = (f32[18,8,256]{2,1,0:T(8,128)S(1)}, f32[18,8,256]{2,1,0:T(8,128)S(1)}, u32[]{:S(2)}, u32[]{:S(2)}) collective-permute-start(f32[18,8,256]{2,1,0:T(8,128)S(1)} %get-tuple-element.73), channel_id=1, source_target_pairs={{0,31},{1,2},{2,1},{3,4},{4,3},{5,6},{6,5},{7,8},{8,7},{9,10},{10,... | collective-permute-start | bytes 442376 | tf_op jit(solution)/shard_map/ppermute | solution.py:101
  32.6 7.3 %collective-permute-start.12 = (f32[18,8,256]{2,1,0:T(8,128)S(1)}, f32[18,8,256]{2,1,0:T(8,128)S(1)}, u32[]{:S(2)}, u32[]{:S(2)}) collective-permute-start(f32[18,8,256]{2,1,0:T(8,128)S(1)} %get-tuple-element.74), channel_id=1, source_target_pairs={{0,1},{1,0},{2,3},{3,2},{4,5},{5,4},{6,7},{7,6},{8,9},{9,8},{10,11... | collective-permute-start | bytes 442376 | tf_op jit(solution)/shard_map/ppermute | solution.py:101
  32.6 9.4 %collective-permute-start.13 = (f32[15,16,256]{2,1,0:T(8,128)S(1)}, f32[15,16,256]{2,1,0:T(8,128)S(1)}, u32[]{:S(2)}, u32[]{:S(2)}) collective-permute-start(f32[15,16,256]{2,1,0:T(8,128)S(1)} %get-tuple-element.76), channel_id=1, source_target_pairs={{0,32},{32,0},{64,96},{96,64},{1,33},{33,1},{65,97},{97,65},{2,34}... | collective-permute-start | bytes 737288 | tf_op jit(solution)/shard_map/ppermute | solution.py:101
  33.6 9.3 %collective-permute-start.14 = (f32[15,16,256]{2,1,0:T(8,128)S(1)}, f32[15,16,256]{2,1,0:T(8,128)S(1)}, u32[]{:S(2)}, u32[]{:S(2)}) collective-permute-start(f32[15,16,256]{2,1,0:T(8,128)S(1)} %get-tuple-element.77), channel_id=1, source_target_pairs={{0,96},{32,64},{64,32},{96,0},{1,97},{33,65},{65,33},{97,1},{2,98}... | collective-permute-start | bytes 737288 | tf_op jit(solution)/shard_map/ppermute | solution.py:101
  34.9 7.1 %collective-permute-start.15 = (f32[6,8,256]{2,1,0:T(8,128)S(1)}, f32[6,8,256]{2,1,0:T(8,128)S(1)}, u32[]{:S(2)}, u32[]{:S(2)}) collective-permute-start(f32[6,8,256]{2,1,0:T(8,128)S(1)} %get-tuple-element.78), channel_id=1, source_target_pairs={{0,31},{1,2},{2,1},{3,4},{4,3},{5,6},{6,5},{7,8},{8,7},{9,10},{10,... | collective-permute-start | bytes 147464 | tf_op jit(solution)/shard_map/ppermute | solution.py:101
  39.9 2.1 %collective-permute-start.16 = (f32[6,8,256]{2,1,0:T(8,128)S(1)}, f32[6,8,256]{2,1,0:T(8,128)S(1)}, u32[]{:S(2)}, u32[]{:S(2)}) collective-permute-start(f32[6,8,256]{2,1,0:T(8,128)S(1)} %get-tuple-element.79), channel_id=1, source_target_pairs={{0,1},{1,0},{2,3},{3,2},{4,5},{5,4},{6,7},{7,6},{8,9},{9,8},{10,11... | collective-permute-start | bytes 147464 | tf_op jit(solution)/shard_map/ppermute | solution.py:101
  41.3 8.0 %collective-permute-start.17 = (f32[18,8,256]{2,1,0:T(8,128)S(1)}, f32[18,8,256]{2,1,0:T(8,128)S(1)}, u32[]{:S(2)}, u32[]{:S(2)}) collective-permute-start(f32[18,8,256]{2,1,0:T(8,128)S(1)} %get-tuple-element.81), channel_id=1, source_target_pairs={{0,31},{1,2},{2,1},{3,4},{4,3},{5,6},{6,5},{7,8},{8,7},{9,10},{10,... | collective-permute-start | bytes 442376 | tf_op jit(solution)/shard_map/ppermute | solution.py:101
  42.0 7.3 %collective-permute-start.18 = (f32[18,8,256]{2,1,0:T(8,128)S(1)}, f32[18,8,256]{2,1,0:T(8,128)S(1)}, u32[]{:S(2)}, u32[]{:S(2)}) collective-permute-start(f32[18,8,256]{2,1,0:T(8,128)S(1)} %get-tuple-element.82), channel_id=1, source_target_pairs={{0,1},{1,0},{2,3},{3,2},{4,5},{5,4},{6,7},{7,6},{8,9},{9,8},{10,11... | collective-permute-start | bytes 442376 | tf_op jit(solution)/shard_map/ppermute | solution.py:101
  43.5 8.9 %collective-permute-start.19 = (f32[15,16,256]{2,1,0:T(8,128)S(1)}, f32[15,16,256]{2,1,0:T(8,128)S(1)}, u32[]{:S(2)}, u32[]{:S(2)}) collective-permute-start(f32[15,16,256]{2,1,0:T(8,128)S(1)} %get-tuple-element.84), channel_id=1, source_target_pairs={{0,32},{32,0},{64,96},{96,64},{1,33},{33,1},{65,97},{97,65},{2,34}... | collective-permute-start | bytes 737288 | tf_op jit(solution)/shard_map/ppermute | solution.py:101
  43.8 9.3 %collective-permute-start.20 = (f32[15,16,256]{2,1,0:T(8,128)S(1)}, f32[15,16,256]{2,1,0:T(8,128)S(1)}, u32[]{:S(2)}, u32[]{:S(2)}) collective-permute-start(f32[15,16,256]{2,1,0:T(8,128)S(1)} %get-tuple-element.85), channel_id=1, source_target_pairs={{0,96},{32,64},{64,32},{96,0},{1,97},{33,65},{65,33},{97,1},{2,98}... | collective-permute-start | bytes 737288 | tf_op jit(solution)/shard_map/ppermute | solution.py:101
  45.6 6.8 %collective-permute-start.21 = (f32[6,8,256]{2,1,0:T(8,128)S(1)}, f32[6,8,256]{2,1,0:T(8,128)S(1)}, u32[]{:S(2)}, u32[]{:S(2)}) collective-permute-start(f32[6,8,256]{2,1,0:T(8,128)S(1)} %get-tuple-element.86), channel_id=1, source_target_pairs={{0,31},{1,2},{2,1},{3,4},{4,3},{5,6},{6,5},{7,8},{8,7},{9,10},{10,... | collective-permute-start | bytes 147464 | tf_op jit(solution)/shard_map/ppermute | solution.py:101
  49.3 3.2 %collective-permute-start.22 = (f32[6,8,256]{2,1,0:T(8,128)S(1)}, f32[6,8,256]{2,1,0:T(8,128)S(1)}, u32[]{:S(2)}, u32[]{:S(2)}) collective-permute-start(f32[6,8,256]{2,1,0:T(8,128)S(1)} %get-tuple-element.87), channel_id=1, source_target_pairs={{0,1},{1,0},{2,3},{3,2},{4,5},{5,4},{6,7},{7,6},{8,9},{9,8},{10,11... | collective-permute-start | bytes 147464 | tf_op jit(solution)/shard_map/ppermute | solution.py:101
  50.6 8.0 %collective-permute-start.23 = (f32[18,8,256]{2,1,0:T(8,128)S(1)}, f32[18,8,256]{2,1,0:T(8,128)S(1)}, u32[]{:S(2)}, u32[]{:S(2)}) collective-permute-start(f32[18,8,256]{2,1,0:T(8,128)S(1)} %get-tuple-element.89), channel_id=1, source_target_pairs={{0,31},{1,2},{2,1},{3,4},{4,3},{5,6},{6,5},{7,8},{8,7},{9,10},{10,... | collective-permute-start | bytes 442376 | tf_op jit(solution)/shard_map/ppermute | solution.py:101
  52.4 6.2 %collective-permute-start.24 = (f32[18,8,256]{2,1,0:T(8,128)S(1)}, f32[18,8,256]{2,1,0:T(8,128)S(1)}, u32[]{:S(2)}, u32[]{:S(2)}) collective-permute-start(f32[18,8,256]{2,1,0:T(8,128)S(1)} %get-tuple-element.90), channel_id=1, source_target_pairs={{0,1},{1,0},{2,3},{3,2},{4,5},{5,4},{6,7},{7,6},{8,9},{9,8},{10,11... | collective-permute-start | bytes 442376 | tf_op jit(solution)/shard_map/ppermute | solution.py:101
  53.0 5.6 %copy-start.2 = (f32[5,32,16,256]{3,2,1,0:T(8,128)S(1)}, f32[5,32,16,256]{3,2,1,0:T(8,128)}, u32[]{:S(2)}) copy-start(f32[5,32,16,256]{3,2,1,0:T(8,128)} %refs_7_.1) | copy-start | bytes 7864324
  53.6 9.0 %collective-permute-start.25 = (f32[15,16,256]{2,1,0:T(8,128)S(1)}, f32[15,16,256]{2,1,0:T(8,128)S(1)}, u32[]{:S(2)}, u32[]{:S(2)}) collective-permute-start(f32[15,16,256]{2,1,0:T(8,128)S(1)} %get-tuple-element.91), channel_id=1, source_target_pairs={{0,32},{32,0},{64,96},{96,64},{1,33},{33,1},{65,97},{97,65},{2,34}... | collective-permute-start | bytes 737288 | tf_op jit(solution)/shard_map/ppermute | solution.py:101
  54.0 9.3 %collective-permute-start.26 = (f32[15,16,256]{2,1,0:T(8,128)S(1)}, f32[15,16,256]{2,1,0:T(8,128)S(1)}, u32[]{:S(2)}, u32[]{:S(2)}) collective-permute-start(f32[15,16,256]{2,1,0:T(8,128)S(1)} %get-tuple-element.92), channel_id=1, source_target_pairs={{0,96},{32,64},{64,32},{96,0},{1,97},{33,65},{65,33},{97,1},{2,98}... | collective-permute-start | bytes 737288 | tf_op jit(solution)/shard_map/ppermute | solution.py:101
  55.8 6.8 %collective-permute-start.27 = (f32[6,8,256]{2,1,0:T(8,128)S(1)}, f32[6,8,256]{2,1,0:T(8,128)S(1)}, u32[]{:S(2)}, u32[]{:S(2)}) collective-permute-start(f32[6,8,256]{2,1,0:T(8,128)S(1)} %get-tuple-element.93), channel_id=1, source_target_pairs={{0,31},{1,2},{2,1},{3,4},{4,3},{5,6},{6,5},{7,8},{8,7},{9,10},{10,... | collective-permute-start | bytes 147464 | tf_op jit(solution)/shard_map/ppermute | solution.py:101
  58.6 4.1 %collective-permute-start.28 = (f32[6,8,256]{2,1,0:T(8,128)S(1)}, f32[6,8,256]{2,1,0:T(8,128)S(1)}, u32[]{:S(2)}, u32[]{:S(2)}) collective-permute-start(f32[6,8,256]{2,1,0:T(8,128)S(1)} %get-tuple-element.94), channel_id=1, source_target_pairs={{0,1},{1,0},{2,3},{3,2},{4,5},{5,4},{6,7},{7,6},{8,9},{9,8},{10,11... | collective-permute-start | bytes 147464 | tf_op jit(solution)/shard_map/ppermute | solution.py:101
